TPU v7x, 1024 devices: a whole 4x4x32 slice. The times are simulated.
1024 devices in a mesh: dp: 64 (over y, z_lo, core), tensor: 16 (over z_hi, x).
Axes of the slice: x: 4, y: 4, z: 32 (z_hi: 4, z_lo: 8; z = z_hi * 8 + z_lo), core: 2. Of those that a mesh axis runs over, the one named last changes fastest.
Arguments:
- pre_act: bfloat16 [16384, 6912], P('dp', 'tensor'), may hold values from -6 to 6
- weight_out: bfloat16 [2560, 6912], P('dp', 'tensor'), may hold values from -0.21875 to 0.21875
- cotangent: bfloat16 [16384, 2560], P('dp'), may hold values from -16 to 16
Outputs:
- output: bfloat16 [16384, 2560], P('dp', 'tensor')
- grad_pre: bfloat16 [16384, 6912], P('dp', 'tensor')
- grad_weight: float32 [2560, 6912], P('dp', 'tensor')
All inputs are finite; a program needn't handle non-finite values.
Results may differ from a plain program's by a relative error of at most 0.018.
Values may be sent and summed in bfloat16 or wider, within the bound.
No kernel may reach another device: no remote copies, remote signals or barrier semaphores. Data moves between devices by JAX's collectives and lax.ppermute only.
A program may use at most 32 MiB of HBM per device.

v0:
```python
import math

import jax
import jax.numpy as jnp
from jax import lax
from jax.sharding import PartitionSpec as P


def gelu_value(values):
    inner = math.sqrt(2.0 / math.pi) * (values + 0.044715 * values * values * values)
    return 0.5 * values * (1.0 + jnp.tanh(inner))


def gelu_slope(values):
    coeff = math.sqrt(2.0 / math.pi)
    tangent = jnp.tanh(coeff * (values + 0.044715 * values * values * values))
    return 0.5 * (1.0 + tangent) + 0.5 * values * (1.0 - tangent * tangent) * coeff * (
        1.0 + 3.0 * 0.044715 * values * values
    )


def local(pre_act, weight_out, cotangent):
    scaled = pre_act.astype(jnp.float32)
    hidden = gelu_value(scaled).astype(jnp.bfloat16)
    tok_rows = cotangent.shape[0]
    groups = lax.axis_size("dp")
    factor = 1.0 / math.sqrt(tok_rows * groups)
    contract_rows = (((0,), (0,)), ((), ()))
    contract_last = (((1,), (1,)), ((), ()))
    full_weight = lax.all_gather(weight_out, "dp", axis=0, tiled=True)
    partial_value = lax.dot_general(
        hidden, full_weight, contract_last, preferred_element_type=jnp.float32
    )
    grad_hidden = jnp.dot(cotangent, full_weight, preferred_element_type=jnp.float32)
    partial_out = partial_value.astype(jnp.bfloat16)
    term = lax.dot_general(cotangent, hidden, contract_rows, preferred_element_type=jnp.float32)
    grad_weight = lax.psum_scatter(term, "dp", scatter_dimension=0, tiled=True) * factor
    summed = lax.psum_scatter(
        partial_out.astype(jnp.float32).astype(jnp.bfloat16),
        "tensor",
        scatter_dimension=1,
        tiled=True,
    )
    grad_pre = (grad_hidden * gelu_slope(scaled)).astype(jnp.bfloat16)
    return (summed, grad_pre, grad_weight)


def solution(mesh):
    placed = (P("dp", "tensor"), P("dp", "tensor"), P("dp", None))
    return jax.shard_map(
        local,
        mesh=mesh,
        in_specs=placed,
        out_specs=(P("dp", "tensor"), P("dp", "tensor"), P("dp", "tensor")),
        check_vma=False,
    )
```

profile of v0, /device:TPU:1, one launch (start us, length us, event | category | flops | bytes accessed | tf_op | source)
XLA Modules:
  0.0 801.5 jit_solution(14918065735891667869)
XLA Ops:
  7.2 0.0 copy-start
  7.2 0.0 all-gather.2.cloned.1.call-start
  7.2 0.7 all-gather.2.cloned.1.call-update
  7.9 0.0 reduce-scatter.7.cloned.1.call-start
  8.0 0.5 copy-done
  8.5 3.8 convolution_bitcast_fusion
  12.3 5.7 copy.8
  18.0 0.0 copy-start.1
  18.0 0.0 reduce-scatter.7.cloned.1.call-update
  18.0 0.0 reduce-scatter.5.cloned.1.call-start
  18.1 133.3 %all-gather.2.cloned.1.call-done = bf16[2560,432]{1,0:T(8,128)(2,1)} async-done(((bf16[40,432]{1,0:T(8,128)(2,1)}), bf16[2560,432]{1,0:T(8,128)(2,1)}) %all-gather.2.cloned.1.call-update) | async-done | bytes 2211856 | tf_op jit(solution)/shard_map/all_gather | solution.py:30
  151.4 0.0 copy-done.1
  151.4 3.8 convolution_convert_fusion
  155.2 0.0 reduce-scatter.5.cloned.1.call-update
  155.2 3.6 fusion
  158.9 440.4 %reduce-scatter.7.cloned.1.call-done = f32[40,432]{1,0:T(8,128)} async-done(((f32[2560,432]{1,0:T(8,128)}), f32[40,432]{1,0:T(8,128)}) %reduce-scatter.7.cloned.1.call-update) | async-done | bytes 69136
  599.3 1.0 copy.9
  600.4 0.7 copy.7
  601.1 193.9 %reduce-scatter.5.cloned.1.call-done = bf16[256,160]{0,1:T(8,128)(2,1)} async-done(((bf16[256,2560]{0,1:T(8,128)(2,1)}), bf16[256,160]{0,1:T(8,128)(2,1)}) %reduce-scatter.5.cloned.1.call-update) | async-done | bytes 81936 | tf_op jit(solution)/shard_map/reduce_scatter | solution.py:38
  (1 shorter events, 0.0 us)
Async XLA Ops:
  7.2 1.3 copy-start
  7.2 144.2 %all-gather.2.cloned.1.call-start = ((), (), s32[]{:S(2)}) async-start(), calls=%async_computation.2 | async-start | bytes 2662400 | tf_op jit(solution)/shard_map/all_gather | solution.py:30
  7.9 591.4 %reduce-scatter.7.cloned.1.call-start = ((), (), s32[]{:S(2)}) async-start(), calls=%async_computation.4 | async-start | bytes 5324800
  18.0 133.4 %copy-start.1 = (bf16[256,432]{0,1:T(8,128)(2,1)S(1)}, bf16[256,432]{0,1:T(8,128)(2,1)}, u32[]{:S(2)}) copy-start(bf16[256,432]{0,1:T(8,128)(2,1)} %param.3) | copy-start | bytes 663556
  18.0 777.0 %reduce-scatter.5.cloned.1.call-start = ((), (), s32[]{:S(2)}) async-start(), calls=%async_computation.3 | async-start | bytes 1392640 | tf_op jit(solution)/shard_map/reduce_scatter | solution.py:38
Sparse Core Ops, SparseCore 0:
  10.7 140.6 all-gather.1
  154.8 444.4 reduce-scatter.6
  605.1 189.8 reduce-scatter.4
where the time goes:
time: 802 us
  waiting for transfers between devices  768 us (96%)
  between operations  13.8 us (2%)
  matrix products  11.3 us (1%)
    unnamed x4, waiting for transfers between devices  441 us
    reduce_scatter x1, waiting for transfers between devices, local(): lax.psum_scatter(partial_out.astype(jnp.float32).astype(jnp.bfloat16), 't...  194 us
    all_gather x1, waiting for transfers between devices, local(): full_weight = lax.all_gather(weight_out, 'dp', axis=0, tiled=True)  133 us
  transfers between devices with their start and end apart: 3, of which 3 were waited for; matrix products, arithmetic and copies ran while one was open for 2% of the time, Pallas kernels for 0%

commit v1 on v0

v1 whole, which is shorter than its diff:
```python
import math

import jax
import jax.numpy as jnp
import numpy as np
from jax import lax
from jax.sharding import Mesh, PartitionSpec as P

COEFF = math.sqrt(2.0 / math.pi)
AXES = ("y", "zl", "c", "zh", "x")
SIZES = (4, 8, 2, 4, 4)


def gelu_value(values):
    inner = COEFF * (values + 0.044715 * values * values * values)
    return 0.5 * values * (1.0 + jnp.tanh(inner))


def gelu_slope(values):
    tangent = jnp.tanh(COEFF * (values + 0.044715 * values * values * values))
    return 0.5 * (1.0 + tangent) + 0.5 * values * (1.0 - tangent * tangent) * COEFF * (
        1.0 + 3.0 * 0.044715 * values * values
    )


def swap(value, axis, distance):
    size = lax.axis_size(axis)
    return lax.ppermute(value, axis, [(i, i ^ distance) for i in range(size)])


def shift(value, axis, distance):
    size = lax.axis_size(axis)
    return lax.ppermute(value, axis, [(i, (i + distance) % size) for i in range(size)])


def dot(left, right, dims):
    return lax.dot_general(left, right, (dims, ((), ())), preferred_element_type=jnp.float32)


def selector(core, width, block):
    rows = lax.broadcasted_iota(jnp.int32, (2 * width, width), 0)
    cols = lax.broadcasted_iota(jnp.int32, (2 * width, width), 1)
    return (rows == cols // block * (2 * block) + core * block + cols % block).astype(jnp.bfloat16)


def local(pre_act, weight_out, cotangent):
    n_y, n_zl, n_x = lax.axis_size("y"), lax.axis_size("zl"), lax.axis_size("x")
    tokens, hid = pre_act.shape
    block = weight_out.shape[0]
    stripe = n_zl * block
    core, y, zl = lax.axis_index("c"), lax.axis_index("y"), lax.axis_index("zl")
    factor = 1.0 / math.sqrt(tokens * n_y * n_zl * 2)

    rows = weight_out[None]
    distance = n_zl // 2
    while distance:
        other = swap(rows, "zl", distance)
        low = (zl & distance) == 0
        first, second = jnp.where(low, rows, other), jnp.where(low, other, rows)
        rows = jnp.stack([first, second], axis=1).reshape(-1, block, hid)
        distance //= 2
    own = rows.reshape(n_x, stripe // n_x, hid)
    pieces = [own] + [shift(own, "y", -k) for k in range(1, n_y)]
    pieces = jnp.stack(pieces + pieces[:-1], axis=0)
    weight = lax.dynamic_slice_in_dim(pieces, (n_y - y) % n_y, n_y, axis=0)

    mine, theirs = [], []
    for index in range(n_y):
        part = cotangent[:, index * 2 * stripe : (index + 1) * 2 * stripe]
        mine.append(dot(part, selector(core, stripe, block), ((1,), (0,))).astype(jnp.bfloat16))
        theirs.append(dot(part, selector(1 - core, stripe, block), ((1,), (0,))).astype(jnp.bfloat16))
    mine, theirs = jnp.concatenate(mine, axis=1), jnp.concatenate(theirs, axis=1)
    pre_both = jnp.concatenate([pre_act, swap(pre_act, "c", 1)], axis=0)
    cot_both = jnp.concatenate([mine, swap(theirs, "c", 1)], axis=0)
    hidden = gelu_value(pre_both.astype(jnp.float32)).astype(jnp.bfloat16)

    term = dot(cot_both, hidden, ((0,), (0,))).astype(jnp.bfloat16)
    term = lax.all_to_all(term.reshape(n_y, stripe, hid), "y", 0, 0)
    term = jnp.sum(term.astype(jnp.float32), axis=0).astype(jnp.bfloat16)
    term = lax.all_to_all(term.reshape(n_zl, block, hid), "zl", 0, 0)
    grad_weight = jnp.sum(term.astype(jnp.float32), axis=0) * factor

    by_x = jnp.swapaxes(weight, 0, 1).reshape(n_y * stripe, hid)
    partial = dot(by_x, hidden, ((1,), (1,))).astype(jnp.bfloat16)
    partial = lax.all_to_all(partial.reshape(n_x, n_y * stripe // n_x, 2 * tokens), "x", 0, 0)
    partial = jnp.sum(partial.astype(jnp.float32), axis=0).astype(jnp.bfloat16)
    partial = lax.all_to_all(partial.reshape(n_y, stripe // n_x, 2 * tokens), "zh", 0, 0)
    summed = jnp.sum(partial.astype(jnp.float32), axis=0).astype(jnp.bfloat16)
    kept, given = summed[:, :tokens], swap(summed[:, tokens:], "c", 1)
    kept, given = kept.reshape(-1, 1, block, tokens), given.reshape(-1, 1, block, tokens)
    first, second = jnp.where(core == 0, kept, given), jnp.where(core == 0, given, kept)
    output = jnp.concatenate([first, second], axis=1).reshape(-1, tokens).T

    half = dot(cot_both, weight.reshape(-1, hid), ((1,), (0,)))
    grad_hidden = half[:tokens] + swap(half[tokens:], "c", 1)
    grad_pre = (grad_hidden * gelu_slope(pre_act.astype(jnp.float32))).astype(jnp.bfloat16)
    return (output, grad_pre, grad_weight)


def solution(mesh):
    fine = Mesh(np.asarray(mesh.devices).reshape(SIZES), AXES)
    dp, tensor = AXES[:3], AXES[3:]
    return jax.shard_map(
        local,
        mesh=fine,
        in_specs=(P(dp, tensor), P(dp, tensor), P(dp, None)),
        out_specs=(P(dp, tensor), P(dp, tensor), P(dp, tensor)),
        check_vma=False,
    )
```

time: 802 us -> 198 us (0.25)
  the two profiles are of different devices: /device:TPU:1 before, /device:TPU:97 now
where the time goes in v1:
time: 198 us; the launch traced here: 197 us
  starting transfers between devices  86 us (43%)
  waiting for transfers between devices  83.6 us (42%)
  matrix products  11.6 us (6%)
  local copies, waits for them, and re-layouts  10.5 us (5%)
  other arithmetic  4.02 us (2%)
    ppermute x7, starting transfers between devices, swap(): return lax.ppermute(value, axis, [(i, i ^ distance) for i in range(size)])  40.9 us
    all_to_all x1, waiting for transfers between devices, local(): lax.all_to_all(partial.reshape(n_y, stripe // n_x, 2 * tokens), 'zh', 0, 0)  23.6 us
    all_to_all x1, starting transfers between devices, local(): lax.all_to_all(partial.reshape(n_y, stripe // n_x, 2 * tokens), 'zh', 0, 0)  21.3 us
    all_to_all x1, waiting for transfers between devices, local(): lax.all_to_all(partial.reshape(n_x, n_y * stripe // n_x, 2 * tokens), 'x'...  15.3 us
    all_to_all x1, waiting for transfers between devices, local(): term = lax.all_to_all(term.reshape(n_zl, block, hid), 'zl', 0, 0)  13 us
    ppermute x3, waiting for transfers between devices, shift(): lax.ppermute(value, axis, [(i, (i + distance) % size) for i in range(size)])  12.9 us
    all_to_all x1, waiting for transfers between devices, local(): term = lax.all_to_all(term.reshape(n_y, stripe, hid), 'y', 0, 0)  12.3 us
    dot_general x11, matrix products, dot(): lax.dot_general(left, right, (dims, ((), ())), preferred_element_type=jnp...  11.6 us
  transfers between devices with their start and end apart: 14, of which 10 were waited for; matrix products, arithmetic and copies ran while one was open for 12% of the time, Pallas kernels for 0%

profile of v1, /device:TPU:97, one launch (start us, length us, event | category | flops | bytes accessed | tf_op | source)
XLA Modules:
  0.0 196.8 jit_solution(2084527127292667788)
XLA Ops:
  0.6 8.8 %collective-permute-start = (bf16[1,40,432]{2,1,0:T(8,128)(2,1)}, bf16[1,40,432]{2,1,0:T(8,128)(2,1)S(1)}, u32[]{:S(2)}, u32[]{:S(2)}) collective-permute-start(bf16[1,40,432]{2,1,0:T(8,128)(2,1)} %bitcast.79), channel_id=1, source_target_pairs={{0,128},{32,160},{64,192},{96,224},{128,0},{160,32},{192,64},{224,... | collective-permute-start | bytes 103688 | tf_op jit(solution)/shard_map/ppermute | solution.py:28
  9.5 1.4 fusion.4
  11.3 0.3 fusion.6
  11.7 0.3 fusion.7
  12.1 3.0 %collective-permute-start.8 = (bf16[256,1280]{0,1:T(8,128)(2,1)S(1)}, bf16[256,1280]{0,1:T(8,128)(2,1)S(1)}, u32[]{:S(2)}, u32[]{:S(2)}) collective-permute-start(bf16[256,1280]{0,1:T(8,128)(2,1)S(1)} %pad_maximum_fusion.1), channel_id=1, source_target_pairs={{0,16},{16,0},{1,17},{17,1},{2,18},{18,2},{3,19},{19,3},{4,20},{20... | collective-permute-start | bytes 1966088 | tf_op jit(solution)/shard_map/ppermute | solution.py:28
  15.1 1.9 collective-permute-start.6
  17.0 1.3 fusion
  18.5 1.9 collective-permute-start.1
  20.4 1.3 fusion.1
  21.7 2.8 %collective-permute-done.1 = bf16[2,40,432]{2,1,0:T(8,128)(2,1)S(1)} collective-permute-done((bf16[2,40,432]{2,1,0:T(8,128)(2,1)S(1)}, bf16[2,40,432]{2,1,0:T(8,128)(2,1)S(1)}, u32[]{:S(2)}, u32[]{:S(2)}) %collective-permute-start.1) | collective-permute-done | bytes 69152 | tf_op jit(solution)/shard_map/ppermute | solution.py:28
  24.6 4.8 %collective-permute-start.2 = (bf16[4,40,432]{2,1,0:T(8,128)(2,1)S(1)}, bf16[4,40,432]{2,1,0:T(8,128)(2,1)S(1)}, u32[]{:S(2)}, u32[]{:S(2)}) collective-permute-start(bf16[4,40,432]{2,1,0:T(8,128)(2,1)S(1)} %bitcast.75), channel_id=1, source_target_pairs={{0,32},{32,0},{64,96},{96,64},{128,160},{160,128},{192,224},{224,1... | collective-permute-start | bytes 414728 | tf_op jit(solution)/shard_map/ppermute | solution.py:28
  29.4 1.3 fusion.2
  30.7 2.2 %collective-permute-done.2 = bf16[4,40,432]{2,1,0:T(8,128)(2,1)S(1)} collective-permute-done((bf16[4,40,432]{2,1,0:T(8,128)(2,1)S(1)}, bf16[4,40,432]{2,1,0:T(8,128)(2,1)S(1)}, u32[]{:S(2)}, u32[]{:S(2)}) %collective-permute-start.2) | collective-permute-done | bytes 138272 | tf_op jit(solution)/shard_map/ppermute | solution.py:28
  33.0 5.9 %collective-permute-start.3 = (bf16[4,80,432]{2,1,0:T(8,128)(2,1)S(1)}, bf16[4,80,432]{2,1,0:T(8,128)(2,1)S(1)}, u32[]{:S(2)}, u32[]{:S(2)}) collective-permute-start(bf16[4,80,432]{2,1,0:T(8,128)(2,1)S(1)} %bitcast.67), channel_id=1, source_target_pairs={{0,768},{256,0},{512,256},{768,512},{1,769},{257,1},{513,257},{769... | collective-permute-start | bytes 829448 | tf_op jit(solution)/shard_map/ppermute | solution.py:33
  38.9 1.3 fusion.3
  40.2 2.3 %collective-permute-start.4 = (bf16[4,80,432]{2,1,0:T(8,128)(2,1)S(1)}, bf16[4,80,432]{2,1,0:T(8,128)(2,1)S(1)}, u32[]{:S(2)}, u32[]{:S(2)}) collective-permute-start(bf16[4,80,432]{2,1,0:T(8,128)(2,1)S(1)} %bitcast.68), channel_id=1, source_target_pairs={{0,512},{256,768},{512,0},{768,256},{1,513},{257,769},{513,1},{769... | collective-permute-start | bytes 829448 | tf_op jit(solution)/shard_map/ppermute | solution.py:33
  42.5 2.6 %collective-permute-start.5 = (bf16[4,80,432]{2,1,0:T(8,128)(2,1)S(1)}, bf16[4,80,432]{2,1,0:T(8,128)(2,1)S(1)}, u32[]{:S(2)}, u32[]{:S(2)}) collective-permute-start(bf16[4,80,432]{2,1,0:T(8,128)(2,1)S(1)} %bitcast.69), channel_id=1, source_target_pairs={{0,256},{256,512},{512,768},{768,0},{1,257},{257,513},{513,769},{7... | collective-permute-start | bytes 829448 | tf_op jit(solution)/shard_map/ppermute | solution.py:33
  45.1 0.8 constant_dynamic-update-slice_fusion.1
  45.9 0.8 bitcast_dynamic-update-slice_fusion.3
  46.6 4.6 %collective-permute-done.4 = bf16[4,80,432]{2,1,0:T(8,128)(2,1)S(1)} collective-permute-done((bf16[4,80,432]{2,1,0:T(8,128)(2,1)S(1)}, bf16[4,80,432]{2,1,0:T(8,128)(2,1)S(1)}, u32[]{:S(2)}, u32[]{:S(2)}) %collective-permute-start.4) | collective-permute-done | bytes 276512 | tf_op jit(solution)/shard_map/ppermute | solution.py:33
  51.3 0.7 bitcast_dynamic-update-slice_fusion.1
  52.0 8.3 %collective-permute-done.5 = bf16[4,80,432]{2,1,0:T(8,128)(2,1)S(1)} collective-permute-done((bf16[4,80,432]{2,1,0:T(8,128)(2,1)S(1)}, bf16[4,80,432]{2,1,0:T(8,128)(2,1)S(1)}, u32[]{:S(2)}, u32[]{:S(2)}) %collective-permute-start.5) | collective-permute-done | bytes 276512 | tf_op jit(solution)/shard_map/ppermute | solution.py:33
  60.3 0.8 bitcast_dynamic-update-slice_fusion
  61.1 0.8 constant_dynamic-update-slice_fusion
  61.8 0.9 convolution_convert_fusion.1
  62.8 1.5 copy.31
  64.3 3.5 %all-to-all-start.2 = ((bf16[4,320,432]{2,1,0:T(8,128)(2,1)}), bf16[4,320,432]{2,1,0:T(8,128)(2,1)S(1)}, u32[]{:S(2)}, u32[]{:S(2)}) async-start(bf16[4,320,432]{2,1,0:T(8,128)(2,1)} %bitcast.32), calls=%async_computation.2 | async-start | bytes 2621440 | tf_op jit(solution)/shard_map/all_to_all | solution.py:78
  67.8 0.8 bitcast_dynamic-update-slice_fusion.4
  68.6 0.7 bitcast_dynamic-update-slice_fusion.2
  69.3 1.4 fusion.53
  70.9 2.1 %convolution_convert_fusion = bf16[1280,512]{1,0:T(8,128)(2,1)} fusion(bf16[1280,432]{1,0:T(8,128)(2,1)S(1)} %bitcast.73, bf16[256,432]{0,1:T(8,128)(2,1)S(1)} %collective-permute-done.6, bf16[256,432]{0,1:T(8,128)(2,1)S(1)} %copy-done), kind=kOutput, calls=%fused_computation | convolution fusion | flops 569761792 | bytes 2859008 | tf_op jit(solution)/shard_map/dot_general | solution.py:37
  72.9 12.3 %all-to-all-done.2 = bf16[4,320,432]{2,1,0:T(8,128)(2,1)S(1)} async-done(((bf16[4,320,432]{2,1,0:T(8,128)(2,1)}), bf16[4,320,432]{2,1,0:T(8,128)(2,1)S(1)}, u32[]{:S(2)}, u32[]{:S(2)}) %all-to-all-start.2) | async-done | bytes 1105952 | tf_op jit(solution)/shard_map/all_to_all | solution.py:78
  85.3 4.0 %all-to-all-start = ((bf16[4,320,512]{2,1,0:T(8,128)(2,1)}), bf16[4,320,512]{2,1,0:T(8,128)(2,1)S(1)}, u32[]{:S(2)}, u32[]{:S(2)}) async-start(bf16[4,320,512]{2,1,0:T(8,128)(2,1)} %bitcast.72), calls=%async_computation | async-start | bytes 2621440 | tf_op jit(solution)/shard_map/all_to_all | solution.py:85
  89.3 1.1 reduce_sum.47
  90.3 15.3 %all-to-all-done = bf16[4,320,512]{2,1,0:T(8,128)(2,1)S(1)} async-done(((bf16[4,320,512]{2,1,0:T(8,128)(2,1)}), bf16[4,320,512]{2,1,0:T(8,128)(2,1)S(1)}, u32[]{:S(2)}, u32[]{:S(2)}) %all-to-all-start) | async-done | bytes 1310752 | tf_op jit(solution)/shard_map/all_to_all | solution.py:85
  105.6 5.4 %all-to-all-start.3 = ((bf16[8,40,432]{2,1,0:T(8,128)(2,1)}), bf16[8,40,432]{2,1,0:T(8,128)(2,1)S(1)}, u32[]{:S(2)}, u32[]{:S(2)}) async-start(bf16[8,40,432]{2,1,0:T(8,128)(2,1)} %bitcast.33), calls=%async_computation.3 | async-start | bytes 655360 | tf_op jit(solution)/shard_map/all_to_all | solution.py:80
  111.1 1.0 reduce_sum.45
  112.0 13.0 %all-to-all-done.3 = bf16[8,40,432]{2,1,0:T(8,128)(2,1)S(1)} async-done(((bf16[8,40,432]{2,1,0:T(8,128)(2,1)}), bf16[8,40,432]{2,1,0:T(8,128)(2,1)S(1)}, u32[]{:S(2)}, u32[]{:S(2)}) %all-to-all-start.3) | async-done | bytes 276512 | tf_op jit(solution)/shard_map/all_to_all | solution.py:80
  125.0 21.3 %all-to-all-start.1 = ((bf16[4,80,512]{2,1,0:T(8,128)(2,1)}), bf16[4,80,512]{2,1,0:T(8,128)(2,1)S(1)}, u32[]{:S(2)}, u32[]{:S(2)}) async-start(bf16[4,80,512]{2,1,0:T(8,128)(2,1)} %bitcast.18), calls=%async_computation.1 | async-start | bytes 655360 | tf_op jit(solution)/shard_map/all_to_all | solution.py:87
  146.3 1.5 constant_dynamic-slice_fusion
  147.8 0.8 fusion.48
  148.6 6.1 %collective-permute-start.9 = (f32[256,432]{0,1:T(8,128)S(1)}, f32[256,432]{0,1:T(8,128)S(1)}, u32[]{:S(2)}, u32[]{:S(2)}) collective-permute-start(f32[256,432]{0,1:T(8,128)S(1)} %slice.35), channel_id=1, source_target_pairs={{0,16},{16,0},{1,17},{17,1},{2,18},{18,2},{3,19},{19,3},{4,20},{20... | collective-permute-start | bytes 1327112 | tf_op jit(solution)/shard_map/ppermute | solution.py:28
  154.7 1.4 collective-permute-done.9
  156.1 1.0 fusion.24
  157.2 23.6 %all-to-all-done.1 = bf16[4,80,512]{2,1,0:T(8,128)(2,1)S(1)} async-done(((bf16[4,80,512]{2,1,0:T(8,128)(2,1)}), bf16[4,80,512]{2,1,0:T(8,128)(2,1)S(1)}, u32[]{:S(2)}, u32[]{:S(2)}) %all-to-all-start.1) | async-done | bytes 327712 | tf_op jit(solution)/shard_map/all_to_all | solution.py:87
  180.8 14.4 %collective-permute-start.7 = (bf16[80,256]{1,0:T(8,128)(2,1)S(1)}, bf16[80,256]{1,0:T(8,128)(2,1)S(1)}, u32[]{:S(2)}, u32[]{:S(2)}) collective-permute-start(bf16[80,256]{1,0:T(8,128)(2,1)S(1)} %slice.33), channel_id=1, source_target_pairs={{0,16},{16,0},{1,17},{17,1},{2,18},{18,2},{3,19},{19,3},{4,20},{20... | collective-permute-start | bytes 122888 | tf_op jit(solution)/shard_map/ppermute | solution.py:28
  195.2 0.6 broadcast_multiply_fusion
  196.1 0.6 copy.27
  (46 shorter events, 1.1 us)
Async XLA Ops:
  0.6 17.8 %collective-permute-start = (bf16[1,40,432]{2,1,0:T(8,128)(2,1)}, bf16[1,40,432]{2,1,0:T(8,128)(2,1)S(1)}, u32[]{:S(2)}, u32[]{:S(2)}) collective-permute-start(bf16[1,40,432]{2,1,0:T(8,128)(2,1)} %bitcast.79), channel_id=1, source_target_pairs={{0,128},{32,160},{64,192},{96,224},{128,0},{160,32},{192,64},{224,... | collective-permute-start | bytes 103688 | tf_op jit(solution)/shard_map/ppermute | solution.py:28
  9.5 1.4 copy-start.2
  12.0 3.1 %copy-start = (bf16[256,432]{0,1:T(8,128)(2,1)S(1)}, bf16[256,432]{0,1:T(8,128)(2,1)}, u32[]{:S(2)}) copy-start(bf16[256,432]{0,1:T(8,128)(2,1)} %param.3) | copy-start | bytes 663556
  12.1 49.7 %collective-permute-start.8 = (bf16[256,1280]{0,1:T(8,128)(2,1)S(1)}, bf16[256,1280]{0,1:T(8,128)(2,1)S(1)}, u32[]{:S(2)}, u32[]{:S(2)}) collective-permute-start(bf16[256,1280]{0,1:T(8,128)(2,1)S(1)} %pad_maximum_fusion.1), channel_id=1, source_target_pairs={{0,16},{16,0},{1,17},{17,1},{2,18},{18,2},{3,19},{19,3},{4,20},{20... | collective-permute-start | bytes 1966088 | tf_op jit(solution)/shard_map/ppermute | solution.py:28
  15.1 46.7 %collective-permute-start.6 = (bf16[256,432]{0,1:T(8,128)(2,1)S(1)}, bf16[256,432]{0,1:T(8,128)(2,1)S(1)}, u32[]{:S(2)}, u32[]{:S(2)}) collective-permute-start(bf16[256,432]{0,1:T(8,128)(2,1)S(1)} %copy-done), channel_id=1, source_target_pairs={{0,16},{16,0},{1,17},{17,1},{2,18},{18,2},{3,19},{19,3},{4,20},{20... | collective-permute-start | bytes 663560 | tf_op jit(solution)/shard_map/ppermute | solution.py:28
  17.0 1.4 copy-start.1
  18.4 43.4 %copy-start.3 = (bf16[256,320]{0,1:T(8,128)(2,1)}, bf16[256,320]{0,1:T(8,128)(2,1)S(1)}, u32[]{:S(2)}) copy-start(bf16[256,320]{0,1:T(8,128)(2,1)S(1)} %fusion) | copy-start | bytes 491524
  18.5 6.1 %collective-permute-start.1 = (bf16[2,40,432]{2,1,0:T(8,128)(2,1)S(1)}, bf16[2,40,432]{2,1,0:T(8,128)(2,1)S(1)}, u32[]{:S(2)}, u32[]{:S(2)}) collective-permute-start(bf16[2,40,432]{2,1,0:T(8,128)(2,1)S(1)} %maximum_bitcast_fusion), channel_id=1, source_target_pairs={{0,64},{32,96},{64,0},{96,32},{128,192},{160,224},{192,128},{224,1... | collective-permute-start | bytes 207368 | tf_op jit(solution)/shard_map/ppermute | solution.py:28
  21.7 40.1 %copy-start.5 = (bf16[256,320]{0,1:T(8,128)(2,1)}, bf16[256,320]{0,1:T(8,128)(2,1)S(1)}, u32[]{:S(2)}) copy-start(bf16[256,320]{0,1:T(8,128)(2,1)S(1)} %fusion.1) | copy-start | bytes 491524
  24.6 8.3 %collective-permute-start.2 = (bf16[4,40,432]{2,1,0:T(8,128)(2,1)S(1)}, bf16[4,40,432]{2,1,0:T(8,128)(2,1)S(1)}, u32[]{:S(2)}, u32[]{:S(2)}) collective-permute-start(bf16[4,40,432]{2,1,0:T(8,128)(2,1)S(1)} %bitcast.75), channel_id=1, source_target_pairs={{0,32},{32,0},{64,96},{96,64},{128,160},{160,128},{192,224},{224,1... | collective-permute-start | bytes 414728 | tf_op jit(solution)/shard_map/ppermute | solution.py:28
  30.7 31.1 %copy-start.7 = (bf16[256,320]{0,1:T(8,128)(2,1)}, bf16[256,320]{0,1:T(8,128)(2,1)S(1)}, u32[]{:S(2)}) copy-start(bf16[256,320]{0,1:T(8,128)(2,1)S(1)} %fusion.2) | copy-start | bytes 491524
  33.0 12.9 %collective-permute-start.3 = (bf16[4,80,432]{2,1,0:T(8,128)(2,1)S(1)}, bf16[4,80,432]{2,1,0:T(8,128)(2,1)S(1)}, u32[]{:S(2)}, u32[]{:S(2)}) collective-permute-start(bf16[4,80,432]{2,1,0:T(8,128)(2,1)S(1)} %bitcast.67), channel_id=1, source_target_pairs={{0,768},{256,0},{512,256},{768,512},{1,769},{257,1},{513,257},{769... | collective-permute-start | bytes 829448 | tf_op jit(solution)/shard_map/ppermute | solution.py:33
  40.2 21.6 %copy-start.9 = (bf16[256,320]{0,1:T(8,128)(2,1)}, bf16[256,320]{0,1:T(8,128)(2,1)S(1)}, u32[]{:S(2)}) copy-start(bf16[256,320]{0,1:T(8,128)(2,1)S(1)} %fusion.3) | copy-start | bytes 491524
  40.2 11.0 %collective-permute-start.4 = (bf16[4,80,432]{2,1,0:T(8,128)(2,1)S(1)}, bf16[4,80,432]{2,1,0:T(8,128)(2,1)S(1)}, u32[]{:S(2)}, u32[]{:S(2)}) collective-permute-start(bf16[4,80,432]{2,1,0:T(8,128)(2,1)S(1)} %bitcast.68), channel_id=1, source_target_pairs={{0,512},{256,768},{512,0},{768,256},{1,513},{257,769},{513,1},{769... | collective-permute-start | bytes 829448 | tf_op jit(solution)/shard_map/ppermute | solution.py:33
  42.5 17.8 %collective-permute-start.5 = (bf16[4,80,432]{2,1,0:T(8,128)(2,1)S(1)}, bf16[4,80,432]{2,1,0:T(8,128)(2,1)S(1)}, u32[]{:S(2)}, u32[]{:S(2)}) collective-permute-start(bf16[4,80,432]{2,1,0:T(8,128)(2,1)S(1)} %bitcast.69), channel_id=1, source_target_pairs={{0,256},{256,512},{512,768},{768,0},{1,257},{257,513},{513,769},{7... | collective-permute-start | bytes 829448 | tf_op jit(solution)/shard_map/ppermute | solution.py:33
  64.3 21.0 %all-to-all-start.2 = ((bf16[4,320,432]{2,1,0:T(8,128)(2,1)}), bf16[4,320,432]{2,1,0:T(8,128)(2,1)S(1)}, u32[]{:S(2)}, u32[]{:S(2)}) async-start(bf16[4,320,432]{2,1,0:T(8,128)(2,1)} %bitcast.32), calls=%async_computation.2 | async-start | bytes 2621440 | tf_op jit(solution)/shard_map/all_to_all | solution.py:78
  85.3 20.3 %all-to-all-start = ((bf16[4,320,512]{2,1,0:T(8,128)(2,1)}), bf16[4,320,512]{2,1,0:T(8,128)(2,1)S(1)}, u32[]{:S(2)}, u32[]{:S(2)}) async-start(bf16[4,320,512]{2,1,0:T(8,128)(2,1)} %bitcast.72), calls=%async_computation | async-start | bytes 2621440 | tf_op jit(solution)/shard_map/all_to_all | solution.py:85
  105.6 19.4 %all-to-all-start.3 = ((bf16[8,40,432]{2,1,0:T(8,128)(2,1)}), bf16[8,40,432]{2,1,0:T(8,128)(2,1)S(1)}, u32[]{:S(2)}, u32[]{:S(2)}) async-start(bf16[8,40,432]{2,1,0:T(8,128)(2,1)} %bitcast.33), calls=%async_computation.3 | async-start | bytes 655360 | tf_op jit(solution)/shard_map/all_to_all | solution.py:80
  125.0 55.7 %all-to-all-start.1 = ((bf16[4,80,512]{2,1,0:T(8,128)(2,1)}), bf16[4,80,512]{2,1,0:T(8,128)(2,1)S(1)}, u32[]{:S(2)}, u32[]{:S(2)}) async-start(bf16[4,80,512]{2,1,0:T(8,128)(2,1)} %bitcast.18), calls=%async_computation.1 | async-start | bytes 655360 | tf_op jit(solution)/shard_map/all_to_all | solution.py:87
  146.3 1.5 copy-start.4
  146.3 1.5 copy-start.6
  146.3 1.5 copy-start.8
  146.3 1.5 copy-start.10
  148.6 7.5 %collective-permute-start.9 = (f32[256,432]{0,1:T(8,128)S(1)}, f32[256,432]{0,1:T(8,128)S(1)}, u32[]{:S(2)}, u32[]{:S(2)}) collective-permute-start(f32[256,432]{0,1:T(8,128)S(1)} %slice.35), channel_id=1, source_target_pairs={{0,16},{16,0},{1,17},{17,1},{2,18},{18,2},{3,19},{19,3},{4,20},{20... | collective-permute-start | bytes 1327112 | tf_op jit(solution)/shard_map/ppermute | solution.py:28
  180.8 15.3 %collective-permute-start.7 = (bf16[80,256]{1,0:T(8,128)(2,1)S(1)}, bf16[80,256]{1,0:T(8,128)(2,1)S(1)}, u32[]{:S(2)}, u32[]{:S(2)}) collective-permute-start(bf16[80,256]{1,0:T(8,128)(2,1)S(1)} %slice.33), channel_id=1, source_target_pairs={{0,16},{16,0},{1,17},{17,1},{2,18},{18,2},{3,19},{19,3},{4,20},{20... | collective-permute-start | bytes 122888 | tf_op jit(solution)/shard_map/ppermute | solution.py:28

commit v2 on v1

v2 whole, which is shorter than its diff:
```python
import functools
import math

import jax
import jax.numpy as jnp
import numpy as np
from jax import lax
from jax.experimental import pallas as pl
from jax.experimental.pallas import tpu as pltpu
from jax.sharding import Mesh, PartitionSpec as P

COEFF = math.sqrt(2.0 / math.pi)
AXES = ("y", "zl", "c", "zh", "x")
SIZES = (4, 8, 2, 4, 4)
F32, BF16 = jnp.float32, jnp.bfloat16
SMEM = pl.BlockSpec(memory_space=pltpu.SMEM)
VMEM = pl.BlockSpec(memory_space=pltpu.VMEM)
LATER = pl.BlockSpec(memory_space=pl.ANY)


def gelu_value(values):
    inner = COEFF * (values + 0.044715 * values * values * values)
    return 0.5 * values * (1.0 + jnp.tanh(inner))


def gelu_slope(values):
    tangent = jnp.tanh(COEFF * (values + 0.044715 * values * values * values))
    return 0.5 * (1.0 + tangent) + 0.5 * values * (1.0 - tangent * tangent) * COEFF * (
        1.0 + 3.0 * 0.044715 * values * values
    )


def swap(value, axis, distance):
    size = lax.axis_size(axis)
    return lax.ppermute(value, axis, [(i, i ^ distance) for i in range(size)])


def shift(value, axis, distance):
    size = lax.axis_size(axis)
    return lax.ppermute(value, axis, [(i, (i + distance) % size) for i in range(size)])


def dot(left, right, over_left, over_right):
    dims = (((over_left,), (over_right,)), ((), ()))
    return lax.dot_general(left, right, dims, preferred_element_type=F32)


def call(body, outs, specs, args, flops=0, scratch=()):
    moved = sum(a.size * a.dtype.itemsize for a in args) + sum(math.prod(s) * 2 for s, _ in outs)
    return pl.pallas_call(
        body,
        out_shape=[jax.ShapeDtypeStruct(s, d) for s, d in outs],
        in_specs=specs,
        out_specs=[VMEM] * len(outs),
        scratch_shapes=list(scratch),
        compiler_params=pltpu.CompilerParams(vmem_limit_bytes=14 << 20),
        cost_estimate=pl.CostEstimate(flops=flops, bytes_accessed=moved, transcendentals=0),
    )(*args)


def sort_channels(place, pick, cot, pre, send, mine):
    core, stripe = place[0], pick.shape[1]
    for index in range(cot.shape[1] // (2 * stripe)):
        part = cot[:, index * 2 * stripe : (index + 1) * 2 * stripe]
        rows = slice(index * stripe, (index + 1) * stripe)
        send[rows, :] = dot(pick[1 - core], part, 1, 1).astype(BF16)
        mine[rows, :] = dot(pick[core], part, 1, 1).astype(BF16)
    send[mine.shape[0] :, :] = pre[...]


def weight_term(pre, mine, got, after, hidden, term, *, stripe):
    tokens, channels = pre.shape[1], mine.shape[0]
    hidden[:, :tokens] = gelu_value(pre[...].astype(F32)).astype(BF16)
    hidden[:, tokens:] = gelu_value(got[channels:, :].astype(F32)).astype(BF16)
    for start in range(0, channels, stripe):
        rows = slice(start, start + stripe)
        total = dot(mine[rows, :], hidden[:, :tokens], 1, 1)
        total += dot(got[rows, :], hidden[:, tokens:], 1, 1)
        term[rows, :] = total.astype(BF16)


def sum_rounded(parts, after, then, last, out):
    total = parts[0].astype(F32)
    for index in range(1, parts.shape[0]):
        total += parts[index].astype(F32)
    out[...] = total.astype(out.dtype)


def sum_scaled(parts, after, out, *, factor):
    total = parts[0].astype(F32)
    for index in range(1, parts.shape[0]):
        total += parts[index].astype(F32)
    out[...] = total * factor


def order_rows(place, own, one, two, four, after, rows):
    zl = place[2]
    rows[zl] = own[...]
    rows[zl ^ 4] = one[...]
    for index, offset in enumerate((2, 6)):
        rows[zl ^ offset] = two[index]
    for index, offset in enumerate((1, 5, 3, 7)):
        rows[zl ^ offset] = four[index]


def output_terms(place, w0, w1, w2, w3, hidden, o0, o1, o2, o3, held):
    y, zh, x = place[1], place[3], place[4]
    group = held.shape[1]
    for k, piece in enumerate((w0, w1, w2, w3)):
        total = dot(piece[...], hidden[...], 1, 0).astype(BF16)
        for index in range(4):
            held[index] = total[index * group : (index + 1) * group]
        target = (y + k - zh + 4) % 4
        for r, out in enumerate((o0, o1, o2, o3)):
            out[target] = held[(x + r) % 4]


def sum_x(o0, g1, g2, g3, s0, s1, s3, left, right):
    def total(index):
        value = o0[index].astype(F32) + g1[index].astype(F32)
        return (value + (g2[index].astype(F32) + g3[index].astype(F32))).astype(BF16)

    half = left.shape[1]
    both = total(2)
    left[...] = both[:, :half]
    right[...] = both[:, half:]
    s0[...] = total(0)
    s1[...] = total(1)
    s3[...] = total(3)


def sum_step(s1, s3, left, right, t1, t3):
    half = left.shape[1]
    t1[:, :half] = (s1[:, :half].astype(F32) + left[...].astype(F32)).astype(BF16)
    t1[:, half:] = s1[:, half:]
    t3[:, :half] = s3[:, :half]
    t3[:, half:] = (s3[:, half:].astype(F32) + right[...].astype(F32)).astype(BF16)


def sum_last(s0, u, v, kept, given):
    half = kept.shape[1]
    total = (s0[...].astype(F32) + (u[...].astype(F32) + v[...].astype(F32))).astype(BF16)
    kept[...] = total[:, :half]
    given[...] = total[:, half:]


def hidden_terms(place, w0, w1, w2, w3, mine, got, own, other):
    y, stripe = place[1], w0.shape[0]
    own[...] = jnp.zeros_like(own)
    other[...] = jnp.zeros_like(other)
    for k, piece in enumerate((w0, w1, w2, w3)):
        rows = pl.ds(pl.multiple_of((y + k) % 4 * stripe, 16), stripe)
        own[...] += dot(piece[...], mine[rows, :], 0, 0)
        other[...] += dot(piece[...], got[rows, :], 0, 0)


def local(pick, pre_act, weight_out, cotangent):
    n_y, n_zl, n_x = SIZES[0], SIZES[1], SIZES[4]
    tokens, hid = pre_act.shape
    block = weight_out.shape[0]
    stripe = n_zl * block
    group = stripe // n_x
    channels = n_y * stripe
    core = lax.axis_index("c")
    place = jnp.stack([lax.axis_index(a) for a in ("c", "y", "zl", "zh", "x")]).astype(jnp.int32)
    factor = 1.0 / math.sqrt(tokens * n_y * n_zl * 2)
    work = 2 * tokens * channels * hid * 2
    pre = pre_act.T

    one = swap(weight_out, "zl", 4)
    send, mine = call(
        sort_channels,
        [((channels + hid, tokens), BF16), ((channels, tokens), BF16)],
        [SMEM, VMEM, VMEM, VMEM],
        (place, pick, cotangent, pre),
        flops=2 * 4 * tokens * stripe * stripe * 2 * 2,
    )
    got = swap(send, "c", 1)
    hidden, term = call(
        functools.partial(weight_term, stripe=stripe),
        [((hid, 2 * tokens), BF16), ((channels, hid), BF16)],
        [VMEM] * 3 + [LATER],
        (pre, mine, got, one),
        flops=work,
    )

    two = swap(jnp.stack([weight_out, one]), "zl", 2)
    four = swap(jnp.concatenate([weight_out[None], one[None], two]), "zl", 1)
    (rows,) = call(
        order_rows,
        [((n_zl, block, hid), BF16)],
        [SMEM] + [VMEM] * 4 + [LATER],
        (place, weight_out, one, two, four, term),
    )
    w0 = rows.reshape(stripe, hid)
    w1, w3, w2 = shift(w0, "y", -1), shift(w0, "y", 1), shift(w0, "y", 2)

    term = lax.all_to_all(term.reshape(n_y, stripe, hid), "y", 0, 0)
    (term,) = call(sum_rounded, [((stripe, hid), BF16)], [VMEM, LATER, LATER, LATER], (term, w1, w2, w3))
    term = lax.all_to_all(term.reshape(n_zl, block, hid), "zl", 0, 0)

    part = ((n_y, group, 2 * tokens), BF16)
    o0, o1, o2, o3 = call(
        output_terms,
        [part] * 4,
        [SMEM] + [VMEM] * 5,
        (place, w0, w1, w2, w3, hidden),
        flops=work,
        scratch=[pltpu.VMEM((n_x, group, 2 * tokens), BF16)],
    )
    g1, g3, g2 = shift(o1, "x", 1), shift(o3, "x", -1), shift(o2, "x", 2)
    whole, half = ((group, 2 * tokens), BF16), ((group, tokens), BF16)
    s0, s1, s3, left, right = call(
        sum_x, [whole] * 3 + [half] * 2, [VMEM] * 4, (o0, g1, g2, g3)
    )
    (grad_weight,) = call(
        functools.partial(sum_scaled, factor=factor), [((block, hid), F32)], [VMEM, LATER], (term, s0)
    )
    left, right = shift(left, "zh", 1), shift(right, "zh", -1)
    t1, t3 = call(sum_step, [whole] * 2, [VMEM] * 4, (s1, s3, left, right))
    u, v = shift(t1, "zh", 1), shift(t3, "zh", -1)
    kept, given = call(sum_last, [half] * 2, [VMEM] * 3, (s0, u, v))
    given = swap(given, "c", 1)
    kept, given = kept.reshape(-1, 1, block, tokens), given.reshape(-1, 1, block, tokens)
    first, second = jnp.where(core == 0, kept, given), jnp.where(core == 0, given, kept)
    output = jnp.concatenate([first, second], axis=1).reshape(-1, tokens).T

    own, other = call(
        hidden_terms,
        [((hid, tokens), F32)] * 2,
        [SMEM] + [VMEM] * 6,
        (place, w0, w1, w2, w3, mine, got),
        flops=work,
    )
    grad_hidden = own + swap(other, "c", 1)
    grad_pre = (grad_hidden * gelu_slope(pre.astype(F32))).astype(BF16).T
    return (output, grad_pre, grad_weight)


def solution(mesh):
    fine = Mesh(np.asarray(mesh.devices).reshape(SIZES), AXES)
    dp, tensor = AXES[:3], AXES[3:]
    mapped = jax.shard_map(
        local,
        mesh=fine,
        in_specs=(P(None, None, None), P(dp, tensor), P(dp, tensor), P(dp, None)),
        out_specs=(P(dp, tensor), P(dp, tensor), P(dp, tensor)),
        check_vma=False,
    )

    def run(pre_act, weight_out, cotangent):
        block = weight_out.shape[0] // (SIZES[0] * SIZES[1] * SIZES[2])
        stripe = SIZES[1] * block
        k = np.arange(stripe)
        table = np.zeros((2, stripe, 2 * stripe), np.float32)
        for core in range(2):
            table[core, k, k // block * (2 * block) + core * block + k % block] = 1.0
        return mapped(jnp.asarray(table, BF16), pre_act, weight_out, cotangent)

    return run
```

time: 198 us -> 168 us (0.85)
  the two profiles are of different devices: /device:TPU:97 before, /device:TPU:107 now
where the time goes in v2:
time: 168 us; the launch traced here: 167 us
  starting transfers between devices  91.9 us (55%)
  waiting for transfers between devices  55.8 us (33%)
  Pallas kernels  10.1 us (6%)
  local copies, waits for them, and re-layouts  7.55 us (4%)
    ppermute x10, starting transfers between devices, shift(): lax.ppermute(value, axis, [(i, (i + distance) % size) for i in range(size)])  50.9 us
    ppermute x10, waiting for transfers between devices, shift(): lax.ppermute(value, axis, [(i, (i + distance) % size) for i in range(size)])  43.9 us
    ppermute x6, starting transfers between devices, swap(): return lax.ppermute(value, axis, [(i, i ^ distance) for i in range(size)])  25.4 us
    ppermute x6, waiting for transfers between devices, swap(): return lax.ppermute(value, axis, [(i, i ^ distance) for i in range(size)])  11.9 us
    all_to_all x1, starting transfers between devices, local(): term = lax.all_to_all(term.reshape(n_zl, block, hid), 'zl', 0, 0)  11.3 us
    pallas_call x10, Pallas kernels, call(): pl.pallas_call(body, out_shape=[jax.ShapeDtypeStruct(s, d) for s, d in ou...  10.1 us
    unnamed x24, local copies, waits for them, and re-layouts  6.82 us
    all_to_all x1, starting transfers between devices, local(): term = lax.all_to_all(term.reshape(n_y, stripe, hid), 'y', 0, 0)  4.35 us
  transfers between devices with their start and end apart: 18, of which 10 were waited for; matrix products, arithmetic and copies ran while one was open for 1% of the time, Pallas kernels for 3%

profile of v2, /device:TPU:107, one launch (start us, length us, event | category | flops | bytes accessed | tf_op | source)
XLA Modules:
  0.0 167.4 jit_solution(6535674240186552417)
XLA Ops:
  0.6 0.1 stack.32.place
  0.7 0.9 copy-done.5
  1.7 1.3 copy-done.8
  3.0 1.1 copy-done.9
  4.1 1.8 %shard_map.67 = (bf16[1712,256]{1,0:T(8,128)(2,1)S(1)}, bf16[1280,256]{1,0:T(8,128)(2,1)S(1)}) custom-call(s32[5]{0:T(128)S(1)} %stack.32.place, bf16[2,320,640]{2,1,0:T(8,128)(2,1)S(1)} %copy-done.9, bf16[256,2560]{1,0:T(8,128)(2,1)S(1)} %copy-done.8, bf16[432,256]{1,0:T(8,128)(2,1)S(1)} %bitcast.28), custom_call_target="tpu_custom_call" | custom-call | flops 838860800 | bytes 3883028 | tf_op jit(solution)/shard_map/pallas_call | solution.py:50
  5.9 2.6 %collective-permute-start.3 = (bf16[1712,256]{1,0:T(8,128)(2,1)S(1)}, bf16[1712,256]{1,0:T(8,128)(2,1)S(1)}, u32[]{:S(2)}, u32[]{:S(2)}) collective-permute-start(bf16[1712,256]{1,0:T(8,128)(2,1)S(1)} %get-tuple-element.23), channel_id=1, source_target_pairs={{0,16},{16,0},{1,17},{17,1},{2,18},{18,2},{3,19},{19,3},{4,20},{20... | collective-permute-start | bytes 2629640 | tf_op jit(solution)/shard_map/ppermute | solution.py:35
  8.5 8.8 %collective-permute-start = (bf16[40,432]{1,0:T(8,128)(2,1)S(1)}, bf16[40,432]{1,0:T(8,128)(2,1)S(1)}, u32[]{:S(2)}, u32[]{:S(2)}) collective-permute-start(bf16[40,432]{1,0:T(8,128)(2,1)S(1)} %copy-done.4), channel_id=1, source_target_pairs={{0,128},{32,160},{64,192},{96,224},{128,0},{160,32},{192,64},{224,... | collective-permute-start | bytes 103688 | tf_op jit(solution)/shard_map/ppermute | solution.py:35
  17.3 2.4 %collective-permute-done.after.one = bf16[40,432]{1,0:T(8,128)(2,1)S(1)} collective-permute-done((bf16[40,432]{1,0:T(8,128)(2,1)S(1)}, bf16[40,432]{1,0:T(8,128)(2,1)S(1)}, u32[]{:S(2)}, u32[]{:S(2)}) %collective-permute-start) | collective-permute-done | bytes 34592 | tf_op jit(solution)/shard_map/ppermute | solution.py:35
  19.8 2.1 %shard_map.68 = (bf16[432,512]{1,0:T(8,128)(2,1)S(1)}, bf16[1280,432]{1,0:T(8,128)(2,1)}) custom-call(bf16[432,256]{1,0:T(8,128)(2,1)S(1)} %bitcast.29, bf16[1280,256]{1,0:T(8,128)(2,1)S(1)} %get-tuple-element.22.mine, bf16[1712,256]{1,0:T(8,128)(2,1)S(1)} %collective-permute-done.3.got, bf16[40,432]{1,0:T(8,128)(2,1)S(1)} %collective-permute-done.after.one), custom_call_target="tpu_custom_call" | custom-call | flops 566231040 | bytes 3335936 | tf_op jit(solution)/shard_map/pallas_call | solution.py:50
  21.9 0.8 copy-done
  22.8 0.8 copy-done.10
  23.5 4.4 %all-to-all-start = ((bf16[4,320,432]{2,1,0:T(8,128)(2,1)}), bf16[4,320,432]{2,1,0:T(8,128)(2,1)S(1)}, u32[]{:S(2)}, u32[]{:S(2)}) async-start(bf16[4,320,432]{2,1,0:T(8,128)(2,1)} %bitcast.14), calls=%async_computation | async-start | bytes 2621440 | tf_op jit(solution)/shard_map/all_to_all | solution.py:198
  27.9 1.9 %collective-permute-start.1 = (bf16[2,40,432]{2,1,0:T(8,128)(2,1)S(1)}, bf16[2,40,432]{2,1,0:T(8,128)(2,1)S(1)}, u32[]{:S(2)}, u32[]{:S(2)}) collective-permute-start(bf16[2,40,432]{2,1,0:T(8,128)(2,1)S(1)} %pad_maximum_fusion.1), channel_id=1, source_target_pairs={{0,64},{32,96},{64,0},{96,32},{128,192},{160,224},{192,128},{224,1... | collective-permute-start | bytes 207368 | tf_op jit(solution)/shard_map/ppermute | solution.py:35
  29.8 5.0 %collective-permute-done.1.two = bf16[2,40,432]{2,1,0:T(8,128)(2,1)S(1)} collective-permute-done((bf16[2,40,432]{2,1,0:T(8,128)(2,1)S(1)}, bf16[2,40,432]{2,1,0:T(8,128)(2,1)S(1)}, u32[]{:S(2)}, u32[]{:S(2)}) %collective-permute-start.1) | collective-permute-done | bytes 69152 | tf_op jit(solution)/shard_map/ppermute | solution.py:35
  34.9 1.9 %collective-permute-start.2 = (bf16[4,40,432]{2,1,0:T(8,128)(2,1)S(1)}, bf16[4,40,432]{2,1,0:T(8,128)(2,1)S(1)}, u32[]{:S(2)}, u32[]{:S(2)}) collective-permute-start(bf16[4,40,432]{2,1,0:T(8,128)(2,1)S(1)} %pad_maximum_fusion), channel_id=1, source_target_pairs={{0,32},{32,0},{64,96},{96,64},{128,160},{160,128},{192,224},{224,1... | collective-permute-start | bytes 414728 | tf_op jit(solution)/shard_map/ppermute | solution.py:35
  36.8 4.4 %collective-permute-done.2.four = bf16[4,40,432]{2,1,0:T(8,128)(2,1)S(1)} collective-permute-done((bf16[4,40,432]{2,1,0:T(8,128)(2,1)S(1)}, bf16[4,40,432]{2,1,0:T(8,128)(2,1)S(1)}, u32[]{:S(2)}, u32[]{:S(2)}) %collective-permute-start.2) | collective-permute-done | bytes 138272 | tf_op jit(solution)/shard_map/ppermute | solution.py:35
  41.3 0.6 shard_map.69
  41.8 3.1 %collective-permute-start.6 = (bf16[320,432]{1,0:T(8,128)(2,1)S(1)}, bf16[320,432]{1,0:T(8,128)(2,1)S(1)}, u32[]{:S(2)}, u32[]{:S(2)}) collective-permute-start(bf16[320,432]{1,0:T(8,128)(2,1)S(1)} %bitcast.19), channel_id=1, source_target_pairs={{0,256},{256,512},{512,768},{768,0},{1,257},{257,513},{513,769},{7... | collective-permute-start | bytes 829448 | tf_op jit(solution)/shard_map/ppermute | solution.py:40
  44.9 3.3 %collective-permute-start.5 = (bf16[320,432]{1,0:T(8,128)(2,1)S(1)}, bf16[320,432]{1,0:T(8,128)(2,1)S(1)}, u32[]{:S(2)}, u32[]{:S(2)}) collective-permute-start(bf16[320,432]{1,0:T(8,128)(2,1)S(1)} %bitcast.20), channel_id=1, source_target_pairs={{0,512},{256,768},{512,0},{768,256},{1,513},{257,769},{513,1},{769... | collective-permute-start | bytes 829448 | tf_op jit(solution)/shard_map/ppermute | solution.py:40
  48.2 3.5 %collective-permute-start.4 = (bf16[320,432]{1,0:T(8,128)(2,1)S(1)}, bf16[320,432]{1,0:T(8,128)(2,1)S(1)}, u32[]{:S(2)}, u32[]{:S(2)}) collective-permute-start(bf16[320,432]{1,0:T(8,128)(2,1)S(1)} %bitcast.21), channel_id=1, source_target_pairs={{0,768},{256,0},{512,256},{768,512},{1,769},{257,1},{513,257},{769... | collective-permute-start | bytes 829448 | tf_op jit(solution)/shard_map/ppermute | solution.py:40
  51.7 0.0 collective-permute-done.6.w3.last
  51.7 3.1 %collective-permute-done.5.w2.then = bf16[320,432]{1,0:T(8,128)(2,1)S(1)} collective-permute-done((bf16[320,432]{1,0:T(8,128)(2,1)S(1)}, bf16[320,432]{1,0:T(8,128)(2,1)S(1)}, u32[]{:S(2)}, u32[]{:S(2)}) %collective-permute-start.5) | collective-permute-done | bytes 276512 | tf_op jit(solution)/shard_map/ppermute | solution.py:40
  54.9 9.6 %collective-permute-done.4.w1.after = bf16[320,432]{1,0:T(8,128)(2,1)S(1)} collective-permute-done((bf16[320,432]{1,0:T(8,128)(2,1)S(1)}, bf16[320,432]{1,0:T(8,128)(2,1)S(1)}, u32[]{:S(2)}, u32[]{:S(2)}) %collective-permute-start.4) | collective-permute-done | bytes 276512 | tf_op jit(solution)/shard_map/ppermute | solution.py:40
  64.5 0.0 all-to-all-done.parts
  64.5 0.9 shard_map.75
  65.4 11.3 %all-to-all-start.1 = ((bf16[8,40,432]{2,1,0:T(8,128)(2,1)}), bf16[8,40,432]{2,1,0:T(8,128)(2,1)S(1)}, u32[]{:S(2)}, u32[]{:S(2)}) async-start(bf16[8,40,432]{2,1,0:T(8,128)(2,1)} %bitcast.15), calls=%async_computation.1 | async-start | bytes 655360 | tf_op jit(solution)/shard_map/all_to_all | solution.py:200
  76.7 1.0 copy-done.11
  77.7 1.4 shard_map.70
  79.1 3.1 %collective-permute-start.7 = (bf16[4,80,512]{2,1,0:T(8,128)(2,1)S(1)}, bf16[4,80,512]{2,1,0:T(8,128)(2,1)S(1)}, u32[]{:S(2)}, u32[]{:S(2)}) collective-permute-start(bf16[4,80,512]{2,1,0:T(8,128)(2,1)S(1)} %get-tuple-element.27), channel_id=1, source_target_pairs={{0,1},{1,2},{2,3},{3,0},{4,5},{5,6},{6,7},{7,4},{8,9},{9,10},{10,1... | collective-permute-start | bytes 983048 | tf_op jit(solution)/shard_map/ppermute | solution.py:40
  82.3 4.6 %collective-permute-start.8 = (bf16[4,80,512]{2,1,0:T(8,128)(2,1)S(1)}, bf16[4,80,512]{2,1,0:T(8,128)(2,1)S(1)}, u32[]{:S(2)}, u32[]{:S(2)}) collective-permute-start(bf16[4,80,512]{2,1,0:T(8,128)(2,1)S(1)} %get-tuple-element.28), channel_id=1, source_target_pairs={{0,2},{1,3},{2,0},{3,1},{4,6},{5,7},{6,4},{7,5},{8,10},{9,11},{10,... | collective-permute-start | bytes 983048 | tf_op jit(solution)/shard_map/ppermute | solution.py:40
  86.8 2.0 %collective-permute-start.9 = (bf16[4,80,512]{2,1,0:T(8,128)(2,1)S(1)}, bf16[4,80,512]{2,1,0:T(8,128)(2,1)S(1)}, u32[]{:S(2)}, u32[]{:S(2)}) collective-permute-start(bf16[4,80,512]{2,1,0:T(8,128)(2,1)S(1)} %get-tuple-element.29), channel_id=1, source_target_pairs={{0,3},{1,0},{2,1},{3,2},{4,7},{5,4},{6,5},{7,6},{8,11},{9,8},{10,9... | collective-permute-start | bytes 983048 | tf_op jit(solution)/shard_map/ppermute | solution.py:40
  88.8 2.5 %shard_map.74 = (f32[432,256]{1,0:T(8,128)S(1)}, f32[432,256]{1,0:T(8,128)}) custom-call(s32[5]{0:T(128)S(1)} %stack.32.place, bf16[320,432]{1,0:T(8,128)(2,1)S(1)} %bitcast.23, bf16[320,432]{1,0:T(8,128)(2,1)S(1)} %collective-permute-done.4.w1.after, bf16[320,432]{1,0:T(8,128)(2,1)S(1)} %collective-permute-done.5.w2.then, ...), custom_call_target="tpu_custom_call" | custom-call | flops 566231040 | bytes 3080212 | tf_op jit(solution)/shard_map/pallas_call | solution.py:50
  91.3 0.8 copy-done.2
  92.0 4.1 %collective-permute-start.15 = (f32[432,256]{1,0:T(8,128)}, f32[432,256]{1,0:T(8,128)S(1)}, u32[]{:S(2)}, u32[]{:S(2)}) collective-permute-start(f32[432,256]{1,0:T(8,128)} %get-tuple-element.40), channel_id=1, source_target_pairs={{0,16},{16,0},{1,17},{17,1},{2,18},{18,2},{3,19},{19,3},{4,20},{20... | collective-permute-start | bytes 1327112 | tf_op jit(solution)/shard_map/ppermute | solution.py:35
  96.1 6.2 %collective-permute-done.9.g3 = bf16[4,80,512]{2,1,0:T(8,128)(2,1)S(1)} collective-permute-done((bf16[4,80,512]{2,1,0:T(8,128)(2,1)S(1)}, bf16[4,80,512]{2,1,0:T(8,128)(2,1)S(1)}, u32[]{:S(2)}, u32[]{:S(2)}) %collective-permute-start.9) | collective-permute-done | bytes 327712 | tf_op jit(solution)/shard_map/ppermute | solution.py:40
  102.3 0.2 shard_map.71
  102.5 15.5 %collective-permute-start.10 = (bf16[80,256]{1,0:T(8,128)(2,1)S(1)}, bf16[80,256]{1,0:T(8,128)(2,1)S(1)}, u32[]{:S(2)}, u32[]{:S(2)}) collective-permute-start(bf16[80,256]{1,0:T(8,128)(2,1)S(1)} %get-tuple-element.33), channel_id=1, source_target_pairs={{0,4},{4,8},{8,12},{12,0},{1,5},{5,9},{9,13},{13,1},{2,6},{6,10},{... | collective-permute-start | bytes 122888 | tf_op jit(solution)/shard_map/ppermute | solution.py:40
  117.9 1.9 %collective-permute-start.11 = (bf16[80,256]{1,0:T(8,128)(2,1)S(1)}, bf16[80,256]{1,0:T(8,128)(2,1)S(1)}, u32[]{:S(2)}, u32[]{:S(2)}) collective-permute-start(bf16[80,256]{1,0:T(8,128)(2,1)S(1)} %get-tuple-element.34), channel_id=1, source_target_pairs={{0,12},{4,0},{8,4},{12,8},{1,13},{5,1},{9,5},{13,9},{2,14},{6,2},{... | collective-permute-start | bytes 122888 | tf_op jit(solution)/shard_map/ppermute | solution.py:40
  119.9 4.9 %collective-permute-done.10.left = bf16[80,256]{1,0:T(8,128)(2,1)S(1)} collective-permute-done((bf16[80,256]{1,0:T(8,128)(2,1)S(1)}, bf16[80,256]{1,0:T(8,128)(2,1)S(1)}, u32[]{:S(2)}, u32[]{:S(2)}) %collective-permute-start.10) | collective-permute-done | bytes 40992 | tf_op jit(solution)/shard_map/ppermute | solution.py:40
  124.8 7.3 %collective-permute-done.11.right = bf16[80,256]{1,0:T(8,128)(2,1)S(1)} collective-permute-done((bf16[80,256]{1,0:T(8,128)(2,1)S(1)}, bf16[80,256]{1,0:T(8,128)(2,1)S(1)}, u32[]{:S(2)}, u32[]{:S(2)}) %collective-permute-start.11) | collective-permute-done | bytes 40992 | tf_op jit(solution)/shard_map/ppermute | solution.py:40
  132.1 5.7 %collective-permute-start.12 = (bf16[80,512]{1,0:T(8,128)(2,1)S(1)}, bf16[80,512]{1,0:T(8,128)(2,1)S(1)}, u32[]{:S(2)}, u32[]{:S(2)}) collective-permute-start(bf16[80,512]{1,0:T(8,128)(2,1)S(1)} %get-tuple-element.35), channel_id=1, source_target_pairs={{0,4},{4,8},{8,12},{12,0},{1,5},{5,9},{9,13},{13,1},{2,6},{6,10},{... | collective-permute-start | bytes 245768 | tf_op jit(solution)/shard_map/ppermute | solution.py:40
  137.8 8.3 %collective-permute-start.13 = (bf16[80,512]{1,0:T(8,128)(2,1)S(1)}, bf16[80,512]{1,0:T(8,128)(2,1)S(1)}, u32[]{:S(2)}, u32[]{:S(2)}) collective-permute-start(bf16[80,512]{1,0:T(8,128)(2,1)S(1)} %get-tuple-element.36), channel_id=1, source_target_pairs={{0,12},{4,0},{8,4},{12,8},{1,13},{5,1},{9,5},{13,9},{2,14},{6,2},{... | collective-permute-start | bytes 245768 | tf_op jit(solution)/shard_map/ppermute | solution.py:40
  146.1 5.5 %collective-permute-done.12.u = bf16[80,512]{1,0:T(8,128)(2,1)S(1)} collective-permute-done((bf16[80,512]{1,0:T(8,128)(2,1)S(1)}, bf16[80,512]{1,0:T(8,128)(2,1)S(1)}, u32[]{:S(2)}, u32[]{:S(2)}) %collective-permute-start.12) | collective-permute-done | bytes 81952 | tf_op jit(solution)/shard_map/ppermute | solution.py:40
  151.7 7.2 %collective-permute-done.13.v = bf16[80,512]{1,0:T(8,128)(2,1)S(1)} collective-permute-done((bf16[80,512]{1,0:T(8,128)(2,1)S(1)}, bf16[80,512]{1,0:T(8,128)(2,1)S(1)}, u32[]{:S(2)}, u32[]{:S(2)}) %collective-permute-start.13) | collective-permute-done | bytes 81952 | tf_op jit(solution)/shard_map/ppermute | solution.py:40
  158.9 6.1 %collective-permute-start.14 = (bf16[80,256]{1,0:T(8,128)(2,1)S(1)}, bf16[80,256]{1,0:T(8,128)(2,1)S(1)}, u32[]{:S(2)}, u32[]{:S(2)}) collective-permute-start(bf16[80,256]{1,0:T(8,128)(2,1)S(1)} %get-tuple-element.38), channel_id=1, source_target_pairs={{0,16},{16,0},{1,17},{17,1},{2,18},{18,2},{3,19},{19,3},{4,20},{20... | collective-permute-start | bytes 122888 | tf_op jit(solution)/shard_map/ppermute | solution.py:35
  165.0 1.0 fusion.9
  166.1 0.6 copy.7
  166.7 0.7 shard_map.76
  (29 shorter events, 0.2 us)
Async XLA Ops:
  0.7 0.9 copy-start.5
  1.7 1.3 copy-start.8
  3.0 1.1 copy-start.9
  4.1 4.4 %copy-start.4 = (bf16[40,432]{1,0:T(8,128)(2,1)S(1)}, bf16[40,432]{1,0:T(8,128)(2,1)}, u32[]{:S(2)}) copy-start(bf16[40,432]{1,0:T(8,128)(2,1)} %own.1) | copy-start | bytes 103684
  4.1 15.7 %copy-start.6 = (bf16[256,432]{0,1:T(8,128)(2,1)S(1)}, bf16[256,432]{0,1:T(8,128)(2,1)}, u32[]{:S(2)}) copy-start(bf16[256,432]{0,1:T(8,128)(2,1)} %param.4) | copy-start | bytes 663556
  5.9 13.9 %collective-permute-start.3 = (bf16[1712,256]{1,0:T(8,128)(2,1)S(1)}, bf16[1712,256]{1,0:T(8,128)(2,1)S(1)}, u32[]{:S(2)}, u32[]{:S(2)}) collective-permute-start(bf16[1712,256]{1,0:T(8,128)(2,1)S(1)} %get-tuple-element.23), channel_id=1, source_target_pairs={{0,16},{16,0},{1,17},{17,1},{2,18},{18,2},{3,19},{19,3},{4,20},{20... | collective-permute-start | bytes 2629640 | tf_op jit(solution)/shard_map/ppermute | solution.py:35
  8.5 11.3 %collective-permute-start = (bf16[40,432]{1,0:T(8,128)(2,1)S(1)}, bf16[40,432]{1,0:T(8,128)(2,1)S(1)}, u32[]{:S(2)}, u32[]{:S(2)}) collective-permute-start(bf16[40,432]{1,0:T(8,128)(2,1)S(1)} %copy-done.4), channel_id=1, source_target_pairs={{0,128},{32,160},{64,192},{96,224},{128,0},{160,32},{192,64},{224,... | collective-permute-start | bytes 103688 | tf_op jit(solution)/shard_map/ppermute | solution.py:35
  21.9 0.8 copy-start
  22.8 0.8 copy-start.10
  23.5 41.0 %all-to-all-start = ((bf16[4,320,432]{2,1,0:T(8,128)(2,1)}), bf16[4,320,432]{2,1,0:T(8,128)(2,1)S(1)}, u32[]{:S(2)}, u32[]{:S(2)}) async-start(bf16[4,320,432]{2,1,0:T(8,128)(2,1)} %bitcast.14), calls=%async_computation | async-start | bytes 2621440 | tf_op jit(solution)/shard_map/all_to_all | solution.py:198
  27.9 7.0 %collective-permute-start.1 = (bf16[2,40,432]{2,1,0:T(8,128)(2,1)S(1)}, bf16[2,40,432]{2,1,0:T(8,128)(2,1)S(1)}, u32[]{:S(2)}, u32[]{:S(2)}) collective-permute-start(bf16[2,40,432]{2,1,0:T(8,128)(2,1)S(1)} %pad_maximum_fusion.1), channel_id=1, source_target_pairs={{0,64},{32,96},{64,0},{96,32},{128,192},{160,224},{192,128},{224,1... | collective-permute-start | bytes 207368 | tf_op jit(solution)/shard_map/ppermute | solution.py:35
  34.9 6.4 %collective-permute-start.2 = (bf16[4,40,432]{2,1,0:T(8,128)(2,1)S(1)}, bf16[4,40,432]{2,1,0:T(8,128)(2,1)S(1)}, u32[]{:S(2)}, u32[]{:S(2)}) collective-permute-start(bf16[4,40,432]{2,1,0:T(8,128)(2,1)S(1)} %pad_maximum_fusion), channel_id=1, source_target_pairs={{0,32},{32,0},{64,96},{96,64},{128,160},{160,128},{192,224},{224,1... | collective-permute-start | bytes 414728 | tf_op jit(solution)/shard_map/ppermute | solution.py:35
  41.8 9.9 %collective-permute-start.6 = (bf16[320,432]{1,0:T(8,128)(2,1)S(1)}, bf16[320,432]{1,0:T(8,128)(2,1)S(1)}, u32[]{:S(2)}, u32[]{:S(2)}) collective-permute-start(bf16[320,432]{1,0:T(8,128)(2,1)S(1)} %bitcast.19), channel_id=1, source_target_pairs={{0,256},{256,512},{512,768},{768,0},{1,257},{257,513},{513,769},{7... | collective-permute-start | bytes 829448 | tf_op jit(solution)/shard_map/ppermute | solution.py:40
  44.9 9.9 %collective-permute-start.5 = (bf16[320,432]{1,0:T(8,128)(2,1)S(1)}, bf16[320,432]{1,0:T(8,128)(2,1)S(1)}, u32[]{:S(2)}, u32[]{:S(2)}) collective-permute-start(bf16[320,432]{1,0:T(8,128)(2,1)S(1)} %bitcast.20), channel_id=1, source_target_pairs={{0,512},{256,768},{512,0},{768,256},{1,513},{257,769},{513,1},{769... | collective-permute-start | bytes 829448 | tf_op jit(solution)/shard_map/ppermute | solution.py:40
  48.2 16.3 %collective-permute-start.4 = (bf16[320,432]{1,0:T(8,128)(2,1)S(1)}, bf16[320,432]{1,0:T(8,128)(2,1)S(1)}, u32[]{:S(2)}, u32[]{:S(2)}) collective-permute-start(bf16[320,432]{1,0:T(8,128)(2,1)S(1)} %bitcast.21), channel_id=1, source_target_pairs={{0,768},{256,0},{512,256},{768,512},{1,769},{257,1},{513,257},{769... | collective-permute-start | bytes 829448 | tf_op jit(solution)/shard_map/ppermute | solution.py:40
  65.4 23.4 %copy-start.1 = (bf16[1280,256]{1,0:T(8,128)(2,1)S(1)}, bf16[1280,256]{1,0:T(8,128)(2,1)}, u32[]{:S(2)}) copy-start(bf16[1280,256]{1,0:T(8,128)(2,1)} %copy-done) | copy-start | bytes 1966084
  65.4 101.3 %all-to-all-start.1 = ((bf16[8,40,432]{2,1,0:T(8,128)(2,1)}), bf16[8,40,432]{2,1,0:T(8,128)(2,1)S(1)}, u32[]{:S(2)}, u32[]{:S(2)}) async-start(bf16[8,40,432]{2,1,0:T(8,128)(2,1)} %bitcast.15), calls=%async_computation.1 | async-start | bytes 655360 | tf_op jit(solution)/shard_map/all_to_all | solution.py:200
  76.7 1.0 copy-start.11
  79.1 17.0 %collective-permute-start.7 = (bf16[4,80,512]{2,1,0:T(8,128)(2,1)S(1)}, bf16[4,80,512]{2,1,0:T(8,128)(2,1)S(1)}, u32[]{:S(2)}, u32[]{:S(2)}) collective-permute-start(bf16[4,80,512]{2,1,0:T(8,128)(2,1)S(1)} %get-tuple-element.27), channel_id=1, source_target_pairs={{0,1},{1,2},{2,3},{3,0},{4,5},{5,6},{6,7},{7,4},{8,9},{9,10},{10,1... | collective-permute-start | bytes 983048 | tf_op jit(solution)/shard_map/ppermute | solution.py:40
  82.3 13.9 %collective-permute-start.8 = (bf16[4,80,512]{2,1,0:T(8,128)(2,1)S(1)}, bf16[4,80,512]{2,1,0:T(8,128)(2,1)S(1)}, u32[]{:S(2)}, u32[]{:S(2)}) collective-permute-start(bf16[4,80,512]{2,1,0:T(8,128)(2,1)S(1)} %get-tuple-element.28), channel_id=1, source_target_pairs={{0,2},{1,3},{2,0},{3,1},{4,6},{5,7},{6,4},{7,5},{8,10},{9,11},{10,... | collective-permute-start | bytes 983048 | tf_op jit(solution)/shard_map/ppermute | solution.py:40
  86.8 15.5 %collective-permute-start.9 = (bf16[4,80,512]{2,1,0:T(8,128)(2,1)S(1)}, bf16[4,80,512]{2,1,0:T(8,128)(2,1)S(1)}, u32[]{:S(2)}, u32[]{:S(2)}) collective-permute-start(bf16[4,80,512]{2,1,0:T(8,128)(2,1)S(1)} %get-tuple-element.29), channel_id=1, source_target_pairs={{0,3},{1,0},{2,1},{3,2},{4,7},{5,4},{6,5},{7,6},{8,11},{9,8},{10,9... | collective-permute-start | bytes 983048 | tf_op jit(solution)/shard_map/ppermute | solution.py:40
  91.3 0.8 copy-start.2
  92.0 73.0 %copy-start.7 = (bf16[256,432]{0,1:T(8,128)(2,1)S(1)}, bf16[256,432]{0,1:T(8,128)(2,1)}, u32[]{:S(2)}) copy-start(bf16[256,432]{0,1:T(8,128)(2,1)} %param.4) | copy-start | bytes 663556
  92.0 73.0 %copy-start.3 = (f32[432,256]{1,0:T(8,128)S(1)}, f32[432,256]{1,0:T(8,128)}, u32[]{:S(2)}) copy-start(f32[432,256]{1,0:T(8,128)} %copy-done.2) | copy-start | bytes 1327108
  92.0 72.9 %collective-permute-start.15 = (f32[432,256]{1,0:T(8,128)}, f32[432,256]{1,0:T(8,128)S(1)}, u32[]{:S(2)}, u32[]{:S(2)}) collective-permute-start(f32[432,256]{1,0:T(8,128)} %get-tuple-element.40), channel_id=1, source_target_pairs={{0,16},{16,0},{1,17},{17,1},{2,18},{18,2},{3,19},{19,3},{4,20},{20... | collective-permute-start | bytes 1327112 | tf_op jit(solution)/shard_map/ppermute | solution.py:35
  102.5 22.3 %collective-permute-start.10 = (bf16[80,256]{1,0:T(8,128)(2,1)S(1)}, bf16[80,256]{1,0:T(8,128)(2,1)S(1)}, u32[]{:S(2)}, u32[]{:S(2)}) collective-permute-start(bf16[80,256]{1,0:T(8,128)(2,1)S(1)} %get-tuple-element.33), channel_id=1, source_target_pairs={{0,4},{4,8},{8,12},{12,0},{1,5},{5,9},{9,13},{13,1},{2,6},{6,10},{... | collective-permute-start | bytes 122888 | tf_op jit(solution)/shard_map/ppermute | solution.py:40
  117.9 14.1 %collective-permute-start.11 = (bf16[80,256]{1,0:T(8,128)(2,1)S(1)}, bf16[80,256]{1,0:T(8,128)(2,1)S(1)}, u32[]{:S(2)}, u32[]{:S(2)}) collective-permute-start(bf16[80,256]{1,0:T(8,128)(2,1)S(1)} %get-tuple-element.34), channel_id=1, source_target_pairs={{0,12},{4,0},{8,4},{12,8},{1,13},{5,1},{9,5},{13,9},{2,14},{6,2},{... | collective-permute-start | bytes 122888 | tf_op jit(solution)/shard_map/ppermute | solution.py:40
  132.1 19.6 %collective-permute-start.12 = (bf16[80,512]{1,0:T(8,128)(2,1)S(1)}, bf16[80,512]{1,0:T(8,128)(2,1)S(1)}, u32[]{:S(2)}, u32[]{:S(2)}) collective-permute-start(bf16[80,512]{1,0:T(8,128)(2,1)S(1)} %get-tuple-element.35), channel_id=1, source_target_pairs={{0,4},{4,8},{8,12},{12,0},{1,5},{5,9},{9,13},{13,1},{2,6},{6,10},{... | collective-permute-start | bytes 245768 | tf_op jit(solution)/shard_map/ppermute | solution.py:40
  137.8 21.1 %collective-permute-start.13 = (bf16[80,512]{1,0:T(8,128)(2,1)S(1)}, bf16[80,512]{1,0:T(8,128)(2,1)S(1)}, u32[]{:S(2)}, u32[]{:S(2)}) collective-permute-start(bf16[80,512]{1,0:T(8,128)(2,1)S(1)} %get-tuple-element.36), channel_id=1, source_target_pairs={{0,12},{4,0},{8,4},{12,8},{1,13},{5,1},{9,5},{13,9},{2,14},{6,2},{... | collective-permute-start | bytes 245768 | tf_op jit(solution)/shard_map/ppermute | solution.py:40
  158.9 7.1 %collective-permute-start.14 = (bf16[80,256]{1,0:T(8,128)(2,1)S(1)}, bf16[80,256]{1,0:T(8,128)(2,1)S(1)}, u32[]{:S(2)}, u32[]{:S(2)}) collective-permute-start(bf16[80,256]{1,0:T(8,128)(2,1)S(1)} %get-tuple-element.38), channel_id=1, source_target_pairs={{0,16},{16,0},{1,17},{17,1},{2,18},{18,2},{3,19},{19,3},{4,20},{20... | collective-permute-start | bytes 122888 | tf_op jit(solution)/shard_map/ppermute | solution.py:35

commit v3 on v2

--- a/solution.py
+++ b/solution.py
@@ -38,6 +38,16 @@
 def shift(value, axis, distance):
     size = lax.axis_size(axis)
     return lax.ppermute(value, axis, [(i, (i + distance) % size) for i in range(size)])
+
+
+def shift_both(value, distance):
+    size = lax.axis_size("zh")
+    pairs = [
+        (core * size + i, core * size + (i + distance * (1 - 2 * core)) % size)
+        for core in range(2)
+        for i in range(size)
+    ]
+    return lax.ppermute(value, ("c", "zh"), pairs)
 
 
 def dot(left, right, over_left, over_right):
@@ -58,7 +68,7 @@
     )(*args)
 
 
-def sort_channels(place, pick, cot, pre, send, mine):
+def sort_channels(place, pick, cot, pre, after, send, mine):
     core, stripe = place[0], pick.shape[1]
     for index in range(cot.shape[1] // (2 * stripe)):
         part = cot[:, index * 2 * stripe : (index + 1) * 2 * stripe]
@@ -68,7 +78,7 @@
     send[mine.shape[0] :, :] = pre[...]
 
 
-def weight_term(pre, mine, got, after, hidden, term, *, stripe):
+def weight_term(pre, mine, got, hidden, term, *, stripe):
     tokens, channels = pre.shape[1], mine.shape[0]
     hidden[:, :tokens] = gelu_value(pre[...].astype(F32)).astype(BF16)
     hidden[:, tokens:] = gelu_value(got[channels:, :].astype(F32)).astype(BF16)
@@ -79,18 +89,30 @@
         term[rows, :] = total.astype(BF16)
 
 
-def sum_rounded(parts, after, then, last, out):
-    total = parts[0].astype(F32)
-    for index in range(1, parts.shape[0]):
-        total += parts[index].astype(F32)
-    out[...] = total.astype(out.dtype)
-
-
-def sum_scaled(parts, after, out, *, factor):
-    total = parts[0].astype(F32)
-    for index in range(1, parts.shape[0]):
-        total += parts[index].astype(F32)
-    out[...] = total * factor
+def split_y(place, parts, after, keep, send):
+    bit = place[2] % 2
+
+    def total(index):
+        value = parts[0, index].astype(F32)
+        for source in range(1, parts.shape[0]):
+            value += parts[source, index].astype(F32)
+        return value
+
+    for index in range(keep.shape[0]):
+        keep[index] = total(2 * index + bit)
+        send[index] = total(2 * index + 1 - bit).astype(BF16)
+
+
+def split_zl(place, kept, got, keep, send, *, width):
+    bit = place[2] // width % 2
+    for index in range(keep.shape[0]):
+        near, far = 2 * index + bit, 2 * index + 1 - bit
+        keep[index] = kept[near] + got[near].astype(F32)
+        send[index] = (kept[far] + got[far].astype(F32)).astype(BF16)
+
+
+def sum_scaled(kept, got, out, *, factor):
+    out[...] = (kept[0] + got[0].astype(F32)) * factor
 
 
 def order_rows(place, own, one, two, four, after, rows):
@@ -104,40 +126,28 @@
 
 
 def output_terms(place, w0, w1, w2, w3, hidden, o0, o1, o2, o3, held):
-    y, zh, x = place[1], place[3], place[4]
+    core, y, zh, x = place[0], place[1], place[3], place[4]
     group = held.shape[1]
     for k, piece in enumerate((w0, w1, w2, w3)):
         total = dot(piece[...], hidden[...], 1, 0).astype(BF16)
         for index in range(4):
             held[index] = total[index * group : (index + 1) * group]
-        target = (y + k - zh + 4) % 4
+        target = (y + k - zh + 4) * (1 + 2 * core) % 4
         for r, out in enumerate((o0, o1, o2, o3)):
             out[target] = held[(x + r) % 4]
 
 
-def sum_x(o0, g1, g2, g3, s0, s1, s3, left, right):
-    def total(index):
+def sum_x(o0, g1, g2, g3, after, s0, s1, s2, s3):
+    for index, out in enumerate((s0, s1, s2, s3)):
         value = o0[index].astype(F32) + g1[index].astype(F32)
-        return (value + (g2[index].astype(F32) + g3[index].astype(F32))).astype(BF16)
-
-    half = left.shape[1]
-    both = total(2)
-    left[...] = both[:, :half]
-    right[...] = both[:, half:]
-    s0[...] = total(0)
-    s1[...] = total(1)
-    s3[...] = total(3)
-
-
-def sum_step(s1, s3, left, right, t1, t3):
-    half = left.shape[1]
-    t1[:, :half] = (s1[:, :half].astype(F32) + left[...].astype(F32)).astype(BF16)
-    t1[:, half:] = s1[:, half:]
-    t3[:, :half] = s3[:, :half]
-    t3[:, half:] = (s3[:, half:].astype(F32) + right[...].astype(F32)).astype(BF16)
-
-
-def sum_last(s0, u, v, kept, given):
+        out[...] = (value + (g2[index].astype(F32) + g3[index].astype(F32))).astype(BF16)
+
+
+def sum_step(s1, got, after, t1):
+    t1[...] = (s1[...].astype(F32) + got[...].astype(F32)).astype(BF16)
+
+
+def sum_last(s0, u, v, after, kept, given):
     half = kept.shape[1]
     total = (s0[...].astype(F32) + (u[...].astype(F32) + v[...].astype(F32))).astype(BF16)
     kept[...] = total[:, :half]
@@ -171,16 +181,16 @@
     send, mine = call(
         sort_channels,
         [((channels + hid, tokens), BF16), ((channels, tokens), BF16)],
-        [SMEM, VMEM, VMEM, VMEM],
-        (place, pick, cotangent, pre),
+        [SMEM, VMEM, VMEM, VMEM, LATER],
+        (place, pick, cotangent, pre, one),
         flops=2 * 4 * tokens * stripe * stripe * 2 * 2,
     )
     got = swap(send, "c", 1)
     hidden, term = call(
         functools.partial(weight_term, stripe=stripe),
         [((hid, 2 * tokens), BF16), ((channels, hid), BF16)],
-        [VMEM] * 3 + [LATER],
-        (pre, mine, got, one),
+        [VMEM] * 3,
+        (pre, mine, got),
         flops=work,
     )
 
@@ -196,8 +206,6 @@
     w1, w3, w2 = shift(w0, "y", -1), shift(w0, "y", 1), shift(w0, "y", 2)
 
     term = lax.all_to_all(term.reshape(n_y, stripe, hid), "y", 0, 0)
-    (term,) = call(sum_rounded, [((stripe, hid), BF16)], [VMEM, LATER, LATER, LATER], (term, w1, w2, w3))
-    term = lax.all_to_all(term.reshape(n_zl, block, hid), "zl", 0, 0)
 
     part = ((n_y, group, 2 * tokens), BF16)
     o0, o1, o2, o3 = call(
@@ -209,22 +217,6 @@
         scratch=[pltpu.VMEM((n_x, group, 2 * tokens), BF16)],
     )
     g1, g3, g2 = shift(o1, "x", 1), shift(o3, "x", -1), shift(o2, "x", 2)
-    whole, half = ((group, 2 * tokens), BF16), ((group, tokens), BF16)
-    s0, s1, s3, left, right = call(
-        sum_x, [whole] * 3 + [half] * 2, [VMEM] * 4, (o0, g1, g2, g3)
-    )
-    (grad_weight,) = call(
-        functools.partial(sum_scaled, factor=factor), [((block, hid), F32)], [VMEM, LATER], (term, s0)
-    )
-    left, right = shift(left, "zh", 1), shift(right, "zh", -1)
-    t1, t3 = call(sum_step, [whole] * 2, [VMEM] * 4, (s1, s3, left, right))
-    u, v = shift(t1, "zh", 1), shift(t3, "zh", -1)
-    kept, given = call(sum_last, [half] * 2, [VMEM] * 3, (s0, u, v))
-    given = swap(given, "c", 1)
-    kept, given = kept.reshape(-1, 1, block, tokens), given.reshape(-1, 1, block, tokens)
-    first, second = jnp.where(core == 0, kept, given), jnp.where(core == 0, given, kept)
-    output = jnp.concatenate([first, second], axis=1).reshape(-1, tokens).T
-
     own, other = call(
         hidden_terms,
         [((hid, tokens), F32)] * 2,
@@ -232,6 +224,42 @@
         (place, w0, w1, w2, w3, mine, got),
         flops=work,
     )
+    whole, half = ((group, 2 * tokens), BF16), ((group, tokens), BF16)
+    quarter = n_zl // 2
+    keep, send = call(
+        split_y,
+        [((quarter, block, hid), F32), ((quarter, block, hid), BF16)],
+        [SMEM, VMEM, LATER],
+        (place, term.reshape(n_y, n_zl, block, hid), own),
+    )
+    s0, s1, s2, s3 = call(sum_x, [whole] * 4, [VMEM] * 4 + [LATER], (o0, g1, g2, g3, keep))
+    got2 = shift_both(s2, 1)
+    keep, send = call(
+        functools.partial(split_zl, width=2),
+        [((quarter // 2, block, hid), F32), ((quarter // 2, block, hid), BF16)],
+        [SMEM, VMEM, VMEM],
+        (place, keep, swap(send, "zl", 1)),
+    )
+    (t1,) = call(sum_step, [whole], [VMEM] * 2 + [LATER], (s1, got2, keep))
+    u, v = shift_both(t1, 1), shift_both(s3, -1)
+    keep, send = call(
+        functools.partial(split_zl, width=4),
+        [((quarter // 4, block, hid), F32), ((quarter // 4, block, hid), BF16)],
+        [SMEM, VMEM, VMEM],
+        (place, keep, swap(send, "zl", 2)),
+    )
+    kept, given = call(sum_last, [half] * 2, [VMEM] * 3 + [LATER], (s0, u, v, keep))
+    (grad_weight,) = call(
+        functools.partial(sum_scaled, factor=factor),
+        [((block, hid), F32)],
+        [VMEM] * 2,
+        (keep, swap(send, "zl", 4)),
+    )
+    given = swap(given, "c", 1)
+    kept, given = kept.reshape(-1, 1, block, tokens), given.reshape(-1, 1, block, tokens)
+    first, second = jnp.where(core == 0, kept, given), jnp.where(core == 0, given, kept)
+    output = jnp.concatenate([first, second], axis=1).reshape(-1, tokens).T
+
     grad_hidden = own + swap(other, "c", 1)
     grad_pre = (grad_hidden * gelu_slope(pre.astype(F32))).astype(BF16).T
     return (output, grad_pre, grad_weight)

time: 168 us -> 156 us (0.929)
  the two profiles are of different devices: /device:TPU:107 before, /device:TPU:11 now
where the time goes in v3:
time: 156 us; the launch traced here: 155 us
  starting transfers between devices  103 us (66%)
  waiting for transfers between devices  32.3 us (21%)
  Pallas kernels  13.2 us (8%)
  local copies, waits for them, and re-layouts  4.94 us (3%)
    ppermute x9, starting transfers between devices, swap(): return lax.ppermute(value, axis, [(i, i ^ distance) for i in range(size)])  44.4 us
    ppermute x3, starting transfers between devices, shift_both(): return lax.ppermute(value, ('c', 'zh'), pairs)  29.1 us
    ppermute x6, starting transfers between devices, shift(): lax.ppermute(value, axis, [(i, (i + distance) % size) for i in range(size)])  24.9 us
    ppermute x6, waiting for transfers between devices, shift(): lax.ppermute(value, axis, [(i, (i + distance) % size) for i in range(size)])  18.9 us
    ppermute x9, waiting for transfers between devices, swap(): return lax.ppermute(value, axis, [(i, i ^ distance) for i in range(size)])  13.4 us
    pallas_call x12, Pallas kernels, call(): pl.pallas_call(body, out_shape=[jax.ShapeDtypeStruct(s, d) for s, d in ou...  13.2 us
    all_to_all x1, starting transfers between devices, local(): term = lax.all_to_all(term.reshape(n_y, stripe, hid), 'y', 0, 0)  4.36 us
    unnamed x18, local copies, waits for them, and re-layouts  4.21 us
  transfers between devices with their start and end apart: 19, of which 8 were waited for; matrix products, arithmetic and copies ran while one was open for 1% of the time, Pallas kernels for 7%

profile of v3, /device:TPU:11, one launch (start us, length us, event | category | flops | bytes accessed | tf_op | source)
XLA Modules:
  0.0 155.3 jit_solution(6243475309163302358)
XLA Ops:
  0.6 8.8 %collective-permute-start = (bf16[40,432]{1,0:T(8,128)(2,1)}, bf16[40,432]{1,0:T(8,128)(2,1)S(1)}, u32[]{:S(2)}, u32[]{:S(2)}) collective-permute-start(bf16[40,432]{1,0:T(8,128)(2,1)} %own.1), channel_id=1, source_target_pairs={{0,128},{32,160},{64,192},{96,224},{128,0},{160,32},{192,64},{224,... | collective-permute-start | bytes 103688 | tf_op jit(solution)/shard_map/ppermute | solution.py:35
  9.5 0.1 stack.32.place
  9.6 1.5 collective-permute-done.after.one
  11.0 0.9 copy-done.3
  12.0 1.3 copy-done.5
  13.3 1.1 copy-done.6
  14.4 1.8 %shard_map.67 = (bf16[1712,256]{1,0:T(8,128)(2,1)S(1)}, bf16[1280,256]{1,0:T(8,128)(2,1)S(1)}) custom-call(s32[5]{0:T(128)S(1)} %stack.32.place, bf16[2,320,640]{2,1,0:T(8,128)(2,1)S(1)} %copy-done.6, bf16[256,2560]{1,0:T(8,128)(2,1)S(1)} %copy-done.5, bf16[432,256]{1,0:T(8,128)(2,1)S(1)} %bitcast.29, bf16[40,432]{1,0:T(8,128)(2,1)S(1)} %collective-permute-done.after.one), custom_call_target="tpu_custom_call" | custom-call | flops 838860800 | bytes 3917588 | tf_op jit(solution)/shard_map/pallas_call | solution.py:60
  16.2 3.4 %collective-permute-start.3 = (bf16[1712,256]{1,0:T(8,128)(2,1)S(1)}, bf16[1712,256]{1,0:T(8,128)(2,1)S(1)}, u32[]{:S(2)}, u32[]{:S(2)}) collective-permute-start(bf16[1712,256]{1,0:T(8,128)(2,1)S(1)} %get-tuple-element.26), channel_id=1, source_target_pairs={{0,16},{16,0},{1,17},{17,1},{2,18},{18,2},{3,19},{19,3},{4,20},{20... | collective-permute-start | bytes 2629640 | tf_op jit(solution)/shard_map/ppermute | solution.py:35
  19.7 4.9 %collective-permute-start.1 = (bf16[2,40,432]{2,1,0:T(8,128)(2,1)S(1)}, bf16[2,40,432]{2,1,0:T(8,128)(2,1)S(1)}, u32[]{:S(2)}, u32[]{:S(2)}) collective-permute-start(bf16[2,40,432]{2,1,0:T(8,128)(2,1)S(1)} %pad_maximum_fusion.1), channel_id=1, source_target_pairs={{0,64},{32,96},{64,0},{96,32},{128,192},{160,224},{192,128},{224,1... | collective-permute-start | bytes 207368 | tf_op jit(solution)/shard_map/ppermute | solution.py:35
  24.6 0.0 collective-permute-done.3.got
  24.6 2.1 %shard_map.68 = (bf16[432,512]{1,0:T(8,128)(2,1)S(1)}, bf16[1280,432]{1,0:T(8,128)(2,1)}) custom-call(bf16[432,256]{1,0:T(8,128)(2,1)S(1)} %bitcast.30, bf16[1280,256]{1,0:T(8,128)(2,1)S(1)} %get-tuple-element.25.mine, bf16[1712,256]{1,0:T(8,128)(2,1)S(1)} %collective-permute-done.3.got), custom_call_target="tpu_custom_call" | custom-call | flops 566231040 | bytes 3301376 | tf_op jit(solution)/shard_map/pallas_call | solution.py:60
  26.8 0.8 copy-done.7
  27.5 4.4 %all-to-all-start = ((bf16[4,320,432]{2,1,0:T(8,128)(2,1)}), bf16[4,320,432]{2,1,0:T(8,128)(2,1)S(1)}, u32[]{:S(2)}, u32[]{:S(2)}) async-start(bf16[4,320,432]{2,1,0:T(8,128)(2,1)} %bitcast.9), calls=%async_computation | async-start | bytes 2621440 | tf_op jit(solution)/shard_map/all_to_all | solution.py:208
  31.9 0.0 collective-permute-done.1.two
  31.9 4.0 %collective-permute-start.2 = (bf16[4,40,432]{2,1,0:T(8,128)(2,1)S(1)}, bf16[4,40,432]{2,1,0:T(8,128)(2,1)S(1)}, u32[]{:S(2)}, u32[]{:S(2)}) collective-permute-start(bf16[4,40,432]{2,1,0:T(8,128)(2,1)S(1)} %pad_maximum_fusion), channel_id=1, source_target_pairs={{0,32},{32,0},{64,96},{96,64},{128,160},{160,128},{192,224},{224,1... | collective-permute-start | bytes 414728 | tf_op jit(solution)/shard_map/ppermute | solution.py:35
  35.9 3.7 %collective-permute-done.2.four = bf16[4,40,432]{2,1,0:T(8,128)(2,1)S(1)} collective-permute-done((bf16[4,40,432]{2,1,0:T(8,128)(2,1)S(1)}, bf16[4,40,432]{2,1,0:T(8,128)(2,1)S(1)}, u32[]{:S(2)}, u32[]{:S(2)}) %collective-permute-start.2) | collective-permute-done | bytes 138272 | tf_op jit(solution)/shard_map/ppermute | solution.py:35
  39.6 0.6 shard_map.69
  40.2 3.1 %collective-permute-start.6 = (bf16[320,432]{1,0:T(8,128)(2,1)S(1)}, bf16[320,432]{1,0:T(8,128)(2,1)S(1)}, u32[]{:S(2)}, u32[]{:S(2)}) collective-permute-start(bf16[320,432]{1,0:T(8,128)(2,1)S(1)} %bitcast.20), channel_id=1, source_target_pairs={{0,256},{256,512},{512,768},{768,0},{1,257},{257,513},{513,769},{7... | collective-permute-start | bytes 829448 | tf_op jit(solution)/shard_map/ppermute | solution.py:40
  43.3 2.8 %collective-permute-start.5 = (bf16[320,432]{1,0:T(8,128)(2,1)S(1)}, bf16[320,432]{1,0:T(8,128)(2,1)S(1)}, u32[]{:S(2)}, u32[]{:S(2)}) collective-permute-start(bf16[320,432]{1,0:T(8,128)(2,1)S(1)} %bitcast.21), channel_id=1, source_target_pairs={{0,512},{256,768},{512,0},{768,256},{1,513},{257,769},{513,1},{769... | collective-permute-start | bytes 829448 | tf_op jit(solution)/shard_map/ppermute | solution.py:40
  46.1 3.7 %collective-permute-start.4 = (bf16[320,432]{1,0:T(8,128)(2,1)S(1)}, bf16[320,432]{1,0:T(8,128)(2,1)S(1)}, u32[]{:S(2)}, u32[]{:S(2)}) collective-permute-start(bf16[320,432]{1,0:T(8,128)(2,1)S(1)} %bitcast.22), channel_id=1, source_target_pairs={{0,768},{256,0},{512,256},{768,512},{1,769},{257,1},{513,257},{769... | collective-permute-start | bytes 829448 | tf_op jit(solution)/shard_map/ppermute | solution.py:40
  49.8 4.1 %collective-permute-done.6.w3 = bf16[320,432]{1,0:T(8,128)(2,1)S(1)} collective-permute-done((bf16[320,432]{1,0:T(8,128)(2,1)S(1)}, bf16[320,432]{1,0:T(8,128)(2,1)S(1)}, u32[]{:S(2)}, u32[]{:S(2)}) %collective-permute-start.6) | collective-permute-done | bytes 276512 | tf_op jit(solution)/shard_map/ppermute | solution.py:40
  53.9 0.3 collective-permute-done.5.w2
  54.2 9.1 %collective-permute-done.4.w1 = bf16[320,432]{1,0:T(8,128)(2,1)S(1)} collective-permute-done((bf16[320,432]{1,0:T(8,128)(2,1)S(1)}, bf16[320,432]{1,0:T(8,128)(2,1)S(1)}, u32[]{:S(2)}, u32[]{:S(2)}) %collective-permute-start.4) | collective-permute-done | bytes 276512 | tf_op jit(solution)/shard_map/ppermute | solution.py:40
  63.3 2.4 %shard_map.70 = (bf16[4,80,512]{2,1,0:T(8,128)(2,1)S(1)}, bf16[4,80,512]{2,1,0:T(8,128)(2,1)}, bf16[4,80,512]{2,1,0:T(8,128)(2,1)}, bf16[4,80,512]{2,1,0:T(8,128)(2,1)}) custom-call(s32[5]{0:T(128)S(1)} %stack.32.place, bf16[320,432]{1,0:T(8,128)(2,1)S(1)} %bitcast.23, bf16[320,432]{1,0:T(8,128)(2,1)S(1)} %collective-permute-done.4.w1, ...), custom_call_target="tpu_custom_call" | custom-call | flops 566231040 | bytes 2859028 | tf_op jit(solution)/shard_map/pallas_call | solution.py:60
  65.7 3.1 %collective-permute-start.7 = (bf16[4,80,512]{2,1,0:T(8,128)(2,1)}, bf16[4,80,512]{2,1,0:T(8,128)(2,1)}, u32[]{:S(2)}, u32[]{:S(2)}) collective-permute-start(bf16[4,80,512]{2,1,0:T(8,128)(2,1)} %get-tuple-element.30), channel_id=1, source_target_pairs={{0,1},{1,2},{2,3},{3,0},{4,5},{5,6},{6,7},{7,4},{8,9},{9,10},{10,1... | collective-permute-start | bytes 983048 | tf_op jit(solution)/shard_map/ppermute | solution.py:40
  68.8 10.3 %collective-permute-start.8 = (bf16[4,80,512]{2,1,0:T(8,128)(2,1)}, bf16[4,80,512]{2,1,0:T(8,128)(2,1)}, u32[]{:S(2)}, u32[]{:S(2)}) collective-permute-start(bf16[4,80,512]{2,1,0:T(8,128)(2,1)} %get-tuple-element.31), channel_id=1, source_target_pairs={{0,2},{1,3},{2,0},{3,1},{4,6},{5,7},{6,4},{7,5},{8,10},{9,11},{10,... | collective-permute-start | bytes 983048 | tf_op jit(solution)/shard_map/ppermute | solution.py:40
  79.2 1.9 %collective-permute-start.9 = (bf16[4,80,512]{2,1,0:T(8,128)(2,1)}, bf16[4,80,512]{2,1,0:T(8,128)(2,1)}, u32[]{:S(2)}, u32[]{:S(2)}) collective-permute-start(bf16[4,80,512]{2,1,0:T(8,128)(2,1)} %get-tuple-element.32), channel_id=1, source_target_pairs={{0,3},{1,0},{2,1},{3,2},{4,7},{5,4},{6,5},{7,6},{8,11},{9,8},{10,9... | collective-permute-start | bytes 983048 | tf_op jit(solution)/shard_map/ppermute | solution.py:40
  81.1 2.5 %shard_map.71 = (f32[432,256]{1,0:T(8,128)S(1)}, f32[432,256]{1,0:T(8,128)}) custom-call(s32[5]{0:T(128)S(1)} %stack.32.place, bf16[320,432]{1,0:T(8,128)(2,1)S(1)} %bitcast.24, bf16[320,432]{1,0:T(8,128)(2,1)S(1)} %collective-permute-done.4.w1, bf16[320,432]{1,0:T(8,128)(2,1)S(1)} %collective-permute-done.5.w2, ...), custom_call_target="tpu_custom_call" | custom-call | flops 566231040 | bytes 3080212 | tf_op jit(solution)/shard_map/pallas_call | solution.py:60
  83.6 3.1 %collective-permute-start.16 = (f32[432,256]{1,0:T(8,128)}, f32[432,256]{1,0:T(8,128)S(1)}, u32[]{:S(2)}, u32[]{:S(2)}) collective-permute-start(f32[432,256]{1,0:T(8,128)} %get-tuple-element.45), channel_id=1, source_target_pairs={{0,16},{16,0},{1,17},{17,1},{2,18},{18,2},{3,19},{19,3},{4,20},{20... | collective-permute-start | bytes 1327112 | tf_op jit(solution)/shard_map/ppermute | solution.py:35
  86.7 0.0 all-to-all-done
  86.7 0.7 shard_map.72
  87.4 1.9 %collective-permute-start.11 = (bf16[4,40,432]{2,1,0:T(8,128)(2,1)S(1)}, bf16[4,40,432]{2,1,0:T(8,128)(2,1)S(1)}, u32[]{:S(2)}, u32[]{:S(2)}) collective-permute-start(bf16[4,40,432]{2,1,0:T(8,128)(2,1)S(1)} %get-tuple-element.38), channel_id=1, source_target_pairs={{0,32},{32,0},{64,96},{96,64},{128,160},{160,128},{192,224},{224,1... | collective-permute-start | bytes 414728 | tf_op jit(solution)/shard_map/ppermute | solution.py:35
  89.3 0.0 collective-permute-done.7.g1
  89.4 5.3 %collective-permute-done.9.g3 = bf16[4,80,512]{2,1,0:T(8,128)(2,1)} collective-permute-done((bf16[4,80,512]{2,1,0:T(8,128)(2,1)}, bf16[4,80,512]{2,1,0:T(8,128)(2,1)}, u32[]{:S(2)}, u32[]{:S(2)}) %collective-permute-start.9) | collective-permute-done | bytes 327712 | tf_op jit(solution)/shard_map/ppermute | solution.py:40
  94.7 1.3 shard_map.73
  96.0 14.8 %collective-permute-start.10 = (bf16[80,512]{1,0:T(8,128)(2,1)S(1)}, bf16[80,512]{1,0:T(8,128)(2,1)S(1)}, u32[]{:S(2)}, u32[]{:S(2)}) collective-permute-start(bf16[80,512]{1,0:T(8,128)(2,1)S(1)} %get-tuple-element.37), channel_id=1, source_target_pairs={{0,4},{4,8},{8,12},{12,0},{16,28},{20,16},{24,20},{28,24},{1,5},{5... | collective-permute-start | bytes 245768 | tf_op jit(solution)/shard_map/ppermute | solution.py:50
  110.9 1.9 %collective-permute-start.13 = (bf16[80,512]{1,0:T(8,128)(2,1)S(1)}, bf16[80,512]{1,0:T(8,128)(2,1)S(1)}, u32[]{:S(2)}, u32[]{:S(2)}) collective-permute-start(bf16[80,512]{1,0:T(8,128)(2,1)S(1)} %get-tuple-element.40), channel_id=1, source_target_pairs={{0,12},{4,0},{8,4},{12,8},{16,20},{20,24},{24,28},{28,16},{1,13},{... | collective-permute-start | bytes 245768 | tf_op jit(solution)/shard_map/ppermute | solution.py:50
  112.8 0.6 shard_map.74
  113.4 12.3 %collective-permute-start.12 = (bf16[80,512]{1,0:T(8,128)(2,1)S(1)}, bf16[80,512]{1,0:T(8,128)(2,1)S(1)}, u32[]{:S(2)}, u32[]{:S(2)}) collective-permute-start(bf16[80,512]{1,0:T(8,128)(2,1)S(1)} %shard_map.75), channel_id=1, source_target_pairs={{0,4},{4,8},{8,12},{12,0},{16,28},{20,16},{24,20},{28,24},{1,5},{5... | collective-permute-start | bytes 245768 | tf_op jit(solution)/shard_map/ppermute | solution.py:50
  125.8 14.4 %collective-permute-start.14 = (bf16[2,40,432]{2,1,0:T(8,128)(2,1)S(1)}, bf16[2,40,432]{2,1,0:T(8,128)(2,1)S(1)}, u32[]{:S(2)}, u32[]{:S(2)}) collective-permute-start(bf16[2,40,432]{2,1,0:T(8,128)(2,1)S(1)} %get-tuple-element.41), channel_id=1, source_target_pairs={{0,64},{32,96},{64,0},{96,32},{128,192},{160,224},{192,128},{224,1... | collective-permute-start | bytes 207368 | tf_op jit(solution)/shard_map/ppermute | solution.py:35
  140.2 2.7 %collective-permute-done.14.got = bf16[2,40,432]{2,1,0:T(8,128)(2,1)S(1)} collective-permute-done((bf16[2,40,432]{2,1,0:T(8,128)(2,1)S(1)}, bf16[2,40,432]{2,1,0:T(8,128)(2,1)S(1)}, u32[]{:S(2)}, u32[]{:S(2)}) %collective-permute-start.14) | collective-permute-done | bytes 69152 | tf_op jit(solution)/shard_map/ppermute | solution.py:35
  142.9 0.6 shard_map.76
  143.5 1.9 %collective-permute-start.17 = (bf16[1,40,432]{2,1,0:T(8,128)(2,1)S(1)}, bf16[1,40,432]{2,1,0:T(8,128)(2,1)S(1)}, u32[]{:S(2)}, u32[]{:S(2)}) collective-permute-start(bf16[1,40,432]{2,1,0:T(8,128)(2,1)S(1)} %get-tuple-element.46), channel_id=1, source_target_pairs={{0,128},{32,160},{64,192},{96,224},{128,0},{160,32},{192,64},{224,... | collective-permute-start | bytes 103688 | tf_op jit(solution)/shard_map/ppermute | solution.py:35
  145.5 1.9 %collective-permute-start.15 = (bf16[80,256]{1,0:T(8,128)(2,1)S(1)}, bf16[80,256]{1,0:T(8,128)(2,1)S(1)}, u32[]{:S(2)}, u32[]{:S(2)}) collective-permute-start(bf16[80,256]{1,0:T(8,128)(2,1)S(1)} %get-tuple-element.44), channel_id=1, source_target_pairs={{0,16},{16,0},{1,17},{17,1},{2,18},{18,2},{3,19},{19,3},{4,20},{20... | collective-permute-start | bytes 122888 | tf_op jit(solution)/shard_map/ppermute | solution.py:35
  147.5 1.0 fusion.9
  148.5 5.5 %collective-permute-done.17.got = bf16[1,40,432]{2,1,0:T(8,128)(2,1)S(1)} collective-permute-done((bf16[1,40,432]{2,1,0:T(8,128)(2,1)S(1)}, bf16[1,40,432]{2,1,0:T(8,128)(2,1)S(1)}, u32[]{:S(2)}, u32[]{:S(2)}) %collective-permute-start.17) | collective-permute-done | bytes 34592 | tf_op jit(solution)/shard_map/ppermute | solution.py:35
  153.9 0.6 shard_map.78
  154.6 0.6 copy.7
  (27 shorter events, 0.2 us)
Async XLA Ops:
  0.6 10.4 %collective-permute-start = (bf16[40,432]{1,0:T(8,128)(2,1)}, bf16[40,432]{1,0:T(8,128)(2,1)S(1)}, u32[]{:S(2)}, u32[]{:S(2)}) collective-permute-start(bf16[40,432]{1,0:T(8,128)(2,1)} %own.1), channel_id=1, source_target_pairs={{0,128},{32,160},{64,192},{96,224},{128,0},{160,32},{192,64},{224,... | collective-permute-start | bytes 103688 | tf_op jit(solution)/shard_map/ppermute | solution.py:35
  11.0 0.9 copy-start.3
  12.0 1.3 copy-start.5
  13.3 1.1 copy-start.6
  14.4 5.2 %copy-start = (bf16[40,432]{1,0:T(8,128)(2,1)S(1)}, bf16[40,432]{1,0:T(8,128)(2,1)}, u32[]{:S(2)}) copy-start(bf16[40,432]{1,0:T(8,128)(2,1)} %own.1) | copy-start | bytes 103684
  14.4 10.2 %copy-start.4 = (bf16[256,432]{0,1:T(8,128)(2,1)S(1)}, bf16[256,432]{0,1:T(8,128)(2,1)}, u32[]{:S(2)}) copy-start(bf16[256,432]{0,1:T(8,128)(2,1)} %param.4) | copy-start | bytes 663556
  16.2 8.4 %collective-permute-start.3 = (bf16[1712,256]{1,0:T(8,128)(2,1)S(1)}, bf16[1712,256]{1,0:T(8,128)(2,1)S(1)}, u32[]{:S(2)}, u32[]{:S(2)}) collective-permute-start(bf16[1712,256]{1,0:T(8,128)(2,1)S(1)} %get-tuple-element.26), channel_id=1, source_target_pairs={{0,16},{16,0},{1,17},{17,1},{2,18},{18,2},{3,19},{19,3},{4,20},{20... | collective-permute-start | bytes 2629640 | tf_op jit(solution)/shard_map/ppermute | solution.py:35
  19.7 12.2 %collective-permute-start.1 = (bf16[2,40,432]{2,1,0:T(8,128)(2,1)S(1)}, bf16[2,40,432]{2,1,0:T(8,128)(2,1)S(1)}, u32[]{:S(2)}, u32[]{:S(2)}) collective-permute-start(bf16[2,40,432]{2,1,0:T(8,128)(2,1)S(1)} %pad_maximum_fusion.1), channel_id=1, source_target_pairs={{0,64},{32,96},{64,0},{96,32},{128,192},{160,224},{192,128},{224,1... | collective-permute-start | bytes 207368 | tf_op jit(solution)/shard_map/ppermute | solution.py:35
  26.7 0.8 copy-start.7
  27.5 59.1 %all-to-all-start = ((bf16[4,320,432]{2,1,0:T(8,128)(2,1)}), bf16[4,320,432]{2,1,0:T(8,128)(2,1)S(1)}, u32[]{:S(2)}, u32[]{:S(2)}) async-start(bf16[4,320,432]{2,1,0:T(8,128)(2,1)} %bitcast.9), calls=%async_computation | async-start | bytes 2621440 | tf_op jit(solution)/shard_map/all_to_all | solution.py:208
  31.9 31.4 %copy-start.8 = (bf16[432,512]{1,0:T(8,128)(2,1)S(1)}, bf16[432,512]{1,0:T(8,128)(2,1)}, u32[]{:S(2)}) copy-start(bf16[432,512]{1,0:T(8,128)(2,1)} %copy-done.7) | copy-start | bytes 1327108
  31.9 7.7 %collective-permute-start.2 = (bf16[4,40,432]{2,1,0:T(8,128)(2,1)S(1)}, bf16[4,40,432]{2,1,0:T(8,128)(2,1)S(1)}, u32[]{:S(2)}, u32[]{:S(2)}) collective-permute-start(bf16[4,40,432]{2,1,0:T(8,128)(2,1)S(1)} %pad_maximum_fusion), channel_id=1, source_target_pairs={{0,32},{32,0},{64,96},{96,64},{128,160},{160,128},{192,224},{224,1... | collective-permute-start | bytes 414728 | tf_op jit(solution)/shard_map/ppermute | solution.py:35
  40.2 13.7 %collective-permute-start.6 = (bf16[320,432]{1,0:T(8,128)(2,1)S(1)}, bf16[320,432]{1,0:T(8,128)(2,1)S(1)}, u32[]{:S(2)}, u32[]{:S(2)}) collective-permute-start(bf16[320,432]{1,0:T(8,128)(2,1)S(1)} %bitcast.20), channel_id=1, source_target_pairs={{0,256},{256,512},{512,768},{768,0},{1,257},{257,513},{513,769},{7... | collective-permute-start | bytes 829448 | tf_op jit(solution)/shard_map/ppermute | solution.py:40
  43.3 10.9 %collective-permute-start.5 = (bf16[320,432]{1,0:T(8,128)(2,1)S(1)}, bf16[320,432]{1,0:T(8,128)(2,1)S(1)}, u32[]{:S(2)}, u32[]{:S(2)}) collective-permute-start(bf16[320,432]{1,0:T(8,128)(2,1)S(1)} %bitcast.21), channel_id=1, source_target_pairs={{0,512},{256,768},{512,0},{768,256},{1,513},{257,769},{513,1},{769... | collective-permute-start | bytes 829448 | tf_op jit(solution)/shard_map/ppermute | solution.py:40
  46.1 17.2 %collective-permute-start.4 = (bf16[320,432]{1,0:T(8,128)(2,1)S(1)}, bf16[320,432]{1,0:T(8,128)(2,1)S(1)}, u32[]{:S(2)}, u32[]{:S(2)}) collective-permute-start(bf16[320,432]{1,0:T(8,128)(2,1)S(1)} %bitcast.22), channel_id=1, source_target_pairs={{0,768},{256,0},{512,256},{768,512},{1,769},{257,1},{513,257},{769... | collective-permute-start | bytes 829448 | tf_op jit(solution)/shard_map/ppermute | solution.py:40
  65.7 17.9 %copy-start.1 = (bf16[4,80,512]{2,1,0:T(8,128)(2,1)}, bf16[4,80,512]{2,1,0:T(8,128)(2,1)S(1)}, u32[]{:S(2)}) copy-start(bf16[4,80,512]{2,1,0:T(8,128)(2,1)S(1)} %get-tuple-element.29.o0) | copy-start | bytes 983044
  65.7 23.6 %collective-permute-start.7 = (bf16[4,80,512]{2,1,0:T(8,128)(2,1)}, bf16[4,80,512]{2,1,0:T(8,128)(2,1)}, u32[]{:S(2)}, u32[]{:S(2)}) collective-permute-start(bf16[4,80,512]{2,1,0:T(8,128)(2,1)} %get-tuple-element.30), channel_id=1, source_target_pairs={{0,1},{1,2},{2,3},{3,0},{4,5},{5,6},{6,7},{7,4},{8,9},{9,10},{10,1... | collective-permute-start | bytes 983048 | tf_op jit(solution)/shard_map/ppermute | solution.py:40
  68.8 20.5 %collective-permute-start.8 = (bf16[4,80,512]{2,1,0:T(8,128)(2,1)}, bf16[4,80,512]{2,1,0:T(8,128)(2,1)}, u32[]{:S(2)}, u32[]{:S(2)}) collective-permute-start(bf16[4,80,512]{2,1,0:T(8,128)(2,1)} %get-tuple-element.31), channel_id=1, source_target_pairs={{0,2},{1,3},{2,0},{3,1},{4,6},{5,7},{6,4},{7,5},{8,10},{9,11},{10,... | collective-permute-start | bytes 983048 | tf_op jit(solution)/shard_map/ppermute | solution.py:40
  79.2 15.5 %collective-permute-start.9 = (bf16[4,80,512]{2,1,0:T(8,128)(2,1)}, bf16[4,80,512]{2,1,0:T(8,128)(2,1)}, u32[]{:S(2)}, u32[]{:S(2)}) collective-permute-start(bf16[4,80,512]{2,1,0:T(8,128)(2,1)} %get-tuple-element.32), channel_id=1, source_target_pairs={{0,3},{1,0},{2,1},{3,2},{4,7},{5,4},{6,5},{7,6},{8,11},{9,8},{10,9... | collective-permute-start | bytes 983048 | tf_op jit(solution)/shard_map/ppermute | solution.py:40
  83.6 11.1 %copy-start.2 = (bf16[4,80,512]{2,1,0:T(8,128)(2,1)S(1)}, bf16[4,80,512]{2,1,0:T(8,128)(2,1)}, u32[]{:S(2)}) copy-start(bf16[4,80,512]{2,1,0:T(8,128)(2,1)} %copy-done.1) | copy-start | bytes 983044
  83.6 63.9 %collective-permute-start.16 = (f32[432,256]{1,0:T(8,128)}, f32[432,256]{1,0:T(8,128)S(1)}, u32[]{:S(2)}, u32[]{:S(2)}) collective-permute-start(f32[432,256]{1,0:T(8,128)} %get-tuple-element.45), channel_id=1, source_target_pairs={{0,16},{16,0},{1,17},{17,1},{2,18},{18,2},{3,19},{19,3},{4,20},{20... | collective-permute-start | bytes 1327112 | tf_op jit(solution)/shard_map/ppermute | solution.py:35
  87.4 25.4 %collective-permute-start.11 = (bf16[4,40,432]{2,1,0:T(8,128)(2,1)S(1)}, bf16[4,40,432]{2,1,0:T(8,128)(2,1)S(1)}, u32[]{:S(2)}, u32[]{:S(2)}) collective-permute-start(bf16[4,40,432]{2,1,0:T(8,128)(2,1)S(1)} %get-tuple-element.38), channel_id=1, source_target_pairs={{0,32},{32,0},{64,96},{96,64},{128,160},{160,128},{192,224},{224,1... | collective-permute-start | bytes 414728 | tf_op jit(solution)/shard_map/ppermute | solution.py:35
  96.0 17.4 %collective-permute-start.10 = (bf16[80,512]{1,0:T(8,128)(2,1)S(1)}, bf16[80,512]{1,0:T(8,128)(2,1)S(1)}, u32[]{:S(2)}, u32[]{:S(2)}) collective-permute-start(bf16[80,512]{1,0:T(8,128)(2,1)S(1)} %get-tuple-element.37), channel_id=1, source_target_pairs={{0,4},{4,8},{8,12},{12,0},{16,28},{20,16},{24,20},{28,24},{1,5},{5... | collective-permute-start | bytes 245768 | tf_op jit(solution)/shard_map/ppermute | solution.py:50
  110.9 34.6 %collective-permute-start.13 = (bf16[80,512]{1,0:T(8,128)(2,1)S(1)}, bf16[80,512]{1,0:T(8,128)(2,1)S(1)}, u32[]{:S(2)}, u32[]{:S(2)}) collective-permute-start(bf16[80,512]{1,0:T(8,128)(2,1)S(1)} %get-tuple-element.40), channel_id=1, source_target_pairs={{0,12},{4,0},{8,4},{12,8},{16,20},{20,24},{24,28},{28,16},{1,13},{... | collective-permute-start | bytes 245768 | tf_op jit(solution)/shard_map/ppermute | solution.py:50
  113.4 32.0 %collective-permute-start.12 = (bf16[80,512]{1,0:T(8,128)(2,1)S(1)}, bf16[80,512]{1,0:T(8,128)(2,1)S(1)}, u32[]{:S(2)}, u32[]{:S(2)}) collective-permute-start(bf16[80,512]{1,0:T(8,128)(2,1)S(1)} %shard_map.75), channel_id=1, source_target_pairs={{0,4},{4,8},{8,12},{12,0},{16,28},{20,16},{24,20},{28,24},{1,5},{5... | collective-permute-start | bytes 245768 | tf_op jit(solution)/shard_map/ppermute | solution.py:50
  125.8 17.2 %collective-permute-start.14 = (bf16[2,40,432]{2,1,0:T(8,128)(2,1)S(1)}, bf16[2,40,432]{2,1,0:T(8,128)(2,1)S(1)}, u32[]{:S(2)}, u32[]{:S(2)}) collective-permute-start(bf16[2,40,432]{2,1,0:T(8,128)(2,1)S(1)} %get-tuple-element.41), channel_id=1, source_target_pairs={{0,64},{32,96},{64,0},{96,32},{128,192},{160,224},{192,128},{224,1... | collective-permute-start | bytes 207368 | tf_op jit(solution)/shard_map/ppermute | solution.py:35
  143.5 10.4 %collective-permute-start.17 = (bf16[1,40,432]{2,1,0:T(8,128)(2,1)S(1)}, bf16[1,40,432]{2,1,0:T(8,128)(2,1)S(1)}, u32[]{:S(2)}, u32[]{:S(2)}) collective-permute-start(bf16[1,40,432]{2,1,0:T(8,128)(2,1)S(1)} %get-tuple-element.46), channel_id=1, source_target_pairs={{0,128},{32,160},{64,192},{96,224},{128,0},{160,32},{192,64},{224,... | collective-permute-start | bytes 103688 | tf_op jit(solution)/shard_map/ppermute | solution.py:35
  145.5 9.1 %collective-permute-start.15 = (bf16[80,256]{1,0:T(8,128)(2,1)S(1)}, bf16[80,256]{1,0:T(8,128)(2,1)S(1)}, u32[]{:S(2)}, u32[]{:S(2)}) collective-permute-start(bf16[80,256]{1,0:T(8,128)(2,1)S(1)} %get-tuple-element.44), channel_id=1, source_target_pairs={{0,16},{16,0},{1,17},{17,1},{2,18},{18,2},{3,19},{19,3},{4,20},{20... | collective-permute-start | bytes 122888 | tf_op jit(solution)/shard_map/ppermute | solution.py:35

commit v4 on v3

v4 whole, which is shorter than its diff:
```python
import functools
import math

import jax
import jax.numpy as jnp
import numpy as np
from jax import lax
from jax.experimental import pallas as pl
from jax.experimental.pallas import tpu as pltpu
from jax.sharding import Mesh, PartitionSpec as P

COEFF = math.sqrt(2.0 / math.pi)
AXES = ("y", "zl", "c", "zh", "x")
SIZES = (4, 8, 2, 4, 4)
F32, BF16 = jnp.float32, jnp.bfloat16
SMEM = pl.BlockSpec(memory_space=pltpu.SMEM)
VMEM = pl.BlockSpec(memory_space=pltpu.VMEM)
LATER = pl.BlockSpec(memory_space=pl.ANY)
HBM = pl.BlockSpec(memory_space=pltpu.HBM)


def gelu_value(values):
    inner = COEFF * (values + 0.044715 * values * values * values)
    return 0.5 * values * (1.0 + jnp.tanh(inner))


def gelu_slope(values):
    tangent = jnp.tanh(COEFF * (values + 0.044715 * values * values * values))
    return 0.5 * (1.0 + tangent) + 0.5 * values * (1.0 - tangent * tangent) * COEFF * (
        1.0 + 3.0 * 0.044715 * values * values
    )


def swap(value, axis, distance):
    size = lax.axis_size(axis)
    return lax.ppermute(value, axis, [(i, i ^ distance) for i in range(size)])


def shift(value, axis, distance):
    size = lax.axis_size(axis)
    return lax.ppermute(value, axis, [(i, (i + distance) % size) for i in range(size)])


def shift_both(value, distance):
    size = lax.axis_size("zh")
    pairs = [
        (core * size + i, core * size + (i + distance * (1 - 2 * core)) % size)
        for core in range(2)
        for i in range(size)
    ]
    return lax.ppermute(value, ("c", "zh"), pairs)


def dot(left, right, over_left, over_right):
    dims = (((over_left,), (over_right,)), ((), ()))
    return lax.dot_general(left, right, dims, preferred_element_type=F32)


def call(body, outs, specs, args, flops=0, scratch=(), out_specs=None, limit=14):
    moved = sum(a.size * a.dtype.itemsize for a in args) + sum(a.size for a in args)
    return pl.pallas_call(
        body,
        out_shape=[s if isinstance(s, pl.MemoryRef) else jax.ShapeDtypeStruct(*s) for s in outs],
        in_specs=specs,
        out_specs=out_specs or [VMEM] * len(outs),
        scratch_shapes=list(scratch),
        compiler_params=pltpu.CompilerParams(vmem_limit_bytes=limit << 20),
        cost_estimate=pl.CostEstimate(flops=flops, bytes_accessed=moved, transcendentals=0),
    )(*args)


def sort_channels(place, base, cot, pre, send, mine, *, block):
    core, stripe = place[0], base.shape[0]
    lanes = lax.broadcasted_iota(jnp.int32, (stripe, 2 * stripe), 1)
    own = jnp.where(lanes == base[...] + core * block, 1.0, 0.0).astype(BF16)
    other = jnp.where(lanes == base[...] + (1 - core) * block, 1.0, 0.0).astype(BF16)
    for index in range(cot.shape[1] // (2 * stripe)):
        part = cot[:, index * 2 * stripe : (index + 1) * 2 * stripe]
        rows = slice(index * stripe, (index + 1) * stripe)
        send[rows, :] = dot(other, part, 1, 1).astype(BF16)
        mine[rows, :] = dot(own, part, 1, 1).astype(BF16)
    send[mine.shape[0] :, :] = pre[...]


def weight_term(pre, mine, got, after, hidden, term, both, held, sems, *, stripe):
    tokens, channels = pre.shape[1], mine.shape[0]
    copies = [
        pltpu.make_async_copy(mine, both.at[0], sems.at[0]),
        pltpu.make_async_copy(got.at[pl.ds(0, channels)], both.at[1], sems.at[1]),
    ]
    for copy in copies:
        copy.start()
    hidden[:, :tokens] = gelu_value(pre[...].astype(F32)).astype(BF16)
    hidden[:, tokens:] = gelu_value(got[channels:, :].astype(F32)).astype(BF16)
    for index in range(channels // stripe):
        rows = slice(index * stripe, (index + 1) * stripe)
        total = dot(mine[rows, :], hidden[:, :tokens], 1, 1)
        total += dot(got[rows, :], hidden[:, tokens:], 1, 1)
        held[index] = total.astype(BF16)
        copies.append(pltpu.make_async_copy(held.at[index], term.at[index], sems.at[2 + index]))
        copies[-1].start()
    for copy in copies:
        copy.wait()


def split_y(place, parts, after, keep, send):
    bit = place[2] % 2

    def total(index):
        value = parts[0, index].astype(F32)
        for source in range(1, parts.shape[0]):
            value += parts[source, index].astype(F32)
        return value

    for index in range(keep.shape[0]):
        keep[index] = total(2 * index + bit)
        send[index] = total(2 * index + 1 - bit).astype(BF16)


def split_zl(place, kept, got, keep, send, *, width):
    bit = place[2] // width % 2
    for index in range(keep.shape[0]):
        near, far = 2 * index + bit, 2 * index + 1 - bit
        keep[index] = kept[near] + got[near].astype(F32)
        send[index] = (kept[far] + got[far].astype(F32)).astype(BF16)


def sum_scaled(kept, got, out, *, factor):
    out[...] = (kept[0] + got[0].astype(F32)) * factor


def order_rows(place, own, one, two, four, after, rows):
    zl = place[2]
    rows[zl] = own[...]
    rows[zl ^ 4] = one[...]
    for index, offset in enumerate((2, 6)):
        rows[zl ^ offset] = two[index]
    for index, offset in enumerate((1, 5, 3, 7)):
        rows[zl ^ offset] = four[index]


def output_terms(place, w0, w1, w2, w3, hidden, out, weight, held, sems):
    core, y, zh = place[0], place[1], place[3]
    group = out.shape[2]
    pieces = (w0, w1, w2, w3)
    copies = [pltpu.make_async_copy(p, weight.at[k], sems.at[k]) for k, p in enumerate(pieces)]
    for copy in copies:
        copy.start()
    for k, piece in enumerate(pieces):
        total = dot(piece[...], hidden[...], 1, 0).astype(BF16)
        target = (y + k - zh + 4) * (1 + 2 * core) % 4
        for x in range(out.shape[0]):
            held[k, x] = total[x * group : (x + 1) * group]
        copies.append(pltpu.make_async_copy(held.at[k], out.at[:, target], sems.at[4 + k]))
        copies[-1].start()
    for copy in copies:
        copy.wait()


def sum_x(parts, after, s0, s1, s2, s3):
    for index, out in enumerate((s0, s1, s2, s3)):
        value = parts[0, index].astype(F32) + parts[1, index].astype(F32)
        value += parts[2, index].astype(F32) + parts[3, index].astype(F32)
        out[...] = value.astype(BF16)


def sum_step(s1, got, after, t1):
    t1[...] = (s1[...].astype(F32) + got[...].astype(F32)).astype(BF16)


def sum_last(s0, u, v, kept, given):
    half = kept.shape[1]
    total = (s0[...].astype(F32) + (u[...].astype(F32) + v[...].astype(F32))).astype(BF16)
    kept[...] = total[:, :half]
    given[...] = total[:, half:]


def gate(value, after, out):
    pass


def hold(value, after):
    return pl.pallas_call(
        gate,
        out_shape=pltpu.HBM(value.shape, value.dtype),
        in_specs=[HBM, LATER],
        out_specs=HBM,
        input_output_aliases={0: 0},
        compiler_params=pltpu.CompilerParams(vmem_limit_bytes=14 << 20),
    )(value, after)


def interleave(place, kept, given, out):
    core = place[0]
    for index in range(kept.shape[0]):
        out[index, core] = kept[index]
        out[index, 1 - core] = given[index]


def hidden_terms(place, weight, both, own, other):
    y, count, stripe = place[1], weight.shape[0], weight.shape[1]
    own[...] = jnp.zeros_like(own)
    other[...] = jnp.zeros_like(other)
    for k in range(count):
        rows = pl.ds(pl.multiple_of((y + k) % count * stripe, 16), stripe)
        own[...] += dot(weight[k], both[0, rows, :], 0, 0)
        other[...] += dot(weight[k], both[1, rows, :], 0, 0)


def local(base, pre_act, weight_out, cotangent):
    n_y, n_zl, n_x = SIZES[0], SIZES[1], SIZES[4]
    tokens, hid = pre_act.shape
    block = weight_out.shape[0]
    stripe = n_zl * block
    group = stripe // n_x
    channels = n_y * stripe
    place = jnp.stack([lax.axis_index(a) for a in ("c", "y", "zl", "zh", "x")]).astype(jnp.int32)
    factor = 1.0 / math.sqrt(tokens * n_y * n_zl * 2)
    work = 2 * tokens * channels * hid * 2
    pre = pre_act.T

    one = swap(weight_out, "zl", 4)
    first = jnp.stack([weight_out, one])
    send, mine = call(
        functools.partial(sort_channels, block=block),
        [((channels + hid, tokens), BF16), ((channels, tokens), BF16)],
        [SMEM, VMEM, VMEM, VMEM],
        (place, base, cotangent, pre),
        flops=2 * 4 * tokens * stripe * stripe * 2 * 2,
        limit=56,
    )
    two = swap(first, "zl", 2)
    second = jnp.concatenate([first, two])
    got = swap(hold(send, two), "c", 1)
    hidden, term, both = call(
        functools.partial(weight_term, stripe=stripe),
        [((hid, 2 * tokens), BF16), pltpu.HBM((n_y, stripe, hid), BF16), pltpu.HBM((2, channels, tokens), BF16)],
        [VMEM] * 3 + [LATER],
        (pre, mine, got, second),
        flops=work,
        scratch=[pltpu.VMEM((n_y, stripe, hid), BF16), pltpu.SemaphoreType.DMA((2 + n_y,))],
        out_specs=[VMEM, HBM, HBM],
    )

    four = swap(second, "zl", 1)
    (rows,) = call(
        order_rows,
        [((n_zl, block, hid), BF16)],
        [SMEM] + [VMEM] * 4 + [LATER],
        (place, weight_out, one, two, four, hidden),
    )
    w0 = rows.reshape(stripe, hid)
    w1, w3, w2 = shift(w0, "y", -1), shift(w0, "y", 1), shift(w0, "y", 2)

    term = lax.all_to_all(hold(term, rows), "y", 0, 0)

    parts, weight = call(
        output_terms,
        [pltpu.HBM((n_x, n_y, group, 2 * tokens), BF16), pltpu.HBM((n_y, stripe, hid), BF16)],
        [SMEM] + [VMEM] * 5,
        (place, w0, w1, w2, w3, hidden),
        flops=work,
        scratch=[pltpu.VMEM((n_y, n_x, group, 2 * tokens), BF16), pltpu.SemaphoreType.DMA((2 * n_y,))],
        out_specs=[HBM, HBM],
    )
    parts = lax.all_to_all(parts, "x", 0, 0)

    own, other = call(
        hidden_terms,
        [((hid, tokens), F32)] * 2,
        [SMEM, VMEM, VMEM],
        (place, weight, both),
        flops=work,
    )
    whole, half = ((group, 2 * tokens), BF16), ((group, tokens), BF16)
    quarter = n_zl // 2
    keep, send = call(
        split_y,
        [((quarter, block, hid), F32), ((quarter, block, hid), BF16)],
        [SMEM, VMEM, LATER],
        (place, term.reshape(n_y, n_zl, block, hid), own),
    )
    keep, send = call(
        functools.partial(split_zl, width=2),
        [((quarter // 2, block, hid), F32), ((quarter // 2, block, hid), BF16)],
        [SMEM, VMEM, VMEM],
        (place, keep, swap(send, "zl", 1)),
    )
    s0, s1, s2, s3 = call(sum_x, [whole] * 4, [VMEM, LATER], (parts, keep))
    got2 = shift_both(s2, 1)
    keep, send = call(
        functools.partial(split_zl, width=4),
        [((quarter // 4, block, hid), F32), ((quarter // 4, block, hid), BF16)],
        [SMEM, VMEM, VMEM],
        (place, keep, swap(send, "zl", 2)),
    )
    (t1,) = call(sum_step, [whole], [VMEM] * 2 + [LATER], (s1, got2, keep))
    u, v = shift_both(t1, 1), shift_both(s3, -1)
    kept, given = call(sum_last, [half] * 2, [VMEM] * 3, (s0, u, v))
    (grad_weight,) = call(
        functools.partial(sum_scaled, factor=factor),
        [((block, hid), F32)],
        [VMEM] * 2,
        (keep, swap(send, "zl", 4)),
    )
    given = swap(given, "c", 1)
    (output,) = call(
        interleave,
        [((group // block, 2, block, tokens), BF16)],
        [SMEM, VMEM, VMEM],
        (place, kept.reshape(-1, block, tokens), given.reshape(-1, block, tokens)),
    )
    output = output.reshape(-1, tokens).T
    grad_hidden = own + swap(other, "c", 1)
    grad_pre = (grad_hidden * gelu_slope(pre.astype(F32))).astype(BF16).T
    return (output, grad_pre, grad_weight)


def solution(mesh):
    fine = Mesh(np.asarray(mesh.devices).reshape(SIZES), AXES)
    dp, tensor = AXES[:3], AXES[3:]
    mapped = jax.shard_map(
        local,
        mesh=fine,
        in_specs=(P(None, None), P(dp, tensor), P(dp, tensor), P(dp, None)),
        out_specs=(P(dp, tensor), P(dp, tensor), P(dp, tensor)),
        check_vma=False,
    )

    def run(pre_act, weight_out, cotangent):
        block = weight_out.shape[0] // (SIZES[0] * SIZES[1] * SIZES[2])
        k = np.arange(SIZES[1] * block)
        base = (k // block * (2 * block) + k % block).astype(np.int32)[:, None]
        return mapped(jnp.asarray(base), pre_act, weight_out, cotangent)

    return run
```

time: 156 us -> 159 us (1.019)
  the two profiles are of different devices: /device:TPU:11 before, /device:TPU:1 now
where the time goes in v4:
time: 159 us; the launch traced here: 156 us
  starting transfers between devices  88.4 us (56%)
  waiting for transfers between devices  45.6 us (29%)
  Pallas kernels  14.8 us (9%)
  local copies, waits for them, and re-layouts  3.25 us (2%)
  other arithmetic  2.85 us (2%)
    ppermute x9, starting transfers between devices, swap(): return lax.ppermute(value, axis, [(i, i ^ distance) for i in range(size)])  42.6 us
    ppermute x3, starting transfers between devices, shift_both(): return lax.ppermute(value, ('c', 'zh'), pairs)  28 us
    ppermute x3, waiting for transfers between devices, shift(): lax.ppermute(value, axis, [(i, (i + distance) % size) for i in range(size)])  20.5 us
    ppermute x9, waiting for transfers between devices, swap(): return lax.ppermute(value, axis, [(i, i ^ distance) for i in range(size)])  18.2 us
    pallas_call x13, Pallas kernels, call(): pl.pallas_call(body, out_shape=[s if isinstance(s, pl.MemoryRef) else jax...  14.8 us
    ppermute x3, starting transfers between devices, shift(): lax.ppermute(value, axis, [(i, (i + distance) % size) for i in range(size)])  10.7 us
    ppermute x3, waiting for transfers between devices, shift_both(): return lax.ppermute(value, ('c', 'zh'), pairs)  6.91 us
    all_to_all x1, starting transfers between devices, local(): parts = lax.all_to_all(parts, 'x', 0, 0)  3.55 us
  transfers between devices with their start and end apart: 17, of which 8 were waited for; matrix products, arithmetic and copies ran while one was open for 2% of the time, Pallas kernels for 8%

profile of v4, /device:TPU:1, one launch (start us, length us, event | category | flops | bytes accessed | tf_op | source)
XLA Modules:
  0.0 155.9 jit_solution(15976845081898593919)
XLA Ops:
  0.6 9.6 %collective-permute-start = (bf16[40,432]{1,0:T(8,128)(2,1)}, bf16[40,432]{1,0:T(8,128)(2,1)S(1)}, u32[]{:S(2)}, u32[]{:S(2)}) collective-permute-start(bf16[40,432]{1,0:T(8,128)(2,1)} %own.1), channel_id=1, source_target_pairs={{0,128},{32,160},{64,192},{96,224},{128,0},{160,32},{192,64},{224,... | collective-permute-start | bytes 103688 | tf_op jit(solution)/shard_map/ppermute | solution.py:36
  10.3 0.6 stack.32.place
  10.9 1.0 collective-permute-done.one
  11.9 0.8 pad_maximum_fusion.1
  12.7 4.9 %collective-permute-start.1 = (bf16[2,40,432]{2,1,0:T(8,128)(2,1)S(1)}, bf16[2,40,432]{2,1,0:T(8,128)(2,1)S(1)}, u32[]{:S(2)}, u32[]{:S(2)}) collective-permute-start(bf16[2,40,432]{2,1,0:T(8,128)(2,1)S(1)} %pad_maximum_fusion.1), channel_id=1, source_target_pairs={{0,64},{32,96},{64,0},{96,32},{128,192},{160,224},{192,128},{224,1... | collective-permute-start | bytes 207368 | tf_op jit(solution)/shard_map/ppermute | solution.py:36
  17.6 3.8 %shard_map.67 = (bf16[1712,256]{1,0:T(8,128)(2,1)}, bf16[1280,256]{1,0:T(8,128)(2,1)}) custom-call(s32[5]{0:T(128)} %stack.32.place, s32[320,1]{1,0:T(8,128)} %constant.35.clone.base, bf16[256,2560]{1,0:T(8,128)(2,1)} %cot.1, bf16[432,256]{1,0:T(8,128)(2,1)} %bitcast.27), custom_call_target="tpu_custom_call" | custom-call | flops 838860800 | bytes 2299481 | tf_op jit(solution)/shard_map/pallas_call | solution.py:61
  21.4 13.4 %collective-permute-start.3 = (bf16[1712,256]{1,0:T(8,128)(2,1)}, bf16[1712,256]{1,0:T(8,128)(2,1)S(1)}, u32[]{:S(2)}, u32[]{:S(2)}) collective-permute-start(bf16[1712,256]{1,0:T(8,128)(2,1)} %shard_map.68), channel_id=1, source_target_pairs={{0,16},{16,0},{1,17},{17,1},{2,18},{18,2},{3,19},{19,3},{4,20},{20... | collective-permute-start | bytes 2629640 | tf_op jit(solution)/shard_map/ppermute | solution.py:36
  34.9 1.9 %collective-permute-start.2 = (bf16[4,40,432]{2,1,0:T(8,128)(2,1)S(1)}, bf16[4,40,432]{2,1,0:T(8,128)(2,1)S(1)}, u32[]{:S(2)}, u32[]{:S(2)}) collective-permute-start(bf16[4,40,432]{2,1,0:T(8,128)(2,1)S(1)} %pad_maximum_fusion.after), channel_id=1, source_target_pairs={{0,32},{32,0},{64,96},{96,64},{128,160},{160,128},{192,224},{224,1... | collective-permute-start | bytes 414728 | tf_op jit(solution)/shard_map/ppermute | solution.py:36
  36.8 0.3 collective-permute-done.3.got
  37.1 1.8 %shard_map.69 = (bf16[432,512]{1,0:T(8,128)(2,1)S(1)}, bf16[4,320,432]{2,1,0:T(8,128)(2,1)}, bf16[2,1280,256]{2,1,0:T(8,128)(2,1)}) custom-call(bf16[432,256]{1,0:T(8,128)(2,1)S(1)} %bitcast.28, bf16[1280,256]{1,0:T(8,128)(2,1)S(1)} %copy-done.5, bf16[1712,256]{1,0:T(8,128)(2,1)S(1)} %collective-permute-done.3.got, bf16[4,40,432]{2,1,0:T(8,128)(2,1)S(1)} %pad_maximum_fusion.after), custom_call_target="tpu_custom_call" | custom-call | flops 566231040 | bytes 2836992 | tf_op jit(solution)/shard_map/pallas_call | solution.py:61
  38.9 3.7 %collective-permute-done.2.four = bf16[4,40,432]{2,1,0:T(8,128)(2,1)S(1)} collective-permute-done((bf16[4,40,432]{2,1,0:T(8,128)(2,1)S(1)}, bf16[4,40,432]{2,1,0:T(8,128)(2,1)S(1)}, u32[]{:S(2)}, u32[]{:S(2)}) %collective-permute-start.2) | collective-permute-done | bytes 138272 | tf_op jit(solution)/shard_map/ppermute | solution.py:36
  42.6 0.6 shard_map.70.after
  43.2 3.6 %all-to-all-start.1 = ((bf16[4,320,432]{2,1,0:T(8,128)(2,1)}), bf16[4,320,432]{2,1,0:T(8,128)(2,1)S(1)}, u32[]{:S(2)}, u32[]{:S(2)}) async-start(bf16[4,320,432]{2,1,0:T(8,128)(2,1)} %shard_map.72), calls=%async_computation.1 | async-start | bytes 2621440 | tf_op jit(solution)/shard_map/all_to_all | solution.py:255
  46.8 3.3 %collective-permute-start.6 = (bf16[320,432]{1,0:T(8,128)(2,1)S(1)}, bf16[320,432]{1,0:T(8,128)(2,1)S(1)}, u32[]{:S(2)}, u32[]{:S(2)}) collective-permute-start(bf16[320,432]{1,0:T(8,128)(2,1)S(1)} %bitcast.19), channel_id=1, source_target_pairs={{0,256},{256,512},{512,768},{768,0},{1,257},{257,513},{513,769},{7... | collective-permute-start | bytes 829448 | tf_op jit(solution)/shard_map/ppermute | solution.py:41
  50.1 4.3 %collective-permute-start.5 = (bf16[320,432]{1,0:T(8,128)(2,1)S(1)}, bf16[320,432]{1,0:T(8,128)(2,1)S(1)}, u32[]{:S(2)}, u32[]{:S(2)}) collective-permute-start(bf16[320,432]{1,0:T(8,128)(2,1)S(1)} %bitcast.20), channel_id=1, source_target_pairs={{0,512},{256,768},{512,0},{768,256},{1,513},{257,769},{513,1},{769... | collective-permute-start | bytes 829448 | tf_op jit(solution)/shard_map/ppermute | solution.py:41
  54.4 3.1 %collective-permute-start.4 = (bf16[320,432]{1,0:T(8,128)(2,1)S(1)}, bf16[320,432]{1,0:T(8,128)(2,1)S(1)}, u32[]{:S(2)}, u32[]{:S(2)}) collective-permute-start(bf16[320,432]{1,0:T(8,128)(2,1)S(1)} %bitcast.21), channel_id=1, source_target_pairs={{0,768},{256,0},{512,256},{768,512},{1,769},{257,1},{513,257},{769... | collective-permute-start | bytes 829448 | tf_op jit(solution)/shard_map/ppermute | solution.py:41
  57.5 13.1 %collective-permute-done.6.w3 = bf16[320,432]{1,0:T(8,128)(2,1)S(1)} collective-permute-done((bf16[320,432]{1,0:T(8,128)(2,1)S(1)}, bf16[320,432]{1,0:T(8,128)(2,1)S(1)}, u32[]{:S(2)}, u32[]{:S(2)}) %collective-permute-start.6) | collective-permute-done | bytes 276512 | tf_op jit(solution)/shard_map/ppermute | solution.py:41
  70.6 7.4 %collective-permute-done.5.w2 = bf16[320,432]{1,0:T(8,128)(2,1)S(1)} collective-permute-done((bf16[320,432]{1,0:T(8,128)(2,1)S(1)}, bf16[320,432]{1,0:T(8,128)(2,1)S(1)}, u32[]{:S(2)}, u32[]{:S(2)}) %collective-permute-start.5) | collective-permute-done | bytes 276512 | tf_op jit(solution)/shard_map/ppermute | solution.py:41
  78.0 0.0 collective-permute-done.4.w1
  78.0 2.2 %shard_map.71 = (bf16[4,4,80,512]{3,2,1,0:T(8,128)(2,1)}, bf16[4,320,432]{2,1,0:T(8,128)(2,1)}) custom-call(s32[5]{0:T(128)S(1)} %copy-done.4, bf16[320,432]{1,0:T(8,128)(2,1)S(1)} %bitcast.22, bf16[320,432]{1,0:T(8,128)(2,1)S(1)} %collective-permute-done.4.w1, bf16[320,432]{1,0:T(8,128)(2,1)S(1)} %collective-permute-done.5.w2, ...), custom_call_target="tpu_custom_call" | custom-call | flops 566231040 | bytes 2322457 | tf_op jit(solution)/shard_map/pallas_call | solution.py:61
  80.2 0.0 all-to-all-done.1
  80.2 3.6 %all-to-all-start = ((bf16[4,4,80,512]{3,2,1,0:T(8,128)(2,1)}), bf16[4,4,80,512]{3,2,1,0:T(8,128)(2,1)S(1)}, u32[]{:S(2)}, u32[]{:S(2)}) async-start(bf16[4,4,80,512]{3,2,1,0:T(8,128)(2,1)} %get-tuple-element.27), calls=%async_computation | async-start | bytes 2621440 | tf_op jit(solution)/shard_map/all_to_all | solution.py:266
  83.8 1.3 copy-done
  85.1 1.3 copy-done.1
  86.4 2.4 %shard_map.73 = (f32[432,256]{1,0:T(8,128)S(1)}, f32[432,256]{1,0:T(8,128)}) custom-call(s32[5]{0:T(128)S(1)} %copy-done.4, bf16[4,320,432]{2,1,0:T(8,128)(2,1)S(1)} %copy-done.1, bf16[2,1280,256]{2,1,0:T(8,128)(2,1)S(1)} %copy-done), custom_call_target="tpu_custom_call" | custom-call | flops 566231040 | bytes 3624985 | tf_op jit(solution)/shard_map/pallas_call | solution.py:61
  88.9 3.6 %collective-permute-start.13 = (f32[432,256]{1,0:T(8,128)}, f32[432,256]{1,0:T(8,128)}, u32[]{:S(2)}, u32[]{:S(2)}) collective-permute-start(f32[432,256]{1,0:T(8,128)} %get-tuple-element.43), channel_id=1, source_target_pairs={{0,16},{16,0},{1,17},{17,1},{2,18},{18,2},{3,19},{19,3},{4,20},{20... | collective-permute-start | bytes 1327112 | tf_op jit(solution)/shard_map/ppermute | solution.py:36
  92.5 0.7 shard_map.74
  93.2 2.1 %collective-permute-start.7 = (bf16[4,40,432]{2,1,0:T(8,128)(2,1)S(1)}, bf16[4,40,432]{2,1,0:T(8,128)(2,1)S(1)}, u32[]{:S(2)}, u32[]{:S(2)}) collective-permute-start(bf16[4,40,432]{2,1,0:T(8,128)(2,1)S(1)} %get-tuple-element.33), channel_id=1, source_target_pairs={{0,32},{32,0},{64,96},{96,64},{128,160},{160,128},{192,224},{224,1... | collective-permute-start | bytes 414728 | tf_op jit(solution)/shard_map/ppermute | solution.py:36
  95.3 5.6 %collective-permute-done.7.got = bf16[4,40,432]{2,1,0:T(8,128)(2,1)S(1)} collective-permute-done((bf16[4,40,432]{2,1,0:T(8,128)(2,1)S(1)}, bf16[4,40,432]{2,1,0:T(8,128)(2,1)S(1)}, u32[]{:S(2)}, u32[]{:S(2)}) %collective-permute-start.7) | collective-permute-done | bytes 138272 | tf_op jit(solution)/shard_map/ppermute | solution.py:36
  100.9 0.6 shard_map.75
  101.5 0.0 all-to-all-done.parts
  101.5 0.2 shard_map.76
  101.7 14.0 %collective-permute-start.8 = (bf16[80,512]{1,0:T(8,128)(2,1)S(1)}, bf16[80,512]{1,0:T(8,128)(2,1)S(1)}, u32[]{:S(2)}, u32[]{:S(2)}) collective-permute-start(bf16[80,512]{1,0:T(8,128)(2,1)S(1)} %get-tuple-element.37), channel_id=1, source_target_pairs={{0,4},{4,8},{8,12},{12,0},{16,28},{20,16},{24,20},{28,24},{1,5},{5... | collective-permute-start | bytes 245768 | tf_op jit(solution)/shard_map/ppermute | solution.py:51
  115.7 2.6 %collective-permute-start.9 = (bf16[2,40,432]{2,1,0:T(8,128)(2,1)S(1)}, bf16[2,40,432]{2,1,0:T(8,128)(2,1)S(1)}, u32[]{:S(2)}, u32[]{:S(2)}) collective-permute-start(bf16[2,40,432]{2,1,0:T(8,128)(2,1)S(1)} %get-tuple-element.38), channel_id=1, source_target_pairs={{0,64},{32,96},{64,0},{96,32},{128,192},{160,224},{192,128},{224,1... | collective-permute-start | bytes 207368 | tf_op jit(solution)/shard_map/ppermute | solution.py:36
  118.2 7.7 %collective-permute-done.9.got = bf16[2,40,432]{2,1,0:T(8,128)(2,1)S(1)} collective-permute-done((bf16[2,40,432]{2,1,0:T(8,128)(2,1)S(1)}, bf16[2,40,432]{2,1,0:T(8,128)(2,1)S(1)}, u32[]{:S(2)}, u32[]{:S(2)}) %collective-permute-start.9) | collective-permute-done | bytes 69152 | tf_op jit(solution)/shard_map/ppermute | solution.py:36
  125.9 0.6 shard_map.77
  126.5 1.9 %collective-permute-start.11 = (bf16[80,512]{1,0:T(8,128)(2,1)S(1)}, bf16[80,512]{1,0:T(8,128)(2,1)S(1)}, u32[]{:S(2)}, u32[]{:S(2)}) collective-permute-start(bf16[80,512]{1,0:T(8,128)(2,1)S(1)} %get-tuple-element.40), channel_id=1, source_target_pairs={{0,12},{4,0},{8,4},{12,8},{16,20},{20,24},{24,28},{28,16},{1,13},{... | collective-permute-start | bytes 245768 | tf_op jit(solution)/shard_map/ppermute | solution.py:51
  128.5 12.1 %collective-permute-start.10 = (bf16[80,512]{1,0:T(8,128)(2,1)S(1)}, bf16[80,512]{1,0:T(8,128)(2,1)S(1)}, u32[]{:S(2)}, u32[]{:S(2)}) collective-permute-start(bf16[80,512]{1,0:T(8,128)(2,1)S(1)} %shard_map.78), channel_id=1, source_target_pairs={{0,4},{4,8},{8,12},{12,0},{16,28},{20,16},{24,20},{28,24},{1,5},{5... | collective-permute-start | bytes 245768 | tf_op jit(solution)/shard_map/ppermute | solution.py:51
  140.5 2.5 %collective-permute-start.14 = (bf16[1,40,432]{2,1,0:T(8,128)(2,1)S(1)}, bf16[1,40,432]{2,1,0:T(8,128)(2,1)S(1)}, u32[]{:S(2)}, u32[]{:S(2)}) collective-permute-start(bf16[1,40,432]{2,1,0:T(8,128)(2,1)S(1)} %get-tuple-element.44), channel_id=1, source_target_pairs={{0,128},{32,160},{64,192},{96,224},{128,0},{160,32},{192,64},{224,... | collective-permute-start | bytes 103688 | tf_op jit(solution)/shard_map/ppermute | solution.py:36
  143.1 0.0 collective-permute-done.11.v
  143.1 6.9 %collective-permute-done.10.u = bf16[80,512]{1,0:T(8,128)(2,1)S(1)} collective-permute-done((bf16[80,512]{1,0:T(8,128)(2,1)S(1)}, bf16[80,512]{1,0:T(8,128)(2,1)S(1)}, u32[]{:S(2)}, u32[]{:S(2)}) %collective-permute-start.10) | collective-permute-done | bytes 81952 | tf_op jit(solution)/shard_map/ppermute | solution.py:51
  150.1 1.9 %collective-permute-start.12 = (bf16[80,256]{1,0:T(8,128)(2,1)S(1)}, bf16[80,256]{1,0:T(8,128)(2,1)S(1)}, u32[]{:S(2)}, u32[]{:S(2)}) collective-permute-start(bf16[80,256]{1,0:T(8,128)(2,1)S(1)} %get-tuple-element.42), channel_id=1, source_target_pairs={{0,16},{16,0},{1,17},{17,1},{2,18},{18,2},{3,19},{19,3},{4,20},{20... | collective-permute-start | bytes 122888 | tf_op jit(solution)/shard_map/ppermute | solution.py:36
  152.0 0.0 collective-permute-done.13
  152.0 2.0 %fusion.9 = bf16[256,432]{0,1:T(8,128)(2,1)} fusion(f32[432,256]{1,0:T(8,128)S(1)} %get-tuple-element.31.after, f32[432,256]{1,0:T(8,128)} %collective-permute-done.13, bf16[256,432]{0,1:T(8,128)(2,1)S(1)} %copy-done.3), kind=kLoop, calls=%fused_computation.16 | loop fusion | flops 2322432 | bytes 1327104 | tf_op jit(solution)/shard_map/transpose | solution.py:315
  154.0 0.0 collective-permute-done.14.got
  154.0 0.6 shard_map.81
  154.7 0.0 collective-permute-done.12
  154.7 1.2 shard_map.80
  (17 shorter events, 0.1 us)
Async XLA Ops:
  0.6 11.2 %collective-permute-start = (bf16[40,432]{1,0:T(8,128)(2,1)}, bf16[40,432]{1,0:T(8,128)(2,1)S(1)}, u32[]{:S(2)}, u32[]{:S(2)}) collective-permute-start(bf16[40,432]{1,0:T(8,128)(2,1)} %own.1), channel_id=1, source_target_pairs={{0,128},{32,160},{64,192},{96,224},{128,0},{160,32},{192,64},{224,... | collective-permute-start | bytes 103688 | tf_op jit(solution)/shard_map/ppermute | solution.py:36
  12.7 8.7 %collective-permute-start.1 = (bf16[2,40,432]{2,1,0:T(8,128)(2,1)S(1)}, bf16[2,40,432]{2,1,0:T(8,128)(2,1)S(1)}, u32[]{:S(2)}, u32[]{:S(2)}) collective-permute-start(bf16[2,40,432]{2,1,0:T(8,128)(2,1)S(1)} %pad_maximum_fusion.1), channel_id=1, source_target_pairs={{0,64},{32,96},{64,0},{96,32},{128,192},{160,224},{192,128},{224,1... | collective-permute-start | bytes 207368 | tf_op jit(solution)/shard_map/ppermute | solution.py:36
  21.4 13.5 %copy-start.2 = (bf16[40,432]{1,0:T(8,128)(2,1)S(1)}, bf16[40,432]{1,0:T(8,128)(2,1)}, u32[]{:S(2)}) copy-start(bf16[40,432]{1,0:T(8,128)(2,1)} %own.1) | copy-start | bytes 103684
  21.4 15.7 %copy-start.3 = (bf16[256,432]{0,1:T(8,128)(2,1)S(1)}, bf16[256,432]{0,1:T(8,128)(2,1)}, u32[]{:S(2)}) copy-start(bf16[256,432]{0,1:T(8,128)(2,1)} %param.4) | copy-start | bytes 663556
  21.4 15.7 %copy-start.5 = (bf16[1280,256]{1,0:T(8,128)(2,1)S(1)}, bf16[1280,256]{1,0:T(8,128)(2,1)}, u32[]{:S(2)}) copy-start(bf16[1280,256]{1,0:T(8,128)(2,1)} %get-tuple-element.24.mine) | copy-start | bytes 1966084
  21.4 21.2 %copy-start.4 = (s32[5]{0:T(128)S(1)}, s32[5]{0:T(128)}, u32[]{:S(2)}) copy-start(s32[5]{0:T(128)} %stack.32.place) | copy-start | bytes 64
  21.4 15.7 %collective-permute-start.3 = (bf16[1712,256]{1,0:T(8,128)(2,1)}, bf16[1712,256]{1,0:T(8,128)(2,1)S(1)}, u32[]{:S(2)}, u32[]{:S(2)}) collective-permute-start(bf16[1712,256]{1,0:T(8,128)(2,1)} %shard_map.68), channel_id=1, source_target_pairs={{0,16},{16,0},{1,17},{17,1},{2,18},{18,2},{3,19},{19,3},{4,20},{20... | collective-permute-start | bytes 2629640 | tf_op jit(solution)/shard_map/ppermute | solution.py:36
  34.9 7.7 %collective-permute-start.2 = (bf16[4,40,432]{2,1,0:T(8,128)(2,1)S(1)}, bf16[4,40,432]{2,1,0:T(8,128)(2,1)S(1)}, u32[]{:S(2)}, u32[]{:S(2)}) collective-permute-start(bf16[4,40,432]{2,1,0:T(8,128)(2,1)S(1)} %pad_maximum_fusion.after), channel_id=1, source_target_pairs={{0,32},{32,0},{64,96},{96,64},{128,160},{160,128},{192,224},{224,1... | collective-permute-start | bytes 414728 | tf_op jit(solution)/shard_map/ppermute | solution.py:36
  43.2 37.0 %all-to-all-start.1 = ((bf16[4,320,432]{2,1,0:T(8,128)(2,1)}), bf16[4,320,432]{2,1,0:T(8,128)(2,1)S(1)}, u32[]{:S(2)}, u32[]{:S(2)}) async-start(bf16[4,320,432]{2,1,0:T(8,128)(2,1)} %shard_map.72), calls=%async_computation.1 | async-start | bytes 2621440 | tf_op jit(solution)/shard_map/all_to_all | solution.py:255
  46.8 23.9 %collective-permute-start.6 = (bf16[320,432]{1,0:T(8,128)(2,1)S(1)}, bf16[320,432]{1,0:T(8,128)(2,1)S(1)}, u32[]{:S(2)}, u32[]{:S(2)}) collective-permute-start(bf16[320,432]{1,0:T(8,128)(2,1)S(1)} %bitcast.19), channel_id=1, source_target_pairs={{0,256},{256,512},{512,768},{768,0},{1,257},{257,513},{513,769},{7... | collective-permute-start | bytes 829448 | tf_op jit(solution)/shard_map/ppermute | solution.py:41
  50.1 27.9 %collective-permute-start.5 = (bf16[320,432]{1,0:T(8,128)(2,1)S(1)}, bf16[320,432]{1,0:T(8,128)(2,1)S(1)}, u32[]{:S(2)}, u32[]{:S(2)}) collective-permute-start(bf16[320,432]{1,0:T(8,128)(2,1)S(1)} %bitcast.20), channel_id=1, source_target_pairs={{0,512},{256,768},{512,0},{768,256},{1,513},{257,769},{513,1},{769... | collective-permute-start | bytes 829448 | tf_op jit(solution)/shard_map/ppermute | solution.py:41
  54.4 23.6 %collective-permute-start.4 = (bf16[320,432]{1,0:T(8,128)(2,1)S(1)}, bf16[320,432]{1,0:T(8,128)(2,1)S(1)}, u32[]{:S(2)}, u32[]{:S(2)}) collective-permute-start(bf16[320,432]{1,0:T(8,128)(2,1)S(1)} %bitcast.21), channel_id=1, source_target_pairs={{0,768},{256,0},{512,256},{768,512},{1,769},{257,1},{513,257},{769... | collective-permute-start | bytes 829448 | tf_op jit(solution)/shard_map/ppermute | solution.py:41
  80.2 21.2 %all-to-all-start = ((bf16[4,4,80,512]{3,2,1,0:T(8,128)(2,1)}), bf16[4,4,80,512]{3,2,1,0:T(8,128)(2,1)S(1)}, u32[]{:S(2)}, u32[]{:S(2)}) async-start(bf16[4,4,80,512]{3,2,1,0:T(8,128)(2,1)} %get-tuple-element.27), calls=%async_computation | async-start | bytes 2621440 | tf_op jit(solution)/shard_map/all_to_all | solution.py:266
  83.8 1.3 copy-start
  85.1 1.3 copy-start.1
  88.9 63.1 %collective-permute-start.13 = (f32[432,256]{1,0:T(8,128)}, f32[432,256]{1,0:T(8,128)}, u32[]{:S(2)}, u32[]{:S(2)}) collective-permute-start(f32[432,256]{1,0:T(8,128)} %get-tuple-element.43), channel_id=1, source_target_pairs={{0,16},{16,0},{1,17},{17,1},{2,18},{18,2},{3,19},{19,3},{4,20},{20... | collective-permute-start | bytes 1327112 | tf_op jit(solution)/shard_map/ppermute | solution.py:36
  93.2 7.7 %collective-permute-start.7 = (bf16[4,40,432]{2,1,0:T(8,128)(2,1)S(1)}, bf16[4,40,432]{2,1,0:T(8,128)(2,1)S(1)}, u32[]{:S(2)}, u32[]{:S(2)}) collective-permute-start(bf16[4,40,432]{2,1,0:T(8,128)(2,1)S(1)} %get-tuple-element.33), channel_id=1, source_target_pairs={{0,32},{32,0},{64,96},{96,64},{128,160},{160,128},{192,224},{224,1... | collective-permute-start | bytes 414728 | tf_op jit(solution)/shard_map/ppermute | solution.py:36
  101.7 26.8 %collective-permute-start.8 = (bf16[80,512]{1,0:T(8,128)(2,1)S(1)}, bf16[80,512]{1,0:T(8,128)(2,1)S(1)}, u32[]{:S(2)}, u32[]{:S(2)}) collective-permute-start(bf16[80,512]{1,0:T(8,128)(2,1)S(1)} %get-tuple-element.37), channel_id=1, source_target_pairs={{0,4},{4,8},{8,12},{12,0},{16,28},{20,16},{24,20},{28,24},{1,5},{5... | collective-permute-start | bytes 245768 | tf_op jit(solution)/shard_map/ppermute | solution.py:51
  115.7 10.3 %collective-permute-start.9 = (bf16[2,40,432]{2,1,0:T(8,128)(2,1)S(1)}, bf16[2,40,432]{2,1,0:T(8,128)(2,1)S(1)}, u32[]{:S(2)}, u32[]{:S(2)}) collective-permute-start(bf16[2,40,432]{2,1,0:T(8,128)(2,1)S(1)} %get-tuple-element.38), channel_id=1, source_target_pairs={{0,64},{32,96},{64,0},{96,32},{128,192},{160,224},{192,128},{224,1... | collective-permute-start | bytes 207368 | tf_op jit(solution)/shard_map/ppermute | solution.py:36
  126.5 16.6 %collective-permute-start.11 = (bf16[80,512]{1,0:T(8,128)(2,1)S(1)}, bf16[80,512]{1,0:T(8,128)(2,1)S(1)}, u32[]{:S(2)}, u32[]{:S(2)}) collective-permute-start(bf16[80,512]{1,0:T(8,128)(2,1)S(1)} %get-tuple-element.40), channel_id=1, source_target_pairs={{0,12},{4,0},{8,4},{12,8},{16,20},{20,24},{24,28},{28,16},{1,13},{... | collective-permute-start | bytes 245768 | tf_op jit(solution)/shard_map/ppermute | solution.py:51
  128.5 21.6 %collective-permute-start.10 = (bf16[80,512]{1,0:T(8,128)(2,1)S(1)}, bf16[80,512]{1,0:T(8,128)(2,1)S(1)}, u32[]{:S(2)}, u32[]{:S(2)}) collective-permute-start(bf16[80,512]{1,0:T(8,128)(2,1)S(1)} %shard_map.78), channel_id=1, source_target_pairs={{0,4},{4,8},{8,12},{12,0},{16,28},{20,16},{24,20},{28,24},{1,5},{5... | collective-permute-start | bytes 245768 | tf_op jit(solution)/shard_map/ppermute | solution.py:51
  140.5 13.5 %collective-permute-start.14 = (bf16[1,40,432]{2,1,0:T(8,128)(2,1)S(1)}, bf16[1,40,432]{2,1,0:T(8,128)(2,1)S(1)}, u32[]{:S(2)}, u32[]{:S(2)}) collective-permute-start(bf16[1,40,432]{2,1,0:T(8,128)(2,1)S(1)} %get-tuple-element.44), channel_id=1, source_target_pairs={{0,128},{32,160},{64,192},{96,224},{128,0},{160,32},{192,64},{224,... | collective-permute-start | bytes 103688 | tf_op jit(solution)/shard_map/ppermute | solution.py:36
  150.1 4.6 %collective-permute-start.12 = (bf16[80,256]{1,0:T(8,128)(2,1)S(1)}, bf16[80,256]{1,0:T(8,128)(2,1)S(1)}, u32[]{:S(2)}, u32[]{:S(2)}) collective-permute-start(bf16[80,256]{1,0:T(8,128)(2,1)S(1)} %get-tuple-element.42), channel_id=1, source_target_pairs={{0,16},{16,0},{1,17},{17,1},{2,18},{18,2},{3,19},{19,3},{4,20},{20... | collective-permute-start | bytes 122888 | tf_op jit(solution)/shard_map/ppermute | solution.py:36

commit v5 on v4

--- a/solution.py
+++ b/solution.py
@@ -82,8 +82,8 @@
     send[mine.shape[0] :, :] = pre[...]
 
 
-def weight_term(pre, mine, got, after, hidden, term, both, held, sems, *, stripe):
-    tokens, channels = pre.shape[1], mine.shape[0]
+def weight_term(place, pre, mine, got, after, hidden, t0, t1, t2, t3, both, held, sems, *, stripe):
+    y, tokens, channels = place[1], pre.shape[1], mine.shape[0]
     copies = [
         pltpu.make_async_copy(mine, both.at[0], sems.at[0]),
         pltpu.make_async_copy(got.at[pl.ds(0, channels)], both.at[1], sems.at[1]),
@@ -92,25 +92,23 @@
         copy.start()
     hidden[:, :tokens] = gelu_value(pre[...].astype(F32)).astype(BF16)
     hidden[:, tokens:] = gelu_value(got[channels:, :].astype(F32)).astype(BF16)
-    for index in range(channels // stripe):
-        rows = slice(index * stripe, (index + 1) * stripe)
+    for index, term in enumerate((t0, t1, t2, t3)):
+        rows = pl.ds(pl.multiple_of((y + index) % 4 * stripe, 16), stripe)
         total = dot(mine[rows, :], hidden[:, :tokens], 1, 1)
         total += dot(got[rows, :], hidden[:, tokens:], 1, 1)
         held[index] = total.astype(BF16)
-        copies.append(pltpu.make_async_copy(held.at[index], term.at[index], sems.at[2 + index]))
+        copies.append(pltpu.make_async_copy(held.at[index], term, sems.at[2 + index]))
         copies[-1].start()
     for copy in copies:
         copy.wait()
 
 
-def split_y(place, parts, after, keep, send):
+def split_y(place, p0, p1, p2, p3, after, keep, send):
     bit = place[2] % 2
 
     def total(index):
-        value = parts[0, index].astype(F32)
-        for source in range(1, parts.shape[0]):
-            value += parts[source, index].astype(F32)
-        return value
+        value = p0[index].astype(F32) + p1[index].astype(F32)
+        return value + (p2[index].astype(F32) + p3[index].astype(F32))
 
     for index in range(keep.shape[0]):
         keep[index] = total(2 * index + bit)
@@ -164,11 +162,11 @@
         out[...] = value.astype(BF16)
 
 
-def sum_step(s1, got, after, t1):
+def sum_step(s1, got, t1):
     t1[...] = (s1[...].astype(F32) + got[...].astype(F32)).astype(BF16)
 
 
-def sum_last(s0, u, v, kept, given):
+def sum_last(s0, u, v, after, then, kept, given):
     half = kept.shape[1]
     total = (s0[...].astype(F32) + (u[...].astype(F32) + v[...].astype(F32))).astype(BF16)
     kept[...] = total[:, :half]
@@ -179,11 +177,11 @@
     pass
 
 
-def hold(value, after):
+def hold(value, after, place=LATER):
     return pl.pallas_call(
         gate,
         out_shape=pltpu.HBM(value.shape, value.dtype),
-        in_specs=[HBM, LATER],
+        in_specs=[HBM, place],
         out_specs=HBM,
         input_output_aliases={0: 0},
         compiler_params=pltpu.CompilerParams(vmem_limit_bytes=14 << 20),
@@ -232,14 +230,16 @@
     two = swap(first, "zl", 2)
     second = jnp.concatenate([first, two])
     got = swap(hold(send, two), "c", 1)
-    hidden, term, both = call(
+    hidden, t0, t1, t2, t3, both = call(
         functools.partial(weight_term, stripe=stripe),
-        [((hid, 2 * tokens), BF16), pltpu.HBM((n_y, stripe, hid), BF16), pltpu.HBM((2, channels, tokens), BF16)],
-        [VMEM] * 3 + [LATER],
-        (pre, mine, got, second),
+        [((hid, 2 * tokens), BF16)]
+        + [pltpu.HBM((stripe, hid), BF16)] * n_y
+        + [pltpu.HBM((2, channels, tokens), BF16)],
+        [SMEM] + [VMEM] * 3 + [LATER],
+        (place, pre, mine, got, second),
         flops=work,
         scratch=[pltpu.VMEM((n_y, stripe, hid), BF16), pltpu.SemaphoreType.DMA((2 + n_y,))],
-        out_specs=[VMEM, HBM, HBM],
+        out_specs=[VMEM] + [HBM] * (n_y + 1),
     )
 
     four = swap(second, "zl", 1)
@@ -251,8 +251,6 @@
     )
     w0 = rows.reshape(stripe, hid)
     w1, w3, w2 = shift(w0, "y", -1), shift(w0, "y", 1), shift(w0, "y", 2)
-
-    term = lax.all_to_all(hold(term, rows), "y", 0, 0)
 
     parts, weight = call(
         output_terms,
@@ -263,8 +261,22 @@
         scratch=[pltpu.VMEM((n_y, n_x, group, 2 * tokens), BF16), pltpu.SemaphoreType.DMA((2 * n_y,))],
         out_specs=[HBM, HBM],
     )
+    t1, t2, t3 = (shift(hold(t, parts, HBM), "y", k) for k, t in ((1, t1), (2, t2), (3, t3)))
     parts = lax.all_to_all(parts, "x", 0, 0)
 
+    whole, half = ((group, 2 * tokens), BF16), ((group, tokens), BF16)
+    quarter = n_zl // 2
+    terms = [t.reshape(n_zl, block, hid) for t in (t0, t1, t2, t3)]
+    s0, s1, s2, s3 = call(sum_x, [whole] * 4, [VMEM, LATER], (parts, terms[3]))
+    got2 = shift_both(s2, 1)
+    (s1,) = call(sum_step, [whole], [VMEM] * 2, (s1, got2))
+    u, v = shift_both(s1, 1), shift_both(s3, -1)
+    keep, send = call(
+        split_y,
+        [((quarter, block, hid), F32), ((quarter, block, hid), BF16)],
+        [SMEM] + [VMEM] * 4 + [LATER],
+        (place, *terms, s1),
+    )
     own, other = call(
         hidden_terms,
         [((hid, tokens), F32)] * 2,
@@ -272,31 +284,19 @@
         (place, weight, both),
         flops=work,
     )
-    whole, half = ((group, 2 * tokens), BF16), ((group, tokens), BF16)
-    quarter = n_zl // 2
-    keep, send = call(
-        split_y,
-        [((quarter, block, hid), F32), ((quarter, block, hid), BF16)],
-        [SMEM, VMEM, LATER],
-        (place, term.reshape(n_y, n_zl, block, hid), own),
-    )
     keep, send = call(
         functools.partial(split_zl, width=2),
         [((quarter // 2, block, hid), F32), ((quarter // 2, block, hid), BF16)],
         [SMEM, VMEM, VMEM],
         (place, keep, swap(send, "zl", 1)),
     )
-    s0, s1, s2, s3 = call(sum_x, [whole] * 4, [VMEM, LATER], (parts, keep))
-    got2 = shift_both(s2, 1)
+    kept, given = call(sum_last, [half] * 2, [VMEM] * 3 + [LATER] * 2, (s0, u, v, keep, own))
     keep, send = call(
         functools.partial(split_zl, width=4),
         [((quarter // 4, block, hid), F32), ((quarter // 4, block, hid), BF16)],
         [SMEM, VMEM, VMEM],
         (place, keep, swap(send, "zl", 2)),
     )
-    (t1,) = call(sum_step, [whole], [VMEM] * 2 + [LATER], (s1, got2, keep))
-    u, v = shift_both(t1, 1), shift_both(s3, -1)
-    kept, given = call(sum_last, [half] * 2, [VMEM] * 3, (s0, u, v))
     (grad_weight,) = call(
         functools.partial(sum_scaled, factor=factor),
         [((block, hid), F32)],

time: 159 us -> 155 us (0.975)
  the two profiles are of different devices: /device:TPU:1 before, /device:TPU:73 now
where the time goes in v5:
time: 155 us; the launch traced here: 154 us
  starting transfers between devices  103 us (66%)
  waiting for transfers between devices  31 us (20%)
  Pallas kernels  15.3 us (10%)
  other arithmetic  2.83 us (2%)
    ppermute x9, starting transfers between devices, swap(): return lax.ppermute(value, axis, [(i, i ^ distance) for i in range(size)])  43 us
    ppermute x3, starting transfers between devices, shift_both(): return lax.ppermute(value, ('c', 'zh'), pairs)  29 us
    ppermute x6, starting transfers between devices, shift(): lax.ppermute(value, axis, [(i, (i + distance) % size) for i in range(size)])  27.6 us
    pallas_call x13, Pallas kernels, call(): pl.pallas_call(body, out_shape=[s if isinstance(s, pl.MemoryRef) else jax...  15.3 us
    ppermute x3, waiting for transfers between devices, shift_both(): return lax.ppermute(value, ('c', 'zh'), pairs)  14.2 us
    ppermute x6, waiting for transfers between devices, shift(): lax.ppermute(value, axis, [(i, (i + distance) % size) for i in range(size)])  13.3 us
    all_to_all x1, starting transfers between devices, local(): parts = lax.all_to_all(parts, 'x', 0, 0)  3.68 us
    ppermute x9, waiting for transfers between devices, swap(): return lax.ppermute(value, axis, [(i, i ^ distance) for i in range(size)])  3.47 us
  transfers between devices with their start and end apart: 19, of which 8 were waited for; matrix products, arithmetic and copies ran while one was open for 2% of the time, Pallas kernels for 8%

profile of v5, /device:TPU:73, one launch (start us, length us, event | category | flops | bytes accessed | tf_op | source)
XLA Modules:
  0.0 154.1 jit_solution(16137606130659143811)
XLA Ops:
  0.6 8.8 %collective-permute-start = (bf16[40,432]{1,0:T(8,128)(2,1)}, bf16[40,432]{1,0:T(8,128)(2,1)S(1)}, u32[]{:S(2)}, u32[]{:S(2)}) collective-permute-start(bf16[40,432]{1,0:T(8,128)(2,1)} %own.1), channel_id=1, source_target_pairs={{0,128},{32,160},{64,192},{96,224},{128,0},{160,32},{192,64},{224,... | collective-permute-start | bytes 103688 | tf_op jit(solution)/shard_map/ppermute | solution.py:36
  9.5 0.6 stack.32.place
  10.0 1.0 collective-permute-done.one
  11.0 0.8 pad_maximum_fusion.1
  11.8 1.9 %collective-permute-start.1 = (bf16[2,40,432]{2,1,0:T(8,128)(2,1)S(1)}, bf16[2,40,432]{2,1,0:T(8,128)(2,1)S(1)}, u32[]{:S(2)}, u32[]{:S(2)}) collective-permute-start(bf16[2,40,432]{2,1,0:T(8,128)(2,1)S(1)} %pad_maximum_fusion.1), channel_id=1, source_target_pairs={{0,64},{32,96},{64,0},{96,32},{128,192},{160,224},{192,128},{224,1... | collective-permute-start | bytes 207368 | tf_op jit(solution)/shard_map/ppermute | solution.py:36
  13.8 3.8 %shard_map.67 = (bf16[1712,256]{1,0:T(8,128)(2,1)}, bf16[1280,256]{1,0:T(8,128)(2,1)}) custom-call(s32[5]{0:T(128)} %stack.32.place, s32[320,1]{1,0:T(8,128)} %constant.35.clone.base, bf16[256,2560]{1,0:T(8,128)(2,1)} %cot.1, bf16[432,256]{1,0:T(8,128)(2,1)} %bitcast.34), custom_call_target="tpu_custom_call" | custom-call | flops 838860800 | bytes 2299481 | tf_op jit(solution)/shard_map/pallas_call | solution.py:61
  17.6 0.3 collective-permute-done.1.after.two
  17.9 4.7 %collective-permute-start.3 = (bf16[1712,256]{1,0:T(8,128)(2,1)}, bf16[1712,256]{1,0:T(8,128)(2,1)S(1)}, u32[]{:S(2)}, u32[]{:S(2)}) collective-permute-start(bf16[1712,256]{1,0:T(8,128)(2,1)} %shard_map.68), channel_id=1, source_target_pairs={{0,16},{16,0},{1,17},{17,1},{2,18},{18,2},{3,19},{19,3},{4,20},{20... | collective-permute-start | bytes 2629640 | tf_op jit(solution)/shard_map/ppermute | solution.py:36
  22.7 4.3 %collective-permute-start.2 = (bf16[4,40,432]{2,1,0:T(8,128)(2,1)S(1)}, bf16[4,40,432]{2,1,0:T(8,128)(2,1)S(1)}, u32[]{:S(2)}, u32[]{:S(2)}) collective-permute-start(bf16[4,40,432]{2,1,0:T(8,128)(2,1)S(1)} %pad_maximum_fusion.after), channel_id=1, source_target_pairs={{0,32},{32,0},{64,96},{96,64},{128,160},{160,128},{192,224},{224,1... | collective-permute-start | bytes 414728 | tf_op jit(solution)/shard_map/ppermute | solution.py:36
  27.1 2.4 %shard_map.69 = (bf16[432,512]{1,0:T(8,128)(2,1)S(1)}, bf16[320,432]{1,0:T(8,128)(2,1)}, bf16[320,432]{1,0:T(8,128)(2,1)}, bf16[320,432]{1,0:T(8,128)(2,1)}, bf1...) custom-call(s32[5]{0:T(128)S(1)} %copy-done.6, bf16[432,256]{1,0:T(8,128)(2,1)S(1)} %bitcast.35, ...), custom_call_target="tpu_custom_call" | custom-call | flops 566231040 | bytes 2837017 | tf_op jit(solution)/shard_map/pallas_call | solution.py:61
  29.5 2.1 %collective-permute-done.2.four = bf16[4,40,432]{2,1,0:T(8,128)(2,1)S(1)} collective-permute-done((bf16[4,40,432]{2,1,0:T(8,128)(2,1)S(1)}, bf16[4,40,432]{2,1,0:T(8,128)(2,1)S(1)}, u32[]{:S(2)}, u32[]{:S(2)}) %collective-permute-start.2) | collective-permute-done | bytes 138272 | tf_op jit(solution)/shard_map/ppermute | solution.py:36
  31.6 0.6 shard_map.70
  32.1 3.2 %collective-permute-start.6 = (bf16[320,432]{1,0:T(8,128)(2,1)S(1)}, bf16[320,432]{1,0:T(8,128)(2,1)S(1)}, u32[]{:S(2)}, u32[]{:S(2)}) collective-permute-start(bf16[320,432]{1,0:T(8,128)(2,1)S(1)} %bitcast.30), channel_id=1, source_target_pairs={{0,256},{256,512},{512,768},{768,0},{1,257},{257,513},{513,769},{7... | collective-permute-start | bytes 829448 | tf_op jit(solution)/shard_map/ppermute | solution.py:41
  35.4 11.0 %collective-permute-start.5 = (bf16[320,432]{1,0:T(8,128)(2,1)S(1)}, bf16[320,432]{1,0:T(8,128)(2,1)S(1)}, u32[]{:S(2)}, u32[]{:S(2)}) collective-permute-start(bf16[320,432]{1,0:T(8,128)(2,1)S(1)} %bitcast.31), channel_id=1, source_target_pairs={{0,512},{256,768},{512,0},{768,256},{1,513},{257,769},{513,1},{769... | collective-permute-start | bytes 829448 | tf_op jit(solution)/shard_map/ppermute | solution.py:41
  46.3 1.9 %collective-permute-start.4 = (bf16[320,432]{1,0:T(8,128)(2,1)S(1)}, bf16[320,432]{1,0:T(8,128)(2,1)S(1)}, u32[]{:S(2)}, u32[]{:S(2)}) collective-permute-start(bf16[320,432]{1,0:T(8,128)(2,1)S(1)} %bitcast.32), channel_id=1, source_target_pairs={{0,768},{256,0},{512,256},{768,512},{1,769},{257,1},{513,257},{769... | collective-permute-start | bytes 829448 | tf_op jit(solution)/shard_map/ppermute | solution.py:41
  48.3 1.7 %collective-permute-done.6.w3 = bf16[320,432]{1,0:T(8,128)(2,1)S(1)} collective-permute-done((bf16[320,432]{1,0:T(8,128)(2,1)S(1)}, bf16[320,432]{1,0:T(8,128)(2,1)S(1)}, u32[]{:S(2)}, u32[]{:S(2)}) %collective-permute-start.6) | collective-permute-done | bytes 276512 | tf_op jit(solution)/shard_map/ppermute | solution.py:41
  49.9 3.4 %collective-permute-done.5.w2 = bf16[320,432]{1,0:T(8,128)(2,1)S(1)} collective-permute-done((bf16[320,432]{1,0:T(8,128)(2,1)S(1)}, bf16[320,432]{1,0:T(8,128)(2,1)S(1)}, u32[]{:S(2)}, u32[]{:S(2)}) %collective-permute-start.5) | collective-permute-done | bytes 276512 | tf_op jit(solution)/shard_map/ppermute | solution.py:41
  53.4 8.2 %collective-permute-done.4.w1 = bf16[320,432]{1,0:T(8,128)(2,1)S(1)} collective-permute-done((bf16[320,432]{1,0:T(8,128)(2,1)S(1)}, bf16[320,432]{1,0:T(8,128)(2,1)S(1)}, u32[]{:S(2)}, u32[]{:S(2)}) %collective-permute-start.4) | collective-permute-done | bytes 276512 | tf_op jit(solution)/shard_map/ppermute | solution.py:41
  61.5 2.2 %shard_map.71 = (bf16[4,4,80,512]{3,2,1,0:T(8,128)(2,1)}, bf16[4,320,432]{2,1,0:T(8,128)(2,1)}) custom-call(s32[5]{0:T(128)S(1)} %copy-done.6, bf16[320,432]{1,0:T(8,128)(2,1)S(1)} %bitcast.33, bf16[320,432]{1,0:T(8,128)(2,1)S(1)} %collective-permute-done.4.w1, bf16[320,432]{1,0:T(8,128)(2,1)S(1)} %collective-permute-done.5.w2, ...), custom_call_target="tpu_custom_call" | custom-call | flops 566231040 | bytes 2322457 | tf_op jit(solution)/shard_map/pallas_call | solution.py:61
  63.7 3.7 %all-to-all-start = ((bf16[4,4,80,512]{3,2,1,0:T(8,128)(2,1)}), bf16[4,4,80,512]{3,2,1,0:T(8,128)(2,1)S(1)}, u32[]{:S(2)}, u32[]{:S(2)}) async-start(bf16[4,4,80,512]{3,2,1,0:T(8,128)(2,1)} %get-tuple-element.30.after), calls=%async_computation | async-start | bytes 2621440 | tf_op jit(solution)/shard_map/all_to_all | solution.py:265
  67.4 2.4 %collective-permute-start.7 = (bf16[320,432]{1,0:T(8,128)(2,1)}, bf16[320,432]{1,0:T(8,128)(2,1)S(1)}, u32[]{:S(2)}, u32[]{:S(2)}) collective-permute-start(bf16[320,432]{1,0:T(8,128)(2,1)} %shard_map.72), channel_id=1, source_target_pairs={{0,768},{256,0},{512,256},{768,512},{1,769},{257,1},{513,257},{769... | collective-permute-start | bytes 829448 | tf_op jit(solution)/shard_map/ppermute | solution.py:41
  69.8 3.0 %collective-permute-start.11 = (bf16[320,432]{1,0:T(8,128)(2,1)}, bf16[320,432]{1,0:T(8,128)(2,1)S(1)}, u32[]{:S(2)}, u32[]{:S(2)}) collective-permute-start(bf16[320,432]{1,0:T(8,128)(2,1)} %shard_map.75), channel_id=1, source_target_pairs={{0,256},{256,512},{512,768},{768,0},{1,257},{257,513},{513,769},{7... | collective-permute-start | bytes 829448 | tf_op jit(solution)/shard_map/ppermute | solution.py:41
  72.9 6.1 %collective-permute-start.12 = (bf16[320,432]{1,0:T(8,128)(2,1)}, bf16[320,432]{1,0:T(8,128)(2,1)S(1)}, u32[]{:S(2)}, u32[]{:S(2)}) collective-permute-start(bf16[320,432]{1,0:T(8,128)(2,1)} %shard_map.76), channel_id=1, source_target_pairs={{0,512},{256,768},{512,0},{768,256},{1,513},{257,769},{513,1},{769... | collective-permute-start | bytes 829448 | tf_op jit(solution)/shard_map/ppermute | solution.py:41
  79.0 2.5 %shard_map.79 = (f32[432,256]{1,0:T(8,128)S(1)}, f32[432,256]{1,0:T(8,128)}) custom-call(s32[5]{0:T(128)S(1)} %copy-done.6, bf16[4,320,432]{2,1,0:T(8,128)(2,1)S(1)} %copy-done.2, bf16[2,1280,256]{2,1,0:T(8,128)(2,1)S(1)} %copy-done.1), custom_call_target="tpu_custom_call" | custom-call | flops 566231040 | bytes 3624985 | tf_op jit(solution)/shard_map/pallas_call | solution.py:61
  81.5 3.4 %collective-permute-start.15 = (f32[432,256]{1,0:T(8,128)}, f32[432,256]{1,0:T(8,128)}, u32[]{:S(2)}, u32[]{:S(2)}) collective-permute-start(f32[432,256]{1,0:T(8,128)} %get-tuple-element.47), channel_id=1, source_target_pairs={{0,16},{16,0},{1,17},{17,1},{2,18},{18,2},{3,19},{19,3},{4,20},{20... | collective-permute-start | bytes 1327112 | tf_op jit(solution)/shard_map/ppermute | solution.py:36
  84.8 0.0 collective-permute-done.7
  84.9 0.0 all-to-all-done.parts
  84.9 0.2 shard_map.73
  85.0 14.5 %collective-permute-start.8 = (bf16[80,512]{1,0:T(8,128)(2,1)S(1)}, bf16[80,512]{1,0:T(8,128)(2,1)S(1)}, u32[]{:S(2)}, u32[]{:S(2)}) collective-permute-start(bf16[80,512]{1,0:T(8,128)(2,1)S(1)} %get-tuple-element.34), channel_id=1, source_target_pairs={{0,4},{4,8},{8,12},{12,0},{16,28},{20,16},{24,20},{28,24},{1,5},{5... | collective-permute-start | bytes 245768 | tf_op jit(solution)/shard_map/ppermute | solution.py:51
  99.6 6.3 %collective-permute-done.8.got = bf16[80,512]{1,0:T(8,128)(2,1)S(1)} collective-permute-done((bf16[80,512]{1,0:T(8,128)(2,1)S(1)}, bf16[80,512]{1,0:T(8,128)(2,1)S(1)}, u32[]{:S(2)}, u32[]{:S(2)}) %collective-permute-start.8) | collective-permute-done | bytes 81952 | tf_op jit(solution)/shard_map/ppermute | solution.py:51
  105.9 0.0 collective-permute-done.11
  105.9 0.7 shard_map.77
  106.6 1.9 %collective-permute-start.13 = (bf16[4,40,432]{2,1,0:T(8,128)(2,1)S(1)}, bf16[4,40,432]{2,1,0:T(8,128)(2,1)S(1)}, u32[]{:S(2)}, u32[]{:S(2)}) collective-permute-start(bf16[4,40,432]{2,1,0:T(8,128)(2,1)S(1)} %get-tuple-element.40), channel_id=1, source_target_pairs={{0,32},{32,0},{64,96},{96,64},{128,160},{160,128},{192,224},{224,1... | collective-permute-start | bytes 414728 | tf_op jit(solution)/shard_map/ppermute | solution.py:36
  108.6 4.8 %collective-permute-start.10 = (bf16[80,512]{1,0:T(8,128)(2,1)S(1)}, bf16[80,512]{1,0:T(8,128)(2,1)S(1)}, u32[]{:S(2)}, u32[]{:S(2)}) collective-permute-start(bf16[80,512]{1,0:T(8,128)(2,1)S(1)} %get-tuple-element.35), channel_id=1, source_target_pairs={{0,12},{4,0},{8,4},{12,8},{16,20},{20,24},{24,28},{28,16},{1,13},{... | collective-permute-start | bytes 245768 | tf_op jit(solution)/shard_map/ppermute | solution.py:51
  113.4 9.7 %collective-permute-start.9 = (bf16[80,512]{1,0:T(8,128)(2,1)S(1)}, bf16[80,512]{1,0:T(8,128)(2,1)S(1)}, u32[]{:S(2)}, u32[]{:S(2)}) collective-permute-start(bf16[80,512]{1,0:T(8,128)(2,1)S(1)} %shard_map.74.after), channel_id=1, source_target_pairs={{0,4},{4,8},{8,12},{12,0},{16,28},{20,16},{24,20},{28,24},{1,5},{5... | collective-permute-start | bytes 245768 | tf_op jit(solution)/shard_map/ppermute | solution.py:51
  123.1 0.0 collective-permute-done.13.got
  123.1 0.6 shard_map.78
  123.7 4.7 %collective-permute-start.16 = (bf16[2,40,432]{2,1,0:T(8,128)(2,1)S(1)}, bf16[2,40,432]{2,1,0:T(8,128)(2,1)S(1)}, u32[]{:S(2)}, u32[]{:S(2)}) collective-permute-start(bf16[2,40,432]{2,1,0:T(8,128)(2,1)S(1)} %get-tuple-element.48), channel_id=1, source_target_pairs={{0,64},{32,96},{64,0},{96,32},{128,192},{160,224},{192,128},{224,1... | collective-permute-start | bytes 207368 | tf_op jit(solution)/shard_map/ppermute | solution.py:36
  128.4 0.0 collective-permute-done.10.v
  128.4 7.9 %collective-permute-done.9.u = bf16[80,512]{1,0:T(8,128)(2,1)S(1)} collective-permute-done((bf16[80,512]{1,0:T(8,128)(2,1)S(1)}, bf16[80,512]{1,0:T(8,128)(2,1)S(1)}, u32[]{:S(2)}, u32[]{:S(2)}) %collective-permute-start.9) | collective-permute-done | bytes 81952 | tf_op jit(solution)/shard_map/ppermute | solution.py:51
  136.3 4.0 %collective-permute-start.14 = (bf16[80,256]{1,0:T(8,128)(2,1)S(1)}, bf16[80,256]{1,0:T(8,128)(2,1)S(1)}, u32[]{:S(2)}, u32[]{:S(2)}) collective-permute-start(bf16[80,256]{1,0:T(8,128)(2,1)S(1)} %get-tuple-element.46), channel_id=1, source_target_pairs={{0,16},{16,0},{1,17},{17,1},{2,18},{18,2},{3,19},{19,3},{4,20},{20... | collective-permute-start | bytes 122888 | tf_op jit(solution)/shard_map/ppermute | solution.py:36
  140.4 0.6 shard_map.82
  140.9 9.3 %collective-permute-start.17 = (bf16[1,40,432]{2,1,0:T(8,128)(2,1)S(1)}, bf16[1,40,432]{2,1,0:T(8,128)(2,1)S(1)}, u32[]{:S(2)}, u32[]{:S(2)}) collective-permute-start(bf16[1,40,432]{2,1,0:T(8,128)(2,1)S(1)} %get-tuple-element.50), channel_id=1, source_target_pairs={{0,128},{32,160},{64,192},{96,224},{128,0},{160,32},{192,64},{224,... | collective-permute-start | bytes 103688 | tf_op jit(solution)/shard_map/ppermute | solution.py:36
  150.2 0.0 collective-permute-done.15
  150.2 2.0 %fusion.9 = bf16[256,432]{0,1:T(8,128)(2,1)} fusion(f32[432,256]{1,0:T(8,128)S(1)} %get-tuple-element.44.then, f32[432,256]{1,0:T(8,128)} %collective-permute-done.15, bf16[256,432]{0,1:T(8,128)(2,1)S(1)} %copy-done.5), kind=kLoop, calls=%fused_computation.16 | loop fusion | flops 2322432 | bytes 1327104 | tf_op jit(solution)/shard_map/transpose | solution.py:315
  152.3 0.0 collective-permute-done.14
  152.3 1.2 shard_map.81
  153.4 0.6 shard_map.83
  (27 shorter events, 0.1 us)
Async XLA Ops:
  0.6 10.4 %collective-permute-start = (bf16[40,432]{1,0:T(8,128)(2,1)}, bf16[40,432]{1,0:T(8,128)(2,1)S(1)}, u32[]{:S(2)}, u32[]{:S(2)}) collective-permute-start(bf16[40,432]{1,0:T(8,128)(2,1)} %own.1), channel_id=1, source_target_pairs={{0,128},{32,160},{64,192},{96,224},{128,0},{160,32},{192,64},{224,... | collective-permute-start | bytes 103688 | tf_op jit(solution)/shard_map/ppermute | solution.py:36
  11.8 6.1 %collective-permute-start.1 = (bf16[2,40,432]{2,1,0:T(8,128)(2,1)S(1)}, bf16[2,40,432]{2,1,0:T(8,128)(2,1)S(1)}, u32[]{:S(2)}, u32[]{:S(2)}) collective-permute-start(bf16[2,40,432]{2,1,0:T(8,128)(2,1)S(1)} %pad_maximum_fusion.1), channel_id=1, source_target_pairs={{0,64},{32,96},{64,0},{96,32},{128,192},{160,224},{192,128},{224,1... | collective-permute-start | bytes 207368 | tf_op jit(solution)/shard_map/ppermute | solution.py:36
  17.6 5.1 %copy-start.3 = (bf16[40,432]{1,0:T(8,128)(2,1)S(1)}, bf16[40,432]{1,0:T(8,128)(2,1)}, u32[]{:S(2)}) copy-start(bf16[40,432]{1,0:T(8,128)(2,1)} %own.1) | copy-start | bytes 103684
  17.6 9.5 %copy-start.5 = (bf16[256,432]{0,1:T(8,128)(2,1)S(1)}, bf16[256,432]{0,1:T(8,128)(2,1)}, u32[]{:S(2)}) copy-start(bf16[256,432]{0,1:T(8,128)(2,1)} %param.4) | copy-start | bytes 663556
  17.6 9.5 %copy-start.6 = (s32[5]{0:T(128)S(1)}, s32[5]{0:T(128)}, u32[]{:S(2)}) copy-start(s32[5]{0:T(128)} %stack.32.place) | copy-start | bytes 64
  17.6 9.5 %copy-start.7 = (bf16[1280,256]{1,0:T(8,128)(2,1)S(1)}, bf16[1280,256]{1,0:T(8,128)(2,1)}, u32[]{:S(2)}) copy-start(bf16[1280,256]{1,0:T(8,128)(2,1)} %get-tuple-element.27.mine) | copy-start | bytes 1966084
  17.9 9.1 %collective-permute-start.3 = (bf16[1712,256]{1,0:T(8,128)(2,1)}, bf16[1712,256]{1,0:T(8,128)(2,1)S(1)}, u32[]{:S(2)}, u32[]{:S(2)}) collective-permute-start(bf16[1712,256]{1,0:T(8,128)(2,1)} %shard_map.68), channel_id=1, source_target_pairs={{0,16},{16,0},{1,17},{17,1},{2,18},{18,2},{3,19},{19,3},{4,20},{20... | collective-permute-start | bytes 2629640 | tf_op jit(solution)/shard_map/ppermute | solution.py:36
  22.7 8.9 %collective-permute-start.2 = (bf16[4,40,432]{2,1,0:T(8,128)(2,1)S(1)}, bf16[4,40,432]{2,1,0:T(8,128)(2,1)S(1)}, u32[]{:S(2)}, u32[]{:S(2)}) collective-permute-start(bf16[4,40,432]{2,1,0:T(8,128)(2,1)S(1)} %pad_maximum_fusion.after), channel_id=1, source_target_pairs={{0,32},{32,0},{64,96},{96,64},{128,160},{160,128},{192,224},{224,1... | collective-permute-start | bytes 414728 | tf_op jit(solution)/shard_map/ppermute | solution.py:36
  32.1 17.8 %collective-permute-start.6 = (bf16[320,432]{1,0:T(8,128)(2,1)S(1)}, bf16[320,432]{1,0:T(8,128)(2,1)S(1)}, u32[]{:S(2)}, u32[]{:S(2)}) collective-permute-start(bf16[320,432]{1,0:T(8,128)(2,1)S(1)} %bitcast.30), channel_id=1, source_target_pairs={{0,256},{256,512},{512,768},{768,0},{1,257},{257,513},{513,769},{7... | collective-permute-start | bytes 829448 | tf_op jit(solution)/shard_map/ppermute | solution.py:41
  35.4 18.0 %collective-permute-start.5 = (bf16[320,432]{1,0:T(8,128)(2,1)S(1)}, bf16[320,432]{1,0:T(8,128)(2,1)S(1)}, u32[]{:S(2)}, u32[]{:S(2)}) collective-permute-start(bf16[320,432]{1,0:T(8,128)(2,1)S(1)} %bitcast.31), channel_id=1, source_target_pairs={{0,512},{256,768},{512,0},{768,256},{1,513},{257,769},{513,1},{769... | collective-permute-start | bytes 829448 | tf_op jit(solution)/shard_map/ppermute | solution.py:41
  46.3 15.2 %collective-permute-start.4 = (bf16[320,432]{1,0:T(8,128)(2,1)S(1)}, bf16[320,432]{1,0:T(8,128)(2,1)S(1)}, u32[]{:S(2)}, u32[]{:S(2)}) collective-permute-start(bf16[320,432]{1,0:T(8,128)(2,1)S(1)} %bitcast.32), channel_id=1, source_target_pairs={{0,768},{256,0},{512,256},{768,512},{1,769},{257,1},{513,257},{769... | collective-permute-start | bytes 829448 | tf_op jit(solution)/shard_map/ppermute | solution.py:41
  63.7 3.7 %copy-start = (bf16[4,4,80,512]{3,2,1,0:T(8,128)(2,1)S(1)}, bf16[4,4,80,512]{3,2,1,0:T(8,128)(2,1)}, u32[]{:S(2)}) copy-start(bf16[4,4,80,512]{3,2,1,0:T(8,128)(2,1)} %get-tuple-element.30.after) | copy-start | bytes 3932164
  63.7 21.2 %all-to-all-start = ((bf16[4,4,80,512]{3,2,1,0:T(8,128)(2,1)}), bf16[4,4,80,512]{3,2,1,0:T(8,128)(2,1)S(1)}, u32[]{:S(2)}, u32[]{:S(2)}) async-start(bf16[4,4,80,512]{3,2,1,0:T(8,128)(2,1)} %get-tuple-element.30.after), calls=%async_computation | async-start | bytes 2621440 | tf_op jit(solution)/shard_map/all_to_all | solution.py:265
  67.4 17.4 %collective-permute-start.7 = (bf16[320,432]{1,0:T(8,128)(2,1)}, bf16[320,432]{1,0:T(8,128)(2,1)S(1)}, u32[]{:S(2)}, u32[]{:S(2)}) collective-permute-start(bf16[320,432]{1,0:T(8,128)(2,1)} %shard_map.72), channel_id=1, source_target_pairs={{0,768},{256,0},{512,256},{768,512},{1,769},{257,1},{513,257},{769... | collective-permute-start | bytes 829448 | tf_op jit(solution)/shard_map/ppermute | solution.py:41
  69.8 9.2 %copy-start.2 = (bf16[4,320,432]{2,1,0:T(8,128)(2,1)S(1)}, bf16[4,320,432]{2,1,0:T(8,128)(2,1)}, u32[]{:S(2)}) copy-start(bf16[4,320,432]{2,1,0:T(8,128)(2,1)} %get-tuple-element.42.weight) | copy-start | bytes 3317764
  69.8 9.2 %copy-start.1 = (bf16[2,1280,256]{2,1,0:T(8,128)(2,1)S(1)}, bf16[2,1280,256]{2,1,0:T(8,128)(2,1)}, u32[]{:S(2)}) copy-start(bf16[2,1280,256]{2,1,0:T(8,128)(2,1)} %get-tuple-element.43.both) | copy-start | bytes 3932164
  69.8 36.1 %collective-permute-start.11 = (bf16[320,432]{1,0:T(8,128)(2,1)}, bf16[320,432]{1,0:T(8,128)(2,1)S(1)}, u32[]{:S(2)}, u32[]{:S(2)}) collective-permute-start(bf16[320,432]{1,0:T(8,128)(2,1)} %shard_map.75), channel_id=1, source_target_pairs={{0,256},{256,512},{512,768},{768,0},{1,257},{257,513},{513,769},{7... | collective-permute-start | bytes 829448 | tf_op jit(solution)/shard_map/ppermute | solution.py:41
  72.9 33.0 %collective-permute-start.12 = (bf16[320,432]{1,0:T(8,128)(2,1)}, bf16[320,432]{1,0:T(8,128)(2,1)S(1)}, u32[]{:S(2)}, u32[]{:S(2)}) collective-permute-start(bf16[320,432]{1,0:T(8,128)(2,1)} %shard_map.76), channel_id=1, source_target_pairs={{0,512},{256,768},{512,0},{768,256},{1,513},{257,769},{513,1},{769... | collective-permute-start | bytes 829448 | tf_op jit(solution)/shard_map/ppermute | solution.py:41
  81.5 24.4 %copy-start.4 = (bf16[320,432]{1,0:T(8,128)(2,1)S(1)}, bf16[320,432]{1,0:T(8,128)(2,1)}, u32[]{:S(2)}) copy-start(bf16[320,432]{1,0:T(8,128)(2,1)} %get-tuple-element.36) | copy-start | bytes 829444
  81.5 68.8 %collective-permute-start.15 = (f32[432,256]{1,0:T(8,128)}, f32[432,256]{1,0:T(8,128)}, u32[]{:S(2)}, u32[]{:S(2)}) collective-permute-start(f32[432,256]{1,0:T(8,128)} %get-tuple-element.47), channel_id=1, source_target_pairs={{0,16},{16,0},{1,17},{17,1},{2,18},{18,2},{3,19},{19,3},{4,20},{20... | collective-permute-start | bytes 1327112 | tf_op jit(solution)/shard_map/ppermute | solution.py:36
  85.0 20.8 %collective-permute-start.8 = (bf16[80,512]{1,0:T(8,128)(2,1)S(1)}, bf16[80,512]{1,0:T(8,128)(2,1)S(1)}, u32[]{:S(2)}, u32[]{:S(2)}) collective-permute-start(bf16[80,512]{1,0:T(8,128)(2,1)S(1)} %get-tuple-element.34), channel_id=1, source_target_pairs={{0,4},{4,8},{8,12},{12,0},{16,28},{20,16},{24,20},{28,24},{1,5},{5... | collective-permute-start | bytes 245768 | tf_op jit(solution)/shard_map/ppermute | solution.py:51
  106.6 16.5 %collective-permute-start.13 = (bf16[4,40,432]{2,1,0:T(8,128)(2,1)S(1)}, bf16[4,40,432]{2,1,0:T(8,128)(2,1)S(1)}, u32[]{:S(2)}, u32[]{:S(2)}) collective-permute-start(bf16[4,40,432]{2,1,0:T(8,128)(2,1)S(1)} %get-tuple-element.40), channel_id=1, source_target_pairs={{0,32},{32,0},{64,96},{96,64},{128,160},{160,128},{192,224},{224,1... | collective-permute-start | bytes 414728 | tf_op jit(solution)/shard_map/ppermute | solution.py:36
  108.6 19.8 %collective-permute-start.10 = (bf16[80,512]{1,0:T(8,128)(2,1)S(1)}, bf16[80,512]{1,0:T(8,128)(2,1)S(1)}, u32[]{:S(2)}, u32[]{:S(2)}) collective-permute-start(bf16[80,512]{1,0:T(8,128)(2,1)S(1)} %get-tuple-element.35), channel_id=1, source_target_pairs={{0,12},{4,0},{8,4},{12,8},{16,20},{20,24},{24,28},{28,16},{1,13},{... | collective-permute-start | bytes 245768 | tf_op jit(solution)/shard_map/ppermute | solution.py:51
  113.4 22.9 %collective-permute-start.9 = (bf16[80,512]{1,0:T(8,128)(2,1)S(1)}, bf16[80,512]{1,0:T(8,128)(2,1)S(1)}, u32[]{:S(2)}, u32[]{:S(2)}) collective-permute-start(bf16[80,512]{1,0:T(8,128)(2,1)S(1)} %shard_map.74.after), channel_id=1, source_target_pairs={{0,4},{4,8},{8,12},{12,0},{16,28},{20,16},{24,20},{28,24},{1,5},{5... | collective-permute-start | bytes 245768 | tf_op jit(solution)/shard_map/ppermute | solution.py:51
  123.7 16.7 %collective-permute-start.16 = (bf16[2,40,432]{2,1,0:T(8,128)(2,1)S(1)}, bf16[2,40,432]{2,1,0:T(8,128)(2,1)S(1)}, u32[]{:S(2)}, u32[]{:S(2)}) collective-permute-start(bf16[2,40,432]{2,1,0:T(8,128)(2,1)S(1)} %get-tuple-element.48), channel_id=1, source_target_pairs={{0,64},{32,96},{64,0},{96,32},{128,192},{160,224},{192,128},{224,1... | collective-permute-start | bytes 207368 | tf_op jit(solution)/shard_map/ppermute | solution.py:36
  136.3 15.9 %collective-permute-start.14 = (bf16[80,256]{1,0:T(8,128)(2,1)S(1)}, bf16[80,256]{1,0:T(8,128)(2,1)S(1)}, u32[]{:S(2)}, u32[]{:S(2)}) collective-permute-start(bf16[80,256]{1,0:T(8,128)(2,1)S(1)} %get-tuple-element.46), channel_id=1, source_target_pairs={{0,16},{16,0},{1,17},{17,1},{2,18},{18,2},{3,19},{19,3},{4,20},{20... | collective-permute-start | bytes 122888 | tf_op jit(solution)/shard_map/ppermute | solution.py:36
  140.9 12.5 %collective-permute-start.17 = (bf16[1,40,432]{2,1,0:T(8,128)(2,1)S(1)}, bf16[1,40,432]{2,1,0:T(8,128)(2,1)S(1)}, u32[]{:S(2)}, u32[]{:S(2)}) collective-permute-start(bf16[1,40,432]{2,1,0:T(8,128)(2,1)S(1)} %get-tuple-element.50), channel_id=1, source_target_pairs={{0,128},{32,160},{64,192},{96,224},{128,0},{160,32},{192,64},{224,... | collective-permute-start | bytes 103688 | tf_op jit(solution)/shard_map/ppermute | solution.py:36

commit v6 on v5

--- a/solution.py
+++ b/solution.py
@@ -82,7 +82,7 @@
     send[mine.shape[0] :, :] = pre[...]
 
 
-def weight_term(place, pre, mine, got, after, hidden, t0, t1, t2, t3, both, held, sems, *, stripe):
+def weight_term(place, pre, mine, got, hidden, t0, t1, t2, t3, both, held, sems, *, stripe):
     y, tokens, channels = place[1], pre.shape[1], mine.shape[0]
     copies = [
         pltpu.make_async_copy(mine, both.at[0], sems.at[0]),
@@ -127,16 +127,6 @@
     out[...] = (kept[0] + got[0].astype(F32)) * factor
 
 
-def order_rows(place, own, one, two, four, after, rows):
-    zl = place[2]
-    rows[zl] = own[...]
-    rows[zl ^ 4] = one[...]
-    for index, offset in enumerate((2, 6)):
-        rows[zl ^ offset] = two[index]
-    for index, offset in enumerate((1, 5, 3, 7)):
-        rows[zl ^ offset] = four[index]
-
-
 def output_terms(place, w0, w1, w2, w3, hidden, out, weight, held, sems):
     core, y, zh = place[0], place[1], place[3]
     group = out.shape[2]
@@ -162,7 +152,7 @@
         out[...] = value.astype(BF16)
 
 
-def sum_step(s1, got, t1):
+def sum_step(s1, got, after, t1):
     t1[...] = (s1[...].astype(F32) + got[...].astype(F32)).astype(BF16)
 
 
@@ -171,6 +161,10 @@
     total = (s0[...].astype(F32) + (u[...].astype(F32) + v[...].astype(F32))).astype(BF16)
     kept[...] = total[:, :half]
     given[...] = total[:, half:]
+
+
+def hidden_grad(pre, own, other, out):
+    out[...] = ((own[...] + other[...]) * gelu_slope(pre[...].astype(F32))).astype(BF16)
 
 
 def gate(value, after, out):
@@ -217,8 +211,7 @@
     work = 2 * tokens * channels * hid * 2
     pre = pre_act.T
 
-    one = swap(weight_out, "zl", 4)
-    first = jnp.stack([weight_out, one])
+    rows = lax.all_to_all(jnp.broadcast_to(weight_out[None], (n_zl, block, hid)), "zl", 0, 0)
     send, mine = call(
         functools.partial(sort_channels, block=block),
         [((channels + hid, tokens), BF16), ((channels, tokens), BF16)],
@@ -227,28 +220,19 @@
         flops=2 * 4 * tokens * stripe * stripe * 2 * 2,
         limit=56,
     )
-    two = swap(first, "zl", 2)
-    second = jnp.concatenate([first, two])
-    got = swap(hold(send, two), "c", 1)
+    got = swap(send, "c", 1)
     hidden, t0, t1, t2, t3, both = call(
         functools.partial(weight_term, stripe=stripe),
         [((hid, 2 * tokens), BF16)]
         + [pltpu.HBM((stripe, hid), BF16)] * n_y
         + [pltpu.HBM((2, channels, tokens), BF16)],
-        [SMEM] + [VMEM] * 3 + [LATER],
-        (place, pre, mine, got, second),
+        [SMEM] + [VMEM] * 3,
+        (place, pre, mine, got),
         flops=work,
         scratch=[pltpu.VMEM((n_y, stripe, hid), BF16), pltpu.SemaphoreType.DMA((2 + n_y,))],
         out_specs=[VMEM] + [HBM] * (n_y + 1),
     )
 
-    four = swap(second, "zl", 1)
-    (rows,) = call(
-        order_rows,
-        [((n_zl, block, hid), BF16)],
-        [SMEM] + [VMEM] * 4 + [LATER],
-        (place, weight_out, one, two, four, hidden),
-    )
     w0 = rows.reshape(stripe, hid)
     w1, w3, w2 = shift(w0, "y", -1), shift(w0, "y", 1), shift(w0, "y", 2)
 
@@ -269,14 +253,20 @@
     terms = [t.reshape(n_zl, block, hid) for t in (t0, t1, t2, t3)]
     s0, s1, s2, s3 = call(sum_x, [whole] * 4, [VMEM, LATER], (parts, terms[3]))
     got2 = shift_both(s2, 1)
-    (s1,) = call(sum_step, [whole], [VMEM] * 2, (s1, got2))
-    u, v = shift_both(s1, 1), shift_both(s3, -1)
     keep, send = call(
         split_y,
         [((quarter, block, hid), F32), ((quarter, block, hid), BF16)],
         [SMEM] + [VMEM] * 4 + [LATER],
-        (place, *terms, s1),
-    )
+        (place, *terms, s0),
+    )
+    keep, send = call(
+        functools.partial(split_zl, width=2),
+        [((quarter // 2, block, hid), F32), ((quarter // 2, block, hid), BF16)],
+        [SMEM, VMEM, VMEM],
+        (place, keep, swap(send, "zl", 1)),
+    )
+    (s1,) = call(sum_step, [whole], [VMEM] * 2 + [LATER], (s1, got2, keep))
+    u, v = shift_both(s1, 1), shift_both(s3, -1)
     own, other = call(
         hidden_terms,
         [((hid, tokens), F32)] * 2,
@@ -285,18 +275,15 @@
         flops=work,
     )
     keep, send = call(
-        functools.partial(split_zl, width=2),
-        [((quarter // 2, block, hid), F32), ((quarter // 2, block, hid), BF16)],
-        [SMEM, VMEM, VMEM],
-        (place, keep, swap(send, "zl", 1)),
-    )
-    kept, given = call(sum_last, [half] * 2, [VMEM] * 3 + [LATER] * 2, (s0, u, v, keep, own))
-    keep, send = call(
         functools.partial(split_zl, width=4),
         [((quarter // 4, block, hid), F32), ((quarter // 4, block, hid), BF16)],
         [SMEM, VMEM, VMEM],
         (place, keep, swap(send, "zl", 2)),
     )
+    (grad_pre,) = call(
+        hidden_grad, [((hid, tokens), BF16)], [VMEM] * 3, (pre, own, swap(other, "c", 1))
+    )
+    kept, given = call(sum_last, [half] * 2, [VMEM] * 3 + [LATER] * 2, (s0, u, v, keep, grad_pre))
     (grad_weight,) = call(
         functools.partial(sum_scaled, factor=factor),
         [((block, hid), F32)],
@@ -311,9 +298,7 @@
         (place, kept.reshape(-1, block, tokens), given.reshape(-1, block, tokens)),
     )
     output = output.reshape(-1, tokens).T
-    grad_hidden = own + swap(other, "c", 1)
-    grad_pre = (grad_hidden * gelu_slope(pre.astype(F32))).astype(BF16).T
-    return (output, grad_pre, grad_weight)
+    return (output, grad_pre.T, grad_weight)
 
 
 def solution(mesh):

time: 155 us -> 153 us (0.987)
  the two profiles are of different devices: /device:TPU:73 before, /device:TPU:1 now
where the time goes in v6:
time: 153 us; the launch traced here: 152 us
  starting transfers between devices  109 us (71%)
  waiting for transfers between devices  21.7 us (14%)
  Pallas kernels  16.2 us (11%)
  local copies, waits for them, and re-layouts  4.25 us (3%)
    ppermute x6, starting transfers between devices, swap(): return lax.ppermute(value, axis, [(i, i ^ distance) for i in range(size)])  35.7 us
    ppermute x3, starting transfers between devices, shift_both(): return lax.ppermute(value, ('c', 'zh'), pairs)  29.2 us
    ppermute x6, starting transfers between devices, shift(): lax.ppermute(value, axis, [(i, (i + distance) % size) for i in range(size)])  25.2 us
    ppermute x6, waiting for transfers between devices, swap(): return lax.ppermute(value, axis, [(i, i ^ distance) for i in range(size)])  16.8 us
    pallas_call x13, Pallas kernels, call(): pl.pallas_call(body, out_shape=[s if isinstance(s, pl.MemoryRef) else jax...  16.2 us
    all_to_all x1, starting transfers between devices, local(): lax.all_to_all(jnp.broadcast_to(weight_out[None], (n_zl, block, hid)), 'z...  13.1 us
    all_to_all x1, starting transfers between devices, local(): parts = lax.all_to_all(parts, 'x', 0, 0)  5.8 us
  transfers between devices with their start and end apart: 17, of which 6 were waited for; matrix products, arithmetic and copies ran while one was open for 0% of the time, Pallas kernels for 8%

profile of v6, /device:TPU:1, one launch (start us, length us, event | category | flops | bytes accessed | tf_op | source)
XLA Modules:
  0.0 152.1 jit_solution(4006548855651676030)
XLA Ops:
  0.6 1.6 %broadcast_in_dim.2 = bf16[8,40,432]{2,1,0:T(8,128)(2,1)} broadcast(bf16[40,432]{1,0:T(8,128)(2,1)} %param.5), dimensions={1,2} | broadcast | bytes 311040 | tf_op jit(solution)/shard_map/broadcast_in_dim | solution.py:214
  2.2 13.1 %all-to-all-start = ((bf16[8,40,432]{2,1,0:T(8,128)(2,1)}), bf16[8,40,432]{2,1,0:T(8,128)(2,1)S(1)}, u32[]{:S(2)}, u32[]{:S(2)}) async-start(bf16[8,40,432]{2,1,0:T(8,128)(2,1)} %broadcast_in_dim.2), calls=%async_computation | async-start | bytes 655360 | tf_op jit(solution)/shard_map/all_to_all | solution.py:214
  15.3 0.7 stack.23.place
  15.9 3.8 %shard_map.67 = (bf16[1712,256]{1,0:T(8,128)(2,1)}, bf16[1280,256]{1,0:T(8,128)(2,1)}) custom-call(s32[5]{0:T(128)} %stack.23.place, s32[320,1]{1,0:T(8,128)} %constant.25.clone.base, bf16[256,2560]{1,0:T(8,128)(2,1)} %cot.1, bf16[432,256]{1,0:T(8,128)(2,1)} %bitcast.26), custom_call_target="tpu_custom_call" | custom-call | flops 838860800 | bytes 2299481 | tf_op jit(solution)/shard_map/pallas_call | solution.py:61
  19.8 6.4 %collective-permute-start.3 = (bf16[1712,256]{1,0:T(8,128)(2,1)}, bf16[1712,256]{1,0:T(8,128)(2,1)S(1)}, u32[]{:S(2)}, u32[]{:S(2)}) collective-permute-start(bf16[1712,256]{1,0:T(8,128)(2,1)} %get-tuple-element.28), channel_id=1, source_target_pairs={{0,16},{16,0},{1,17},{17,1},{2,18},{18,2},{3,19},{19,3},{4,20},{20... | collective-permute-start | bytes 2629640 | tf_op jit(solution)/shard_map/ppermute | solution.py:36
  26.2 1.9 %all-to-all-done = bf16[8,40,432]{2,1,0:T(8,128)(2,1)S(1)} async-done(((bf16[8,40,432]{2,1,0:T(8,128)(2,1)}), bf16[8,40,432]{2,1,0:T(8,128)(2,1)S(1)}, u32[]{:S(2)}, u32[]{:S(2)}) %all-to-all-start) | async-done | bytes 276512 | tf_op jit(solution)/shard_map/all_to_all | solution.py:214
  28.1 6.1 %collective-permute-start.2 = (bf16[320,432]{1,0:T(8,128)(2,1)S(1)}, bf16[320,432]{1,0:T(8,128)(2,1)S(1)}, u32[]{:S(2)}, u32[]{:S(2)}) collective-permute-start(bf16[320,432]{1,0:T(8,128)(2,1)S(1)} %bitcast.22), channel_id=1, source_target_pairs={{0,256},{256,512},{512,768},{768,0},{1,257},{257,513},{513,769},{7... | collective-permute-start | bytes 829448 | tf_op jit(solution)/shard_map/ppermute | solution.py:41
  34.2 4.5 %collective-permute-start.1 = (bf16[320,432]{1,0:T(8,128)(2,1)S(1)}, bf16[320,432]{1,0:T(8,128)(2,1)S(1)}, u32[]{:S(2)}, u32[]{:S(2)}) collective-permute-start(bf16[320,432]{1,0:T(8,128)(2,1)S(1)} %bitcast.23), channel_id=1, source_target_pairs={{0,512},{256,768},{512,0},{768,256},{1,513},{257,769},{513,1},{769... | collective-permute-start | bytes 829448 | tf_op jit(solution)/shard_map/ppermute | solution.py:41
  38.7 3.0 %collective-permute-start = (bf16[320,432]{1,0:T(8,128)(2,1)S(1)}, bf16[320,432]{1,0:T(8,128)(2,1)S(1)}, u32[]{:S(2)}, u32[]{:S(2)}) collective-permute-start(bf16[320,432]{1,0:T(8,128)(2,1)S(1)} %bitcast.24), channel_id=1, source_target_pairs={{0,768},{256,0},{512,256},{768,512},{1,769},{257,1},{513,257},{769... | collective-permute-start | bytes 829448 | tf_op jit(solution)/shard_map/ppermute | solution.py:41
  41.7 0.0 collective-permute-done.3.got
  41.8 1.1 copy-done.7
  42.8 2.4 %shard_map.68 = (bf16[432,512]{1,0:T(8,128)(2,1)S(1)}, bf16[320,432]{1,0:T(8,128)(2,1)}, bf16[320,432]{1,0:T(8,128)(2,1)}, bf16[320,432]{1,0:T(8,128)(2,1)}, bf1...) custom-call(s32[5]{0:T(128)S(1)} %copy-done.6, bf16[432,256]{1,0:T(8,128)(2,1)S(1)} %bitcast.27, ...), custom_call_target="tpu_custom_call" | custom-call | flops 566231040 | bytes 2629657 | tf_op jit(solution)/shard_map/pallas_call | solution.py:61
  45.2 0.0 collective-permute-done.2.w3
  45.2 1.8 %collective-permute-done.1.w2 = bf16[320,432]{1,0:T(8,128)(2,1)S(1)} collective-permute-done((bf16[320,432]{1,0:T(8,128)(2,1)S(1)}, bf16[320,432]{1,0:T(8,128)(2,1)S(1)}, u32[]{:S(2)}, u32[]{:S(2)}) %collective-permute-start.1) | collective-permute-done | bytes 276512 | tf_op jit(solution)/shard_map/ppermute | solution.py:41
  47.0 0.8 collective-permute-done.w1
  47.8 2.2 %shard_map.69 = (bf16[4,4,80,512]{3,2,1,0:T(8,128)(2,1)}, bf16[4,320,432]{2,1,0:T(8,128)(2,1)}) custom-call(s32[5]{0:T(128)S(1)} %copy-done.6, bf16[320,432]{1,0:T(8,128)(2,1)S(1)} %bitcast.25, bf16[320,432]{1,0:T(8,128)(2,1)S(1)} %collective-permute-done.w1, bf16[320,432]{1,0:T(8,128)(2,1)S(1)} %collective-permute-done.1.w2, ...), custom_call_target="tpu_custom_call" | custom-call | flops 566231040 | bytes 2322457 | tf_op jit(solution)/shard_map/pallas_call | solution.py:61
  50.0 5.8 %all-to-all-start.1 = ((bf16[4,4,80,512]{3,2,1,0:T(8,128)(2,1)}), bf16[4,4,80,512]{3,2,1,0:T(8,128)(2,1)S(1)}, u32[]{:S(2)}, u32[]{:S(2)}) async-start(bf16[4,4,80,512]{3,2,1,0:T(8,128)(2,1)} %get-tuple-element.30.after), calls=%async_computation.1 | async-start | bytes 2621440 | tf_op jit(solution)/shard_map/all_to_all | solution.py:249
  55.8 5.4 %collective-permute-start.4 = (bf16[320,432]{1,0:T(8,128)(2,1)}, bf16[320,432]{1,0:T(8,128)(2,1)S(1)}, u32[]{:S(2)}, u32[]{:S(2)}) collective-permute-start(bf16[320,432]{1,0:T(8,128)(2,1)} %shard_map.70), channel_id=1, source_target_pairs={{0,768},{256,0},{512,256},{768,512},{1,769},{257,1},{513,257},{769... | collective-permute-start | bytes 829448 | tf_op jit(solution)/shard_map/ppermute | solution.py:41
  61.2 2.5 %collective-permute-start.6 = (bf16[320,432]{1,0:T(8,128)(2,1)}, bf16[320,432]{1,0:T(8,128)(2,1)S(1)}, u32[]{:S(2)}, u32[]{:S(2)}) collective-permute-start(bf16[320,432]{1,0:T(8,128)(2,1)} %shard_map.72), channel_id=1, source_target_pairs={{0,256},{256,512},{512,768},{768,0},{1,257},{257,513},{513,769},{7... | collective-permute-start | bytes 829448 | tf_op jit(solution)/shard_map/ppermute | solution.py:41
  63.8 3.7 %collective-permute-start.7 = (bf16[320,432]{1,0:T(8,128)(2,1)}, bf16[320,432]{1,0:T(8,128)(2,1)}, u32[]{:S(2)}, u32[]{:S(2)}) collective-permute-start(bf16[320,432]{1,0:T(8,128)(2,1)} %shard_map.73), channel_id=1, source_target_pairs={{0,512},{256,768},{512,0},{768,256},{1,513},{257,769},{513,1},{769... | collective-permute-start | bytes 829448 | tf_op jit(solution)/shard_map/ppermute | solution.py:41
  67.5 2.5 %shard_map.78 = (f32[432,256]{1,0:T(8,128)S(1)}, f32[432,256]{1,0:T(8,128)}) custom-call(s32[5]{0:T(128)S(1)} %copy-done.6, bf16[4,320,432]{2,1,0:T(8,128)(2,1)S(1)} %copy-done.2, bf16[2,1280,256]{2,1,0:T(8,128)(2,1)S(1)} %copy-done.1), custom_call_target="tpu_custom_call" | custom-call | flops 566231040 | bytes 3624985 | tf_op jit(solution)/shard_map/pallas_call | solution.py:61
  69.9 6.2 %collective-permute-start.12 = (f32[432,256]{1,0:T(8,128)}, f32[432,256]{1,0:T(8,128)S(1)}, u32[]{:S(2)}, u32[]{:S(2)}) collective-permute-start(f32[432,256]{1,0:T(8,128)} %get-tuple-element.47), channel_id=1, source_target_pairs={{0,16},{16,0},{1,17},{17,1},{2,18},{18,2},{3,19},{19,3},{4,20},{20... | collective-permute-start | bytes 1327112 | tf_op jit(solution)/shard_map/ppermute | solution.py:36
  76.1 0.0 collective-permute-done.4
  76.1 0.0 all-to-all-done.1.parts
  76.1 0.2 shard_map.71
  76.3 0.4 collective-permute-done.7
  76.7 1.1 shard_map.74
  77.9 10.3 %collective-permute-start.8 = (bf16[4,40,432]{2,1,0:T(8,128)(2,1)S(1)}, bf16[4,40,432]{2,1,0:T(8,128)(2,1)S(1)}, u32[]{:S(2)}, u32[]{:S(2)}) collective-permute-start(bf16[4,40,432]{2,1,0:T(8,128)(2,1)S(1)} %get-tuple-element.39), channel_id=1, source_target_pairs={{0,32},{32,0},{64,96},{96,64},{128,160},{160,128},{192,224},{224,1... | collective-permute-start | bytes 414728 | tf_op jit(solution)/shard_map/ppermute | solution.py:36
  88.2 15.2 %collective-permute-start.5 = (bf16[80,512]{1,0:T(8,128)(2,1)S(1)}, bf16[80,512]{1,0:T(8,128)(2,1)S(1)}, u32[]{:S(2)}, u32[]{:S(2)}) collective-permute-start(bf16[80,512]{1,0:T(8,128)(2,1)S(1)} %get-tuple-element.34), channel_id=1, source_target_pairs={{0,4},{4,8},{8,12},{12,0},{16,28},{20,16},{24,20},{28,24},{1,5},{5... | collective-permute-start | bytes 245768 | tf_op jit(solution)/shard_map/ppermute | solution.py:51
  103.4 2.2 %collective-permute-start.10 = (bf16[80,512]{1,0:T(8,128)(2,1)S(1)}, bf16[80,512]{1,0:T(8,128)(2,1)S(1)}, u32[]{:S(2)}, u32[]{:S(2)}) collective-permute-start(bf16[80,512]{1,0:T(8,128)(2,1)S(1)} %get-tuple-element.41), channel_id=1, source_target_pairs={{0,12},{4,0},{8,4},{12,8},{16,20},{20,24},{24,28},{28,16},{1,13},{... | collective-permute-start | bytes 245768 | tf_op jit(solution)/shard_map/ppermute | solution.py:51
  105.6 0.0 collective-permute-done.8.got
  105.6 0.6 shard_map.75
  106.2 0.0 collective-permute-done.5.got
  106.2 11.8 %collective-permute-start.9 = (bf16[80,512]{1,0:T(8,128)(2,1)S(1)}, bf16[80,512]{1,0:T(8,128)(2,1)S(1)}, u32[]{:S(2)}, u32[]{:S(2)}) collective-permute-start(bf16[80,512]{1,0:T(8,128)(2,1)S(1)} %shard_map.76), channel_id=1, source_target_pairs={{0,4},{4,8},{8,12},{12,0},{16,28},{20,16},{24,20},{28,24},{1,5},{5... | collective-permute-start | bytes 245768 | tf_op jit(solution)/shard_map/ppermute | solution.py:51
  118.1 1.9 %collective-permute-start.11 = (bf16[2,40,432]{2,1,0:T(8,128)(2,1)S(1)}, bf16[2,40,432]{2,1,0:T(8,128)(2,1)S(1)}, u32[]{:S(2)}, u32[]{:S(2)}) collective-permute-start(bf16[2,40,432]{2,1,0:T(8,128)(2,1)S(1)} %get-tuple-element.42), channel_id=1, source_target_pairs={{0,64},{32,96},{64,0},{96,32},{128,192},{160,224},{192,128},{224,1... | collective-permute-start | bytes 207368 | tf_op jit(solution)/shard_map/ppermute | solution.py:36
  120.0 0.0 collective-permute-done.12.other
  120.0 1.0 shard_map.79.then
  121.0 9.8 %collective-permute-done.11.got = bf16[2,40,432]{2,1,0:T(8,128)(2,1)S(1)} collective-permute-done((bf16[2,40,432]{2,1,0:T(8,128)(2,1)S(1)}, bf16[2,40,432]{2,1,0:T(8,128)(2,1)S(1)}, u32[]{:S(2)}, u32[]{:S(2)}) %collective-permute-start.11) | collective-permute-done | bytes 69152 | tf_op jit(solution)/shard_map/ppermute | solution.py:36
  130.8 0.6 shard_map.77
  131.4 0.0 collective-permute-done.9.u
  131.4 0.0 copy-start.3
  131.4 0.9 copy-done.3
  132.3 6.0 %collective-permute-start.13 = (bf16[80,256]{1,0:T(8,128)(2,1)S(1)}, bf16[80,256]{1,0:T(8,128)(2,1)S(1)}, u32[]{:S(2)}, u32[]{:S(2)}) collective-permute-start(bf16[80,256]{1,0:T(8,128)(2,1)S(1)} %get-tuple-element.49), channel_id=1, source_target_pairs={{0,16},{16,0},{1,17},{17,1},{2,18},{18,2},{3,19},{19,3},{4,20},{20... | collective-permute-start | bytes 122888 | tf_op jit(solution)/shard_map/ppermute | solution.py:36
  138.4 4.8 %collective-permute-start.14 = (bf16[1,40,432]{2,1,0:T(8,128)(2,1)S(1)}, bf16[1,40,432]{2,1,0:T(8,128)(2,1)S(1)}, u32[]{:S(2)}, u32[]{:S(2)}) collective-permute-start(bf16[1,40,432]{2,1,0:T(8,128)(2,1)S(1)} %get-tuple-element.50), channel_id=1, source_target_pairs={{0,128},{32,160},{64,192},{96,224},{128,0},{160,32},{192,64},{224,... | collective-permute-start | bytes 103688 | tf_op jit(solution)/shard_map/ppermute | solution.py:36
  143.2 7.0 %collective-permute-done.14.got = bf16[1,40,432]{2,1,0:T(8,128)(2,1)S(1)} collective-permute-done((bf16[1,40,432]{2,1,0:T(8,128)(2,1)S(1)}, bf16[1,40,432]{2,1,0:T(8,128)(2,1)S(1)}, u32[]{:S(2)}, u32[]{:S(2)}) %collective-permute-start.14) | collective-permute-done | bytes 34592 | tf_op jit(solution)/shard_map/ppermute | solution.py:36
  150.3 0.6 shard_map.82
  150.9 0.0 collective-permute-done.13
  150.9 1.2 shard_map.81
  (20 shorter events, 0.1 us)
Async XLA Ops:
  2.2 25.9 %all-to-all-start = ((bf16[8,40,432]{2,1,0:T(8,128)(2,1)}), bf16[8,40,432]{2,1,0:T(8,128)(2,1)S(1)}, u32[]{:S(2)}, u32[]{:S(2)}) async-start(bf16[8,40,432]{2,1,0:T(8,128)(2,1)} %broadcast_in_dim.2), calls=%async_computation | async-start | bytes 655360 | tf_op jit(solution)/shard_map/all_to_all | solution.py:214
  15.9 25.8 %copy-start.5 = (bf16[256,432]{0,1:T(8,128)(2,1)S(1)}, bf16[256,432]{0,1:T(8,128)(2,1)}, u32[]{:S(2)}) copy-start(bf16[256,432]{0,1:T(8,128)(2,1)} %param.4) | copy-start | bytes 663556
  15.9 25.8 %copy-start.6 = (s32[5]{0:T(128)S(1)}, s32[5]{0:T(128)}, u32[]{:S(2)}) copy-start(s32[5]{0:T(128)} %stack.23.place) | copy-start | bytes 64
  19.8 22.0 %collective-permute-start.3 = (bf16[1712,256]{1,0:T(8,128)(2,1)}, bf16[1712,256]{1,0:T(8,128)(2,1)S(1)}, u32[]{:S(2)}, u32[]{:S(2)}) collective-permute-start(bf16[1712,256]{1,0:T(8,128)(2,1)} %get-tuple-element.28), channel_id=1, source_target_pairs={{0,16},{16,0},{1,17},{17,1},{2,18},{18,2},{3,19},{19,3},{4,20},{20... | collective-permute-start | bytes 2629640 | tf_op jit(solution)/shard_map/ppermute | solution.py:36
  28.1 17.1 %collective-permute-start.2 = (bf16[320,432]{1,0:T(8,128)(2,1)S(1)}, bf16[320,432]{1,0:T(8,128)(2,1)S(1)}, u32[]{:S(2)}, u32[]{:S(2)}) collective-permute-start(bf16[320,432]{1,0:T(8,128)(2,1)S(1)} %bitcast.22), channel_id=1, source_target_pairs={{0,256},{256,512},{512,768},{768,0},{1,257},{257,513},{513,769},{7... | collective-permute-start | bytes 829448 | tf_op jit(solution)/shard_map/ppermute | solution.py:41
  34.2 12.8 %collective-permute-start.1 = (bf16[320,432]{1,0:T(8,128)(2,1)S(1)}, bf16[320,432]{1,0:T(8,128)(2,1)S(1)}, u32[]{:S(2)}, u32[]{:S(2)}) collective-permute-start(bf16[320,432]{1,0:T(8,128)(2,1)S(1)} %bitcast.23), channel_id=1, source_target_pairs={{0,512},{256,768},{512,0},{768,256},{1,513},{257,769},{513,1},{769... | collective-permute-start | bytes 829448 | tf_op jit(solution)/shard_map/ppermute | solution.py:41
  38.7 9.0 %collective-permute-start = (bf16[320,432]{1,0:T(8,128)(2,1)S(1)}, bf16[320,432]{1,0:T(8,128)(2,1)S(1)}, u32[]{:S(2)}, u32[]{:S(2)}) collective-permute-start(bf16[320,432]{1,0:T(8,128)(2,1)S(1)} %bitcast.24), channel_id=1, source_target_pairs={{0,768},{256,0},{512,256},{768,512},{1,769},{257,1},{513,257},{769... | collective-permute-start | bytes 829448 | tf_op jit(solution)/shard_map/ppermute | solution.py:41
  41.8 1.1 copy-start.7
  50.0 5.8 %copy-start = (bf16[4,4,80,512]{3,2,1,0:T(8,128)(2,1)S(1)}, bf16[4,4,80,512]{3,2,1,0:T(8,128)(2,1)}, u32[]{:S(2)}) copy-start(bf16[4,4,80,512]{3,2,1,0:T(8,128)(2,1)} %get-tuple-element.30.after) | copy-start | bytes 3932164
  50.0 26.2 %all-to-all-start.1 = ((bf16[4,4,80,512]{3,2,1,0:T(8,128)(2,1)}), bf16[4,4,80,512]{3,2,1,0:T(8,128)(2,1)S(1)}, u32[]{:S(2)}, u32[]{:S(2)}) async-start(bf16[4,4,80,512]{3,2,1,0:T(8,128)(2,1)} %get-tuple-element.30.after), calls=%async_computation.1 | async-start | bytes 2621440 | tf_op jit(solution)/shard_map/all_to_all | solution.py:249
  55.8 20.3 %collective-permute-start.4 = (bf16[320,432]{1,0:T(8,128)(2,1)}, bf16[320,432]{1,0:T(8,128)(2,1)S(1)}, u32[]{:S(2)}, u32[]{:S(2)}) collective-permute-start(bf16[320,432]{1,0:T(8,128)(2,1)} %shard_map.70), channel_id=1, source_target_pairs={{0,768},{256,0},{512,256},{768,512},{1,769},{257,1},{513,257},{769... | collective-permute-start | bytes 829448 | tf_op jit(solution)/shard_map/ppermute | solution.py:41
  61.2 6.3 %copy-start.2 = (bf16[4,320,432]{2,1,0:T(8,128)(2,1)S(1)}, bf16[4,320,432]{2,1,0:T(8,128)(2,1)}, u32[]{:S(2)}) copy-start(bf16[4,320,432]{2,1,0:T(8,128)(2,1)} %get-tuple-element.44.weight) | copy-start | bytes 3317764
  61.2 6.3 %copy-start.1 = (bf16[2,1280,256]{2,1,0:T(8,128)(2,1)S(1)}, bf16[2,1280,256]{2,1,0:T(8,128)(2,1)}, u32[]{:S(2)}) copy-start(bf16[2,1280,256]{2,1,0:T(8,128)(2,1)} %get-tuple-element.45.both) | copy-start | bytes 3932164
  61.2 15.1 %collective-permute-start.6 = (bf16[320,432]{1,0:T(8,128)(2,1)}, bf16[320,432]{1,0:T(8,128)(2,1)S(1)}, u32[]{:S(2)}, u32[]{:S(2)}) collective-permute-start(bf16[320,432]{1,0:T(8,128)(2,1)} %shard_map.72), channel_id=1, source_target_pairs={{0,256},{256,512},{512,768},{768,0},{1,257},{257,513},{513,769},{7... | collective-permute-start | bytes 829448 | tf_op jit(solution)/shard_map/ppermute | solution.py:41
  63.8 13.0 %collective-permute-start.7 = (bf16[320,432]{1,0:T(8,128)(2,1)}, bf16[320,432]{1,0:T(8,128)(2,1)}, u32[]{:S(2)}, u32[]{:S(2)}) collective-permute-start(bf16[320,432]{1,0:T(8,128)(2,1)} %shard_map.73), channel_id=1, source_target_pairs={{0,512},{256,768},{512,0},{768,256},{1,513},{257,769},{513,1},{769... | collective-permute-start | bytes 829448 | tf_op jit(solution)/shard_map/ppermute | solution.py:41
  69.9 6.8 %copy-start.4 = (bf16[320,432]{1,0:T(8,128)(2,1)S(1)}, bf16[320,432]{1,0:T(8,128)(2,1)}, u32[]{:S(2)}) copy-start(bf16[320,432]{1,0:T(8,128)(2,1)} %get-tuple-element.35) | copy-start | bytes 829444
  69.9 50.0 %collective-permute-start.12 = (f32[432,256]{1,0:T(8,128)}, f32[432,256]{1,0:T(8,128)S(1)}, u32[]{:S(2)}, u32[]{:S(2)}) collective-permute-start(f32[432,256]{1,0:T(8,128)} %get-tuple-element.47), channel_id=1, source_target_pairs={{0,16},{16,0},{1,17},{17,1},{2,18},{18,2},{3,19},{19,3},{4,20},{20... | collective-permute-start | bytes 1327112 | tf_op jit(solution)/shard_map/ppermute | solution.py:36
  77.9 27.7 %collective-permute-start.8 = (bf16[4,40,432]{2,1,0:T(8,128)(2,1)S(1)}, bf16[4,40,432]{2,1,0:T(8,128)(2,1)S(1)}, u32[]{:S(2)}, u32[]{:S(2)}) collective-permute-start(bf16[4,40,432]{2,1,0:T(8,128)(2,1)S(1)} %get-tuple-element.39), channel_id=1, source_target_pairs={{0,32},{32,0},{64,96},{96,64},{128,160},{160,128},{192,224},{224,1... | collective-permute-start | bytes 414728 | tf_op jit(solution)/shard_map/ppermute | solution.py:36
  88.2 18.0 %collective-permute-start.5 = (bf16[80,512]{1,0:T(8,128)(2,1)S(1)}, bf16[80,512]{1,0:T(8,128)(2,1)S(1)}, u32[]{:S(2)}, u32[]{:S(2)}) collective-permute-start(bf16[80,512]{1,0:T(8,128)(2,1)S(1)} %get-tuple-element.34), channel_id=1, source_target_pairs={{0,4},{4,8},{8,12},{12,0},{16,28},{20,16},{24,20},{28,24},{1,5},{5... | collective-permute-start | bytes 245768 | tf_op jit(solution)/shard_map/ppermute | solution.py:51
  103.4 27.9 %collective-permute-start.10 = (bf16[80,512]{1,0:T(8,128)(2,1)S(1)}, bf16[80,512]{1,0:T(8,128)(2,1)S(1)}, u32[]{:S(2)}, u32[]{:S(2)}) collective-permute-start(bf16[80,512]{1,0:T(8,128)(2,1)S(1)} %get-tuple-element.41), channel_id=1, source_target_pairs={{0,12},{4,0},{8,4},{12,8},{16,20},{20,24},{24,28},{28,16},{1,13},{... | collective-permute-start | bytes 245768 | tf_op jit(solution)/shard_map/ppermute | solution.py:51
  106.2 25.1 %collective-permute-start.9 = (bf16[80,512]{1,0:T(8,128)(2,1)S(1)}, bf16[80,512]{1,0:T(8,128)(2,1)S(1)}, u32[]{:S(2)}, u32[]{:S(2)}) collective-permute-start(bf16[80,512]{1,0:T(8,128)(2,1)S(1)} %shard_map.76), channel_id=1, source_target_pairs={{0,4},{4,8},{8,12},{12,0},{16,28},{20,16},{24,20},{28,24},{1,5},{5... | collective-permute-start | bytes 245768 | tf_op jit(solution)/shard_map/ppermute | solution.py:51
  118.1 12.7 %collective-permute-start.11 = (bf16[2,40,432]{2,1,0:T(8,128)(2,1)S(1)}, bf16[2,40,432]{2,1,0:T(8,128)(2,1)S(1)}, u32[]{:S(2)}, u32[]{:S(2)}) collective-permute-start(bf16[2,40,432]{2,1,0:T(8,128)(2,1)S(1)} %get-tuple-element.42), channel_id=1, source_target_pairs={{0,64},{32,96},{64,0},{96,32},{128,192},{160,224},{192,128},{224,1... | collective-permute-start | bytes 207368 | tf_op jit(solution)/shard_map/ppermute | solution.py:36
  131.4 0.9 copy-start.3
  132.3 18.6 %collective-permute-start.13 = (bf16[80,256]{1,0:T(8,128)(2,1)S(1)}, bf16[80,256]{1,0:T(8,128)(2,1)S(1)}, u32[]{:S(2)}, u32[]{:S(2)}) collective-permute-start(bf16[80,256]{1,0:T(8,128)(2,1)S(1)} %get-tuple-element.49), channel_id=1, source_target_pairs={{0,16},{16,0},{1,17},{17,1},{2,18},{18,2},{3,19},{19,3},{4,20},{20... | collective-permute-start | bytes 122888 | tf_op jit(solution)/shard_map/ppermute | solution.py:36
  138.4 11.9 %collective-permute-start.14 = (bf16[1,40,432]{2,1,0:T(8,128)(2,1)S(1)}, bf16[1,40,432]{2,1,0:T(8,128)(2,1)S(1)}, u32[]{:S(2)}, u32[]{:S(2)}) collective-permute-start(bf16[1,40,432]{2,1,0:T(8,128)(2,1)S(1)} %get-tuple-element.50), channel_id=1, source_target_pairs={{0,128},{32,160},{64,192},{96,224},{128,0},{160,32},{192,64},{224,... | collective-permute-start | bytes 103688 | tf_op jit(solution)/shard_map/ppermute | solution.py:36

commit v7 on v6

--- a/solution.py
+++ b/solution.py
@@ -103,34 +103,26 @@
         copy.wait()
 
 
-def split_y(place, p0, p1, p2, p3, after, keep, send):
-    bit = place[2] % 2
-
-    def total(index):
-        value = p0[index].astype(F32) + p1[index].astype(F32)
-        return value + (p2[index].astype(F32) + p3[index].astype(F32))
-
-    for index in range(keep.shape[0]):
-        keep[index] = total(2 * index + bit)
-        send[index] = total(2 * index + 1 - bit).astype(BF16)
-
-
-def split_zl(place, kept, got, keep, send, *, width):
-    bit = place[2] // width % 2
-    for index in range(keep.shape[0]):
-        near, far = 2 * index + bit, 2 * index + 1 - bit
-        keep[index] = kept[near] + got[near].astype(F32)
-        send[index] = (kept[far] + got[far].astype(F32)).astype(BF16)
-
-
-def sum_scaled(kept, got, out, *, factor):
-    out[...] = (kept[0] + got[0].astype(F32)) * factor
-
-
-def output_terms(place, w0, w1, w2, w3, hidden, out, weight, held, sems):
+def sum_y(p0, p1, p2, p3, after, then, out, held, sem):
+    value = p0[...].astype(F32) + p1[...].astype(F32)
+    held[...] = (value + (p2[...].astype(F32) + p3[...].astype(F32))).astype(BF16)
+    copy = pltpu.make_async_copy(held, out, sem)
+    copy.start()
+    copy.wait()
+
+
+def sum_scaled(parts, out, *, factor):
+    total = parts[0].astype(F32)
+    for index in range(1, parts.shape[0]):
+        total += parts[index].astype(F32)
+    out[...] = total * factor
+
+
+def output_terms(place, w0, w1, w2, w3, hidden, out, weight, token, held, sems):
     core, y, zh = place[0], place[1], place[3]
     group = out.shape[2]
     pieces = (w0, w1, w2, w3)
+    token[...] = jnp.zeros_like(token)
     copies = [pltpu.make_async_copy(p, weight.at[k], sems.at[k]) for k, p in enumerate(pieces)]
     for copy in copies:
         copy.start()
@@ -156,14 +148,15 @@
     t1[...] = (s1[...].astype(F32) + got[...].astype(F32)).astype(BF16)
 
 
-def sum_last(s0, u, v, after, then, kept, given):
+def sum_last(s0, u, v, kept, given):
     half = kept.shape[1]
     total = (s0[...].astype(F32) + (u[...].astype(F32) + v[...].astype(F32))).astype(BF16)
     kept[...] = total[:, :half]
     given[...] = total[:, half:]
 
 
-def hidden_grad(pre, own, other, out):
+def hidden_grad(pre, own, other, out, token):
+    token[...] = jnp.zeros_like(token)
     out[...] = ((own[...] + other[...]) * gelu_slope(pre[...].astype(F32))).astype(BF16)
 
 
@@ -236,37 +229,20 @@
     w0 = rows.reshape(stripe, hid)
     w1, w3, w2 = shift(w0, "y", -1), shift(w0, "y", 1), shift(w0, "y", 2)
 
-    parts, weight = call(
+    parts, weight, token = call(
         output_terms,
-        [pltpu.HBM((n_x, n_y, group, 2 * tokens), BF16), pltpu.HBM((n_y, stripe, hid), BF16)],
+        [pltpu.HBM((n_x, n_y, group, 2 * tokens), BF16), pltpu.HBM((n_y, stripe, hid), BF16), ((8, 128), F32)],
         [SMEM] + [VMEM] * 5,
         (place, w0, w1, w2, w3, hidden),
         flops=work,
         scratch=[pltpu.VMEM((n_y, n_x, group, 2 * tokens), BF16), pltpu.SemaphoreType.DMA((2 * n_y,))],
-        out_specs=[HBM, HBM],
-    )
-    t1, t2, t3 = (shift(hold(t, parts, HBM), "y", k) for k, t in ((1, t1), (2, t2), (3, t3)))
+        out_specs=[HBM, HBM, VMEM],
+    )
+    t1, t2, t3 = (shift(hold(t, token), "y", k) for k, t in ((1, t1), (2, t2), (3, t3)))
     parts = lax.all_to_all(parts, "x", 0, 0)
 
     whole, half = ((group, 2 * tokens), BF16), ((group, tokens), BF16)
-    quarter = n_zl // 2
     terms = [t.reshape(n_zl, block, hid) for t in (t0, t1, t2, t3)]
-    s0, s1, s2, s3 = call(sum_x, [whole] * 4, [VMEM, LATER], (parts, terms[3]))
-    got2 = shift_both(s2, 1)
-    keep, send = call(
-        split_y,
-        [((quarter, block, hid), F32), ((quarter, block, hid), BF16)],
-        [SMEM] + [VMEM] * 4 + [LATER],
-        (place, *terms, s0),
-    )
-    keep, send = call(
-        functools.partial(split_zl, width=2),
-        [((quarter // 2, block, hid), F32), ((quarter // 2, block, hid), BF16)],
-        [SMEM, VMEM, VMEM],
-        (place, keep, swap(send, "zl", 1)),
-    )
-    (s1,) = call(sum_step, [whole], [VMEM] * 2 + [LATER], (s1, got2, keep))
-    u, v = shift_both(s1, 1), shift_both(s3, -1)
     own, other = call(
         hidden_terms,
         [((hid, tokens), F32)] * 2,
@@ -274,21 +250,27 @@
         (place, weight, both),
         flops=work,
     )
-    keep, send = call(
-        functools.partial(split_zl, width=4),
-        [((quarter // 4, block, hid), F32), ((quarter // 4, block, hid), BF16)],
-        [SMEM, VMEM, VMEM],
-        (place, keep, swap(send, "zl", 2)),
-    )
-    (grad_pre,) = call(
-        hidden_grad, [((hid, tokens), BF16)], [VMEM] * 3, (pre, own, swap(other, "c", 1))
-    )
-    kept, given = call(sum_last, [half] * 2, [VMEM] * 3 + [LATER] * 2, (s0, u, v, keep, grad_pre))
+    grad_pre, token = call(
+        hidden_grad, [((hid, tokens), BF16), ((8, 128), F32)], [VMEM] * 3, (pre, own, swap(other, "c", 1))
+    )
+    s0, s1, s2, s3 = call(sum_x, [whole] * 4, [VMEM, LATER], (parts, token))
+    got2, v = shift_both(s2, 1), shift_both(s3, -1)
+    (term,) = call(
+        sum_y,
+        [pltpu.HBM((n_zl, block, hid), BF16)],
+        [VMEM] * 4 + [LATER] * 2,
+        (*terms, got2, v),
+        scratch=[pltpu.VMEM((n_zl, block, hid), BF16), pltpu.SemaphoreType.DMA],
+        out_specs=[HBM],
+    )
+    (t1,) = call(sum_step, [whole], [VMEM] * 2 + [LATER], (s1, got2, v))
+    u = shift_both(t1, 1)
+    kept, given = call(sum_last, [half] * 2, [VMEM] * 3, (s0, u, v))
     (grad_weight,) = call(
         functools.partial(sum_scaled, factor=factor),
         [((block, hid), F32)],
-        [VMEM] * 2,
-        (keep, swap(send, "zl", 4)),
+        [VMEM],
+        (lax.all_to_all(term, "zl", 0, 0),),
     )
     given = swap(given, "c", 1)
     (output,) = call(

time: 153 us -> 152 us (level)
  the two profiles are of different devices: /device:TPU:1 before, /device:TPU:131 now
where the time goes in v7:
time: 152 us; the launch traced here: 151 us
  starting transfers between devices  85.3 us (56%)
  waiting for transfers between devices  46.3 us (30%)
  Pallas kernels  14.1 us (9%)
  local copies, waits for them, and re-layouts  4.65 us (3%)
    ppermute x3, waiting for transfers between devices, shift_both(): return lax.ppermute(value, ('c', 'zh'), pairs)  34.4 us
    ppermute x3, starting transfers between devices, shift_both(): return lax.ppermute(value, ('c', 'zh'), pairs)  23.7 us
    ppermute x6, starting transfers between devices, shift(): lax.ppermute(value, axis, [(i, (i + distance) % size) for i in range(size)])  21.5 us
    all_to_all x1, starting transfers between devices, local(): lax.all_to_all(term, 'zl', 0, 0)  14.3 us
    pallas_call x11, Pallas kernels, call(): pl.pallas_call(body, out_shape=[s if isinstance(s, pl.MemoryRef) else jax...  14 us
    ppermute x3, starting transfers between devices, swap(): return lax.ppermute(value, axis, [(i, i ^ distance) for i in range(size)])  10.7 us
    all_to_all x1, starting transfers between devices, local(): lax.all_to_all(jnp.broadcast_to(weight_out[None], (n_zl, block, hid)), 'z...  10.7 us
    ppermute x6, waiting for transfers between devices, shift(): lax.ppermute(value, axis, [(i, (i + distance) % size) for i in range(size)])  5.38 us
  transfers between devices with their start and end apart: 15, of which 7 were waited for; matrix products, arithmetic and copies ran while one was open for 0% of the time, Pallas kernels for 7%

profile of v7, /device:TPU:131, one launch (start us, length us, event | category | flops | bytes accessed | tf_op | source)
XLA Modules:
  0.0 151.2 jit_solution(90998085353978793)
XLA Ops:
  0.6 1.6 %broadcast_in_dim.2 = bf16[8,40,432]{2,1,0:T(8,128)(2,1)} broadcast(bf16[40,432]{1,0:T(8,128)(2,1)} %param.5), dimensions={1,2} | broadcast | bytes 311040 | tf_op jit(solution)/shard_map/broadcast_in_dim | solution.py:207
  2.2 10.7 %all-to-all-start = ((bf16[8,40,432]{2,1,0:T(8,128)(2,1)}), bf16[8,40,432]{2,1,0:T(8,128)(2,1)S(1)}, u32[]{:S(2)}, u32[]{:S(2)}) async-start(bf16[8,40,432]{2,1,0:T(8,128)(2,1)} %broadcast_in_dim.2), calls=%async_computation | async-start | bytes 655360 | tf_op jit(solution)/shard_map/all_to_all | solution.py:207
  12.9 0.7 stack.23.place
  13.6 3.8 %shard_map.67 = (bf16[1712,256]{1,0:T(8,128)(2,1)}, bf16[1280,256]{1,0:T(8,128)(2,1)}) custom-call(s32[5]{0:T(128)} %stack.23.place, s32[320,1]{1,0:T(8,128)} %constant.25.clone.base, bf16[256,2560]{1,0:T(8,128)(2,1)} %cot.1, bf16[432,256]{1,0:T(8,128)(2,1)} %bitcast.25), custom_call_target="tpu_custom_call" | custom-call | flops 838860800 | bytes 2299481 | tf_op jit(solution)/shard_map/pallas_call | solution.py:61
  17.4 3.1 %collective-permute-start.3 = (bf16[1712,256]{1,0:T(8,128)(2,1)}, bf16[1712,256]{1,0:T(8,128)(2,1)S(1)}, u32[]{:S(2)}, u32[]{:S(2)}) collective-permute-start(bf16[1712,256]{1,0:T(8,128)(2,1)} %get-tuple-element.25), channel_id=1, source_target_pairs={{0,16},{16,0},{1,17},{17,1},{2,18},{18,2},{3,19},{19,3},{4,20},{20... | collective-permute-start | bytes 2629640 | tf_op jit(solution)/shard_map/ppermute | solution.py:36
  20.6 5.3 %all-to-all-done = bf16[8,40,432]{2,1,0:T(8,128)(2,1)S(1)} async-done(((bf16[8,40,432]{2,1,0:T(8,128)(2,1)}), bf16[8,40,432]{2,1,0:T(8,128)(2,1)S(1)}, u32[]{:S(2)}, u32[]{:S(2)}) %all-to-all-start) | async-done | bytes 276512 | tf_op jit(solution)/shard_map/all_to_all | solution.py:207
  25.9 3.2 %collective-permute-start.2 = (bf16[320,432]{1,0:T(8,128)(2,1)S(1)}, bf16[320,432]{1,0:T(8,128)(2,1)S(1)}, u32[]{:S(2)}, u32[]{:S(2)}) collective-permute-start(bf16[320,432]{1,0:T(8,128)(2,1)S(1)} %bitcast.21), channel_id=1, source_target_pairs={{0,256},{256,512},{512,768},{768,0},{1,257},{257,513},{513,769},{7... | collective-permute-start | bytes 829448 | tf_op jit(solution)/shard_map/ppermute | solution.py:41
  29.1 4.5 %collective-permute-start.1 = (bf16[320,432]{1,0:T(8,128)(2,1)S(1)}, bf16[320,432]{1,0:T(8,128)(2,1)S(1)}, u32[]{:S(2)}, u32[]{:S(2)}) collective-permute-start(bf16[320,432]{1,0:T(8,128)(2,1)S(1)} %bitcast.22), channel_id=1, source_target_pairs={{0,512},{256,768},{512,0},{768,256},{1,513},{257,769},{513,1},{769... | collective-permute-start | bytes 829448 | tf_op jit(solution)/shard_map/ppermute | solution.py:41
  33.6 3.0 %collective-permute-start = (bf16[320,432]{1,0:T(8,128)(2,1)S(1)}, bf16[320,432]{1,0:T(8,128)(2,1)S(1)}, u32[]{:S(2)}, u32[]{:S(2)}) collective-permute-start(bf16[320,432]{1,0:T(8,128)(2,1)S(1)} %bitcast.23), channel_id=1, source_target_pairs={{0,768},{256,0},{512,256},{768,512},{1,769},{257,1},{513,257},{769... | collective-permute-start | bytes 829448 | tf_op jit(solution)/shard_map/ppermute | solution.py:41
  36.6 0.0 collective-permute-done.3.got
  36.6 0.0 copy-done.3
  36.6 0.0 copy-done.4
  36.6 0.0 copy-start.5
  36.6 1.1 copy-done.5
  37.7 2.4 %shard_map.68 = (bf16[432,512]{1,0:T(8,128)(2,1)S(1)}, bf16[320,432]{1,0:T(8,128)(2,1)}, bf16[320,432]{1,0:T(8,128)(2,1)}, bf16[320,432]{1,0:T(8,128)(2,1)}, bf1...) custom-call(s32[5]{0:T(128)S(1)} %copy-done.4, bf16[432,256]{1,0:T(8,128)(2,1)S(1)} %bitcast.26, ...), custom_call_target="tpu_custom_call" | custom-call | flops 566231040 | bytes 2629657 | tf_op jit(solution)/shard_map/pallas_call | solution.py:61
  40.1 0.0 collective-permute-done.2.w3
  40.1 3.8 %collective-permute-done.1.w2 = bf16[320,432]{1,0:T(8,128)(2,1)S(1)} collective-permute-done((bf16[320,432]{1,0:T(8,128)(2,1)S(1)}, bf16[320,432]{1,0:T(8,128)(2,1)S(1)}, u32[]{:S(2)}, u32[]{:S(2)}) %collective-permute-start.1) | collective-permute-done | bytes 276512 | tf_op jit(solution)/shard_map/ppermute | solution.py:41
  43.9 1.6 %collective-permute-done.w1 = bf16[320,432]{1,0:T(8,128)(2,1)S(1)} collective-permute-done((bf16[320,432]{1,0:T(8,128)(2,1)S(1)}, bf16[320,432]{1,0:T(8,128)(2,1)S(1)}, u32[]{:S(2)}, u32[]{:S(2)}) %collective-permute-start) | collective-permute-done | bytes 276512 | tf_op jit(solution)/shard_map/ppermute | solution.py:41
  45.5 2.2 %shard_map.69 = (bf16[4,4,80,512]{3,2,1,0:T(8,128)(2,1)}, bf16[4,320,432]{2,1,0:T(8,128)(2,1)}, f32[8,128]{1,0:T(8,128)S(1)}) custom-call(s32[5]{0:T(128)S(1)} %copy-done.4, bf16[320,432]{1,0:T(8,128)(2,1)S(1)} %bitcast.24, bf16[320,432]{1,0:T(8,128)(2,1)S(1)} %collective-permute-done.w1, bf16[320,432]{1,0:T(8,128)(2,1)S(1)} %collective-permute-done.1.w2, ...), custom_call_target="tpu_custom_call" | custom-call | flops 566231040 | bytes 2322457 | tf_op jit(solution)/shard_map/pallas_call | solution.py:61
  47.6 4.4 %all-to-all-start.1 = ((bf16[4,4,80,512]{3,2,1,0:T(8,128)(2,1)}), bf16[4,4,80,512]{3,2,1,0:T(8,128)(2,1)S(1)}, u32[]{:S(2)}, u32[]{:S(2)}) async-start(bf16[4,4,80,512]{3,2,1,0:T(8,128)(2,1)} %get-tuple-element.27), calls=%async_computation.1 | async-start | bytes 2621440 | tf_op jit(solution)/shard_map/all_to_all | solution.py:242
  52.1 0.0 copy-done
  52.1 1.3 copy-done.1
  53.4 1.7 %shard_map.70 = (f32[432,256]{1,0:T(8,128)S(1)}, f32[432,256]{1,0:T(8,128)S(1)}) custom-call(s32[5]{0:T(128)S(1)} %copy-done.4, bf16[4,320,432]{2,1,0:T(8,128)(2,1)S(1)} %copy-done.1, bf16[2,1280,256]{2,1,0:T(8,128)(2,1)S(1)} %copy-done), custom_call_target="tpu_custom_call" | custom-call | flops 566231040 | bytes 3624985 | tf_op jit(solution)/shard_map/pallas_call | solution.py:61
  55.1 5.7 %collective-permute-start.4 = (f32[432,256]{1,0:T(8,128)S(1)}, f32[432,256]{1,0:T(8,128)S(1)}, u32[]{:S(2)}, u32[]{:S(2)}) collective-permute-start(f32[432,256]{1,0:T(8,128)S(1)} %get-tuple-element.31), channel_id=1, source_target_pairs={{0,16},{16,0},{1,17},{17,1},{2,18},{18,2},{3,19},{19,3},{4,20},{20... | collective-permute-start | bytes 1327112 | tf_op jit(solution)/shard_map/ppermute | solution.py:36
  60.8 4.3 %collective-permute-start.9 = (bf16[320,432]{1,0:T(8,128)(2,1)}, bf16[320,432]{1,0:T(8,128)(2,1)S(1)}, u32[]{:S(2)}, u32[]{:S(2)}) collective-permute-start(bf16[320,432]{1,0:T(8,128)(2,1)} %shard_map.76), channel_id=1, source_target_pairs={{0,256},{256,512},{512,768},{768,0},{1,257},{257,513},{513,769},{7... | collective-permute-start | bytes 829448 | tf_op jit(solution)/shard_map/ppermute | solution.py:41
  65.1 3.3 %collective-permute-start.10 = (bf16[320,432]{1,0:T(8,128)(2,1)}, bf16[320,432]{1,0:T(8,128)(2,1)S(1)}, u32[]{:S(2)}, u32[]{:S(2)}) collective-permute-start(bf16[320,432]{1,0:T(8,128)(2,1)} %shard_map.77), channel_id=1, source_target_pairs={{0,512},{256,768},{512,0},{768,256},{1,513},{257,769},{513,1},{769... | collective-permute-start | bytes 829448 | tf_op jit(solution)/shard_map/ppermute | solution.py:41
  68.3 0.0 copy-done.6
  68.3 3.3 %collective-permute-start.11 = (bf16[320,432]{1,0:T(8,128)(2,1)S(1)}, bf16[320,432]{1,0:T(8,128)(2,1)S(1)}, u32[]{:S(2)}, u32[]{:S(2)}) collective-permute-start(bf16[320,432]{1,0:T(8,128)(2,1)S(1)} %copy-done.6), channel_id=1, source_target_pairs={{0,768},{256,0},{512,256},{768,512},{1,769},{257,1},{513,257},{769... | collective-permute-start | bytes 829448 | tf_op jit(solution)/shard_map/ppermute | solution.py:41
  71.6 0.0 collective-permute-done.4.other
  71.6 1.0 shard_map.71
  72.6 0.0 all-to-all-done.1.parts
  72.6 0.2 shard_map.72
  72.8 15.2 %collective-permute-start.5 = (bf16[80,512]{1,0:T(8,128)(2,1)S(1)}, bf16[80,512]{1,0:T(8,128)(2,1)S(1)}, u32[]{:S(2)}, u32[]{:S(2)}) collective-permute-start(bf16[80,512]{1,0:T(8,128)(2,1)S(1)} %get-tuple-element.35), channel_id=1, source_target_pairs={{0,4},{4,8},{8,12},{12,0},{16,28},{20,16},{24,20},{28,24},{1,5},{5... | collective-permute-start | bytes 245768 | tf_op jit(solution)/shard_map/ppermute | solution.py:51
  88.1 2.1 %collective-permute-start.6 = (bf16[80,512]{1,0:T(8,128)(2,1)S(1)}, bf16[80,512]{1,0:T(8,128)(2,1)S(1)}, u32[]{:S(2)}, u32[]{:S(2)}) collective-permute-start(bf16[80,512]{1,0:T(8,128)(2,1)S(1)} %get-tuple-element.36), channel_id=1, source_target_pairs={{0,12},{4,0},{8,4},{12,8},{16,20},{20,24},{24,28},{28,16},{1,13},{... | collective-permute-start | bytes 245768 | tf_op jit(solution)/shard_map/ppermute | solution.py:51
  90.2 0.0 collective-permute-done.9
  90.2 0.0 collective-permute-done.10
  90.2 0.0 collective-permute-done.11
  90.2 0.9 collective-permute-done.5.got.after
  91.1 10.9 %collective-permute-done.6.after.v.then = bf16[80,512]{1,0:T(8,128)(2,1)S(1)} collective-permute-done((bf16[80,512]{1,0:T(8,128)(2,1)S(1)}, bf16[80,512]{1,0:T(8,128)(2,1)S(1)}, u32[]{:S(2)}, u32[]{:S(2)}) %collective-permute-start.6) | collective-permute-done | bytes 81952 | tf_op jit(solution)/shard_map/ppermute | solution.py:51
  102.0 0.9 shard_map.79
  102.9 14.3 %all-to-all-start.2 = ((bf16[8,40,432]{2,1,0:T(8,128)(2,1)}), bf16[8,40,432]{2,1,0:T(8,128)(2,1)S(1)}, u32[]{:S(2)}, u32[]{:S(2)}) async-start(bf16[8,40,432]{2,1,0:T(8,128)(2,1)} %shard_map.79), calls=%async_computation.2 | async-start | bytes 655360 | tf_op jit(solution)/shard_map/all_to_all | solution.py:273
  117.2 6.3 %collective-permute-start.7 = (bf16[80,512]{1,0:T(8,128)(2,1)S(1)}, bf16[80,512]{1,0:T(8,128)(2,1)S(1)}, u32[]{:S(2)}, u32[]{:S(2)}) collective-permute-start(bf16[80,512]{1,0:T(8,128)(2,1)S(1)} %shard_map.73), channel_id=1, source_target_pairs={{0,4},{4,8},{8,12},{12,0},{16,28},{20,16},{24,20},{28,24},{1,5},{5... | collective-permute-start | bytes 245768 | tf_op jit(solution)/shard_map/ppermute | solution.py:51
  123.5 22.7 %collective-permute-done.7.u = bf16[80,512]{1,0:T(8,128)(2,1)S(1)} collective-permute-done((bf16[80,512]{1,0:T(8,128)(2,1)S(1)}, bf16[80,512]{1,0:T(8,128)(2,1)S(1)}, u32[]{:S(2)}, u32[]{:S(2)}) %collective-permute-start.7) | collective-permute-done | bytes 81952 | tf_op jit(solution)/shard_map/ppermute | solution.py:51
  146.2 1.9 %collective-permute-start.8 = (bf16[80,256]{1,0:T(8,128)(2,1)S(1)}, bf16[80,256]{1,0:T(8,128)(2,1)S(1)}, u32[]{:S(2)}, u32[]{:S(2)}) collective-permute-start(bf16[80,256]{1,0:T(8,128)(2,1)S(1)} %get-tuple-element.38), channel_id=1, source_target_pairs={{0,16},{16,0},{1,17},{17,1},{2,18},{18,2},{3,19},{19,3},{4,20},{20... | collective-permute-start | bytes 122888 | tf_op jit(solution)/shard_map/ppermute | solution.py:36
  148.1 1.2 collective-permute-done.8
  149.3 1.2 shard_map.75
  150.5 0.0 all-to-all-done.2.parts
  150.5 0.7 shard_map.80
  (12 shorter events, 0.1 us)
Async XLA Ops:
  2.2 23.7 %all-to-all-start = ((bf16[8,40,432]{2,1,0:T(8,128)(2,1)}), bf16[8,40,432]{2,1,0:T(8,128)(2,1)S(1)}, u32[]{:S(2)}, u32[]{:S(2)}) async-start(bf16[8,40,432]{2,1,0:T(8,128)(2,1)} %broadcast_in_dim.2), calls=%async_computation | async-start | bytes 655360 | tf_op jit(solution)/shard_map/all_to_all | solution.py:207
  13.6 23.0 %copy-start.3 = (bf16[256,432]{0,1:T(8,128)(2,1)S(1)}, bf16[256,432]{0,1:T(8,128)(2,1)}, u32[]{:S(2)}) copy-start(bf16[256,432]{0,1:T(8,128)(2,1)} %param.4) | copy-start | bytes 663556
  13.6 23.0 %copy-start.4 = (s32[5]{0:T(128)S(1)}, s32[5]{0:T(128)}, u32[]{:S(2)}) copy-start(s32[5]{0:T(128)} %stack.23.place) | copy-start | bytes 64
  17.4 19.2 %collective-permute-start.3 = (bf16[1712,256]{1,0:T(8,128)(2,1)}, bf16[1712,256]{1,0:T(8,128)(2,1)S(1)}, u32[]{:S(2)}, u32[]{:S(2)}) collective-permute-start(bf16[1712,256]{1,0:T(8,128)(2,1)} %get-tuple-element.25), channel_id=1, source_target_pairs={{0,16},{16,0},{1,17},{17,1},{2,18},{18,2},{3,19},{19,3},{4,20},{20... | collective-permute-start | bytes 2629640 | tf_op jit(solution)/shard_map/ppermute | solution.py:36
  25.9 14.2 %collective-permute-start.2 = (bf16[320,432]{1,0:T(8,128)(2,1)S(1)}, bf16[320,432]{1,0:T(8,128)(2,1)S(1)}, u32[]{:S(2)}, u32[]{:S(2)}) collective-permute-start(bf16[320,432]{1,0:T(8,128)(2,1)S(1)} %bitcast.21), channel_id=1, source_target_pairs={{0,256},{256,512},{512,768},{768,0},{1,257},{257,513},{513,769},{7... | collective-permute-start | bytes 829448 | tf_op jit(solution)/shard_map/ppermute | solution.py:41
  29.1 14.9 %collective-permute-start.1 = (bf16[320,432]{1,0:T(8,128)(2,1)S(1)}, bf16[320,432]{1,0:T(8,128)(2,1)S(1)}, u32[]{:S(2)}, u32[]{:S(2)}) collective-permute-start(bf16[320,432]{1,0:T(8,128)(2,1)S(1)} %bitcast.22), channel_id=1, source_target_pairs={{0,512},{256,768},{512,0},{768,256},{1,513},{257,769},{513,1},{769... | collective-permute-start | bytes 829448 | tf_op jit(solution)/shard_map/ppermute | solution.py:41
  33.6 11.9 %collective-permute-start = (bf16[320,432]{1,0:T(8,128)(2,1)S(1)}, bf16[320,432]{1,0:T(8,128)(2,1)S(1)}, u32[]{:S(2)}, u32[]{:S(2)}) collective-permute-start(bf16[320,432]{1,0:T(8,128)(2,1)S(1)} %bitcast.23), channel_id=1, source_target_pairs={{0,768},{256,0},{512,256},{768,512},{1,769},{257,1},{513,257},{769... | collective-permute-start | bytes 829448 | tf_op jit(solution)/shard_map/ppermute | solution.py:41
  36.6 1.1 copy-start.5
  47.6 4.4 %copy-start = (bf16[2,1280,256]{2,1,0:T(8,128)(2,1)S(1)}, bf16[2,1280,256]{2,1,0:T(8,128)(2,1)}, u32[]{:S(2)}) copy-start(bf16[2,1280,256]{2,1,0:T(8,128)(2,1)} %get-tuple-element.29.both) | copy-start | bytes 3932164
  47.6 25.0 %all-to-all-start.1 = ((bf16[4,4,80,512]{3,2,1,0:T(8,128)(2,1)}), bf16[4,4,80,512]{3,2,1,0:T(8,128)(2,1)S(1)}, u32[]{:S(2)}, u32[]{:S(2)}) async-start(bf16[4,4,80,512]{3,2,1,0:T(8,128)(2,1)} %get-tuple-element.27), calls=%async_computation.1 | async-start | bytes 2621440 | tf_op jit(solution)/shard_map/all_to_all | solution.py:242
  52.1 1.3 copy-start.1
  55.1 16.6 %collective-permute-start.4 = (f32[432,256]{1,0:T(8,128)S(1)}, f32[432,256]{1,0:T(8,128)S(1)}, u32[]{:S(2)}, u32[]{:S(2)}) collective-permute-start(f32[432,256]{1,0:T(8,128)S(1)} %get-tuple-element.31), channel_id=1, source_target_pairs={{0,16},{16,0},{1,17},{17,1},{2,18},{18,2},{3,19},{19,3},{4,20},{20... | collective-permute-start | bytes 1327112 | tf_op jit(solution)/shard_map/ppermute | solution.py:36
  60.7 7.6 %copy-start.6 = (bf16[320,432]{1,0:T(8,128)(2,1)S(1)}, bf16[320,432]{1,0:T(8,128)(2,1)}, u32[]{:S(2)}) copy-start(bf16[320,432]{1,0:T(8,128)(2,1)} %shard_map.78) | copy-start | bytes 829444
  60.8 41.2 %copy-start.2 = (bf16[320,432]{1,0:T(8,128)(2,1)S(1)}, bf16[320,432]{1,0:T(8,128)(2,1)}, u32[]{:S(2)}) copy-start(bf16[320,432]{1,0:T(8,128)(2,1)} %get-tuple-element.40) | copy-start | bytes 829444
  60.8 29.4 %collective-permute-start.9 = (bf16[320,432]{1,0:T(8,128)(2,1)}, bf16[320,432]{1,0:T(8,128)(2,1)S(1)}, u32[]{:S(2)}, u32[]{:S(2)}) collective-permute-start(bf16[320,432]{1,0:T(8,128)(2,1)} %shard_map.76), channel_id=1, source_target_pairs={{0,256},{256,512},{512,768},{768,0},{1,257},{257,513},{513,769},{7... | collective-permute-start | bytes 829448 | tf_op jit(solution)/shard_map/ppermute | solution.py:41
  65.1 25.1 %collective-permute-start.10 = (bf16[320,432]{1,0:T(8,128)(2,1)}, bf16[320,432]{1,0:T(8,128)(2,1)S(1)}, u32[]{:S(2)}, u32[]{:S(2)}) collective-permute-start(bf16[320,432]{1,0:T(8,128)(2,1)} %shard_map.77), channel_id=1, source_target_pairs={{0,512},{256,768},{512,0},{768,256},{1,513},{257,769},{513,1},{769... | collective-permute-start | bytes 829448 | tf_op jit(solution)/shard_map/ppermute | solution.py:41
  68.3 21.9 %collective-permute-start.11 = (bf16[320,432]{1,0:T(8,128)(2,1)S(1)}, bf16[320,432]{1,0:T(8,128)(2,1)S(1)}, u32[]{:S(2)}, u32[]{:S(2)}) collective-permute-start(bf16[320,432]{1,0:T(8,128)(2,1)S(1)} %copy-done.6), channel_id=1, source_target_pairs={{0,768},{256,0},{512,256},{768,512},{1,769},{257,1},{513,257},{769... | collective-permute-start | bytes 829448 | tf_op jit(solution)/shard_map/ppermute | solution.py:41
  72.8 18.3 %collective-permute-start.5 = (bf16[80,512]{1,0:T(8,128)(2,1)S(1)}, bf16[80,512]{1,0:T(8,128)(2,1)S(1)}, u32[]{:S(2)}, u32[]{:S(2)}) collective-permute-start(bf16[80,512]{1,0:T(8,128)(2,1)S(1)} %get-tuple-element.35), channel_id=1, source_target_pairs={{0,4},{4,8},{8,12},{12,0},{16,28},{20,16},{24,20},{28,24},{1,5},{5... | collective-permute-start | bytes 245768 | tf_op jit(solution)/shard_map/ppermute | solution.py:51
  88.1 13.9 %collective-permute-start.6 = (bf16[80,512]{1,0:T(8,128)(2,1)S(1)}, bf16[80,512]{1,0:T(8,128)(2,1)S(1)}, u32[]{:S(2)}, u32[]{:S(2)}) collective-permute-start(bf16[80,512]{1,0:T(8,128)(2,1)S(1)} %get-tuple-element.36), channel_id=1, source_target_pairs={{0,12},{4,0},{8,4},{12,8},{16,20},{20,24},{24,28},{28,16},{1,13},{... | collective-permute-start | bytes 245768 | tf_op jit(solution)/shard_map/ppermute | solution.py:51
  102.9 47.6 %all-to-all-start.2 = ((bf16[8,40,432]{2,1,0:T(8,128)(2,1)}), bf16[8,40,432]{2,1,0:T(8,128)(2,1)S(1)}, u32[]{:S(2)}, u32[]{:S(2)}) async-start(bf16[8,40,432]{2,1,0:T(8,128)(2,1)} %shard_map.79), calls=%async_computation.2 | async-start | bytes 655360 | tf_op jit(solution)/shard_map/all_to_all | solution.py:273
  117.2 29.0 %collective-permute-start.7 = (bf16[80,512]{1,0:T(8,128)(2,1)S(1)}, bf16[80,512]{1,0:T(8,128)(2,1)S(1)}, u32[]{:S(2)}, u32[]{:S(2)}) collective-permute-start(bf16[80,512]{1,0:T(8,128)(2,1)S(1)} %shard_map.73), channel_id=1, source_target_pairs={{0,4},{4,8},{8,12},{12,0},{16,28},{20,16},{24,20},{28,24},{1,5},{5... | collective-permute-start | bytes 245768 | tf_op jit(solution)/shard_map/ppermute | solution.py:51
  146.2 3.1 %collective-permute-start.8 = (bf16[80,256]{1,0:T(8,128)(2,1)S(1)}, bf16[80,256]{1,0:T(8,128)(2,1)S(1)}, u32[]{:S(2)}, u32[]{:S(2)}) collective-permute-start(bf16[80,256]{1,0:T(8,128)(2,1)S(1)} %get-tuple-element.38), channel_id=1, source_target_pairs={{0,16},{16,0},{1,17},{17,1},{2,18},{18,2},{3,19},{19,3},{4,20},{20... | collective-permute-start | bytes 122888 | tf_op jit(solution)/shard_map/ppermute | solution.py:36

commit v8 on v6

--- a/solution.py
+++ b/solution.py
@@ -103,7 +103,7 @@
         copy.wait()
 
 
-def split_y(place, p0, p1, p2, p3, after, keep, send):
+def split_y(place, p0, p1, p2, p3, keep, send):
     bit = place[2] % 2
 
     def total(index):
@@ -127,10 +127,11 @@
     out[...] = (kept[0] + got[0].astype(F32)) * factor
 
 
-def output_terms(place, w0, w1, w2, w3, hidden, out, weight, held, sems):
+def output_terms(place, w0, w1, w2, w3, hidden, a0, a1, a2, out, weight, token, held, sems):
     core, y, zh = place[0], place[1], place[3]
     group = out.shape[2]
     pieces = (w0, w1, w2, w3)
+    token[...] = jnp.zeros_like(token)
     copies = [pltpu.make_async_copy(p, weight.at[k], sems.at[k]) for k, p in enumerate(pieces)]
     for copy in copies:
         copy.start()
@@ -145,41 +146,27 @@
         copy.wait()
 
 
-def sum_x(parts, after, s0, s1, s2, s3):
+def sum_x(parts, after, then, s0, s1, s2, s3):
     for index, out in enumerate((s0, s1, s2, s3)):
         value = parts[0, index].astype(F32) + parts[1, index].astype(F32)
         value += parts[2, index].astype(F32) + parts[3, index].astype(F32)
         out[...] = value.astype(BF16)
 
 
-def sum_step(s1, got, after, t1):
+def sum_step(s1, got, after, then, t1):
     t1[...] = (s1[...].astype(F32) + got[...].astype(F32)).astype(BF16)
 
 
-def sum_last(s0, u, v, after, then, kept, given):
+def sum_last(s0, u, v, kept, given):
     half = kept.shape[1]
     total = (s0[...].astype(F32) + (u[...].astype(F32) + v[...].astype(F32))).astype(BF16)
     kept[...] = total[:, :half]
     given[...] = total[:, half:]
 
 
-def hidden_grad(pre, own, other, out):
+def hidden_grad(pre, own, other, out, token):
+    token[...] = jnp.zeros_like(token)
     out[...] = ((own[...] + other[...]) * gelu_slope(pre[...].astype(F32))).astype(BF16)
-
-
-def gate(value, after, out):
-    pass
-
-
-def hold(value, after, place=LATER):
-    return pl.pallas_call(
-        gate,
-        out_shape=pltpu.HBM(value.shape, value.dtype),
-        in_specs=[HBM, place],
-        out_specs=HBM,
-        input_output_aliases={0: 0},
-        compiler_params=pltpu.CompilerParams(vmem_limit_bytes=14 << 20),
-    )(value, after)
 
 
 def interleave(place, kept, given, out):
@@ -236,37 +223,20 @@
     w0 = rows.reshape(stripe, hid)
     w1, w3, w2 = shift(w0, "y", -1), shift(w0, "y", 1), shift(w0, "y", 2)
 
-    parts, weight = call(
+    t1, t2, t3 = (shift(t, "y", k) for k, t in ((1, t1), (2, t2), (3, t3)))
+    parts, weight, token = call(
         output_terms,
-        [pltpu.HBM((n_x, n_y, group, 2 * tokens), BF16), pltpu.HBM((n_y, stripe, hid), BF16)],
-        [SMEM] + [VMEM] * 5,
-        (place, w0, w1, w2, w3, hidden),
+        [pltpu.HBM((n_x, n_y, group, 2 * tokens), BF16), pltpu.HBM((n_y, stripe, hid), BF16), ((8, 128), F32)],
+        [SMEM] + [VMEM] * 5 + [LATER] * 3,
+        (place, w0, w1, w2, w3, hidden, t1, t3, t2),
         flops=work,
         scratch=[pltpu.VMEM((n_y, n_x, group, 2 * tokens), BF16), pltpu.SemaphoreType.DMA((2 * n_y,))],
-        out_specs=[HBM, HBM],
-    )
-    t1, t2, t3 = (shift(hold(t, parts, HBM), "y", k) for k, t in ((1, t1), (2, t2), (3, t3)))
+        out_specs=[HBM, HBM, VMEM],
+    )
     parts = lax.all_to_all(parts, "x", 0, 0)
 
     whole, half = ((group, 2 * tokens), BF16), ((group, tokens), BF16)
-    quarter = n_zl // 2
     terms = [t.reshape(n_zl, block, hid) for t in (t0, t1, t2, t3)]
-    s0, s1, s2, s3 = call(sum_x, [whole] * 4, [VMEM, LATER], (parts, terms[3]))
-    got2 = shift_both(s2, 1)
-    keep, send = call(
-        split_y,
-        [((quarter, block, hid), F32), ((quarter, block, hid), BF16)],
-        [SMEM] + [VMEM] * 4 + [LATER],
-        (place, *terms, s0),
-    )
-    keep, send = call(
-        functools.partial(split_zl, width=2),
-        [((quarter // 2, block, hid), F32), ((quarter // 2, block, hid), BF16)],
-        [SMEM, VMEM, VMEM],
-        (place, keep, swap(send, "zl", 1)),
-    )
-    (s1,) = call(sum_step, [whole], [VMEM] * 2 + [LATER], (s1, got2, keep))
-    u, v = shift_both(s1, 1), shift_both(s3, -1)
     own, other = call(
         hidden_terms,
         [((hid, tokens), F32)] * 2,
@@ -274,22 +244,35 @@
         (place, weight, both),
         flops=work,
     )
+    grad_pre, token = call(
+        hidden_grad, [((hid, tokens), BF16), ((8, 128), F32)], [VMEM] * 3, (pre, own, swap(other, "c", 1))
+    )
+    quarter = n_zl // 2
     keep, send = call(
-        functools.partial(split_zl, width=4),
-        [((quarter // 4, block, hid), F32), ((quarter // 4, block, hid), BF16)],
-        [SMEM, VMEM, VMEM],
-        (place, keep, swap(send, "zl", 2)),
-    )
-    (grad_pre,) = call(
-        hidden_grad, [((hid, tokens), BF16)], [VMEM] * 3, (pre, own, swap(other, "c", 1))
-    )
-    kept, given = call(sum_last, [half] * 2, [VMEM] * 3 + [LATER] * 2, (s0, u, v, keep, grad_pre))
+        split_y,
+        [((quarter, block, hid), F32), ((quarter, block, hid), BF16)],
+        [SMEM] + [VMEM] * 4,
+        (place, *terms),
+    )
+    for width in (2, 4):
+        quarter //= 2
+        keep, send = call(
+            functools.partial(split_zl, width=width),
+            [((quarter, block, hid), F32), ((quarter, block, hid), BF16)],
+            [SMEM, VMEM, VMEM],
+            (place, keep, swap(send, "zl", width // 2)),
+        )
+    s0, s1, s2, s3 = call(sum_x, [whole] * 4, [VMEM] + [LATER] * 2, (parts, token, keep))
+    got2, v = shift_both(s2, 1), shift_both(s3, -1)
     (grad_weight,) = call(
         functools.partial(sum_scaled, factor=factor),
         [((block, hid), F32)],
         [VMEM] * 2,
         (keep, swap(send, "zl", 4)),
     )
+    (t1,) = call(sum_step, [whole], [VMEM] * 2 + [LATER] * 2, (s1, got2, v, grad_weight))
+    u = shift_both(t1, 1)
+    kept, given = call(sum_last, [half] * 2, [VMEM] * 3, (s0, u, v))
     given = swap(given, "c", 1)
     (output,) = call(
         interleave,

time: 153 us -> 160 us (1.046)
  waiting for transfers between devices: 21.7 us -> 35.8 us
  starting transfers between devices: 109 us -> 98.6 us
  local copies, waits for them, and re-layouts: 4.25 us -> 6.83 us
    ppermute x6, waiting for transfers between devices: 2.95 us -> 18.4 us  [shift(): lax.ppermute(value, axis, [(i, (i + distance) % size) for i in range(size)])]
    ppermute x6, starting transfers between devices: 25.2 us -> 16.7 us  [shift(): lax.ppermute(value, axis, [(i, (i + distance) % size) for i in range(size)])]
    ppermute x3, waiting for transfers between devices: 0.01 us -> 6.12 us  [shift_both(): return lax.ppermute(value, ('c', 'zh'), pairs)]
    ppermute x6, waiting for transfers between devices: 16.8 us -> 11.2 us  [swap(): return lax.ppermute(value, axis, [(i, i ^ distance) for i in range(size)])]
    ppermute x3, starting transfers between devices: 29.2 us -> 34 us  [shift_both(): return lax.ppermute(value, ('c', 'zh'), pairs)]
    ppermute x6, starting transfers between devices: 35.7 us -> 31.2 us  [swap(): return lax.ppermute(value, axis, [(i, i ^ distance) for i in range(size)])]
    unnamed x16 -> x14, local copies, waits for them, and re-layouts: 2.04 us -> 4.61 us
    all_to_all x1, starting transfers between devices: 5.8 us -> 3.55 us  [local(): parts = lax.all_to_all(parts, 'x', 0, 0)]
  transfers between devices with their start and end apart: 17 -> 17, of which waited for: 6 -> 9; matrix products, arithmetic and copies ran while one was open for 0% -> 0% of each run, Pallas kernels for 8% -> 7%
where the time goes in v8:
time: 160 us; the launch traced here: 158 us
  starting transfers between devices  98.6 us (62%)
  waiting for transfers between devices  35.8 us (22%)
  Pallas kernels  15.6 us (10%)
  local copies, waits for them, and re-layouts  6.83 us (4%)
    ppermute x3, starting transfers between devices, shift_both(): return lax.ppermute(value, ('c', 'zh'), pairs)  34 us
    ppermute x6, starting transfers between devices, swap(): return lax.ppermute(value, axis, [(i, i ^ distance) for i in range(size)])  31.2 us
    ppermute x6, waiting for transfers between devices, shift(): lax.ppermute(value, axis, [(i, (i + distance) % size) for i in range(size)])  18.4 us
    ppermute x6, starting transfers between devices, shift(): lax.ppermute(value, axis, [(i, (i + distance) % size) for i in range(size)])  16.7 us
    pallas_call x13, Pallas kernels, call(): pl.pallas_call(body, out_shape=[s if isinstance(s, pl.MemoryRef) else jax...  15.6 us
    all_to_all x1, starting transfers between devices, local(): lax.all_to_all(jnp.broadcast_to(weight_out[None], (n_zl, block, hid)), 'z...  13.1 us
    ppermute x6, waiting for transfers between devices, swap(): return lax.ppermute(value, axis, [(i, i ^ distance) for i in range(size)])  11.2 us
    ppermute x3, waiting for transfers between devices, shift_both(): return lax.ppermute(value, ('c', 'zh'), pairs)  6.12 us
  transfers between devices with their start and end apart: 17, of which 9 were waited for; matrix products, arithmetic and copies ran while one was open for 0% of the time, Pallas kernels for 7%

profile of v8, /device:TPU:1, one launch (start us, length us, event | category | flops | bytes accessed | tf_op | source)
XLA Modules:
  0.0 157.6 jit_solution(13954296587293116980)
XLA Ops:
  0.6 1.6 broadcast_in_dim.2
  2.2 13.1 %all-to-all-start = ((bf16[8,40,432]{2,1,0:T(8,128)(2,1)}), bf16[8,40,432]{2,1,0:T(8,128)(2,1)S(1)}, u32[]{:S(2)}, u32[]{:S(2)}) async-start(bf16[8,40,432]{2,1,0:T(8,128)(2,1)} %broadcast_in_dim.2), calls=%async_computation | async-start | bytes 655360 | tf_op jit(solution)/shard_map/all_to_all | solution.py:201
  15.3 0.7 stack.23.place
  15.9 3.8 %shard_map.67 = (bf16[1712,256]{1,0:T(8,128)(2,1)}, bf16[1280,256]{1,0:T(8,128)(2,1)}) custom-call(s32[5]{0:T(128)} %stack.23.place, s32[320,1]{1,0:T(8,128)} %constant.25.clone.base, bf16[256,2560]{1,0:T(8,128)(2,1)} %cot.1, bf16[432,256]{1,0:T(8,128)(2,1)} %bitcast.25), custom_call_target="tpu_custom_call" | custom-call | flops 838860800 | bytes 2299481 | tf_op jit(solution)/shard_map/pallas_call | solution.py:61
  19.8 6.4 %collective-permute-start.3 = (bf16[1712,256]{1,0:T(8,128)(2,1)}, bf16[1712,256]{1,0:T(8,128)(2,1)S(1)}, u32[]{:S(2)}, u32[]{:S(2)}) collective-permute-start(bf16[1712,256]{1,0:T(8,128)(2,1)} %get-tuple-element.30), channel_id=1, source_target_pairs={{0,16},{16,0},{1,17},{17,1},{2,18},{18,2},{3,19},{19,3},{4,20},{20... | collective-permute-start | bytes 2629640 | tf_op jit(solution)/shard_map/ppermute | solution.py:36
  26.2 2.2 %collective-permute-done.3.got = bf16[1712,256]{1,0:T(8,128)(2,1)S(1)} collective-permute-done((bf16[1712,256]{1,0:T(8,128)(2,1)}, bf16[1712,256]{1,0:T(8,128)(2,1)S(1)}, u32[]{:S(2)}, u32[]{:S(2)}) %collective-permute-start.3) | collective-permute-done | bytes 876576 | tf_op jit(solution)/shard_map/ppermute | solution.py:36
  28.4 1.1 copy-done.6
  29.5 2.4 %shard_map.68 = (bf16[432,512]{1,0:T(8,128)(2,1)S(1)}, bf16[320,432]{1,0:T(8,128)(2,1)}, bf16[320,432]{1,0:T(8,128)(2,1)}, bf16[320,432]{1,0:T(8,128)(2,1)}, bf1...) custom-call(s32[5]{0:T(128)S(1)} %copy-done.5, bf16[432,256]{1,0:T(8,128)(2,1)S(1)} %bitcast.26, ...), custom_call_target="tpu_custom_call" | custom-call | flops 566231040 | bytes 2629657 | tf_op jit(solution)/shard_map/pallas_call | solution.py:61
  31.9 1.9 %collective-permute-start.5 = (bf16[320,432]{1,0:T(8,128)(2,1)}, bf16[320,432]{1,0:T(8,128)(2,1)S(1)}, u32[]{:S(2)}, u32[]{:S(2)}) collective-permute-start(bf16[320,432]{1,0:T(8,128)(2,1)} %get-tuple-element.33), channel_id=1, source_target_pairs={{0,768},{256,0},{512,256},{768,512},{1,769},{257,1},{513,257},{769... | collective-permute-start | bytes 829448 | tf_op jit(solution)/shard_map/ppermute | solution.py:41
  33.8 3.4 %collective-permute-start.4 = (bf16[320,432]{1,0:T(8,128)(2,1)}, bf16[320,432]{1,0:T(8,128)(2,1)S(1)}, u32[]{:S(2)}, u32[]{:S(2)}) collective-permute-start(bf16[320,432]{1,0:T(8,128)(2,1)} %get-tuple-element.32), channel_id=1, source_target_pairs={{0,256},{256,512},{512,768},{768,0},{1,257},{257,513},{513,769},{7... | collective-permute-start | bytes 829448 | tf_op jit(solution)/shard_map/ppermute | solution.py:41
  37.2 1.9 %collective-permute-start.6 = (bf16[320,432]{1,0:T(8,128)(2,1)}, bf16[320,432]{1,0:T(8,128)(2,1)S(1)}, u32[]{:S(2)}, u32[]{:S(2)}) collective-permute-start(bf16[320,432]{1,0:T(8,128)(2,1)} %get-tuple-element.34), channel_id=1, source_target_pairs={{0,512},{256,768},{512,0},{768,256},{1,513},{257,769},{513,1},{769... | collective-permute-start | bytes 829448 | tf_op jit(solution)/shard_map/ppermute | solution.py:41
  39.1 4.3 %collective-permute-start = (bf16[320,432]{1,0:T(8,128)(2,1)S(1)}, bf16[320,432]{1,0:T(8,128)(2,1)S(1)}, u32[]{:S(2)}, u32[]{:S(2)}) collective-permute-start(bf16[320,432]{1,0:T(8,128)(2,1)S(1)} %bitcast.17), channel_id=1, source_target_pairs={{0,768},{256,0},{512,256},{768,512},{1,769},{257,1},{513,257},{769... | collective-permute-start | bytes 829448 | tf_op jit(solution)/shard_map/ppermute | solution.py:41
  43.4 3.1 %collective-permute-start.1 = (bf16[320,432]{1,0:T(8,128)(2,1)S(1)}, bf16[320,432]{1,0:T(8,128)(2,1)S(1)}, u32[]{:S(2)}, u32[]{:S(2)}) collective-permute-start(bf16[320,432]{1,0:T(8,128)(2,1)S(1)} %bitcast.18), channel_id=1, source_target_pairs={{0,512},{256,768},{512,0},{768,256},{1,513},{257,769},{513,1},{769... | collective-permute-start | bytes 829448 | tf_op jit(solution)/shard_map/ppermute | solution.py:41
  46.6 2.2 %collective-permute-start.2 = (bf16[320,432]{1,0:T(8,128)(2,1)S(1)}, bf16[320,432]{1,0:T(8,128)(2,1)S(1)}, u32[]{:S(2)}, u32[]{:S(2)}) collective-permute-start(bf16[320,432]{1,0:T(8,128)(2,1)S(1)} %bitcast.19), channel_id=1, source_target_pairs={{0,256},{256,512},{512,768},{768,0},{1,257},{257,513},{513,769},{7... | collective-permute-start | bytes 829448 | tf_op jit(solution)/shard_map/ppermute | solution.py:41
  48.7 11.3 %collective-permute-done.4.a0 = bf16[320,432]{1,0:T(8,128)(2,1)S(1)} collective-permute-done((bf16[320,432]{1,0:T(8,128)(2,1)}, bf16[320,432]{1,0:T(8,128)(2,1)S(1)}, u32[]{:S(2)}, u32[]{:S(2)}) %collective-permute-start.4) | collective-permute-done | bytes 276512 | tf_op jit(solution)/shard_map/ppermute | solution.py:41
  60.0 0.0 collective-permute-done.6.a2
  60.0 0.0 collective-permute-done.w1
  60.0 0.0 collective-permute-done.1.w2
  60.0 7.1 %collective-permute-done.2.w3 = bf16[320,432]{1,0:T(8,128)(2,1)S(1)} collective-permute-done((bf16[320,432]{1,0:T(8,128)(2,1)S(1)}, bf16[320,432]{1,0:T(8,128)(2,1)S(1)}, u32[]{:S(2)}, u32[]{:S(2)}) %collective-permute-start.2) | collective-permute-done | bytes 276512 | tf_op jit(solution)/shard_map/ppermute | solution.py:41
  67.1 2.8 %shard_map.69 = (bf16[4,4,80,512]{3,2,1,0:T(8,128)(2,1)}, bf16[4,320,432]{2,1,0:T(8,128)(2,1)}, f32[8,128]{1,0:T(8,128)}) custom-call(s32[5]{0:T(128)S(1)} %copy-done.5, bf16[320,432]{1,0:T(8,128)(2,1)S(1)} %bitcast.20, bf16[320,432]{1,0:T(8,128)(2,1)S(1)} %collective-permute-done.w1, bf16[320,432]{1,0:T(8,128)(2,1)S(1)} %collective-permute-done.1.w2, ...), custom_call_target="tpu_custom_call" | custom-call | flops 566231040 | bytes 3566617 | tf_op jit(solution)/shard_map/pallas_call | solution.py:61
  69.9 3.6 %all-to-all-start.1 = ((bf16[4,4,80,512]{3,2,1,0:T(8,128)(2,1)}), bf16[4,4,80,512]{3,2,1,0:T(8,128)(2,1)S(1)}, u32[]{:S(2)}, u32[]{:S(2)}) async-start(bf16[4,4,80,512]{3,2,1,0:T(8,128)(2,1)} %get-tuple-element.35), calls=%async_computation.1 | async-start | bytes 2621440 | tf_op jit(solution)/shard_map/all_to_all | solution.py:236
  73.5 1.3 copy-done
  74.8 1.3 copy-done.1
  76.1 1.7 %shard_map.70 = (f32[432,256]{1,0:T(8,128)S(1)}, f32[432,256]{1,0:T(8,128)S(1)}) custom-call(s32[5]{0:T(128)S(1)} %copy-done.5, bf16[4,320,432]{2,1,0:T(8,128)(2,1)S(1)} %copy-done.1, bf16[2,1280,256]{2,1,0:T(8,128)(2,1)S(1)} %copy-done), custom_call_target="tpu_custom_call" | custom-call | flops 566231040 | bytes 3624985 | tf_op jit(solution)/shard_map/pallas_call | solution.py:61
  77.8 3.1 %collective-permute-start.7 = (f32[432,256]{1,0:T(8,128)S(1)}, f32[432,256]{1,0:T(8,128)S(1)}, u32[]{:S(2)}, u32[]{:S(2)}) collective-permute-start(f32[432,256]{1,0:T(8,128)S(1)} %get-tuple-element.39), channel_id=1, source_target_pairs={{0,16},{16,0},{1,17},{17,1},{2,18},{18,2},{3,19},{19,3},{4,20},{20... | collective-permute-start | bytes 1327112 | tf_op jit(solution)/shard_map/ppermute | solution.py:36
  80.9 0.7 shard_map.72
  81.6 3.6 %collective-permute-start.8 = (bf16[4,40,432]{2,1,0:T(8,128)(2,1)S(1)}, bf16[4,40,432]{2,1,0:T(8,128)(2,1)S(1)}, u32[]{:S(2)}, u32[]{:S(2)}) collective-permute-start(bf16[4,40,432]{2,1,0:T(8,128)(2,1)S(1)} %get-tuple-element.43), channel_id=1, source_target_pairs={{0,32},{32,0},{64,96},{96,64},{128,160},{160,128},{192,224},{224,1... | collective-permute-start | bytes 414728 | tf_op jit(solution)/shard_map/ppermute | solution.py:36
  85.2 4.5 %collective-permute-done.8.got = bf16[4,40,432]{2,1,0:T(8,128)(2,1)S(1)} collective-permute-done((bf16[4,40,432]{2,1,0:T(8,128)(2,1)S(1)}, bf16[4,40,432]{2,1,0:T(8,128)(2,1)S(1)}, u32[]{:S(2)}, u32[]{:S(2)}) %collective-permute-start.8) | collective-permute-done | bytes 138272 | tf_op jit(solution)/shard_map/ppermute | solution.py:36
  89.7 0.6 shard_map.73
  90.3 4.1 %collective-permute-start.9 = (bf16[2,40,432]{2,1,0:T(8,128)(2,1)S(1)}, bf16[2,40,432]{2,1,0:T(8,128)(2,1)S(1)}, u32[]{:S(2)}, u32[]{:S(2)}) collective-permute-start(bf16[2,40,432]{2,1,0:T(8,128)(2,1)S(1)} %get-tuple-element.45), channel_id=1, source_target_pairs={{0,64},{32,96},{64,0},{96,32},{128,192},{160,224},{192,128},{224,1... | collective-permute-start | bytes 207368 | tf_op jit(solution)/shard_map/ppermute | solution.py:36
  94.4 1.9 %collective-permute-done.9.got = bf16[2,40,432]{2,1,0:T(8,128)(2,1)S(1)} collective-permute-done((bf16[2,40,432]{2,1,0:T(8,128)(2,1)S(1)}, bf16[2,40,432]{2,1,0:T(8,128)(2,1)S(1)}, u32[]{:S(2)}, u32[]{:S(2)}) %collective-permute-start.9) | collective-permute-done | bytes 69152 | tf_op jit(solution)/shard_map/ppermute | solution.py:36
  96.3 0.6 shard_map.74
  96.9 1.0 shard_map.71
  97.9 0.0 all-to-all-done.1.parts
  97.9 0.2 shard_map.75
  98.1 15.3 %collective-permute-start.10 = (bf16[80,512]{1,0:T(8,128)(2,1)S(1)}, bf16[80,512]{1,0:T(8,128)(2,1)S(1)}, u32[]{:S(2)}, u32[]{:S(2)}) collective-permute-start(bf16[80,512]{1,0:T(8,128)(2,1)S(1)} %get-tuple-element.49), channel_id=1, source_target_pairs={{0,4},{4,8},{8,12},{12,0},{16,28},{20,16},{24,20},{28,24},{1,5},{5... | collective-permute-start | bytes 245768 | tf_op jit(solution)/shard_map/ppermute | solution.py:51
  113.4 2.1 %collective-permute-start.11 = (bf16[80,512]{1,0:T(8,128)(2,1)S(1)}, bf16[80,512]{1,0:T(8,128)(2,1)S(1)}, u32[]{:S(2)}, u32[]{:S(2)}) collective-permute-start(bf16[80,512]{1,0:T(8,128)(2,1)S(1)} %get-tuple-element.50), channel_id=1, source_target_pairs={{0,12},{4,0},{8,4},{12,8},{16,20},{20,24},{24,28},{28,16},{1,13},{... | collective-permute-start | bytes 245768 | tf_op jit(solution)/shard_map/ppermute | solution.py:51
  115.6 7.1 %collective-permute-start.12 = (bf16[1,40,432]{2,1,0:T(8,128)(2,1)S(1)}, bf16[1,40,432]{2,1,0:T(8,128)(2,1)S(1)}, u32[]{:S(2)}, u32[]{:S(2)}) collective-permute-start(bf16[1,40,432]{2,1,0:T(8,128)(2,1)S(1)} %get-tuple-element.51), channel_id=1, source_target_pairs={{0,128},{32,160},{64,192},{96,224},{128,0},{160,32},{192,64},{224,... | collective-permute-start | bytes 103688 | tf_op jit(solution)/shard_map/ppermute | solution.py:36
  122.6 1.8 %collective-permute-done.12.got = bf16[1,40,432]{2,1,0:T(8,128)(2,1)S(1)} collective-permute-done((bf16[1,40,432]{2,1,0:T(8,128)(2,1)S(1)}, bf16[1,40,432]{2,1,0:T(8,128)(2,1)S(1)}, u32[]{:S(2)}, u32[]{:S(2)}) %collective-permute-start.12) | collective-permute-done | bytes 34592 | tf_op jit(solution)/shard_map/ppermute | solution.py:36
  124.4 0.6 shard_map.76.then
  125.0 0.0 collective-permute-done.10.got
  125.0 4.3 %collective-permute-done.11.after.v = bf16[80,512]{1,0:T(8,128)(2,1)S(1)} collective-permute-done((bf16[80,512]{1,0:T(8,128)(2,1)S(1)}, bf16[80,512]{1,0:T(8,128)(2,1)S(1)}, u32[]{:S(2)}, u32[]{:S(2)}) %collective-permute-start.11) | collective-permute-done | bytes 81952 | tf_op jit(solution)/shard_map/ppermute | solution.py:51
  129.3 0.9 copy-done.2
  130.2 16.6 %collective-permute-start.13 = (bf16[80,512]{1,0:T(8,128)(2,1)S(1)}, bf16[80,512]{1,0:T(8,128)(2,1)S(1)}, u32[]{:S(2)}, u32[]{:S(2)}) collective-permute-start(bf16[80,512]{1,0:T(8,128)(2,1)S(1)} %shard_map.77), channel_id=1, source_target_pairs={{0,4},{4,8},{8,12},{12,0},{16,28},{20,16},{24,20},{28,24},{1,5},{5... | collective-permute-start | bytes 245768 | tf_op jit(solution)/shard_map/ppermute | solution.py:51
  146.8 1.8 %collective-permute-done.13.u = bf16[80,512]{1,0:T(8,128)(2,1)S(1)} collective-permute-done((bf16[80,512]{1,0:T(8,128)(2,1)S(1)}, bf16[80,512]{1,0:T(8,128)(2,1)S(1)}, u32[]{:S(2)}, u32[]{:S(2)}) %collective-permute-start.13) | collective-permute-done | bytes 81952 | tf_op jit(solution)/shard_map/ppermute | solution.py:51
  148.7 6.9 %collective-permute-start.14 = (bf16[80,256]{1,0:T(8,128)(2,1)S(1)}, bf16[80,256]{1,0:T(8,128)(2,1)S(1)}, u32[]{:S(2)}, u32[]{:S(2)}) collective-permute-start(bf16[80,256]{1,0:T(8,128)(2,1)S(1)} %get-tuple-element.53), channel_id=1, source_target_pairs={{0,16},{16,0},{1,17},{17,1},{2,18},{18,2},{3,19},{19,3},{4,20},{20... | collective-permute-start | bytes 122888 | tf_op jit(solution)/shard_map/ppermute | solution.py:36
  155.6 0.8 collective-permute-done.14
  156.4 1.2 shard_map.79
  (15 shorter events, 0.1 us)
Async XLA Ops:
  2.2 36.9 %all-to-all-start = ((bf16[8,40,432]{2,1,0:T(8,128)(2,1)}), bf16[8,40,432]{2,1,0:T(8,128)(2,1)S(1)}, u32[]{:S(2)}, u32[]{:S(2)}) async-start(bf16[8,40,432]{2,1,0:T(8,128)(2,1)} %broadcast_in_dim.2), calls=%async_computation | async-start | bytes 655360 | tf_op jit(solution)/shard_map/all_to_all | solution.py:201
  15.9 12.5 %copy-start.4 = (bf16[256,432]{0,1:T(8,128)(2,1)S(1)}, bf16[256,432]{0,1:T(8,128)(2,1)}, u32[]{:S(2)}) copy-start(bf16[256,432]{0,1:T(8,128)(2,1)} %param.4) | copy-start | bytes 663556
  15.9 12.5 %copy-start.5 = (s32[5]{0:T(128)S(1)}, s32[5]{0:T(128)}, u32[]{:S(2)}) copy-start(s32[5]{0:T(128)} %stack.23.place) | copy-start | bytes 64
  19.8 8.7 %collective-permute-start.3 = (bf16[1712,256]{1,0:T(8,128)(2,1)}, bf16[1712,256]{1,0:T(8,128)(2,1)S(1)}, u32[]{:S(2)}, u32[]{:S(2)}) collective-permute-start(bf16[1712,256]{1,0:T(8,128)(2,1)} %get-tuple-element.30), channel_id=1, source_target_pairs={{0,16},{16,0},{1,17},{17,1},{2,18},{18,2},{3,19},{19,3},{4,20},{20... | collective-permute-start | bytes 2629640 | tf_op jit(solution)/shard_map/ppermute | solution.py:36
  28.4 1.1 copy-start.6
  31.9 14.6 %collective-permute-start.5 = (bf16[320,432]{1,0:T(8,128)(2,1)}, bf16[320,432]{1,0:T(8,128)(2,1)S(1)}, u32[]{:S(2)}, u32[]{:S(2)}) collective-permute-start(bf16[320,432]{1,0:T(8,128)(2,1)} %get-tuple-element.33), channel_id=1, source_target_pairs={{0,768},{256,0},{512,256},{768,512},{1,769},{257,1},{513,257},{769... | collective-permute-start | bytes 829448 | tf_op jit(solution)/shard_map/ppermute | solution.py:41
  33.8 26.2 %collective-permute-start.4 = (bf16[320,432]{1,0:T(8,128)(2,1)}, bf16[320,432]{1,0:T(8,128)(2,1)S(1)}, u32[]{:S(2)}, u32[]{:S(2)}) collective-permute-start(bf16[320,432]{1,0:T(8,128)(2,1)} %get-tuple-element.32), channel_id=1, source_target_pairs={{0,256},{256,512},{512,768},{768,0},{1,257},{257,513},{513,769},{7... | collective-permute-start | bytes 829448 | tf_op jit(solution)/shard_map/ppermute | solution.py:41
  37.2 22.8 %collective-permute-start.6 = (bf16[320,432]{1,0:T(8,128)(2,1)}, bf16[320,432]{1,0:T(8,128)(2,1)S(1)}, u32[]{:S(2)}, u32[]{:S(2)}) collective-permute-start(bf16[320,432]{1,0:T(8,128)(2,1)} %get-tuple-element.34), channel_id=1, source_target_pairs={{0,512},{256,768},{512,0},{768,256},{1,513},{257,769},{513,1},{769... | collective-permute-start | bytes 829448 | tf_op jit(solution)/shard_map/ppermute | solution.py:41
  39.1 20.9 %collective-permute-start = (bf16[320,432]{1,0:T(8,128)(2,1)S(1)}, bf16[320,432]{1,0:T(8,128)(2,1)S(1)}, u32[]{:S(2)}, u32[]{:S(2)}) collective-permute-start(bf16[320,432]{1,0:T(8,128)(2,1)S(1)} %bitcast.17), channel_id=1, source_target_pairs={{0,768},{256,0},{512,256},{768,512},{1,769},{257,1},{513,257},{769... | collective-permute-start | bytes 829448 | tf_op jit(solution)/shard_map/ppermute | solution.py:41
  43.4 16.6 %collective-permute-start.1 = (bf16[320,432]{1,0:T(8,128)(2,1)S(1)}, bf16[320,432]{1,0:T(8,128)(2,1)S(1)}, u32[]{:S(2)}, u32[]{:S(2)}) collective-permute-start(bf16[320,432]{1,0:T(8,128)(2,1)S(1)} %bitcast.18), channel_id=1, source_target_pairs={{0,512},{256,768},{512,0},{768,256},{1,513},{257,769},{513,1},{769... | collective-permute-start | bytes 829448 | tf_op jit(solution)/shard_map/ppermute | solution.py:41
  46.6 20.6 %collective-permute-start.2 = (bf16[320,432]{1,0:T(8,128)(2,1)S(1)}, bf16[320,432]{1,0:T(8,128)(2,1)S(1)}, u32[]{:S(2)}, u32[]{:S(2)}) collective-permute-start(bf16[320,432]{1,0:T(8,128)(2,1)S(1)} %bitcast.19), channel_id=1, source_target_pairs={{0,256},{256,512},{512,768},{768,0},{1,257},{257,513},{513,769},{7... | collective-permute-start | bytes 829448 | tf_op jit(solution)/shard_map/ppermute | solution.py:41
  69.9 28.0 %all-to-all-start.1 = ((bf16[4,4,80,512]{3,2,1,0:T(8,128)(2,1)}), bf16[4,4,80,512]{3,2,1,0:T(8,128)(2,1)S(1)}, u32[]{:S(2)}, u32[]{:S(2)}) async-start(bf16[4,4,80,512]{3,2,1,0:T(8,128)(2,1)} %get-tuple-element.35), calls=%async_computation.1 | async-start | bytes 2621440 | tf_op jit(solution)/shard_map/all_to_all | solution.py:236
  73.5 1.3 copy-start
  74.8 1.3 copy-start.1
  76.1 4.8 %copy-start.3 = (bf16[320,432]{1,0:T(8,128)(2,1)S(1)}, bf16[320,432]{1,0:T(8,128)(2,1)}, u32[]{:S(2)}) copy-start(bf16[320,432]{1,0:T(8,128)(2,1)} %get-tuple-element.41) | copy-start | bytes 829444
  77.8 19.1 %collective-permute-start.7 = (f32[432,256]{1,0:T(8,128)S(1)}, f32[432,256]{1,0:T(8,128)S(1)}, u32[]{:S(2)}, u32[]{:S(2)}) collective-permute-start(f32[432,256]{1,0:T(8,128)S(1)} %get-tuple-element.39), channel_id=1, source_target_pairs={{0,16},{16,0},{1,17},{17,1},{2,18},{18,2},{3,19},{19,3},{4,20},{20... | collective-permute-start | bytes 1327112 | tf_op jit(solution)/shard_map/ppermute | solution.py:36
  81.6 8.0 %collective-permute-start.8 = (bf16[4,40,432]{2,1,0:T(8,128)(2,1)S(1)}, bf16[4,40,432]{2,1,0:T(8,128)(2,1)S(1)}, u32[]{:S(2)}, u32[]{:S(2)}) collective-permute-start(bf16[4,40,432]{2,1,0:T(8,128)(2,1)S(1)} %get-tuple-element.43), channel_id=1, source_target_pairs={{0,32},{32,0},{64,96},{96,64},{128,160},{160,128},{192,224},{224,1... | collective-permute-start | bytes 414728 | tf_op jit(solution)/shard_map/ppermute | solution.py:36
  90.3 6.1 %collective-permute-start.9 = (bf16[2,40,432]{2,1,0:T(8,128)(2,1)S(1)}, bf16[2,40,432]{2,1,0:T(8,128)(2,1)S(1)}, u32[]{:S(2)}, u32[]{:S(2)}) collective-permute-start(bf16[2,40,432]{2,1,0:T(8,128)(2,1)S(1)} %get-tuple-element.45), channel_id=1, source_target_pairs={{0,64},{32,96},{64,0},{96,32},{128,192},{160,224},{192,128},{224,1... | collective-permute-start | bytes 207368 | tf_op jit(solution)/shard_map/ppermute | solution.py:36
  98.1 26.9 %collective-permute-start.10 = (bf16[80,512]{1,0:T(8,128)(2,1)S(1)}, bf16[80,512]{1,0:T(8,128)(2,1)S(1)}, u32[]{:S(2)}, u32[]{:S(2)}) collective-permute-start(bf16[80,512]{1,0:T(8,128)(2,1)S(1)} %get-tuple-element.49), channel_id=1, source_target_pairs={{0,4},{4,8},{8,12},{12,0},{16,28},{20,16},{24,20},{28,24},{1,5},{5... | collective-permute-start | bytes 245768 | tf_op jit(solution)/shard_map/ppermute | solution.py:51
  113.4 15.9 %collective-permute-start.11 = (bf16[80,512]{1,0:T(8,128)(2,1)S(1)}, bf16[80,512]{1,0:T(8,128)(2,1)S(1)}, u32[]{:S(2)}, u32[]{:S(2)}) collective-permute-start(bf16[80,512]{1,0:T(8,128)(2,1)S(1)} %get-tuple-element.50), channel_id=1, source_target_pairs={{0,12},{4,0},{8,4},{12,8},{16,20},{20,24},{24,28},{28,16},{1,13},{... | collective-permute-start | bytes 245768 | tf_op jit(solution)/shard_map/ppermute | solution.py:51
  115.6 8.8 %collective-permute-start.12 = (bf16[1,40,432]{2,1,0:T(8,128)(2,1)S(1)}, bf16[1,40,432]{2,1,0:T(8,128)(2,1)S(1)}, u32[]{:S(2)}, u32[]{:S(2)}) collective-permute-start(bf16[1,40,432]{2,1,0:T(8,128)(2,1)S(1)} %get-tuple-element.51), channel_id=1, source_target_pairs={{0,128},{32,160},{64,192},{96,224},{128,0},{160,32},{192,64},{224,... | collective-permute-start | bytes 103688 | tf_op jit(solution)/shard_map/ppermute | solution.py:36
  129.3 0.9 copy-start.2
  130.2 18.4 %collective-permute-start.13 = (bf16[80,512]{1,0:T(8,128)(2,1)S(1)}, bf16[80,512]{1,0:T(8,128)(2,1)S(1)}, u32[]{:S(2)}, u32[]{:S(2)}) collective-permute-start(bf16[80,512]{1,0:T(8,128)(2,1)S(1)} %shard_map.77), channel_id=1, source_target_pairs={{0,4},{4,8},{8,12},{12,0},{16,28},{20,16},{24,20},{28,24},{1,5},{5... | collective-permute-start | bytes 245768 | tf_op jit(solution)/shard_map/ppermute | solution.py:51
  148.7 7.7 %collective-permute-start.14 = (bf16[80,256]{1,0:T(8,128)(2,1)S(1)}, bf16[80,256]{1,0:T(8,128)(2,1)S(1)}, u32[]{:S(2)}, u32[]{:S(2)}) collective-permute-start(bf16[80,256]{1,0:T(8,128)(2,1)S(1)} %get-tuple-element.53), channel_id=1, source_target_pairs={{0,16},{16,0},{1,17},{17,1},{2,18},{18,2},{3,19},{19,3},{4,20},{20... | collective-permute-start | bytes 122888 | tf_op jit(solution)/shard_map/ppermute | solution.py:36

commit v9 on v7

--- a/solution.py
+++ b/solution.py
@@ -103,19 +103,29 @@
         copy.wait()
 
 
-def sum_y(p0, p1, p2, p3, after, then, out, held, sem):
-    value = p0[...].astype(F32) + p1[...].astype(F32)
-    held[...] = (value + (p2[...].astype(F32) + p3[...].astype(F32))).astype(BF16)
-    copy = pltpu.make_async_copy(held, out, sem)
-    copy.start()
-    copy.wait()
-
-
-def sum_scaled(parts, out, *, factor):
-    total = parts[0].astype(F32)
-    for index in range(1, parts.shape[0]):
-        total += parts[index].astype(F32)
-    out[...] = total * factor
+def split_y(place, p0, p1, p2, p3, after, then, keep, send):
+    bit = place[2] % 2
+
+    def total(index):
+        value = p0[index].astype(F32) + p1[index].astype(F32)
+        return value + (p2[index].astype(F32) + p3[index].astype(F32))
+
+    for index in range(keep.shape[0]):
+        keep[index] = total(2 * index + bit)
+        send[index] = total(2 * index + 1 - bit).astype(BF16)
+
+
+def split_pairs(place, kept, got, own, q1, q2, q3):
+    pair = place[2] // 2
+    own[...] = kept[pair] + got[pair].astype(F32)
+    for index, out in enumerate((q1, q2, q3)):
+        block = pair ^ (index + 1)
+        out[...] = (kept[block] + got[block].astype(F32)).astype(BF16)
+
+
+def sum_scaled(own, r1, r2, r3, out, *, factor):
+    total = own[...] + r1[...].astype(F32)
+    out[...] = (total + (r2[...].astype(F32) + r3[...].astype(F32))) * factor
 
 
 def output_terms(place, w0, w1, w2, w3, hidden, out, weight, token, held, sems):
@@ -148,7 +158,7 @@
     t1[...] = (s1[...].astype(F32) + got[...].astype(F32)).astype(BF16)
 
 
-def sum_last(s0, u, v, kept, given):
+def sum_last(s0, u, v, r1, r2, r3, kept, given):
     half = kept.shape[1]
     total = (s0[...].astype(F32) + (u[...].astype(F32) + v[...].astype(F32))).astype(BF16)
     kept[...] = total[:, :half]
@@ -255,22 +265,28 @@
     )
     s0, s1, s2, s3 = call(sum_x, [whole] * 4, [VMEM, LATER], (parts, token))
     got2, v = shift_both(s2, 1), shift_both(s3, -1)
-    (term,) = call(
-        sum_y,
-        [pltpu.HBM((n_zl, block, hid), BF16)],
-        [VMEM] * 4 + [LATER] * 2,
-        (*terms, got2, v),
-        scratch=[pltpu.VMEM((n_zl, block, hid), BF16), pltpu.SemaphoreType.DMA],
-        out_specs=[HBM],
+    quarter = n_zl // 2
+    keep, send = call(
+        split_y,
+        [((quarter, block, hid), F32), ((quarter, block, hid), BF16)],
+        [SMEM] + [VMEM] * 4 + [LATER] * 2,
+        (place, *terms, got2, v),
     )
     (t1,) = call(sum_step, [whole], [VMEM] * 2 + [LATER], (s1, got2, v))
     u = shift_both(t1, 1)
-    kept, given = call(sum_last, [half] * 2, [VMEM] * 3, (s0, u, v))
+    partial, *pairs = call(
+        split_pairs,
+        [((block, hid), F32)] + [((block, hid), BF16)] * 3,
+        [SMEM, VMEM, VMEM],
+        (place, keep, swap(send, "zl", 1)),
+    )
+    pairs = [swap(p, "zl", 2 * (k + 1)) for k, p in enumerate(pairs)]
+    kept, given = call(sum_last, [half] * 2, [VMEM] * 3 + [LATER] * 3, (s0, u, v, *pairs))
     (grad_weight,) = call(
         functools.partial(sum_scaled, factor=factor),
         [((block, hid), F32)],
-        [VMEM],
-        (lax.all_to_all(term, "zl", 0, 0),),
+        [VMEM] * 4,
+        (partial, *pairs),
     )
     given = swap(given, "c", 1)
     (output,) = call(

time: 152 us -> 153 us (level)
  the two profiles are of different devices: /device:TPU:131 before, /device:TPU:1 now
where the time goes in v9:
time: 153 us; the launch traced here: 151 us
  starting transfers between devices  108 us (71%)
  waiting for transfers between devices  22.6 us (15%)
  Pallas kernels  14.5 us (9%)
  local copies, waits for them, and re-layouts  4.63 us (3%)
    ppermute x7, starting transfers between devices, swap(): return lax.ppermute(value, axis, [(i, i ^ distance) for i in range(size)])  39.4 us
    ppermute x3, starting transfers between devices, shift_both(): return lax.ppermute(value, ('c', 'zh'), pairs)  26 us
    ppermute x6, starting transfers between devices, shift(): lax.ppermute(value, axis, [(i, (i + distance) % size) for i in range(size)])  24 us
    ppermute x3, waiting for transfers between devices, shift_both(): return lax.ppermute(value, ('c', 'zh'), pairs)  15.6 us
    pallas_call x12, Pallas kernels, call(): pl.pallas_call(body, out_shape=[s if isinstance(s, pl.MemoryRef) else jax...  14.4 us
    all_to_all x1, starting transfers between devices, local(): lax.all_to_all(jnp.broadcast_to(weight_out[None], (n_zl, block, hid)), 'z...  13.1 us
    all_to_all x1, starting transfers between devices, local(): parts = lax.all_to_all(parts, 'x', 0, 0)  5.8 us
  transfers between devices with their start and end apart: 18, of which 7 were waited for; matrix products, arithmetic and copies ran while one was open for 0% of the time, Pallas kernels for 7%

profile of v9, /device:TPU:1, one launch (start us, length us, event | category | flops | bytes accessed | tf_op | source)
XLA Modules:
  0.0 150.9 jit_solution(2562233929612823662)
XLA Ops:
  0.6 1.6 %broadcast_in_dim.2 = bf16[8,40,432]{2,1,0:T(8,128)(2,1)} broadcast(bf16[40,432]{1,0:T(8,128)(2,1)} %param.5), dimensions={1,2} | broadcast | bytes 311040 | tf_op jit(solution)/shard_map/broadcast_in_dim | solution.py:217
  2.2 13.1 %all-to-all-start = ((bf16[8,40,432]{2,1,0:T(8,128)(2,1)}), bf16[8,40,432]{2,1,0:T(8,128)(2,1)S(1)}, u32[]{:S(2)}, u32[]{:S(2)}) async-start(bf16[8,40,432]{2,1,0:T(8,128)(2,1)} %broadcast_in_dim.2), calls=%async_computation | async-start | bytes 655360 | tf_op jit(solution)/shard_map/all_to_all | solution.py:217
  15.3 0.7 stack.23.place
  15.9 3.8 %shard_map.67 = (bf16[1712,256]{1,0:T(8,128)(2,1)}, bf16[1280,256]{1,0:T(8,128)(2,1)}) custom-call(s32[5]{0:T(128)} %stack.23.place, s32[320,1]{1,0:T(8,128)} %constant.25.clone.base, bf16[256,2560]{1,0:T(8,128)(2,1)} %cot.1, bf16[432,256]{1,0:T(8,128)(2,1)} %bitcast.25), custom_call_target="tpu_custom_call" | custom-call | flops 838860800 | bytes 2299481 | tf_op jit(solution)/shard_map/pallas_call | solution.py:61
  19.8 6.4 %collective-permute-start.3 = (bf16[1712,256]{1,0:T(8,128)(2,1)}, bf16[1712,256]{1,0:T(8,128)(2,1)S(1)}, u32[]{:S(2)}, u32[]{:S(2)}) collective-permute-start(bf16[1712,256]{1,0:T(8,128)(2,1)} %get-tuple-element.31), channel_id=1, source_target_pairs={{0,16},{16,0},{1,17},{17,1},{2,18},{18,2},{3,19},{19,3},{4,20},{20... | collective-permute-start | bytes 2629640 | tf_op jit(solution)/shard_map/ppermute | solution.py:36
  26.2 1.9 %all-to-all-done = bf16[8,40,432]{2,1,0:T(8,128)(2,1)S(1)} async-done(((bf16[8,40,432]{2,1,0:T(8,128)(2,1)}), bf16[8,40,432]{2,1,0:T(8,128)(2,1)S(1)}, u32[]{:S(2)}, u32[]{:S(2)}) %all-to-all-start) | async-done | bytes 276512 | tf_op jit(solution)/shard_map/all_to_all | solution.py:217
  28.1 6.1 %collective-permute-start.2 = (bf16[320,432]{1,0:T(8,128)(2,1)S(1)}, bf16[320,432]{1,0:T(8,128)(2,1)S(1)}, u32[]{:S(2)}, u32[]{:S(2)}) collective-permute-start(bf16[320,432]{1,0:T(8,128)(2,1)S(1)} %bitcast.17), channel_id=1, source_target_pairs={{0,256},{256,512},{512,768},{768,0},{1,257},{257,513},{513,769},{7... | collective-permute-start | bytes 829448 | tf_op jit(solution)/shard_map/ppermute | solution.py:41
  34.2 4.5 %collective-permute-start.1 = (bf16[320,432]{1,0:T(8,128)(2,1)S(1)}, bf16[320,432]{1,0:T(8,128)(2,1)S(1)}, u32[]{:S(2)}, u32[]{:S(2)}) collective-permute-start(bf16[320,432]{1,0:T(8,128)(2,1)S(1)} %bitcast.18), channel_id=1, source_target_pairs={{0,512},{256,768},{512,0},{768,256},{1,513},{257,769},{513,1},{769... | collective-permute-start | bytes 829448 | tf_op jit(solution)/shard_map/ppermute | solution.py:41
  38.7 3.0 %collective-permute-start = (bf16[320,432]{1,0:T(8,128)(2,1)S(1)}, bf16[320,432]{1,0:T(8,128)(2,1)S(1)}, u32[]{:S(2)}, u32[]{:S(2)}) collective-permute-start(bf16[320,432]{1,0:T(8,128)(2,1)S(1)} %bitcast.19), channel_id=1, source_target_pairs={{0,768},{256,0},{512,256},{768,512},{1,769},{257,1},{513,257},{769... | collective-permute-start | bytes 829448 | tf_op jit(solution)/shard_map/ppermute | solution.py:41
  41.7 0.0 collective-permute-done.3.got
  41.8 1.1 copy-done.5
  42.8 2.4 %shard_map.68 = (bf16[432,512]{1,0:T(8,128)(2,1)S(1)}, bf16[320,432]{1,0:T(8,128)(2,1)}, bf16[320,432]{1,0:T(8,128)(2,1)}, bf16[320,432]{1,0:T(8,128)(2,1)}, bf1...) custom-call(s32[5]{0:T(128)S(1)} %copy-done.4, bf16[432,256]{1,0:T(8,128)(2,1)S(1)} %bitcast.26, ...), custom_call_target="tpu_custom_call" | custom-call | flops 566231040 | bytes 2629657 | tf_op jit(solution)/shard_map/pallas_call | solution.py:61
  45.2 0.0 collective-permute-done.2.w3
  45.2 1.7 %collective-permute-done.1.w2 = bf16[320,432]{1,0:T(8,128)(2,1)S(1)} collective-permute-done((bf16[320,432]{1,0:T(8,128)(2,1)S(1)}, bf16[320,432]{1,0:T(8,128)(2,1)S(1)}, u32[]{:S(2)}, u32[]{:S(2)}) %collective-permute-start.1) | collective-permute-done | bytes 276512 | tf_op jit(solution)/shard_map/ppermute | solution.py:41
  47.0 0.8 collective-permute-done.w1
  47.8 2.2 %shard_map.69 = (bf16[4,4,80,512]{3,2,1,0:T(8,128)(2,1)}, bf16[4,320,432]{2,1,0:T(8,128)(2,1)}, f32[8,128]{1,0:T(8,128)S(1)}) custom-call(s32[5]{0:T(128)S(1)} %copy-done.4, bf16[320,432]{1,0:T(8,128)(2,1)S(1)} %bitcast.20, bf16[320,432]{1,0:T(8,128)(2,1)S(1)} %collective-permute-done.w1, bf16[320,432]{1,0:T(8,128)(2,1)S(1)} %collective-permute-done.1.w2, ...), custom_call_target="tpu_custom_call" | custom-call | flops 566231040 | bytes 2322457 | tf_op jit(solution)/shard_map/pallas_call | solution.py:61
  50.0 5.8 %all-to-all-start.1 = ((bf16[4,4,80,512]{3,2,1,0:T(8,128)(2,1)}), bf16[4,4,80,512]{3,2,1,0:T(8,128)(2,1)S(1)}, u32[]{:S(2)}, u32[]{:S(2)}) async-start(bf16[4,4,80,512]{3,2,1,0:T(8,128)(2,1)} %get-tuple-element.33), calls=%async_computation.1 | async-start | bytes 2621440 | tf_op jit(solution)/shard_map/all_to_all | solution.py:252
  55.8 1.3 copy-done.1
  57.1 1.7 %shard_map.70 = (f32[432,256]{1,0:T(8,128)S(1)}, f32[432,256]{1,0:T(8,128)S(1)}) custom-call(s32[5]{0:T(128)S(1)} %copy-done.4, bf16[4,320,432]{2,1,0:T(8,128)(2,1)S(1)} %copy-done.1, bf16[2,1280,256]{2,1,0:T(8,128)(2,1)S(1)} %copy-done), custom_call_target="tpu_custom_call" | custom-call | flops 566231040 | bytes 3624985 | tf_op jit(solution)/shard_map/pallas_call | solution.py:61
  58.8 7.1 %collective-permute-start.4 = (f32[432,256]{1,0:T(8,128)S(1)}, f32[432,256]{1,0:T(8,128)S(1)}, u32[]{:S(2)}, u32[]{:S(2)}) collective-permute-start(f32[432,256]{1,0:T(8,128)S(1)} %get-tuple-element.37), channel_id=1, source_target_pairs={{0,16},{16,0},{1,17},{17,1},{2,18},{18,2},{3,19},{19,3},{4,20},{20... | collective-permute-start | bytes 1327112 | tf_op jit(solution)/shard_map/ppermute | solution.py:36
  65.9 3.8 %collective-permute-start.8 = (bf16[320,432]{1,0:T(8,128)(2,1)}, bf16[320,432]{1,0:T(8,128)(2,1)S(1)}, u32[]{:S(2)}, u32[]{:S(2)}) collective-permute-start(bf16[320,432]{1,0:T(8,128)(2,1)} %shard_map.74), channel_id=1, source_target_pairs={{0,256},{256,512},{512,768},{768,0},{1,257},{257,513},{513,769},{7... | collective-permute-start | bytes 829448 | tf_op jit(solution)/shard_map/ppermute | solution.py:41
  69.7 3.6 %collective-permute-start.9 = (bf16[320,432]{1,0:T(8,128)(2,1)}, bf16[320,432]{1,0:T(8,128)(2,1)S(1)}, u32[]{:S(2)}, u32[]{:S(2)}) collective-permute-start(bf16[320,432]{1,0:T(8,128)(2,1)} %shard_map.75), channel_id=1, source_target_pairs={{0,512},{256,768},{512,0},{768,256},{1,513},{257,769},{513,1},{769... | collective-permute-start | bytes 829448 | tf_op jit(solution)/shard_map/ppermute | solution.py:41
  73.3 3.0 %collective-permute-start.10 = (bf16[320,432]{1,0:T(8,128)(2,1)S(1)}, bf16[320,432]{1,0:T(8,128)(2,1)S(1)}, u32[]{:S(2)}, u32[]{:S(2)}) collective-permute-start(bf16[320,432]{1,0:T(8,128)(2,1)S(1)} %copy-done.6), channel_id=1, source_target_pairs={{0,768},{256,0},{512,256},{768,512},{1,769},{257,1},{513,257},{769... | collective-permute-start | bytes 829448 | tf_op jit(solution)/shard_map/ppermute | solution.py:41
  76.3 0.0 collective-permute-done.4.other
  76.3 1.0 shard_map.71
  77.3 0.0 all-to-all-done.1.parts
  77.3 0.2 shard_map.72
  77.5 15.2 %collective-permute-start.5 = (bf16[80,512]{1,0:T(8,128)(2,1)S(1)}, bf16[80,512]{1,0:T(8,128)(2,1)S(1)}, u32[]{:S(2)}, u32[]{:S(2)}) collective-permute-start(bf16[80,512]{1,0:T(8,128)(2,1)S(1)} %get-tuple-element.41), channel_id=1, source_target_pairs={{0,4},{4,8},{8,12},{12,0},{16,28},{20,16},{24,20},{28,24},{1,5},{5... | collective-permute-start | bytes 245768 | tf_op jit(solution)/shard_map/ppermute | solution.py:51
  92.7 2.1 %collective-permute-start.6 = (bf16[80,512]{1,0:T(8,128)(2,1)S(1)}, bf16[80,512]{1,0:T(8,128)(2,1)S(1)}, u32[]{:S(2)}, u32[]{:S(2)}) collective-permute-start(bf16[80,512]{1,0:T(8,128)(2,1)S(1)} %get-tuple-element.42), channel_id=1, source_target_pairs={{0,12},{4,0},{8,4},{12,8},{16,20},{20,24},{24,28},{28,16},{1,13},{... | collective-permute-start | bytes 245768 | tf_op jit(solution)/shard_map/ppermute | solution.py:51
  94.9 0.0 collective-permute-done.8
  94.9 0.0 collective-permute-done.9
  94.9 0.0 collective-permute-done.10
  94.9 0.1 collective-permute-done.5.got.after
  95.0 15.4 %collective-permute-done.6.after.then.v = bf16[80,512]{1,0:T(8,128)(2,1)S(1)} collective-permute-done((bf16[80,512]{1,0:T(8,128)(2,1)S(1)}, bf16[80,512]{1,0:T(8,128)(2,1)S(1)}, u32[]{:S(2)}, u32[]{:S(2)}) %collective-permute-start.6) | collective-permute-done | bytes 81952 | tf_op jit(solution)/shard_map/ppermute | solution.py:51
  110.5 0.7 shard_map.77
  111.2 5.4 %collective-permute-start.11 = (bf16[4,40,432]{2,1,0:T(8,128)(2,1)S(1)}, bf16[4,40,432]{2,1,0:T(8,128)(2,1)S(1)}, u32[]{:S(2)}, u32[]{:S(2)}) collective-permute-start(bf16[4,40,432]{2,1,0:T(8,128)(2,1)S(1)} %get-tuple-element.49), channel_id=1, source_target_pairs={{0,32},{32,0},{64,96},{96,64},{128,160},{160,128},{192,224},{224,1... | collective-permute-start | bytes 414728 | tf_op jit(solution)/shard_map/ppermute | solution.py:36
  116.6 8.6 %collective-permute-start.7 = (bf16[80,512]{1,0:T(8,128)(2,1)S(1)}, bf16[80,512]{1,0:T(8,128)(2,1)S(1)}, u32[]{:S(2)}, u32[]{:S(2)}) collective-permute-start(bf16[80,512]{1,0:T(8,128)(2,1)S(1)} %shard_map.73), channel_id=1, source_target_pairs={{0,4},{4,8},{8,12},{12,0},{16,28},{20,16},{24,20},{28,24},{1,5},{5... | collective-permute-start | bytes 245768 | tf_op jit(solution)/shard_map/ppermute | solution.py:51
  125.3 0.6 shard_map.78
  125.8 2.1 %collective-permute-start.12 = (bf16[40,432]{1,0:T(8,128)(2,1)S(1)}, bf16[40,432]{1,0:T(8,128)(2,1)S(1)}, u32[]{:S(2)}, u32[]{:S(2)}) collective-permute-start(bf16[40,432]{1,0:T(8,128)(2,1)S(1)} %get-tuple-element.50), channel_id=1, source_target_pairs={{0,64},{32,96},{64,0},{96,32},{128,192},{160,224},{192,128},{224,1... | collective-permute-start | bytes 103688 | tf_op jit(solution)/shard_map/ppermute | solution.py:36
  127.9 2.9 %collective-permute-start.13 = (bf16[40,432]{1,0:T(8,128)(2,1)S(1)}, bf16[40,432]{1,0:T(8,128)(2,1)S(1)}, u32[]{:S(2)}, u32[]{:S(2)}) collective-permute-start(bf16[40,432]{1,0:T(8,128)(2,1)S(1)} %get-tuple-element.51), channel_id=1, source_target_pairs={{0,128},{32,160},{64,192},{96,224},{128,0},{160,32},{192,64},{224,... | collective-permute-start | bytes 103688 | tf_op jit(solution)/shard_map/ppermute | solution.py:36
  130.8 8.2 %collective-permute-start.14 = (bf16[40,432]{1,0:T(8,128)(2,1)S(1)}, bf16[40,432]{1,0:T(8,128)(2,1)S(1)}, u32[]{:S(2)}, u32[]{:S(2)}) collective-permute-start(bf16[40,432]{1,0:T(8,128)(2,1)S(1)} %get-tuple-element.52), channel_id=1, source_target_pairs={{0,192},{32,224},{64,128},{96,160},{128,64},{160,96},{192,0},{224,... | collective-permute-start | bytes 103688 | tf_op jit(solution)/shard_map/ppermute | solution.py:36
  139.1 0.0 collective-permute-done.7.u
  139.1 0.0 collective-permute-done.12.r1
  139.1 2.4 %collective-permute-done.14.r3 = bf16[40,432]{1,0:T(8,128)(2,1)S(1)} collective-permute-done((bf16[40,432]{1,0:T(8,128)(2,1)S(1)}, bf16[40,432]{1,0:T(8,128)(2,1)S(1)}, u32[]{:S(2)}, u32[]{:S(2)}) %collective-permute-start.14) | collective-permute-done | bytes 34592 | tf_op jit(solution)/shard_map/ppermute | solution.py:36
  141.5 7.4 %collective-permute-start.15 = (bf16[80,256]{1,0:T(8,128)(2,1)S(1)}, bf16[80,256]{1,0:T(8,128)(2,1)S(1)}, u32[]{:S(2)}, u32[]{:S(2)}) collective-permute-start(bf16[80,256]{1,0:T(8,128)(2,1)S(1)} %get-tuple-element.54), channel_id=1, source_target_pairs={{0,16},{16,0},{1,17},{17,1},{2,18},{18,2},{3,19},{19,3},{4,20},{20... | collective-permute-start | bytes 122888 | tf_op jit(solution)/shard_map/ppermute | solution.py:36
  148.9 0.7 shard_map.81
  149.6 0.2 collective-permute-done.15
  149.8 1.2 shard_map.80
  (19 shorter events, 0.1 us)
Async XLA Ops:
  2.2 25.9 %all-to-all-start = ((bf16[8,40,432]{2,1,0:T(8,128)(2,1)}), bf16[8,40,432]{2,1,0:T(8,128)(2,1)S(1)}, u32[]{:S(2)}, u32[]{:S(2)}) async-start(bf16[8,40,432]{2,1,0:T(8,128)(2,1)} %broadcast_in_dim.2), calls=%async_computation | async-start | bytes 655360 | tf_op jit(solution)/shard_map/all_to_all | solution.py:217
  15.9 25.8 %copy-start.3 = (bf16[256,432]{0,1:T(8,128)(2,1)S(1)}, bf16[256,432]{0,1:T(8,128)(2,1)}, u32[]{:S(2)}) copy-start(bf16[256,432]{0,1:T(8,128)(2,1)} %param.4) | copy-start | bytes 663556
  15.9 25.8 %copy-start.4 = (s32[5]{0:T(128)S(1)}, s32[5]{0:T(128)}, u32[]{:S(2)}) copy-start(s32[5]{0:T(128)} %stack.23.place) | copy-start | bytes 64
  19.8 22.0 %collective-permute-start.3 = (bf16[1712,256]{1,0:T(8,128)(2,1)}, bf16[1712,256]{1,0:T(8,128)(2,1)S(1)}, u32[]{:S(2)}, u32[]{:S(2)}) collective-permute-start(bf16[1712,256]{1,0:T(8,128)(2,1)} %get-tuple-element.31), channel_id=1, source_target_pairs={{0,16},{16,0},{1,17},{17,1},{2,18},{18,2},{3,19},{19,3},{4,20},{20... | collective-permute-start | bytes 2629640 | tf_op jit(solution)/shard_map/ppermute | solution.py:36
  28.1 17.1 %collective-permute-start.2 = (bf16[320,432]{1,0:T(8,128)(2,1)S(1)}, bf16[320,432]{1,0:T(8,128)(2,1)S(1)}, u32[]{:S(2)}, u32[]{:S(2)}) collective-permute-start(bf16[320,432]{1,0:T(8,128)(2,1)S(1)} %bitcast.17), channel_id=1, source_target_pairs={{0,256},{256,512},{512,768},{768,0},{1,257},{257,513},{513,769},{7... | collective-permute-start | bytes 829448 | tf_op jit(solution)/shard_map/ppermute | solution.py:41
  34.2 12.8 %collective-permute-start.1 = (bf16[320,432]{1,0:T(8,128)(2,1)S(1)}, bf16[320,432]{1,0:T(8,128)(2,1)S(1)}, u32[]{:S(2)}, u32[]{:S(2)}) collective-permute-start(bf16[320,432]{1,0:T(8,128)(2,1)S(1)} %bitcast.18), channel_id=1, source_target_pairs={{0,512},{256,768},{512,0},{768,256},{1,513},{257,769},{513,1},{769... | collective-permute-start | bytes 829448 | tf_op jit(solution)/shard_map/ppermute | solution.py:41
  38.7 9.0 %collective-permute-start = (bf16[320,432]{1,0:T(8,128)(2,1)S(1)}, bf16[320,432]{1,0:T(8,128)(2,1)S(1)}, u32[]{:S(2)}, u32[]{:S(2)}) collective-permute-start(bf16[320,432]{1,0:T(8,128)(2,1)S(1)} %bitcast.19), channel_id=1, source_target_pairs={{0,768},{256,0},{512,256},{768,512},{1,769},{257,1},{513,257},{769... | collective-permute-start | bytes 829448 | tf_op jit(solution)/shard_map/ppermute | solution.py:41
  41.8 1.1 copy-start.5
  50.0 5.8 %copy-start = (bf16[2,1280,256]{2,1,0:T(8,128)(2,1)S(1)}, bf16[2,1280,256]{2,1,0:T(8,128)(2,1)}, u32[]{:S(2)}) copy-start(bf16[2,1280,256]{2,1,0:T(8,128)(2,1)} %get-tuple-element.35.both) | copy-start | bytes 3932164
  50.0 27.4 %all-to-all-start.1 = ((bf16[4,4,80,512]{3,2,1,0:T(8,128)(2,1)}), bf16[4,4,80,512]{3,2,1,0:T(8,128)(2,1)S(1)}, u32[]{:S(2)}, u32[]{:S(2)}) async-start(bf16[4,4,80,512]{3,2,1,0:T(8,128)(2,1)} %get-tuple-element.33), calls=%async_computation.1 | async-start | bytes 2621440 | tf_op jit(solution)/shard_map/all_to_all | solution.py:252
  55.8 1.3 copy-start.1
  58.8 17.5 %collective-permute-start.4 = (f32[432,256]{1,0:T(8,128)S(1)}, f32[432,256]{1,0:T(8,128)S(1)}, u32[]{:S(2)}, u32[]{:S(2)}) collective-permute-start(f32[432,256]{1,0:T(8,128)S(1)} %get-tuple-element.37), channel_id=1, source_target_pairs={{0,16},{16,0},{1,17},{17,1},{2,18},{18,2},{3,19},{19,3},{4,20},{20... | collective-permute-start | bytes 1327112 | tf_op jit(solution)/shard_map/ppermute | solution.py:36
  65.8 7.5 %copy-start.6 = (bf16[320,432]{1,0:T(8,128)(2,1)S(1)}, bf16[320,432]{1,0:T(8,128)(2,1)}, u32[]{:S(2)}) copy-start(bf16[320,432]{1,0:T(8,128)(2,1)} %shard_map.76) | copy-start | bytes 829444
  65.9 44.6 %copy-start.2 = (bf16[320,432]{1,0:T(8,128)(2,1)S(1)}, bf16[320,432]{1,0:T(8,128)(2,1)}, u32[]{:S(2)}) copy-start(bf16[320,432]{1,0:T(8,128)(2,1)} %get-tuple-element.43) | copy-start | bytes 829444
  65.9 29.0 %collective-permute-start.8 = (bf16[320,432]{1,0:T(8,128)(2,1)}, bf16[320,432]{1,0:T(8,128)(2,1)S(1)}, u32[]{:S(2)}, u32[]{:S(2)}) collective-permute-start(bf16[320,432]{1,0:T(8,128)(2,1)} %shard_map.74), channel_id=1, source_target_pairs={{0,256},{256,512},{512,768},{768,0},{1,257},{257,513},{513,769},{7... | collective-permute-start | bytes 829448 | tf_op jit(solution)/shard_map/ppermute | solution.py:41
  69.7 25.2 %collective-permute-start.9 = (bf16[320,432]{1,0:T(8,128)(2,1)}, bf16[320,432]{1,0:T(8,128)(2,1)S(1)}, u32[]{:S(2)}, u32[]{:S(2)}) collective-permute-start(bf16[320,432]{1,0:T(8,128)(2,1)} %shard_map.75), channel_id=1, source_target_pairs={{0,512},{256,768},{512,0},{768,256},{1,513},{257,769},{513,1},{769... | collective-permute-start | bytes 829448 | tf_op jit(solution)/shard_map/ppermute | solution.py:41
  73.3 21.6 %collective-permute-start.10 = (bf16[320,432]{1,0:T(8,128)(2,1)S(1)}, bf16[320,432]{1,0:T(8,128)(2,1)S(1)}, u32[]{:S(2)}, u32[]{:S(2)}) collective-permute-start(bf16[320,432]{1,0:T(8,128)(2,1)S(1)} %copy-done.6), channel_id=1, source_target_pairs={{0,768},{256,0},{512,256},{768,512},{1,769},{257,1},{513,257},{769... | collective-permute-start | bytes 829448 | tf_op jit(solution)/shard_map/ppermute | solution.py:41
  77.5 17.6 %collective-permute-start.5 = (bf16[80,512]{1,0:T(8,128)(2,1)S(1)}, bf16[80,512]{1,0:T(8,128)(2,1)S(1)}, u32[]{:S(2)}, u32[]{:S(2)}) collective-permute-start(bf16[80,512]{1,0:T(8,128)(2,1)S(1)} %get-tuple-element.41), channel_id=1, source_target_pairs={{0,4},{4,8},{8,12},{12,0},{16,28},{20,16},{24,20},{28,24},{1,5},{5... | collective-permute-start | bytes 245768 | tf_op jit(solution)/shard_map/ppermute | solution.py:51
  92.7 17.8 %collective-permute-start.6 = (bf16[80,512]{1,0:T(8,128)(2,1)S(1)}, bf16[80,512]{1,0:T(8,128)(2,1)S(1)}, u32[]{:S(2)}, u32[]{:S(2)}) collective-permute-start(bf16[80,512]{1,0:T(8,128)(2,1)S(1)} %get-tuple-element.42), channel_id=1, source_target_pairs={{0,12},{4,0},{8,4},{12,8},{16,20},{20,24},{24,28},{28,16},{1,13},{... | collective-permute-start | bytes 245768 | tf_op jit(solution)/shard_map/ppermute | solution.py:51
  111.2 14.0 %collective-permute-start.11 = (bf16[4,40,432]{2,1,0:T(8,128)(2,1)S(1)}, bf16[4,40,432]{2,1,0:T(8,128)(2,1)S(1)}, u32[]{:S(2)}, u32[]{:S(2)}) collective-permute-start(bf16[4,40,432]{2,1,0:T(8,128)(2,1)S(1)} %get-tuple-element.49), channel_id=1, source_target_pairs={{0,32},{32,0},{64,96},{96,64},{128,160},{160,128},{192,224},{224,1... | collective-permute-start | bytes 414728 | tf_op jit(solution)/shard_map/ppermute | solution.py:36
  116.6 22.5 %collective-permute-start.7 = (bf16[80,512]{1,0:T(8,128)(2,1)S(1)}, bf16[80,512]{1,0:T(8,128)(2,1)S(1)}, u32[]{:S(2)}, u32[]{:S(2)}) collective-permute-start(bf16[80,512]{1,0:T(8,128)(2,1)S(1)} %shard_map.73), channel_id=1, source_target_pairs={{0,4},{4,8},{8,12},{12,0},{16,28},{20,16},{24,20},{28,24},{1,5},{5... | collective-permute-start | bytes 245768 | tf_op jit(solution)/shard_map/ppermute | solution.py:51
  125.8 13.2 %collective-permute-start.12 = (bf16[40,432]{1,0:T(8,128)(2,1)S(1)}, bf16[40,432]{1,0:T(8,128)(2,1)S(1)}, u32[]{:S(2)}, u32[]{:S(2)}) collective-permute-start(bf16[40,432]{1,0:T(8,128)(2,1)S(1)} %get-tuple-element.50), channel_id=1, source_target_pairs={{0,64},{32,96},{64,0},{96,32},{128,192},{160,224},{192,128},{224,1... | collective-permute-start | bytes 103688 | tf_op jit(solution)/shard_map/ppermute | solution.py:36
  127.9 11.2 %collective-permute-start.13 = (bf16[40,432]{1,0:T(8,128)(2,1)S(1)}, bf16[40,432]{1,0:T(8,128)(2,1)S(1)}, u32[]{:S(2)}, u32[]{:S(2)}) collective-permute-start(bf16[40,432]{1,0:T(8,128)(2,1)S(1)} %get-tuple-element.51), channel_id=1, source_target_pairs={{0,128},{32,160},{64,192},{96,224},{128,0},{160,32},{192,64},{224,... | collective-permute-start | bytes 103688 | tf_op jit(solution)/shard_map/ppermute | solution.py:36
  130.8 10.7 %collective-permute-start.14 = (bf16[40,432]{1,0:T(8,128)(2,1)S(1)}, bf16[40,432]{1,0:T(8,128)(2,1)S(1)}, u32[]{:S(2)}, u32[]{:S(2)}) collective-permute-start(bf16[40,432]{1,0:T(8,128)(2,1)S(1)} %get-tuple-element.52), channel_id=1, source_target_pairs={{0,192},{32,224},{64,128},{96,160},{128,64},{160,96},{192,0},{224,... | collective-permute-start | bytes 103688 | tf_op jit(solution)/shard_map/ppermute | solution.py:36
  141.5 8.3 %collective-permute-start.15 = (bf16[80,256]{1,0:T(8,128)(2,1)S(1)}, bf16[80,256]{1,0:T(8,128)(2,1)S(1)}, u32[]{:S(2)}, u32[]{:S(2)}) collective-permute-start(bf16[80,256]{1,0:T(8,128)(2,1)S(1)} %get-tuple-element.54), channel_id=1, source_target_pairs={{0,16},{16,0},{1,17},{17,1},{2,18},{18,2},{3,19},{19,3},{4,20},{20... | collective-permute-start | bytes 122888 | tf_op jit(solution)/shard_map/ppermute | solution.py:36

commit v10 on v9

--- a/solution.py
+++ b/solution.py
@@ -158,7 +158,7 @@
     t1[...] = (s1[...].astype(F32) + got[...].astype(F32)).astype(BF16)
 
 
-def sum_last(s0, u, v, r1, r2, r3, kept, given):
+def sum_last(s0, u, v, r1, r2, kept, given):
     half = kept.shape[1]
     total = (s0[...].astype(F32) + (u[...].astype(F32) + v[...].astype(F32))).astype(BF16)
     kept[...] = total[:, :half]
@@ -259,6 +259,7 @@
         [SMEM, VMEM, VMEM],
         (place, weight, both),
         flops=work,
+        limit=56,
     )
     grad_pre, token = call(
         hidden_grad, [((hid, tokens), BF16), ((8, 128), F32)], [VMEM] * 3, (pre, own, swap(other, "c", 1))
@@ -281,7 +282,7 @@
         (place, keep, swap(send, "zl", 1)),
     )
     pairs = [swap(p, "zl", 2 * (k + 1)) for k, p in enumerate(pairs)]
-    kept, given = call(sum_last, [half] * 2, [VMEM] * 3 + [LATER] * 3, (s0, u, v, *pairs))
+    kept, given = call(sum_last, [half] * 2, [VMEM] * 3 + [LATER] * 2, (s0, u, v, *pairs[:2]))
     (grad_weight,) = call(
         functools.partial(sum_scaled, factor=factor),
         [((block, hid), F32)],

time: 153 us -> 159 us (1.039)
  waiting for transfers between devices: 22.6 us -> 32.1 us
  starting transfers between devices: 108 us -> 104 us
  Pallas kernels: 14.5 us -> 16.5 us
    ppermute x7, waiting for transfers between devices: 2.58 us -> 9.17 us  [swap(): return lax.ppermute(value, axis, [(i, i ^ distance) for i in range(size)])]
    ppermute x7, starting transfers between devices: 39.4 us -> 35.4 us  [swap(): return lax.ppermute(value, axis, [(i, i ^ distance) for i in range(size)])]
    ppermute x3, waiting for transfers between devices: 15.6 us -> 18.4 us  [shift_both(): return lax.ppermute(value, ('c', 'zh'), pairs)]
    pallas_call x12, Pallas kernels: 14.4 us -> 16.5 us  [call(): pl.pallas_call(body, out_shape=[s if isinstance(s, pl.MemoryRef) else jax...]
  transfers between devices with their start and end apart: 18 -> 18, of which waited for: 7 -> 8; matrix products, arithmetic and copies ran while one was open for 0% -> 0% of each run, Pallas kernels for 7% -> 8%
where the time goes in v10:
time: 159 us; the launch traced here: 157 us
  starting transfers between devices  104 us (65%)
  waiting for transfers between devices  32.1 us (20%)
  Pallas kernels  16.5 us (10%)
  local copies, waits for them, and re-layouts  3.31 us (2%)
    ppermute x7, starting transfers between devices, swap(): return lax.ppermute(value, axis, [(i, i ^ distance) for i in range(size)])  35.4 us
    ppermute x3, starting transfers between devices, shift_both(): return lax.ppermute(value, ('c', 'zh'), pairs)  26.1 us
    ppermute x6, starting transfers between devices, shift(): lax.ppermute(value, axis, [(i, (i + distance) % size) for i in range(size)])  24 us
    ppermute x3, waiting for transfers between devices, shift_both(): return lax.ppermute(value, ('c', 'zh'), pairs)  18.4 us
    pallas_call x12, Pallas kernels, call(): pl.pallas_call(body, out_shape=[s if isinstance(s, pl.MemoryRef) else jax...  16.5 us
    all_to_all x1, starting transfers between devices, local(): lax.all_to_all(jnp.broadcast_to(weight_out[None], (n_zl, block, hid)), 'z...  13.1 us
    ppermute x7, waiting for transfers between devices, swap(): return lax.ppermute(value, axis, [(i, i ^ distance) for i in range(size)])  9.17 us
    all_to_all x1, starting transfers between devices, local(): parts = lax.all_to_all(parts, 'x', 0, 0)  5.67 us
  transfers between devices with their start and end apart: 18, of which 8 were waited for; matrix products, arithmetic and copies ran while one was open for 0% of the time, Pallas kernels for 8%

profile of v10, /device:TPU:1, one launch (start us, length us, event | category | flops | bytes accessed | tf_op | source)
XLA Modules:
  0.0 157.1 jit_solution(16073291399888325602)
XLA Ops:
  0.6 1.6 broadcast_in_dim.2
  2.2 13.1 %all-to-all-start = ((bf16[8,40,432]{2,1,0:T(8,128)(2,1)}), bf16[8,40,432]{2,1,0:T(8,128)(2,1)S(1)}, u32[]{:S(2)}, u32[]{:S(2)}) async-start(bf16[8,40,432]{2,1,0:T(8,128)(2,1)} %broadcast_in_dim.2), calls=%async_computation | async-start | bytes 655360 | tf_op jit(solution)/shard_map/all_to_all | solution.py:217
  15.3 0.6 stack.23.place
  15.9 3.8 %shard_map.67 = (bf16[1712,256]{1,0:T(8,128)(2,1)}, bf16[1280,256]{1,0:T(8,128)(2,1)}) custom-call(s32[5]{0:T(128)} %stack.23.place, s32[320,1]{1,0:T(8,128)} %constant.25.clone.base, bf16[256,2560]{1,0:T(8,128)(2,1)} %cot.1, bf16[432,256]{1,0:T(8,128)(2,1)} %bitcast.25), custom_call_target="tpu_custom_call" | custom-call | flops 838860800 | bytes 2299481 | tf_op jit(solution)/shard_map/pallas_call | solution.py:61
  19.8 6.4 %collective-permute-start.3 = (bf16[1712,256]{1,0:T(8,128)(2,1)}, bf16[1712,256]{1,0:T(8,128)(2,1)S(1)}, u32[]{:S(2)}, u32[]{:S(2)}) collective-permute-start(bf16[1712,256]{1,0:T(8,128)(2,1)} %get-tuple-element.31), channel_id=1, source_target_pairs={{0,16},{16,0},{1,17},{17,1},{2,18},{18,2},{3,19},{19,3},{4,20},{20... | collective-permute-start | bytes 2629640 | tf_op jit(solution)/shard_map/ppermute | solution.py:36
  26.2 1.9 %all-to-all-done = bf16[8,40,432]{2,1,0:T(8,128)(2,1)S(1)} async-done(((bf16[8,40,432]{2,1,0:T(8,128)(2,1)}), bf16[8,40,432]{2,1,0:T(8,128)(2,1)S(1)}, u32[]{:S(2)}, u32[]{:S(2)}) %all-to-all-start) | async-done | bytes 276512 | tf_op jit(solution)/shard_map/all_to_all | solution.py:217
  28.1 6.1 %collective-permute-start.2 = (bf16[320,432]{1,0:T(8,128)(2,1)S(1)}, bf16[320,432]{1,0:T(8,128)(2,1)S(1)}, u32[]{:S(2)}, u32[]{:S(2)}) collective-permute-start(bf16[320,432]{1,0:T(8,128)(2,1)S(1)} %bitcast.17), channel_id=1, source_target_pairs={{0,256},{256,512},{512,768},{768,0},{1,257},{257,513},{513,769},{7... | collective-permute-start | bytes 829448 | tf_op jit(solution)/shard_map/ppermute | solution.py:41
  34.2 4.5 %collective-permute-start.1 = (bf16[320,432]{1,0:T(8,128)(2,1)S(1)}, bf16[320,432]{1,0:T(8,128)(2,1)S(1)}, u32[]{:S(2)}, u32[]{:S(2)}) collective-permute-start(bf16[320,432]{1,0:T(8,128)(2,1)S(1)} %bitcast.18), channel_id=1, source_target_pairs={{0,512},{256,768},{512,0},{768,256},{1,513},{257,769},{513,1},{769... | collective-permute-start | bytes 829448 | tf_op jit(solution)/shard_map/ppermute | solution.py:41
  38.7 3.0 %collective-permute-start = (bf16[320,432]{1,0:T(8,128)(2,1)S(1)}, bf16[320,432]{1,0:T(8,128)(2,1)S(1)}, u32[]{:S(2)}, u32[]{:S(2)}) collective-permute-start(bf16[320,432]{1,0:T(8,128)(2,1)S(1)} %bitcast.19), channel_id=1, source_target_pairs={{0,768},{256,0},{512,256},{768,512},{1,769},{257,1},{513,257},{769... | collective-permute-start | bytes 829448 | tf_op jit(solution)/shard_map/ppermute | solution.py:41
  41.7 0.0 collective-permute-done.3.got
  41.8 1.1 copy-done.5
  42.8 2.4 %shard_map.68 = (bf16[432,512]{1,0:T(8,128)(2,1)S(1)}, bf16[320,432]{1,0:T(8,128)(2,1)}, bf16[320,432]{1,0:T(8,128)(2,1)}, bf16[320,432]{1,0:T(8,128)(2,1)}, bf1...) custom-call(s32[5]{0:T(128)S(1)} %copy-done.3, bf16[432,256]{1,0:T(8,128)(2,1)S(1)} %bitcast.26, ...), custom_call_target="tpu_custom_call" | custom-call | flops 566231040 | bytes 2629657 | tf_op jit(solution)/shard_map/pallas_call | solution.py:61
  45.2 0.0 collective-permute-done.2.w3
  45.2 1.8 %collective-permute-done.1.w2 = bf16[320,432]{1,0:T(8,128)(2,1)S(1)} collective-permute-done((bf16[320,432]{1,0:T(8,128)(2,1)S(1)}, bf16[320,432]{1,0:T(8,128)(2,1)S(1)}, u32[]{:S(2)}, u32[]{:S(2)}) %collective-permute-start.1) | collective-permute-done | bytes 276512 | tf_op jit(solution)/shard_map/ppermute | solution.py:41
  47.0 0.8 collective-permute-done.w1
  47.8 2.2 %shard_map.69 = (bf16[4,4,80,512]{3,2,1,0:T(8,128)(2,1)}, bf16[4,320,432]{2,1,0:T(8,128)(2,1)}, f32[8,128]{1,0:T(8,128)S(1)}) custom-call(s32[5]{0:T(128)S(1)} %copy-done.3, bf16[320,432]{1,0:T(8,128)(2,1)S(1)} %bitcast.20, bf16[320,432]{1,0:T(8,128)(2,1)S(1)} %collective-permute-done.w1, bf16[320,432]{1,0:T(8,128)(2,1)S(1)} %collective-permute-done.1.w2, ...), custom_call_target="tpu_custom_call" | custom-call | flops 566231040 | bytes 2322457 | tf_op jit(solution)/shard_map/pallas_call | solution.py:61
  49.9 5.7 %all-to-all-start.1 = ((bf16[4,4,80,512]{3,2,1,0:T(8,128)(2,1)}), bf16[4,4,80,512]{3,2,1,0:T(8,128)(2,1)S(1)}, u32[]{:S(2)}, u32[]{:S(2)}) async-start(bf16[4,4,80,512]{3,2,1,0:T(8,128)(2,1)} %get-tuple-element.33), calls=%async_computation.1 | async-start | bytes 2621440 | tf_op jit(solution)/shard_map/all_to_all | solution.py:252
  55.6 3.8 %shard_map.70 = (f32[432,256]{1,0:T(8,128)}, f32[432,256]{1,0:T(8,128)}) custom-call(s32[5]{0:T(128)} %stack.23.place, bf16[4,320,432]{2,1,0:T(8,128)(2,1)} %get-tuple-element.34.weight, bf16[2,1280,256]{2,1,0:T(8,128)(2,1)} %get-tuple-element.35.both), custom_call_target="tpu_custom_call" | custom-call | flops 566231040 | bytes 3624985 | tf_op jit(solution)/shard_map/pallas_call | solution.py:61
  59.4 7.2 %collective-permute-start.4 = (f32[432,256]{1,0:T(8,128)}, f32[432,256]{1,0:T(8,128)S(1)}, u32[]{:S(2)}, u32[]{:S(2)}) collective-permute-start(f32[432,256]{1,0:T(8,128)} %get-tuple-element.37), channel_id=1, source_target_pairs={{0,16},{16,0},{1,17},{17,1},{2,18},{18,2},{3,19},{19,3},{4,20},{20... | collective-permute-start | bytes 1327112 | tf_op jit(solution)/shard_map/ppermute | solution.py:36
  66.6 3.8 %collective-permute-start.8 = (bf16[320,432]{1,0:T(8,128)(2,1)}, bf16[320,432]{1,0:T(8,128)(2,1)S(1)}, u32[]{:S(2)}, u32[]{:S(2)}) collective-permute-start(bf16[320,432]{1,0:T(8,128)(2,1)} %shard_map.74), channel_id=1, source_target_pairs={{0,256},{256,512},{512,768},{768,0},{1,257},{257,513},{513,769},{7... | collective-permute-start | bytes 829448 | tf_op jit(solution)/shard_map/ppermute | solution.py:41
  70.4 3.6 %collective-permute-start.9 = (bf16[320,432]{1,0:T(8,128)(2,1)}, bf16[320,432]{1,0:T(8,128)(2,1)S(1)}, u32[]{:S(2)}, u32[]{:S(2)}) collective-permute-start(bf16[320,432]{1,0:T(8,128)(2,1)} %shard_map.75), channel_id=1, source_target_pairs={{0,512},{256,768},{512,0},{768,256},{1,513},{257,769},{513,1},{769... | collective-permute-start | bytes 829448 | tf_op jit(solution)/shard_map/ppermute | solution.py:41
  74.1 3.0 %collective-permute-start.10 = (bf16[320,432]{1,0:T(8,128)(2,1)S(1)}, bf16[320,432]{1,0:T(8,128)(2,1)S(1)}, u32[]{:S(2)}, u32[]{:S(2)}) collective-permute-start(bf16[320,432]{1,0:T(8,128)(2,1)S(1)} %copy-done.6), channel_id=1, source_target_pairs={{0,768},{256,0},{512,256},{768,512},{1,769},{257,1},{513,257},{769... | collective-permute-start | bytes 829448 | tf_op jit(solution)/shard_map/ppermute | solution.py:41
  77.1 0.0 collective-permute-done.4.other
  77.1 1.0 shard_map.71
  78.1 0.0 all-to-all-done.1.parts
  78.1 0.2 shard_map.72
  78.2 15.2 %collective-permute-start.5 = (bf16[80,512]{1,0:T(8,128)(2,1)S(1)}, bf16[80,512]{1,0:T(8,128)(2,1)S(1)}, u32[]{:S(2)}, u32[]{:S(2)}) collective-permute-start(bf16[80,512]{1,0:T(8,128)(2,1)S(1)} %get-tuple-element.41), channel_id=1, source_target_pairs={{0,4},{4,8},{8,12},{12,0},{16,28},{20,16},{24,20},{28,24},{1,5},{5... | collective-permute-start | bytes 245768 | tf_op jit(solution)/shard_map/ppermute | solution.py:51
  93.5 2.1 %collective-permute-start.6 = (bf16[80,512]{1,0:T(8,128)(2,1)S(1)}, bf16[80,512]{1,0:T(8,128)(2,1)S(1)}, u32[]{:S(2)}, u32[]{:S(2)}) collective-permute-start(bf16[80,512]{1,0:T(8,128)(2,1)S(1)} %get-tuple-element.42), channel_id=1, source_target_pairs={{0,12},{4,0},{8,4},{12,8},{16,20},{20,24},{24,28},{28,16},{1,13},{... | collective-permute-start | bytes 245768 | tf_op jit(solution)/shard_map/ppermute | solution.py:51
  95.6 0.0 collective-permute-done.8
  95.6 0.0 collective-permute-done.9
  95.6 0.0 collective-permute-done.10
  95.7 0.1 collective-permute-done.5.got.after
  95.8 15.4 %collective-permute-done.6.after.then.v = bf16[80,512]{1,0:T(8,128)(2,1)S(1)} collective-permute-done((bf16[80,512]{1,0:T(8,128)(2,1)S(1)}, bf16[80,512]{1,0:T(8,128)(2,1)S(1)}, u32[]{:S(2)}, u32[]{:S(2)}) %collective-permute-start.6) | collective-permute-done | bytes 81952 | tf_op jit(solution)/shard_map/ppermute | solution.py:51
  111.3 0.7 shard_map.77
  112.0 5.2 %collective-permute-start.11 = (bf16[4,40,432]{2,1,0:T(8,128)(2,1)S(1)}, bf16[4,40,432]{2,1,0:T(8,128)(2,1)S(1)}, u32[]{:S(2)}, u32[]{:S(2)}) collective-permute-start(bf16[4,40,432]{2,1,0:T(8,128)(2,1)S(1)} %get-tuple-element.49), channel_id=1, source_target_pairs={{0,32},{32,0},{64,96},{96,64},{128,160},{160,128},{192,224},{224,1... | collective-permute-start | bytes 414728 | tf_op jit(solution)/shard_map/ppermute | solution.py:36
  117.3 8.7 %collective-permute-start.7 = (bf16[80,512]{1,0:T(8,128)(2,1)S(1)}, bf16[80,512]{1,0:T(8,128)(2,1)S(1)}, u32[]{:S(2)}, u32[]{:S(2)}) collective-permute-start(bf16[80,512]{1,0:T(8,128)(2,1)S(1)} %shard_map.73), channel_id=1, source_target_pairs={{0,4},{4,8},{8,12},{12,0},{16,28},{20,16},{24,20},{28,24},{1,5},{5... | collective-permute-start | bytes 245768 | tf_op jit(solution)/shard_map/ppermute | solution.py:51
  126.0 0.0 collective-permute-done.11.got
  126.0 0.6 shard_map.78
  126.6 2.1 %collective-permute-start.12 = (bf16[40,432]{1,0:T(8,128)(2,1)S(1)}, bf16[40,432]{1,0:T(8,128)(2,1)S(1)}, u32[]{:S(2)}, u32[]{:S(2)}) collective-permute-start(bf16[40,432]{1,0:T(8,128)(2,1)S(1)} %get-tuple-element.50), channel_id=1, source_target_pairs={{0,64},{32,96},{64,0},{96,32},{128,192},{160,224},{192,128},{224,1... | collective-permute-start | bytes 103688 | tf_op jit(solution)/shard_map/ppermute | solution.py:36
  128.7 2.9 %collective-permute-start.13 = (bf16[40,432]{1,0:T(8,128)(2,1)S(1)}, bf16[40,432]{1,0:T(8,128)(2,1)S(1)}, u32[]{:S(2)}, u32[]{:S(2)}) collective-permute-start(bf16[40,432]{1,0:T(8,128)(2,1)S(1)} %get-tuple-element.51), channel_id=1, source_target_pairs={{0,128},{32,160},{64,192},{96,224},{128,0},{160,32},{192,64},{224,... | collective-permute-start | bytes 103688 | tf_op jit(solution)/shard_map/ppermute | solution.py:36
  131.6 2.8 %collective-permute-done.7.u = bf16[80,512]{1,0:T(8,128)(2,1)S(1)} collective-permute-done((bf16[80,512]{1,0:T(8,128)(2,1)S(1)}, bf16[80,512]{1,0:T(8,128)(2,1)S(1)}, u32[]{:S(2)}, u32[]{:S(2)}) %collective-permute-start.7) | collective-permute-done | bytes 81952 | tf_op jit(solution)/shard_map/ppermute | solution.py:51
  134.5 3.1 %collective-permute-done.13.r2 = bf16[40,432]{1,0:T(8,128)(2,1)S(1)} collective-permute-done((bf16[40,432]{1,0:T(8,128)(2,1)S(1)}, bf16[40,432]{1,0:T(8,128)(2,1)S(1)}, u32[]{:S(2)}, u32[]{:S(2)}) %collective-permute-start.13) | collective-permute-done | bytes 34592 | tf_op jit(solution)/shard_map/ppermute | solution.py:36
  137.7 7.1 %collective-permute-start.14 = (bf16[80,256]{1,0:T(8,128)(2,1)S(1)}, bf16[80,256]{1,0:T(8,128)(2,1)S(1)}, u32[]{:S(2)}, u32[]{:S(2)}) collective-permute-start(bf16[80,256]{1,0:T(8,128)(2,1)S(1)} %get-tuple-element.53), channel_id=1, source_target_pairs={{0,16},{16,0},{1,17},{17,1},{2,18},{18,2},{3,19},{19,3},{4,20},{20... | collective-permute-start | bytes 122888 | tf_op jit(solution)/shard_map/ppermute | solution.py:36
  144.8 4.4 %collective-permute-start.15 = (bf16[40,432]{1,0:T(8,128)(2,1)S(1)}, bf16[40,432]{1,0:T(8,128)(2,1)S(1)}, u32[]{:S(2)}, u32[]{:S(2)}) collective-permute-start(bf16[40,432]{1,0:T(8,128)(2,1)S(1)} %get-tuple-element.56), channel_id=1, source_target_pairs={{0,192},{32,224},{64,128},{96,160},{128,64},{160,96},{192,0},{224,... | collective-permute-start | bytes 103688 | tf_op jit(solution)/shard_map/ppermute | solution.py:36
  149.2 6.0 %collective-permute-done.15.r3 = bf16[40,432]{1,0:T(8,128)(2,1)S(1)} collective-permute-done((bf16[40,432]{1,0:T(8,128)(2,1)S(1)}, bf16[40,432]{1,0:T(8,128)(2,1)S(1)}, u32[]{:S(2)}, u32[]{:S(2)}) %collective-permute-start.15) | collective-permute-done | bytes 34592 | tf_op jit(solution)/shard_map/ppermute | solution.py:36
  155.3 0.7 shard_map.81
  155.9 0.0 collective-permute-done.14
  155.9 1.2 shard_map.80
  (19 shorter events, 0.1 us)
Async XLA Ops:
  2.2 25.9 %all-to-all-start = ((bf16[8,40,432]{2,1,0:T(8,128)(2,1)}), bf16[8,40,432]{2,1,0:T(8,128)(2,1)S(1)}, u32[]{:S(2)}, u32[]{:S(2)}) async-start(bf16[8,40,432]{2,1,0:T(8,128)(2,1)} %broadcast_in_dim.2), calls=%async_computation | async-start | bytes 655360 | tf_op jit(solution)/shard_map/all_to_all | solution.py:217
  15.9 25.8 %copy-start.2 = (bf16[256,432]{0,1:T(8,128)(2,1)S(1)}, bf16[256,432]{0,1:T(8,128)(2,1)}, u32[]{:S(2)}) copy-start(bf16[256,432]{0,1:T(8,128)(2,1)} %param.4) | copy-start | bytes 663556
  15.9 25.8 %copy-start.3 = (s32[5]{0:T(128)S(1)}, s32[5]{0:T(128)}, u32[]{:S(2)}) copy-start(s32[5]{0:T(128)} %stack.23.place) | copy-start | bytes 64
  19.8 22.0 %collective-permute-start.3 = (bf16[1712,256]{1,0:T(8,128)(2,1)}, bf16[1712,256]{1,0:T(8,128)(2,1)S(1)}, u32[]{:S(2)}, u32[]{:S(2)}) collective-permute-start(bf16[1712,256]{1,0:T(8,128)(2,1)} %get-tuple-element.31), channel_id=1, source_target_pairs={{0,16},{16,0},{1,17},{17,1},{2,18},{18,2},{3,19},{19,3},{4,20},{20... | collective-permute-start | bytes 2629640 | tf_op jit(solution)/shard_map/ppermute | solution.py:36
  28.1 17.1 %collective-permute-start.2 = (bf16[320,432]{1,0:T(8,128)(2,1)S(1)}, bf16[320,432]{1,0:T(8,128)(2,1)S(1)}, u32[]{:S(2)}, u32[]{:S(2)}) collective-permute-start(bf16[320,432]{1,0:T(8,128)(2,1)S(1)} %bitcast.17), channel_id=1, source_target_pairs={{0,256},{256,512},{512,768},{768,0},{1,257},{257,513},{513,769},{7... | collective-permute-start | bytes 829448 | tf_op jit(solution)/shard_map/ppermute | solution.py:41
  34.2 12.8 %collective-permute-start.1 = (bf16[320,432]{1,0:T(8,128)(2,1)S(1)}, bf16[320,432]{1,0:T(8,128)(2,1)S(1)}, u32[]{:S(2)}, u32[]{:S(2)}) collective-permute-start(bf16[320,432]{1,0:T(8,128)(2,1)S(1)} %bitcast.18), channel_id=1, source_target_pairs={{0,512},{256,768},{512,0},{768,256},{1,513},{257,769},{513,1},{769... | collective-permute-start | bytes 829448 | tf_op jit(solution)/shard_map/ppermute | solution.py:41
  38.7 9.0 %collective-permute-start = (bf16[320,432]{1,0:T(8,128)(2,1)S(1)}, bf16[320,432]{1,0:T(8,128)(2,1)S(1)}, u32[]{:S(2)}, u32[]{:S(2)}) collective-permute-start(bf16[320,432]{1,0:T(8,128)(2,1)S(1)} %bitcast.19), channel_id=1, source_target_pairs={{0,768},{256,0},{512,256},{768,512},{1,769},{257,1},{513,257},{769... | collective-permute-start | bytes 829448 | tf_op jit(solution)/shard_map/ppermute | solution.py:41
  41.8 1.1 copy-start.5
  49.9 28.1 %all-to-all-start.1 = ((bf16[4,4,80,512]{3,2,1,0:T(8,128)(2,1)}), bf16[4,4,80,512]{3,2,1,0:T(8,128)(2,1)S(1)}, u32[]{:S(2)}, u32[]{:S(2)}) async-start(bf16[4,4,80,512]{3,2,1,0:T(8,128)(2,1)} %get-tuple-element.33), calls=%async_computation.1 | async-start | bytes 2621440 | tf_op jit(solution)/shard_map/all_to_all | solution.py:252
  59.4 17.7 %copy-start = (f32[432,256]{1,0:T(8,128)S(1)}, f32[432,256]{1,0:T(8,128)}, u32[]{:S(2)}) copy-start(f32[432,256]{1,0:T(8,128)} %get-tuple-element.36.own) | copy-start | bytes 1327108
  59.4 17.7 %collective-permute-start.4 = (f32[432,256]{1,0:T(8,128)}, f32[432,256]{1,0:T(8,128)S(1)}, u32[]{:S(2)}, u32[]{:S(2)}) collective-permute-start(f32[432,256]{1,0:T(8,128)} %get-tuple-element.37), channel_id=1, source_target_pairs={{0,16},{16,0},{1,17},{17,1},{2,18},{18,2},{3,19},{19,3},{4,20},{20... | collective-permute-start | bytes 1327112 | tf_op jit(solution)/shard_map/ppermute | solution.py:36
  66.6 7.5 %copy-start.6 = (bf16[320,432]{1,0:T(8,128)(2,1)S(1)}, bf16[320,432]{1,0:T(8,128)(2,1)}, u32[]{:S(2)}) copy-start(bf16[320,432]{1,0:T(8,128)(2,1)} %shard_map.76) | copy-start | bytes 829444
  66.6 44.6 %copy-start.1 = (bf16[320,432]{1,0:T(8,128)(2,1)S(1)}, bf16[320,432]{1,0:T(8,128)(2,1)}, u32[]{:S(2)}) copy-start(bf16[320,432]{1,0:T(8,128)(2,1)} %get-tuple-element.43) | copy-start | bytes 829444
  66.6 44.6 %copy-start.4 = (s32[5]{0:T(128)S(1)}, s32[5]{0:T(128)}, u32[]{:S(2)}) copy-start(s32[5]{0:T(128)} %stack.23.place) | copy-start | bytes 64
  66.6 29.0 %collective-permute-start.8 = (bf16[320,432]{1,0:T(8,128)(2,1)}, bf16[320,432]{1,0:T(8,128)(2,1)S(1)}, u32[]{:S(2)}, u32[]{:S(2)}) collective-permute-start(bf16[320,432]{1,0:T(8,128)(2,1)} %shard_map.74), channel_id=1, source_target_pairs={{0,256},{256,512},{512,768},{768,0},{1,257},{257,513},{513,769},{7... | collective-permute-start | bytes 829448 | tf_op jit(solution)/shard_map/ppermute | solution.py:41
  70.4 25.2 %collective-permute-start.9 = (bf16[320,432]{1,0:T(8,128)(2,1)}, bf16[320,432]{1,0:T(8,128)(2,1)S(1)}, u32[]{:S(2)}, u32[]{:S(2)}) collective-permute-start(bf16[320,432]{1,0:T(8,128)(2,1)} %shard_map.75), channel_id=1, source_target_pairs={{0,512},{256,768},{512,0},{768,256},{1,513},{257,769},{513,1},{769... | collective-permute-start | bytes 829448 | tf_op jit(solution)/shard_map/ppermute | solution.py:41
  74.1 21.6 %collective-permute-start.10 = (bf16[320,432]{1,0:T(8,128)(2,1)S(1)}, bf16[320,432]{1,0:T(8,128)(2,1)S(1)}, u32[]{:S(2)}, u32[]{:S(2)}) collective-permute-start(bf16[320,432]{1,0:T(8,128)(2,1)S(1)} %copy-done.6), channel_id=1, source_target_pairs={{0,768},{256,0},{512,256},{768,512},{1,769},{257,1},{513,257},{769... | collective-permute-start | bytes 829448 | tf_op jit(solution)/shard_map/ppermute | solution.py:41
  78.2 17.6 %collective-permute-start.5 = (bf16[80,512]{1,0:T(8,128)(2,1)S(1)}, bf16[80,512]{1,0:T(8,128)(2,1)S(1)}, u32[]{:S(2)}, u32[]{:S(2)}) collective-permute-start(bf16[80,512]{1,0:T(8,128)(2,1)S(1)} %get-tuple-element.41), channel_id=1, source_target_pairs={{0,4},{4,8},{8,12},{12,0},{16,28},{20,16},{24,20},{28,24},{1,5},{5... | collective-permute-start | bytes 245768 | tf_op jit(solution)/shard_map/ppermute | solution.py:51
  93.5 17.8 %collective-permute-start.6 = (bf16[80,512]{1,0:T(8,128)(2,1)S(1)}, bf16[80,512]{1,0:T(8,128)(2,1)S(1)}, u32[]{:S(2)}, u32[]{:S(2)}) collective-permute-start(bf16[80,512]{1,0:T(8,128)(2,1)S(1)} %get-tuple-element.42), channel_id=1, source_target_pairs={{0,12},{4,0},{8,4},{12,8},{16,20},{20,24},{24,28},{28,16},{1,13},{... | collective-permute-start | bytes 245768 | tf_op jit(solution)/shard_map/ppermute | solution.py:51
  112.0 14.0 %collective-permute-start.11 = (bf16[4,40,432]{2,1,0:T(8,128)(2,1)S(1)}, bf16[4,40,432]{2,1,0:T(8,128)(2,1)S(1)}, u32[]{:S(2)}, u32[]{:S(2)}) collective-permute-start(bf16[4,40,432]{2,1,0:T(8,128)(2,1)S(1)} %get-tuple-element.49), channel_id=1, source_target_pairs={{0,32},{32,0},{64,96},{96,64},{128,160},{160,128},{192,224},{224,1... | collective-permute-start | bytes 414728 | tf_op jit(solution)/shard_map/ppermute | solution.py:36
  117.3 17.2 %collective-permute-start.7 = (bf16[80,512]{1,0:T(8,128)(2,1)S(1)}, bf16[80,512]{1,0:T(8,128)(2,1)S(1)}, u32[]{:S(2)}, u32[]{:S(2)}) collective-permute-start(bf16[80,512]{1,0:T(8,128)(2,1)S(1)} %shard_map.73), channel_id=1, source_target_pairs={{0,4},{4,8},{8,12},{12,0},{16,28},{20,16},{24,20},{28,24},{1,5},{5... | collective-permute-start | bytes 245768 | tf_op jit(solution)/shard_map/ppermute | solution.py:51
  126.6 7.9 %collective-permute-start.12 = (bf16[40,432]{1,0:T(8,128)(2,1)S(1)}, bf16[40,432]{1,0:T(8,128)(2,1)S(1)}, u32[]{:S(2)}, u32[]{:S(2)}) collective-permute-start(bf16[40,432]{1,0:T(8,128)(2,1)S(1)} %get-tuple-element.50), channel_id=1, source_target_pairs={{0,64},{32,96},{64,0},{96,32},{128,192},{160,224},{192,128},{224,1... | collective-permute-start | bytes 103688 | tf_op jit(solution)/shard_map/ppermute | solution.py:36
  128.7 8.9 %collective-permute-start.13 = (bf16[40,432]{1,0:T(8,128)(2,1)S(1)}, bf16[40,432]{1,0:T(8,128)(2,1)S(1)}, u32[]{:S(2)}, u32[]{:S(2)}) collective-permute-start(bf16[40,432]{1,0:T(8,128)(2,1)S(1)} %get-tuple-element.51), channel_id=1, source_target_pairs={{0,128},{32,160},{64,192},{96,224},{128,0},{160,32},{192,64},{224,... | collective-permute-start | bytes 103688 | tf_op jit(solution)/shard_map/ppermute | solution.py:36
  137.7 18.2 %collective-permute-start.14 = (bf16[80,256]{1,0:T(8,128)(2,1)S(1)}, bf16[80,256]{1,0:T(8,128)(2,1)S(1)}, u32[]{:S(2)}, u32[]{:S(2)}) collective-permute-start(bf16[80,256]{1,0:T(8,128)(2,1)S(1)} %get-tuple-element.53), channel_id=1, source_target_pairs={{0,16},{16,0},{1,17},{17,1},{2,18},{18,2},{3,19},{19,3},{4,20},{20... | collective-permute-start | bytes 122888 | tf_op jit(solution)/shard_map/ppermute | solution.py:36
  144.8 10.5 %collective-permute-start.15 = (bf16[40,432]{1,0:T(8,128)(2,1)S(1)}, bf16[40,432]{1,0:T(8,128)(2,1)S(1)}, u32[]{:S(2)}, u32[]{:S(2)}) collective-permute-start(bf16[40,432]{1,0:T(8,128)(2,1)S(1)} %get-tuple-element.56), channel_id=1, source_target_pairs={{0,192},{32,224},{64,128},{96,160},{128,64},{160,96},{192,0},{224,... | collective-permute-start | bytes 103688 | tf_op jit(solution)/shard_map/ppermute | solution.py:36

commit v11 on v7

--- a/solution.py
+++ b/solution.py
@@ -144,7 +144,7 @@
         out[...] = value.astype(BF16)
 
 
-def sum_step(s1, got, after, t1):
+def sum_step(s1, got, t1):
     t1[...] = (s1[...].astype(F32) + got[...].astype(F32)).astype(BF16)
 
 
@@ -255,22 +255,22 @@
     )
     s0, s1, s2, s3 = call(sum_x, [whole] * 4, [VMEM, LATER], (parts, token))
     got2, v = shift_both(s2, 1), shift_both(s3, -1)
+    (t1,) = call(sum_step, [whole], [VMEM] * 2, (s1, got2))
+    u = shift_both(t1, 1)
     (term,) = call(
         sum_y,
         [pltpu.HBM((n_zl, block, hid), BF16)],
         [VMEM] * 4 + [LATER] * 2,
-        (*terms, got2, v),
+        (*terms, t1, v),
         scratch=[pltpu.VMEM((n_zl, block, hid), BF16), pltpu.SemaphoreType.DMA],
         out_specs=[HBM],
     )
-    (t1,) = call(sum_step, [whole], [VMEM] * 2 + [LATER], (s1, got2, v))
-    u = shift_both(t1, 1)
     kept, given = call(sum_last, [half] * 2, [VMEM] * 3, (s0, u, v))
     (grad_weight,) = call(
         functools.partial(sum_scaled, factor=factor),
         [((block, hid), F32)],
         [VMEM],
-        (lax.all_to_all(term, "zl", 0, 0),),
+        (lax.all_to_all(hold(term, u), "zl", 0, 0),),
     )
     given = swap(given, "c", 1)
     (output,) = call(

time: 152 us -> 150 us (0.987)
  the two profiles are of different devices: /device:TPU:131 before, /device:TPU:2 now
where the time goes in v11:
time: 150 us; the launch traced here: 149 us
  starting transfers between devices  94.6 us (63%)
  waiting for transfers between devices  35 us (23%)
  Pallas kernels  14.1 us (9%)
  local copies, waits for them, and re-layouts  4.65 us (3%)
    ppermute x3, starting transfers between devices, shift_both(): return lax.ppermute(value, ('c', 'zh'), pairs)  31.3 us
    ppermute x6, starting transfers between devices, shift(): lax.ppermute(value, axis, [(i, (i + distance) % size) for i in range(size)])  22.8 us
    all_to_all x1, starting transfers between devices, local(): lax.all_to_all(hold(term, u), 'zl', 0, 0)  17.2 us
    pallas_call x11, Pallas kernels, call(): pl.pallas_call(body, out_shape=[s if isinstance(s, pl.MemoryRef) else jax...  14.1 us
    all_to_all x1, waiting for transfers between devices, local(): lax.all_to_all(hold(term, u), 'zl', 0, 0)  12.7 us
    all_to_all x1, waiting for transfers between devices, local(): lax.all_to_all(jnp.broadcast_to(weight_out[None], (n_zl, block, hid)), 'z...  12.6 us
    all_to_all x1, starting transfers between devices, local(): lax.all_to_all(jnp.broadcast_to(weight_out[None], (n_zl, block, hid)), 'z...  12.5 us
    ppermute x3, starting transfers between devices, swap(): return lax.ppermute(value, axis, [(i, i ^ distance) for i in range(size)])  5.75 us
  transfers between devices with their start and end apart: 15, of which 7 were waited for; matrix products, arithmetic and copies ran while one was open for 0% of the time, Pallas kernels for 8%

profile of v11, /device:TPU:2, one launch (start us, length us, event | category | flops | bytes accessed | tf_op | source)
XLA Modules:
  0.0 149.2 jit_solution(7898244763325877776)
XLA Ops:
  0.6 1.6 %broadcast_in_dim.2 = bf16[8,40,432]{2,1,0:T(8,128)(2,1)} broadcast(bf16[40,432]{1,0:T(8,128)(2,1)} %param.5), dimensions={1,2} | broadcast | bytes 311040 | tf_op jit(solution)/shard_map/broadcast_in_dim | solution.py:207
  2.2 12.5 %all-to-all-start = ((bf16[8,40,432]{2,1,0:T(8,128)(2,1)}), bf16[8,40,432]{2,1,0:T(8,128)(2,1)S(1)}, u32[]{:S(2)}, u32[]{:S(2)}) async-start(bf16[8,40,432]{2,1,0:T(8,128)(2,1)} %broadcast_in_dim.2), calls=%async_computation | async-start | bytes 655360 | tf_op jit(solution)/shard_map/all_to_all | solution.py:207
  14.7 0.7 stack.23.place
  15.4 3.8 %shard_map.67 = (bf16[1712,256]{1,0:T(8,128)(2,1)}, bf16[1280,256]{1,0:T(8,128)(2,1)}) custom-call(s32[5]{0:T(128)} %stack.23.place, s32[320,1]{1,0:T(8,128)} %constant.25.clone.base, bf16[256,2560]{1,0:T(8,128)(2,1)} %cot.1, bf16[432,256]{1,0:T(8,128)(2,1)} %bitcast.25), custom_call_target="tpu_custom_call" | custom-call | flops 838860800 | bytes 2299481 | tf_op jit(solution)/shard_map/pallas_call | solution.py:61
  19.2 1.9 %collective-permute-start.3 = (bf16[1712,256]{1,0:T(8,128)(2,1)}, bf16[1712,256]{1,0:T(8,128)(2,1)S(1)}, u32[]{:S(2)}, u32[]{:S(2)}) collective-permute-start(bf16[1712,256]{1,0:T(8,128)(2,1)} %get-tuple-element.25), channel_id=1, source_target_pairs={{0,16},{16,0},{1,17},{17,1},{2,18},{18,2},{3,19},{19,3},{4,20},{20... | collective-permute-start | bytes 2629640 | tf_op jit(solution)/shard_map/ppermute | solution.py:36
  21.2 12.6 %all-to-all-done = bf16[8,40,432]{2,1,0:T(8,128)(2,1)S(1)} async-done(((bf16[8,40,432]{2,1,0:T(8,128)(2,1)}), bf16[8,40,432]{2,1,0:T(8,128)(2,1)S(1)}, u32[]{:S(2)}, u32[]{:S(2)}) %all-to-all-start) | async-done | bytes 276512 | tf_op jit(solution)/shard_map/all_to_all | solution.py:207
  33.8 3.5 %collective-permute-start.2 = (bf16[320,432]{1,0:T(8,128)(2,1)S(1)}, bf16[320,432]{1,0:T(8,128)(2,1)S(1)}, u32[]{:S(2)}, u32[]{:S(2)}) collective-permute-start(bf16[320,432]{1,0:T(8,128)(2,1)S(1)} %bitcast.21), channel_id=1, source_target_pairs={{0,256},{256,512},{512,768},{768,0},{1,257},{257,513},{513,769},{7... | collective-permute-start | bytes 829448 | tf_op jit(solution)/shard_map/ppermute | solution.py:41
  37.3 4.8 %collective-permute-start.1 = (bf16[320,432]{1,0:T(8,128)(2,1)S(1)}, bf16[320,432]{1,0:T(8,128)(2,1)S(1)}, u32[]{:S(2)}, u32[]{:S(2)}) collective-permute-start(bf16[320,432]{1,0:T(8,128)(2,1)S(1)} %bitcast.22), channel_id=1, source_target_pairs={{0,512},{256,768},{512,0},{768,256},{1,513},{257,769},{513,1},{769... | collective-permute-start | bytes 829448 | tf_op jit(solution)/shard_map/ppermute | solution.py:41
  42.1 3.3 %collective-permute-start = (bf16[320,432]{1,0:T(8,128)(2,1)S(1)}, bf16[320,432]{1,0:T(8,128)(2,1)S(1)}, u32[]{:S(2)}, u32[]{:S(2)}) collective-permute-start(bf16[320,432]{1,0:T(8,128)(2,1)S(1)} %bitcast.23), channel_id=1, source_target_pairs={{0,768},{256,0},{512,256},{768,512},{1,769},{257,1},{513,257},{769... | collective-permute-start | bytes 829448 | tf_op jit(solution)/shard_map/ppermute | solution.py:41
  45.3 0.0 collective-permute-done.3.got
  45.3 0.0 copy-done.3
  45.4 0.0 copy-done.4
  45.4 0.0 copy-start.5
  45.4 1.1 copy-done.5
  46.5 2.4 %shard_map.68 = (bf16[432,512]{1,0:T(8,128)(2,1)S(1)}, bf16[320,432]{1,0:T(8,128)(2,1)}, bf16[320,432]{1,0:T(8,128)(2,1)}, bf16[320,432]{1,0:T(8,128)(2,1)}, bf1...) custom-call(s32[5]{0:T(128)S(1)} %copy-done.4, bf16[432,256]{1,0:T(8,128)(2,1)S(1)} %bitcast.26, ...), custom_call_target="tpu_custom_call" | custom-call | flops 566231040 | bytes 2629657 | tf_op jit(solution)/shard_map/pallas_call | solution.py:61
  48.8 0.0 collective-permute-done.2.w3
  48.8 2.2 %collective-permute-done.1.w2 = bf16[320,432]{1,0:T(8,128)(2,1)S(1)} collective-permute-done((bf16[320,432]{1,0:T(8,128)(2,1)S(1)}, bf16[320,432]{1,0:T(8,128)(2,1)S(1)}, u32[]{:S(2)}, u32[]{:S(2)}) %collective-permute-start.1) | collective-permute-done | bytes 276512 | tf_op jit(solution)/shard_map/ppermute | solution.py:41
  51.0 1.7 %collective-permute-done.w1 = bf16[320,432]{1,0:T(8,128)(2,1)S(1)} collective-permute-done((bf16[320,432]{1,0:T(8,128)(2,1)S(1)}, bf16[320,432]{1,0:T(8,128)(2,1)S(1)}, u32[]{:S(2)}, u32[]{:S(2)}) %collective-permute-start) | collective-permute-done | bytes 276512 | tf_op jit(solution)/shard_map/ppermute | solution.py:41
  52.8 2.2 %shard_map.69 = (bf16[4,4,80,512]{3,2,1,0:T(8,128)(2,1)}, bf16[4,320,432]{2,1,0:T(8,128)(2,1)}, f32[8,128]{1,0:T(8,128)S(1)}) custom-call(s32[5]{0:T(128)S(1)} %copy-done.4, bf16[320,432]{1,0:T(8,128)(2,1)S(1)} %bitcast.24, bf16[320,432]{1,0:T(8,128)(2,1)S(1)} %collective-permute-done.w1, bf16[320,432]{1,0:T(8,128)(2,1)S(1)} %collective-permute-done.1.w2, ...), custom_call_target="tpu_custom_call" | custom-call | flops 566231040 | bytes 2322457 | tf_op jit(solution)/shard_map/pallas_call | solution.py:61
  55.0 0.0 copy-start
  55.0 5.0 %all-to-all-start.1 = ((bf16[4,4,80,512]{3,2,1,0:T(8,128)(2,1)}), bf16[4,4,80,512]{3,2,1,0:T(8,128)(2,1)S(1)}, u32[]{:S(2)}, u32[]{:S(2)}) async-start(bf16[4,4,80,512]{3,2,1,0:T(8,128)(2,1)} %get-tuple-element.27), calls=%async_computation.1 | async-start | bytes 2621440 | tf_op jit(solution)/shard_map/all_to_all | solution.py:242
  59.9 0.0 copy-done
  59.9 1.3 copy-done.1
  61.3 1.7 %shard_map.70 = (f32[432,256]{1,0:T(8,128)S(1)}, f32[432,256]{1,0:T(8,128)S(1)}) custom-call(s32[5]{0:T(128)S(1)} %copy-done.4, bf16[4,320,432]{2,1,0:T(8,128)(2,1)S(1)} %copy-done.1, bf16[2,1280,256]{2,1,0:T(8,128)(2,1)S(1)} %copy-done), custom_call_target="tpu_custom_call" | custom-call | flops 566231040 | bytes 3624985 | tf_op jit(solution)/shard_map/pallas_call | solution.py:61
  62.9 1.9 %collective-permute-start.4 = (f32[432,256]{1,0:T(8,128)S(1)}, f32[432,256]{1,0:T(8,128)S(1)}, u32[]{:S(2)}, u32[]{:S(2)}) collective-permute-start(f32[432,256]{1,0:T(8,128)S(1)} %get-tuple-element.31), channel_id=1, source_target_pairs={{0,16},{16,0},{1,17},{17,1},{2,18},{18,2},{3,19},{19,3},{4,20},{20... | collective-permute-start | bytes 1327112 | tf_op jit(solution)/shard_map/ppermute | solution.py:36
  64.9 4.1 %collective-permute-start.9 = (bf16[320,432]{1,0:T(8,128)(2,1)}, bf16[320,432]{1,0:T(8,128)(2,1)S(1)}, u32[]{:S(2)}, u32[]{:S(2)}) collective-permute-start(bf16[320,432]{1,0:T(8,128)(2,1)} %shard_map.76), channel_id=1, source_target_pairs={{0,256},{256,512},{512,768},{768,0},{1,257},{257,513},{513,769},{7... | collective-permute-start | bytes 829448 | tf_op jit(solution)/shard_map/ppermute | solution.py:41
  69.0 3.9 %collective-permute-start.10 = (bf16[320,432]{1,0:T(8,128)(2,1)}, bf16[320,432]{1,0:T(8,128)(2,1)S(1)}, u32[]{:S(2)}, u32[]{:S(2)}) collective-permute-start(bf16[320,432]{1,0:T(8,128)(2,1)} %shard_map.77), channel_id=1, source_target_pairs={{0,512},{256,768},{512,0},{768,256},{1,513},{257,769},{513,1},{769... | collective-permute-start | bytes 829448 | tf_op jit(solution)/shard_map/ppermute | solution.py:41
  72.9 3.2 %collective-permute-start.11 = (bf16[320,432]{1,0:T(8,128)(2,1)S(1)}, bf16[320,432]{1,0:T(8,128)(2,1)S(1)}, u32[]{:S(2)}, u32[]{:S(2)}) collective-permute-start(bf16[320,432]{1,0:T(8,128)(2,1)S(1)} %copy-done.6), channel_id=1, source_target_pairs={{0,768},{256,0},{512,256},{768,512},{1,769},{257,1},{513,257},{769... | collective-permute-start | bytes 829448 | tf_op jit(solution)/shard_map/ppermute | solution.py:41
  76.2 0.0 collective-permute-done.4.other
  76.2 1.0 shard_map.71
  77.2 0.0 all-to-all-done.1.parts
  77.2 0.2 shard_map.72
  77.4 15.7 %collective-permute-start.5 = (bf16[80,512]{1,0:T(8,128)(2,1)S(1)}, bf16[80,512]{1,0:T(8,128)(2,1)S(1)}, u32[]{:S(2)}, u32[]{:S(2)}) collective-permute-start(bf16[80,512]{1,0:T(8,128)(2,1)S(1)} %get-tuple-element.35), channel_id=1, source_target_pairs={{0,4},{4,8},{8,12},{12,0},{16,28},{20,16},{24,20},{28,24},{1,5},{5... | collective-permute-start | bytes 245768 | tf_op jit(solution)/shard_map/ppermute | solution.py:51
  93.1 1.9 %collective-permute-start.7 = (bf16[80,512]{1,0:T(8,128)(2,1)S(1)}, bf16[80,512]{1,0:T(8,128)(2,1)S(1)}, u32[]{:S(2)}, u32[]{:S(2)}) collective-permute-start(bf16[80,512]{1,0:T(8,128)(2,1)S(1)} %get-tuple-element.36), channel_id=1, source_target_pairs={{0,12},{4,0},{8,4},{12,8},{16,20},{20,24},{24,28},{28,16},{1,13},{... | collective-permute-start | bytes 245768 | tf_op jit(solution)/shard_map/ppermute | solution.py:51
  95.0 2.8 %collective-permute-done.5.got = bf16[80,512]{1,0:T(8,128)(2,1)S(1)} collective-permute-done((bf16[80,512]{1,0:T(8,128)(2,1)S(1)}, bf16[80,512]{1,0:T(8,128)(2,1)S(1)}, u32[]{:S(2)}, u32[]{:S(2)}) %collective-permute-start.5) | collective-permute-done | bytes 81952 | tf_op jit(solution)/shard_map/ppermute | solution.py:51
  97.9 13.7 %collective-permute-start.6 = (bf16[80,512]{1,0:T(8,128)(2,1)S(1)}, bf16[80,512]{1,0:T(8,128)(2,1)S(1)}, u32[]{:S(2)}, u32[]{:S(2)}) collective-permute-start(bf16[80,512]{1,0:T(8,128)(2,1)S(1)} %shard_map.73.after), channel_id=1, source_target_pairs={{0,4},{4,8},{8,12},{12,0},{16,28},{20,16},{24,20},{28,24},{1,5},{5... | collective-permute-start | bytes 245768 | tf_op jit(solution)/shard_map/ppermute | solution.py:51
  111.5 0.0 collective-permute-done.9
  111.6 0.0 collective-permute-done.10
  111.6 0.0 collective-permute-done.11
  111.6 0.0 collective-permute-done.7.v.then
  111.6 0.9 shard_map.79.value
  112.5 1.8 %collective-permute-done.6.u.after = bf16[80,512]{1,0:T(8,128)(2,1)S(1)} collective-permute-done((bf16[80,512]{1,0:T(8,128)(2,1)S(1)}, bf16[80,512]{1,0:T(8,128)(2,1)S(1)}, u32[]{:S(2)}, u32[]{:S(2)}) %collective-permute-start.6) | collective-permute-done | bytes 81952 | tf_op jit(solution)/shard_map/ppermute | solution.py:51
  114.3 17.2 %all-to-all-start.2 = ((bf16[8,40,432]{2,1,0:T(8,128)(2,1)}), bf16[8,40,432]{2,1,0:T(8,128)(2,1)S(1)}, u32[]{:S(2)}, u32[]{:S(2)}) async-start(bf16[8,40,432]{2,1,0:T(8,128)(2,1)} %shard_map.80), calls=%async_computation.2 | async-start | bytes 655360 | tf_op jit(solution)/shard_map/all_to_all | solution.py:273
  131.5 1.9 %collective-permute-start.8 = (bf16[80,256]{1,0:T(8,128)(2,1)S(1)}, bf16[80,256]{1,0:T(8,128)(2,1)S(1)}, u32[]{:S(2)}, u32[]{:S(2)}) collective-permute-start(bf16[80,256]{1,0:T(8,128)(2,1)S(1)} %get-tuple-element.38), channel_id=1, source_target_pairs={{0,16},{16,0},{1,17},{17,1},{2,18},{18,2},{3,19},{19,3},{4,20},{20... | collective-permute-start | bytes 122888 | tf_op jit(solution)/shard_map/ppermute | solution.py:36
  133.5 1.2 collective-permute-done.8
  134.6 1.2 shard_map.75
  135.8 12.7 %all-to-all-done.2.parts = bf16[8,40,432]{2,1,0:T(8,128)(2,1)S(1)} async-done(((bf16[8,40,432]{2,1,0:T(8,128)(2,1)}), bf16[8,40,432]{2,1,0:T(8,128)(2,1)S(1)}, u32[]{:S(2)}, u32[]{:S(2)}) %all-to-all-start.2) | async-done | bytes 276512 | tf_op jit(solution)/shard_map/all_to_all | solution.py:273
  148.6 0.7 shard_map.81
  (13 shorter events, 0.1 us)
Async XLA Ops:
  2.2 31.6 %all-to-all-start = ((bf16[8,40,432]{2,1,0:T(8,128)(2,1)}), bf16[8,40,432]{2,1,0:T(8,128)(2,1)S(1)}, u32[]{:S(2)}, u32[]{:S(2)}) async-start(bf16[8,40,432]{2,1,0:T(8,128)(2,1)} %broadcast_in_dim.2), calls=%async_computation | async-start | bytes 655360 | tf_op jit(solution)/shard_map/all_to_all | solution.py:207
  15.4 30.0 %copy-start.3 = (bf16[256,432]{0,1:T(8,128)(2,1)S(1)}, bf16[256,432]{0,1:T(8,128)(2,1)}, u32[]{:S(2)}) copy-start(bf16[256,432]{0,1:T(8,128)(2,1)} %param.4) | copy-start | bytes 663556
  15.4 30.0 %copy-start.4 = (s32[5]{0:T(128)S(1)}, s32[5]{0:T(128)}, u32[]{:S(2)}) copy-start(s32[5]{0:T(128)} %stack.23.place) | copy-start | bytes 64
  19.2 26.1 %collective-permute-start.3 = (bf16[1712,256]{1,0:T(8,128)(2,1)}, bf16[1712,256]{1,0:T(8,128)(2,1)S(1)}, u32[]{:S(2)}, u32[]{:S(2)}) collective-permute-start(bf16[1712,256]{1,0:T(8,128)(2,1)} %get-tuple-element.25), channel_id=1, source_target_pairs={{0,16},{16,0},{1,17},{17,1},{2,18},{18,2},{3,19},{19,3},{4,20},{20... | collective-permute-start | bytes 2629640 | tf_op jit(solution)/shard_map/ppermute | solution.py:36
  33.8 15.1 %collective-permute-start.2 = (bf16[320,432]{1,0:T(8,128)(2,1)S(1)}, bf16[320,432]{1,0:T(8,128)(2,1)S(1)}, u32[]{:S(2)}, u32[]{:S(2)}) collective-permute-start(bf16[320,432]{1,0:T(8,128)(2,1)S(1)} %bitcast.21), channel_id=1, source_target_pairs={{0,256},{256,512},{512,768},{768,0},{1,257},{257,513},{513,769},{7... | collective-permute-start | bytes 829448 | tf_op jit(solution)/shard_map/ppermute | solution.py:41
  37.3 13.8 %collective-permute-start.1 = (bf16[320,432]{1,0:T(8,128)(2,1)S(1)}, bf16[320,432]{1,0:T(8,128)(2,1)S(1)}, u32[]{:S(2)}, u32[]{:S(2)}) collective-permute-start(bf16[320,432]{1,0:T(8,128)(2,1)S(1)} %bitcast.22), channel_id=1, source_target_pairs={{0,512},{256,768},{512,0},{768,256},{1,513},{257,769},{513,1},{769... | collective-permute-start | bytes 829448 | tf_op jit(solution)/shard_map/ppermute | solution.py:41
  42.1 10.7 %collective-permute-start = (bf16[320,432]{1,0:T(8,128)(2,1)S(1)}, bf16[320,432]{1,0:T(8,128)(2,1)S(1)}, u32[]{:S(2)}, u32[]{:S(2)}) collective-permute-start(bf16[320,432]{1,0:T(8,128)(2,1)S(1)} %bitcast.23), channel_id=1, source_target_pairs={{0,768},{256,0},{512,256},{768,512},{1,769},{257,1},{513,257},{769... | collective-permute-start | bytes 829448 | tf_op jit(solution)/shard_map/ppermute | solution.py:41
  45.4 1.1 copy-start.5
  55.0 5.0 %copy-start = (bf16[2,1280,256]{2,1,0:T(8,128)(2,1)S(1)}, bf16[2,1280,256]{2,1,0:T(8,128)(2,1)}, u32[]{:S(2)}) copy-start(bf16[2,1280,256]{2,1,0:T(8,128)(2,1)} %get-tuple-element.29.both) | copy-start | bytes 3932164
  55.0 22.2 %all-to-all-start.1 = ((bf16[4,4,80,512]{3,2,1,0:T(8,128)(2,1)}), bf16[4,4,80,512]{3,2,1,0:T(8,128)(2,1)S(1)}, u32[]{:S(2)}, u32[]{:S(2)}) async-start(bf16[4,4,80,512]{3,2,1,0:T(8,128)(2,1)} %get-tuple-element.27), calls=%async_computation.1 | async-start | bytes 2621440 | tf_op jit(solution)/shard_map/all_to_all | solution.py:242
  59.9 1.3 copy-start.1
  62.9 13.2 %collective-permute-start.4 = (f32[432,256]{1,0:T(8,128)S(1)}, f32[432,256]{1,0:T(8,128)S(1)}, u32[]{:S(2)}, u32[]{:S(2)}) collective-permute-start(f32[432,256]{1,0:T(8,128)S(1)} %get-tuple-element.31), channel_id=1, source_target_pairs={{0,16},{16,0},{1,17},{17,1},{2,18},{18,2},{3,19},{19,3},{4,20},{20... | collective-permute-start | bytes 1327112 | tf_op jit(solution)/shard_map/ppermute | solution.py:36
  64.9 8.0 %copy-start.6 = (bf16[320,432]{1,0:T(8,128)(2,1)S(1)}, bf16[320,432]{1,0:T(8,128)(2,1)}, u32[]{:S(2)}) copy-start(bf16[320,432]{1,0:T(8,128)(2,1)} %shard_map.78) | copy-start | bytes 829444
  64.9 46.6 %collective-permute-start.9 = (bf16[320,432]{1,0:T(8,128)(2,1)}, bf16[320,432]{1,0:T(8,128)(2,1)S(1)}, u32[]{:S(2)}, u32[]{:S(2)}) collective-permute-start(bf16[320,432]{1,0:T(8,128)(2,1)} %shard_map.76), channel_id=1, source_target_pairs={{0,256},{256,512},{512,768},{768,0},{1,257},{257,513},{513,769},{7... | collective-permute-start | bytes 829448 | tf_op jit(solution)/shard_map/ppermute | solution.py:41
  69.0 42.6 %collective-permute-start.10 = (bf16[320,432]{1,0:T(8,128)(2,1)}, bf16[320,432]{1,0:T(8,128)(2,1)S(1)}, u32[]{:S(2)}, u32[]{:S(2)}) collective-permute-start(bf16[320,432]{1,0:T(8,128)(2,1)} %shard_map.77), channel_id=1, source_target_pairs={{0,512},{256,768},{512,0},{768,256},{1,513},{257,769},{513,1},{769... | collective-permute-start | bytes 829448 | tf_op jit(solution)/shard_map/ppermute | solution.py:41
  72.9 38.7 %collective-permute-start.11 = (bf16[320,432]{1,0:T(8,128)(2,1)S(1)}, bf16[320,432]{1,0:T(8,128)(2,1)S(1)}, u32[]{:S(2)}, u32[]{:S(2)}) collective-permute-start(bf16[320,432]{1,0:T(8,128)(2,1)S(1)} %copy-done.6), channel_id=1, source_target_pairs={{0,768},{256,0},{512,256},{768,512},{1,769},{257,1},{513,257},{769... | collective-permute-start | bytes 829448 | tf_op jit(solution)/shard_map/ppermute | solution.py:41
  76.2 35.4 %copy-start.2 = (bf16[320,432]{1,0:T(8,128)(2,1)S(1)}, bf16[320,432]{1,0:T(8,128)(2,1)}, u32[]{:S(2)}) copy-start(bf16[320,432]{1,0:T(8,128)(2,1)} %get-tuple-element.40) | copy-start | bytes 829444
  77.4 20.5 %collective-permute-start.5 = (bf16[80,512]{1,0:T(8,128)(2,1)S(1)}, bf16[80,512]{1,0:T(8,128)(2,1)S(1)}, u32[]{:S(2)}, u32[]{:S(2)}) collective-permute-start(bf16[80,512]{1,0:T(8,128)(2,1)S(1)} %get-tuple-element.35), channel_id=1, source_target_pairs={{0,4},{4,8},{8,12},{12,0},{16,28},{20,16},{24,20},{28,24},{1,5},{5... | collective-permute-start | bytes 245768 | tf_op jit(solution)/shard_map/ppermute | solution.py:51
  93.1 18.5 %collective-permute-start.7 = (bf16[80,512]{1,0:T(8,128)(2,1)S(1)}, bf16[80,512]{1,0:T(8,128)(2,1)S(1)}, u32[]{:S(2)}, u32[]{:S(2)}) collective-permute-start(bf16[80,512]{1,0:T(8,128)(2,1)S(1)} %get-tuple-element.36), channel_id=1, source_target_pairs={{0,12},{4,0},{8,4},{12,8},{16,20},{20,24},{24,28},{28,16},{1,13},{... | collective-permute-start | bytes 245768 | tf_op jit(solution)/shard_map/ppermute | solution.py:51
  97.9 16.4 %collective-permute-start.6 = (bf16[80,512]{1,0:T(8,128)(2,1)S(1)}, bf16[80,512]{1,0:T(8,128)(2,1)S(1)}, u32[]{:S(2)}, u32[]{:S(2)}) collective-permute-start(bf16[80,512]{1,0:T(8,128)(2,1)S(1)} %shard_map.73.after), channel_id=1, source_target_pairs={{0,4},{4,8},{8,12},{12,0},{16,28},{20,16},{24,20},{28,24},{1,5},{5... | collective-permute-start | bytes 245768 | tf_op jit(solution)/shard_map/ppermute | solution.py:51
  114.3 34.3 %all-to-all-start.2 = ((bf16[8,40,432]{2,1,0:T(8,128)(2,1)}), bf16[8,40,432]{2,1,0:T(8,128)(2,1)S(1)}, u32[]{:S(2)}, u32[]{:S(2)}) async-start(bf16[8,40,432]{2,1,0:T(8,128)(2,1)} %shard_map.80), calls=%async_computation.2 | async-start | bytes 655360 | tf_op jit(solution)/shard_map/all_to_all | solution.py:273
  131.5 3.1 %collective-permute-start.8 = (bf16[80,256]{1,0:T(8,128)(2,1)S(1)}, bf16[80,256]{1,0:T(8,128)(2,1)S(1)}, u32[]{:S(2)}, u32[]{:S(2)}) collective-permute-start(bf16[80,256]{1,0:T(8,128)(2,1)S(1)} %get-tuple-element.38), channel_id=1, source_target_pairs={{0,16},{16,0},{1,17},{17,1},{2,18},{18,2},{3,19},{19,3},{4,20},{20... | collective-permute-start | bytes 122888 | tf_op jit(solution)/shard_map/ppermute | solution.py:36

commit v12 on v11

--- a/solution.py
+++ b/solution.py
@@ -10,8 +10,8 @@
 from jax.sharding import Mesh, PartitionSpec as P
 
 COEFF = math.sqrt(2.0 / math.pi)
-AXES = ("y", "zl", "c", "zh", "x")
-SIZES = (4, 8, 2, 4, 4)
+AXES = ("y", "zq", "zb", "c", "zh", "x")
+SIZES = (4, 4, 2, 2, 4, 4)
 F32, BF16 = jnp.float32, jnp.bfloat16
 SMEM = pl.BlockSpec(memory_space=pltpu.SMEM)
 VMEM = pl.BlockSpec(memory_space=pltpu.VMEM)
@@ -103,9 +103,20 @@
         copy.wait()
 
 
-def sum_y(p0, p1, p2, p3, after, then, out, held, sem):
-    value = p0[...].astype(F32) + p1[...].astype(F32)
-    held[...] = (value + (p2[...].astype(F32) + p3[...].astype(F32))).astype(BF16)
+def split_y(place, p0, p1, p2, p3, after, then, keep, send):
+    bit = place[2]
+
+    def total(index):
+        value = p0[index].astype(F32) + p1[index].astype(F32)
+        return value + (p2[index].astype(F32) + p3[index].astype(F32))
+
+    for index in range(keep.shape[0]):
+        keep[index] = total(2 * index + bit)
+        send[index] = total(2 * index + 1 - bit).astype(BF16)
+
+
+def sum_pair(kept, got, after, out, held, sem):
+    held[...] = (kept[...] + got[...].astype(F32)).astype(BF16)
     copy = pltpu.make_async_copy(held, out, sem)
     copy.start()
     copy.wait()
@@ -193,18 +204,18 @@
 
 
 def local(base, pre_act, weight_out, cotangent):
-    n_y, n_zl, n_x = SIZES[0], SIZES[1], SIZES[4]
+    n_y, n_zl, n_x = SIZES[0], SIZES[1] * SIZES[2], SIZES[5]
     tokens, hid = pre_act.shape
     block = weight_out.shape[0]
     stripe = n_zl * block
     group = stripe // n_x
     channels = n_y * stripe
-    place = jnp.stack([lax.axis_index(a) for a in ("c", "y", "zl", "zh", "x")]).astype(jnp.int32)
+    place = jnp.stack([lax.axis_index(a) for a in ("c", "y", "zb", "zh", "x")]).astype(jnp.int32)
     factor = 1.0 / math.sqrt(tokens * n_y * n_zl * 2)
     work = 2 * tokens * channels * hid * 2
     pre = pre_act.T
 
-    rows = lax.all_to_all(jnp.broadcast_to(weight_out[None], (n_zl, block, hid)), "zl", 0, 0)
+    rows = lax.all_to_all(jnp.broadcast_to(weight_out[None], (n_zl, block, hid)), ("zq", "zb"), 0, 0)
     send, mine = call(
         functools.partial(sort_channels, block=block),
         [((channels + hid, tokens), BF16), ((channels, tokens), BF16)],
@@ -257,12 +268,19 @@
     got2, v = shift_both(s2, 1), shift_both(s3, -1)
     (t1,) = call(sum_step, [whole], [VMEM] * 2, (s1, got2))
     u = shift_both(t1, 1)
+    quarter = SIZES[1]
+    keep, send = call(
+        split_y,
+        [((quarter, block, hid), F32), ((quarter, block, hid), BF16)],
+        [SMEM] + [VMEM] * 4 + [LATER] * 2,
+        (place, *terms, t1, v),
+    )
     (term,) = call(
-        sum_y,
-        [pltpu.HBM((n_zl, block, hid), BF16)],
-        [VMEM] * 4 + [LATER] * 2,
-        (*terms, t1, v),
-        scratch=[pltpu.VMEM((n_zl, block, hid), BF16), pltpu.SemaphoreType.DMA],
+        sum_pair,
+        [pltpu.HBM((quarter, block, hid), BF16)],
+        [VMEM] * 2 + [LATER],
+        (keep, swap(hold(send, u), "zb", 1), u),
+        scratch=[pltpu.VMEM((quarter, block, hid), BF16), pltpu.SemaphoreType.DMA],
         out_specs=[HBM],
     )
     kept, given = call(sum_last, [half] * 2, [VMEM] * 3, (s0, u, v))
@@ -270,7 +288,7 @@
         functools.partial(sum_scaled, factor=factor),
         [((block, hid), F32)],
         [VMEM],
-        (lax.all_to_all(hold(term, u), "zl", 0, 0),),
+        (lax.all_to_all(term, "zq", 0, 0),),
     )
     given = swap(given, "c", 1)
     (output,) = call(
@@ -285,7 +303,7 @@
 
 def solution(mesh):
     fine = Mesh(np.asarray(mesh.devices).reshape(SIZES), AXES)
-    dp, tensor = AXES[:3], AXES[3:]
+    dp, tensor = AXES[:4], AXES[4:]
     mapped = jax.shard_map(
         local,
         mesh=fine,
@@ -295,8 +313,8 @@
     )
 
     def run(pre_act, weight_out, cotangent):
-        block = weight_out.shape[0] // (SIZES[0] * SIZES[1] * SIZES[2])
-        k = np.arange(SIZES[1] * block)
+        block = weight_out.shape[0] // math.prod(SIZES[:4])
+        k = np.arange(SIZES[1] * SIZES[2] * block)
         base = (k // block * (2 * block) + k % block).astype(np.int32)[:, None]
         return mapped(jnp.asarray(base), pre_act, weight_out, cotangent)
 

time: 150 us -> 152 us (1.013)
  starting transfers between devices: 94.6 us -> 97 us
    ppermute x3 -> x4, starting transfers between devices: 5.75 us -> 20.1 us  [swap(): return lax.ppermute(value, axis, [(i, i ^ distance) for i in range(size)])]
    all_to_all x2, starting transfers between devices: 29.8 us -> 18.1 us  [the longest x1 12.5 us: local(): lax.all_to_all(jnp.broadcast_to(weight_out[None], (n_zl, block, hid)), ('...]
    all_to_all x2, waiting for transfers between devices: 25.3 us -> 20.1 us  [the longest x1 12.7 us: local(): lax.all_to_all(jnp.broadcast_to(weight_out[None], (n_zl, block, hid)), ('...]
    ppermute x3 -> x4, waiting for transfers between devices: 1.19 us -> 4.68 us  [swap(): return lax.ppermute(value, axis, [(i, i ^ distance) for i in range(size)])]
    pallas_call x11 -> x12, Pallas kernels: 14.1 us -> 14.6 us  [call(): pl.pallas_call(body, out_shape=[s if isinstance(s, pl.MemoryRef) else jax...]
  transfers between devices with their start and end apart: 15 -> 16, of which waited for: 7 -> 8; matrix products, arithmetic and copies ran while one was open for 0% -> 0% of each run, Pallas kernels for 8% -> 7%
where the time goes in v12:
time: 152 us; the launch traced here: 151 us
  starting transfers between devices  97 us (64%)
  waiting for transfers between devices  33.6 us (22%)
  Pallas kernels  14.6 us (10%)
  local copies, waits for them, and re-layouts  4.57 us (3%)
    ppermute x3, starting transfers between devices, shift_both(): return lax.ppermute(value, ('c', 'zh'), pairs)  31.1 us
    ppermute x6, starting transfers between devices, shift(): lax.ppermute(value, axis, [(i, (i + distance) % size) for i in range(size)])  22.7 us
    ppermute x4, starting transfers between devices, swap(): return lax.ppermute(value, axis, [(i, i ^ distance) for i in range(size)])  20.1 us
    pallas_call x12, Pallas kernels, call(): pl.pallas_call(body, out_shape=[s if isinstance(s, pl.MemoryRef) else jax...  14.6 us
    all_to_all x1, waiting for transfers between devices, local(): lax.all_to_all(jnp.broadcast_to(weight_out[None], (n_zl, block, hid)), ('...  12.7 us
    all_to_all x1, starting transfers between devices, local(): lax.all_to_all(jnp.broadcast_to(weight_out[None], (n_zl, block, hid)), ('...  12.5 us
    all_to_all x1, waiting for transfers between devices, local(): lax.all_to_all(term, 'zq', 0, 0)  7.34 us
    all_to_all x1, starting transfers between devices, local(): lax.all_to_all(term, 'zq', 0, 0)  5.55 us
  transfers between devices with their start and end apart: 16, of which 8 were waited for; matrix products, arithmetic and copies ran while one was open for 0% of the time, Pallas kernels for 7%

profile of v12, /device:TPU:2, one launch (start us, length us, event | category | flops | bytes accessed | tf_op | source)
XLA Modules:
  0.0 150.7 jit_solution(6359930001432985804)
XLA Ops:
  0.6 1.6 %broadcast_in_dim.2 = bf16[8,40,432]{2,1,0:T(8,128)(2,1)} broadcast(bf16[40,432]{1,0:T(8,128)(2,1)} %param.5), dimensions={1,2} | broadcast | bytes 311040 | tf_op jit(solution)/shard_map/broadcast_in_dim | solution.py:218
  2.2 12.5 %all-to-all-start = ((bf16[8,40,432]{2,1,0:T(8,128)(2,1)}), bf16[8,40,432]{2,1,0:T(8,128)(2,1)S(1)}, u32[]{:S(2)}, u32[]{:S(2)}) async-start(bf16[8,40,432]{2,1,0:T(8,128)(2,1)} %broadcast_in_dim.2), calls=%async_computation | async-start | bytes 655360 | tf_op jit(solution)/shard_map/all_to_all | solution.py:218
  14.7 0.6 stack.23.place
  15.3 3.8 %shard_map.67 = (bf16[1712,256]{1,0:T(8,128)(2,1)}, bf16[1280,256]{1,0:T(8,128)(2,1)}) custom-call(s32[5]{0:T(128)} %stack.23.place, s32[320,1]{1,0:T(8,128)} %constant.23.clone.base, bf16[256,2560]{1,0:T(8,128)(2,1)} %cot.1, bf16[432,256]{1,0:T(8,128)(2,1)} %bitcast.25), custom_call_target="tpu_custom_call" | custom-call | flops 838860800 | bytes 2299481 | tf_op jit(solution)/shard_map/pallas_call | solution.py:61
  19.1 1.9 %collective-permute-start.3 = (bf16[1712,256]{1,0:T(8,128)(2,1)}, bf16[1712,256]{1,0:T(8,128)(2,1)S(1)}, u32[]{:S(2)}, u32[]{:S(2)}) collective-permute-start(bf16[1712,256]{1,0:T(8,128)(2,1)} %get-tuple-element.27), channel_id=1, source_target_pairs={{0,16},{16,0},{1,17},{17,1},{2,18},{18,2},{3,19},{19,3},{4,20},{20... | collective-permute-start | bytes 2629640 | tf_op jit(solution)/shard_map/ppermute | solution.py:36
  21.0 12.7 %all-to-all-done = bf16[8,40,432]{2,1,0:T(8,128)(2,1)S(1)} async-done(((bf16[8,40,432]{2,1,0:T(8,128)(2,1)}), bf16[8,40,432]{2,1,0:T(8,128)(2,1)S(1)}, u32[]{:S(2)}, u32[]{:S(2)}) %all-to-all-start) | async-done | bytes 276512 | tf_op jit(solution)/shard_map/all_to_all | solution.py:218
  33.8 3.5 %collective-permute-start.2 = (bf16[320,432]{1,0:T(8,128)(2,1)S(1)}, bf16[320,432]{1,0:T(8,128)(2,1)S(1)}, u32[]{:S(2)}, u32[]{:S(2)}) collective-permute-start(bf16[320,432]{1,0:T(8,128)(2,1)S(1)} %bitcast.17), channel_id=1, source_target_pairs={{0,256},{256,512},{512,768},{768,0},{1,257},{257,513},{513,769},{7... | collective-permute-start | bytes 829448 | tf_op jit(solution)/shard_map/ppermute | solution.py:41
  37.2 4.8 %collective-permute-start.1 = (bf16[320,432]{1,0:T(8,128)(2,1)S(1)}, bf16[320,432]{1,0:T(8,128)(2,1)S(1)}, u32[]{:S(2)}, u32[]{:S(2)}) collective-permute-start(bf16[320,432]{1,0:T(8,128)(2,1)S(1)} %bitcast.18), channel_id=1, source_target_pairs={{0,512},{256,768},{512,0},{768,256},{1,513},{257,769},{513,1},{769... | collective-permute-start | bytes 829448 | tf_op jit(solution)/shard_map/ppermute | solution.py:41
  42.1 3.3 %collective-permute-start = (bf16[320,432]{1,0:T(8,128)(2,1)S(1)}, bf16[320,432]{1,0:T(8,128)(2,1)S(1)}, u32[]{:S(2)}, u32[]{:S(2)}) collective-permute-start(bf16[320,432]{1,0:T(8,128)(2,1)S(1)} %bitcast.19), channel_id=1, source_target_pairs={{0,768},{256,0},{512,256},{768,512},{1,769},{257,1},{513,257},{769... | collective-permute-start | bytes 829448 | tf_op jit(solution)/shard_map/ppermute | solution.py:41
  45.3 0.0 collective-permute-done.3.got
  45.3 0.0 copy-done.3
  45.4 1.1 copy-done.6
  46.5 2.4 %shard_map.68 = (bf16[432,512]{1,0:T(8,128)(2,1)S(1)}, bf16[320,432]{1,0:T(8,128)(2,1)}, bf16[320,432]{1,0:T(8,128)(2,1)}, bf16[320,432]{1,0:T(8,128)(2,1)}, bf1...) custom-call(s32[5]{0:T(128)S(1)} %copy-done.5, bf16[432,256]{1,0:T(8,128)(2,1)S(1)} %bitcast.26, ...), custom_call_target="tpu_custom_call" | custom-call | flops 566231040 | bytes 2629657 | tf_op jit(solution)/shard_map/pallas_call | solution.py:61
  48.8 0.0 collective-permute-done.2.w3
  48.9 2.2 %collective-permute-done.1.w2 = bf16[320,432]{1,0:T(8,128)(2,1)S(1)} collective-permute-done((bf16[320,432]{1,0:T(8,128)(2,1)S(1)}, bf16[320,432]{1,0:T(8,128)(2,1)S(1)}, u32[]{:S(2)}, u32[]{:S(2)}) %collective-permute-start.1) | collective-permute-done | bytes 276512 | tf_op jit(solution)/shard_map/ppermute | solution.py:41
  51.0 1.7 %collective-permute-done.w1 = bf16[320,432]{1,0:T(8,128)(2,1)S(1)} collective-permute-done((bf16[320,432]{1,0:T(8,128)(2,1)S(1)}, bf16[320,432]{1,0:T(8,128)(2,1)S(1)}, u32[]{:S(2)}, u32[]{:S(2)}) %collective-permute-start) | collective-permute-done | bytes 276512 | tf_op jit(solution)/shard_map/ppermute | solution.py:41
  52.8 2.2 %shard_map.69 = (bf16[4,4,80,512]{3,2,1,0:T(8,128)(2,1)}, bf16[4,320,432]{2,1,0:T(8,128)(2,1)}, f32[8,128]{1,0:T(8,128)S(1)}) custom-call(s32[5]{0:T(128)S(1)} %copy-done.5, bf16[320,432]{1,0:T(8,128)(2,1)S(1)} %bitcast.20, bf16[320,432]{1,0:T(8,128)(2,1)S(1)} %collective-permute-done.w1, bf16[320,432]{1,0:T(8,128)(2,1)S(1)} %collective-permute-done.1.w2, ...), custom_call_target="tpu_custom_call" | custom-call | flops 566231040 | bytes 2322457 | tf_op jit(solution)/shard_map/pallas_call | solution.py:61
  55.0 5.0 %all-to-all-start.1 = ((bf16[4,4,80,512]{3,2,1,0:T(8,128)(2,1)}), bf16[4,4,80,512]{3,2,1,0:T(8,128)(2,1)S(1)}, u32[]{:S(2)}, u32[]{:S(2)}) async-start(bf16[4,4,80,512]{3,2,1,0:T(8,128)(2,1)} %get-tuple-element.29), calls=%async_computation.1 | async-start | bytes 2621440 | tf_op jit(solution)/shard_map/all_to_all | solution.py:253
  60.0 0.0 copy-done
  60.0 1.3 copy-done.1
  61.3 1.7 %shard_map.70 = (f32[432,256]{1,0:T(8,128)S(1)}, f32[432,256]{1,0:T(8,128)S(1)}) custom-call(s32[5]{0:T(128)S(1)} %copy-done.5, bf16[4,320,432]{2,1,0:T(8,128)(2,1)S(1)} %copy-done.1, bf16[2,1280,256]{2,1,0:T(8,128)(2,1)S(1)} %copy-done), custom_call_target="tpu_custom_call" | custom-call | flops 566231040 | bytes 3624985 | tf_op jit(solution)/shard_map/pallas_call | solution.py:61
  63.0 1.9 %collective-permute-start.4 = (f32[432,256]{1,0:T(8,128)S(1)}, f32[432,256]{1,0:T(8,128)S(1)}, u32[]{:S(2)}, u32[]{:S(2)}) collective-permute-start(f32[432,256]{1,0:T(8,128)S(1)} %get-tuple-element.33), channel_id=1, source_target_pairs={{0,16},{16,0},{1,17},{17,1},{2,18},{18,2},{3,19},{19,3},{4,20},{20... | collective-permute-start | bytes 1327112 | tf_op jit(solution)/shard_map/ppermute | solution.py:36
  64.9 4.1 %collective-permute-start.9 = (bf16[320,432]{1,0:T(8,128)(2,1)}, bf16[320,432]{1,0:T(8,128)(2,1)S(1)}, u32[]{:S(2)}, u32[]{:S(2)}) collective-permute-start(bf16[320,432]{1,0:T(8,128)(2,1)} %shard_map.76), channel_id=1, source_target_pairs={{0,256},{256,512},{512,768},{768,0},{1,257},{257,513},{513,769},{7... | collective-permute-start | bytes 829448 | tf_op jit(solution)/shard_map/ppermute | solution.py:41
  69.0 3.9 %collective-permute-start.10 = (bf16[320,432]{1,0:T(8,128)(2,1)}, bf16[320,432]{1,0:T(8,128)(2,1)S(1)}, u32[]{:S(2)}, u32[]{:S(2)}) collective-permute-start(bf16[320,432]{1,0:T(8,128)(2,1)} %shard_map.77), channel_id=1, source_target_pairs={{0,512},{256,768},{512,0},{768,256},{1,513},{257,769},{513,1},{769... | collective-permute-start | bytes 829448 | tf_op jit(solution)/shard_map/ppermute | solution.py:41
  72.9 3.3 %collective-permute-start.11 = (bf16[320,432]{1,0:T(8,128)(2,1)S(1)}, bf16[320,432]{1,0:T(8,128)(2,1)S(1)}, u32[]{:S(2)}, u32[]{:S(2)}) collective-permute-start(bf16[320,432]{1,0:T(8,128)(2,1)S(1)} %copy-done.7), channel_id=1, source_target_pairs={{0,768},{256,0},{512,256},{768,512},{1,769},{257,1},{513,257},{769... | collective-permute-start | bytes 829448 | tf_op jit(solution)/shard_map/ppermute | solution.py:41
  76.2 0.0 collective-permute-done.4.other
  76.2 1.0 shard_map.71
  77.2 0.0 all-to-all-done.1.parts
  77.2 0.2 shard_map.72
  77.4 15.7 %collective-permute-start.5 = (bf16[80,512]{1,0:T(8,128)(2,1)S(1)}, bf16[80,512]{1,0:T(8,128)(2,1)S(1)}, u32[]{:S(2)}, u32[]{:S(2)}) collective-permute-start(bf16[80,512]{1,0:T(8,128)(2,1)S(1)} %get-tuple-element.37), channel_id=1, source_target_pairs={{0,4},{4,8},{8,12},{12,0},{16,28},{20,16},{24,20},{28,24},{1,5},{5... | collective-permute-start | bytes 245768 | tf_op jit(solution)/shard_map/ppermute | solution.py:51
  93.1 1.9 %collective-permute-start.7 = (bf16[80,512]{1,0:T(8,128)(2,1)S(1)}, bf16[80,512]{1,0:T(8,128)(2,1)S(1)}, u32[]{:S(2)}, u32[]{:S(2)}) collective-permute-start(bf16[80,512]{1,0:T(8,128)(2,1)S(1)} %get-tuple-element.38), channel_id=1, source_target_pairs={{0,12},{4,0},{8,4},{12,8},{16,20},{20,24},{24,28},{28,16},{1,13},{... | collective-permute-start | bytes 245768 | tf_op jit(solution)/shard_map/ppermute | solution.py:51
  95.1 3.0 %collective-permute-done.5.got = bf16[80,512]{1,0:T(8,128)(2,1)S(1)} collective-permute-done((bf16[80,512]{1,0:T(8,128)(2,1)S(1)}, bf16[80,512]{1,0:T(8,128)(2,1)S(1)}, u32[]{:S(2)}, u32[]{:S(2)}) %collective-permute-start.5) | collective-permute-done | bytes 81952 | tf_op jit(solution)/shard_map/ppermute | solution.py:51
  98.1 13.5 %collective-permute-start.6 = (bf16[80,512]{1,0:T(8,128)(2,1)S(1)}, bf16[80,512]{1,0:T(8,128)(2,1)S(1)}, u32[]{:S(2)}, u32[]{:S(2)}) collective-permute-start(bf16[80,512]{1,0:T(8,128)(2,1)S(1)} %shard_map.73.after), channel_id=1, source_target_pairs={{0,4},{4,8},{8,12},{12,0},{16,28},{20,16},{24,20},{28,24},{1,5},{5... | collective-permute-start | bytes 245768 | tf_op jit(solution)/shard_map/ppermute | solution.py:51
  111.6 0.0 collective-permute-done.9
  111.6 0.0 collective-permute-done.10
  111.6 0.0 collective-permute-done.11
  111.6 0.0 collective-permute-done.7.v.then
  111.6 0.7 shard_map.79
  112.4 1.9 %collective-permute-done.6.u.after = bf16[80,512]{1,0:T(8,128)(2,1)S(1)} collective-permute-done((bf16[80,512]{1,0:T(8,128)(2,1)S(1)}, bf16[80,512]{1,0:T(8,128)(2,1)S(1)}, u32[]{:S(2)}, u32[]{:S(2)}) %collective-permute-start.6) | collective-permute-done | bytes 81952 | tf_op jit(solution)/shard_map/ppermute | solution.py:51
  114.2 14.3 %collective-permute-start.12 = (bf16[4,40,432]{2,1,0:T(8,128)(2,1)}, bf16[4,40,432]{2,1,0:T(8,128)(2,1)S(1)}, u32[]{:S(2)}, u32[]{:S(2)}) collective-permute-start(bf16[4,40,432]{2,1,0:T(8,128)(2,1)} %shard_map.80), channel_id=1, source_target_pairs={{0,32},{32,0},{1,33},{33,1},{2,34},{34,2},{3,35},{35,3},{4,36},{36... | collective-permute-start | bytes 414728 | tf_op jit(solution)/shard_map/ppermute | solution.py:36
  128.6 3.5 %collective-permute-done.12.got = bf16[4,40,432]{2,1,0:T(8,128)(2,1)S(1)} collective-permute-done((bf16[4,40,432]{2,1,0:T(8,128)(2,1)}, bf16[4,40,432]{2,1,0:T(8,128)(2,1)S(1)}, u32[]{:S(2)}, u32[]{:S(2)}) %collective-permute-start.12) | collective-permute-done | bytes 138272 | tf_op jit(solution)/shard_map/ppermute | solution.py:36
  132.1 0.7 shard_map.81
  132.8 5.6 %all-to-all-start.2 = ((bf16[4,40,432]{2,1,0:T(8,128)(2,1)}), bf16[4,40,432]{2,1,0:T(8,128)(2,1)S(1)}, u32[]{:S(2)}, u32[]{:S(2)}) async-start(bf16[4,40,432]{2,1,0:T(8,128)(2,1)} %shard_map.81), calls=%async_computation.2 | async-start | bytes 327680 | tf_op jit(solution)/shard_map/all_to_all | solution.py:291
  138.4 1.9 %collective-permute-start.8 = (bf16[80,256]{1,0:T(8,128)(2,1)S(1)}, bf16[80,256]{1,0:T(8,128)(2,1)S(1)}, u32[]{:S(2)}, u32[]{:S(2)}) collective-permute-start(bf16[80,256]{1,0:T(8,128)(2,1)S(1)} %get-tuple-element.40), channel_id=1, source_target_pairs={{0,16},{16,0},{1,17},{17,1},{2,18},{18,2},{3,19},{19,3},{4,20},{20... | collective-permute-start | bytes 122888 | tf_op jit(solution)/shard_map/ppermute | solution.py:36
  140.3 1.2 collective-permute-done.8
  141.5 1.2 shard_map.75
  142.7 7.3 %all-to-all-done.2.parts = bf16[4,40,432]{2,1,0:T(8,128)(2,1)S(1)} async-done(((bf16[4,40,432]{2,1,0:T(8,128)(2,1)}), bf16[4,40,432]{2,1,0:T(8,128)(2,1)S(1)}, u32[]{:S(2)}, u32[]{:S(2)}) %all-to-all-start.2) | async-done | bytes 138272 | tf_op jit(solution)/shard_map/all_to_all | solution.py:291
  150.0 0.7 shard_map.82
  (18 shorter events, 0.1 us)
Async XLA Ops:
  2.2 31.6 %all-to-all-start = ((bf16[8,40,432]{2,1,0:T(8,128)(2,1)}), bf16[8,40,432]{2,1,0:T(8,128)(2,1)S(1)}, u32[]{:S(2)}, u32[]{:S(2)}) async-start(bf16[8,40,432]{2,1,0:T(8,128)(2,1)} %broadcast_in_dim.2), calls=%async_computation | async-start | bytes 655360 | tf_op jit(solution)/shard_map/all_to_all | solution.py:218
  15.3 30.0 %copy-start.3 = (bf16[256,432]{0,1:T(8,128)(2,1)S(1)}, bf16[256,432]{0,1:T(8,128)(2,1)}, u32[]{:S(2)}) copy-start(bf16[256,432]{0,1:T(8,128)(2,1)} %param.4) | copy-start | bytes 663556
  15.3 30.0 %copy-start.5 = (s32[5]{0:T(128)S(1)}, s32[5]{0:T(128)}, u32[]{:S(2)}) copy-start(s32[5]{0:T(128)} %stack.23.place) | copy-start | bytes 64
  19.1 26.2 %collective-permute-start.3 = (bf16[1712,256]{1,0:T(8,128)(2,1)}, bf16[1712,256]{1,0:T(8,128)(2,1)S(1)}, u32[]{:S(2)}, u32[]{:S(2)}) collective-permute-start(bf16[1712,256]{1,0:T(8,128)(2,1)} %get-tuple-element.27), channel_id=1, source_target_pairs={{0,16},{16,0},{1,17},{17,1},{2,18},{18,2},{3,19},{19,3},{4,20},{20... | collective-permute-start | bytes 2629640 | tf_op jit(solution)/shard_map/ppermute | solution.py:36
  33.8 15.1 %collective-permute-start.2 = (bf16[320,432]{1,0:T(8,128)(2,1)S(1)}, bf16[320,432]{1,0:T(8,128)(2,1)S(1)}, u32[]{:S(2)}, u32[]{:S(2)}) collective-permute-start(bf16[320,432]{1,0:T(8,128)(2,1)S(1)} %bitcast.17), channel_id=1, source_target_pairs={{0,256},{256,512},{512,768},{768,0},{1,257},{257,513},{513,769},{7... | collective-permute-start | bytes 829448 | tf_op jit(solution)/shard_map/ppermute | solution.py:41
  37.2 13.8 %collective-permute-start.1 = (bf16[320,432]{1,0:T(8,128)(2,1)S(1)}, bf16[320,432]{1,0:T(8,128)(2,1)S(1)}, u32[]{:S(2)}, u32[]{:S(2)}) collective-permute-start(bf16[320,432]{1,0:T(8,128)(2,1)S(1)} %bitcast.18), channel_id=1, source_target_pairs={{0,512},{256,768},{512,0},{768,256},{1,513},{257,769},{513,1},{769... | collective-permute-start | bytes 829448 | tf_op jit(solution)/shard_map/ppermute | solution.py:41
  42.1 10.7 %collective-permute-start = (bf16[320,432]{1,0:T(8,128)(2,1)S(1)}, bf16[320,432]{1,0:T(8,128)(2,1)S(1)}, u32[]{:S(2)}, u32[]{:S(2)}) collective-permute-start(bf16[320,432]{1,0:T(8,128)(2,1)S(1)} %bitcast.19), channel_id=1, source_target_pairs={{0,768},{256,0},{512,256},{768,512},{1,769},{257,1},{513,257},{769... | collective-permute-start | bytes 829448 | tf_op jit(solution)/shard_map/ppermute | solution.py:41
  45.4 1.1 copy-start.6
  55.0 5.0 %copy-start = (bf16[2,1280,256]{2,1,0:T(8,128)(2,1)S(1)}, bf16[2,1280,256]{2,1,0:T(8,128)(2,1)}, u32[]{:S(2)}) copy-start(bf16[2,1280,256]{2,1,0:T(8,128)(2,1)} %get-tuple-element.31.both) | copy-start | bytes 3932164
  55.0 22.2 %all-to-all-start.1 = ((bf16[4,4,80,512]{3,2,1,0:T(8,128)(2,1)}), bf16[4,4,80,512]{3,2,1,0:T(8,128)(2,1)S(1)}, u32[]{:S(2)}, u32[]{:S(2)}) async-start(bf16[4,4,80,512]{3,2,1,0:T(8,128)(2,1)} %get-tuple-element.29), calls=%async_computation.1 | async-start | bytes 2621440 | tf_op jit(solution)/shard_map/all_to_all | solution.py:253
  60.0 1.3 copy-start.1
  63.0 13.2 %collective-permute-start.4 = (f32[432,256]{1,0:T(8,128)S(1)}, f32[432,256]{1,0:T(8,128)S(1)}, u32[]{:S(2)}, u32[]{:S(2)}) collective-permute-start(f32[432,256]{1,0:T(8,128)S(1)} %get-tuple-element.33), channel_id=1, source_target_pairs={{0,16},{16,0},{1,17},{17,1},{2,18},{18,2},{3,19},{19,3},{4,20},{20... | collective-permute-start | bytes 1327112 | tf_op jit(solution)/shard_map/ppermute | solution.py:36
  64.9 8.0 %copy-start.7 = (bf16[320,432]{1,0:T(8,128)(2,1)S(1)}, bf16[320,432]{1,0:T(8,128)(2,1)}, u32[]{:S(2)}) copy-start(bf16[320,432]{1,0:T(8,128)(2,1)} %shard_map.78) | copy-start | bytes 829444
  64.9 46.7 %collective-permute-start.9 = (bf16[320,432]{1,0:T(8,128)(2,1)}, bf16[320,432]{1,0:T(8,128)(2,1)S(1)}, u32[]{:S(2)}, u32[]{:S(2)}) collective-permute-start(bf16[320,432]{1,0:T(8,128)(2,1)} %shard_map.76), channel_id=1, source_target_pairs={{0,256},{256,512},{512,768},{768,0},{1,257},{257,513},{513,769},{7... | collective-permute-start | bytes 829448 | tf_op jit(solution)/shard_map/ppermute | solution.py:41
  69.0 42.6 %collective-permute-start.10 = (bf16[320,432]{1,0:T(8,128)(2,1)}, bf16[320,432]{1,0:T(8,128)(2,1)S(1)}, u32[]{:S(2)}, u32[]{:S(2)}) collective-permute-start(bf16[320,432]{1,0:T(8,128)(2,1)} %shard_map.77), channel_id=1, source_target_pairs={{0,512},{256,768},{512,0},{768,256},{1,513},{257,769},{513,1},{769... | collective-permute-start | bytes 829448 | tf_op jit(solution)/shard_map/ppermute | solution.py:41
  72.9 38.7 %collective-permute-start.11 = (bf16[320,432]{1,0:T(8,128)(2,1)S(1)}, bf16[320,432]{1,0:T(8,128)(2,1)S(1)}, u32[]{:S(2)}, u32[]{:S(2)}) collective-permute-start(bf16[320,432]{1,0:T(8,128)(2,1)S(1)} %copy-done.7), channel_id=1, source_target_pairs={{0,768},{256,0},{512,256},{768,512},{1,769},{257,1},{513,257},{769... | collective-permute-start | bytes 829448 | tf_op jit(solution)/shard_map/ppermute | solution.py:41
  76.2 35.5 %copy-start.2 = (bf16[320,432]{1,0:T(8,128)(2,1)S(1)}, bf16[320,432]{1,0:T(8,128)(2,1)}, u32[]{:S(2)}) copy-start(bf16[320,432]{1,0:T(8,128)(2,1)} %get-tuple-element.42) | copy-start | bytes 829444
  77.4 20.7 %collective-permute-start.5 = (bf16[80,512]{1,0:T(8,128)(2,1)S(1)}, bf16[80,512]{1,0:T(8,128)(2,1)S(1)}, u32[]{:S(2)}, u32[]{:S(2)}) collective-permute-start(bf16[80,512]{1,0:T(8,128)(2,1)S(1)} %get-tuple-element.37), channel_id=1, source_target_pairs={{0,4},{4,8},{8,12},{12,0},{16,28},{20,16},{24,20},{28,24},{1,5},{5... | collective-permute-start | bytes 245768 | tf_op jit(solution)/shard_map/ppermute | solution.py:51
  93.1 18.5 %collective-permute-start.7 = (bf16[80,512]{1,0:T(8,128)(2,1)S(1)}, bf16[80,512]{1,0:T(8,128)(2,1)S(1)}, u32[]{:S(2)}, u32[]{:S(2)}) collective-permute-start(bf16[80,512]{1,0:T(8,128)(2,1)S(1)} %get-tuple-element.38), channel_id=1, source_target_pairs={{0,12},{4,0},{8,4},{12,8},{16,20},{20,24},{24,28},{28,16},{1,13},{... | collective-permute-start | bytes 245768 | tf_op jit(solution)/shard_map/ppermute | solution.py:51
  98.1 16.1 %collective-permute-start.6 = (bf16[80,512]{1,0:T(8,128)(2,1)S(1)}, bf16[80,512]{1,0:T(8,128)(2,1)S(1)}, u32[]{:S(2)}, u32[]{:S(2)}) collective-permute-start(bf16[80,512]{1,0:T(8,128)(2,1)S(1)} %shard_map.73.after), channel_id=1, source_target_pairs={{0,4},{4,8},{8,12},{12,0},{16,28},{20,16},{24,20},{28,24},{1,5},{5... | collective-permute-start | bytes 245768 | tf_op jit(solution)/shard_map/ppermute | solution.py:51
  112.4 1.9 %copy-start.4 = (bf16[4,40,432]{2,1,0:T(8,128)(2,1)}, bf16[4,40,432]{2,1,0:T(8,128)(2,1)S(1)}, u32[]{:S(2)}) copy-start(bf16[4,40,432]{2,1,0:T(8,128)(2,1)S(1)} %get-tuple-element.48.value) | copy-start | bytes 414724
  114.2 17.8 %collective-permute-start.12 = (bf16[4,40,432]{2,1,0:T(8,128)(2,1)}, bf16[4,40,432]{2,1,0:T(8,128)(2,1)S(1)}, u32[]{:S(2)}, u32[]{:S(2)}) collective-permute-start(bf16[4,40,432]{2,1,0:T(8,128)(2,1)} %shard_map.80), channel_id=1, source_target_pairs={{0,32},{32,0},{1,33},{33,1},{2,34},{34,2},{3,35},{35,3},{4,36},{36... | collective-permute-start | bytes 414728 | tf_op jit(solution)/shard_map/ppermute | solution.py:36
  132.8 17.2 %all-to-all-start.2 = ((bf16[4,40,432]{2,1,0:T(8,128)(2,1)}), bf16[4,40,432]{2,1,0:T(8,128)(2,1)S(1)}, u32[]{:S(2)}, u32[]{:S(2)}) async-start(bf16[4,40,432]{2,1,0:T(8,128)(2,1)} %shard_map.81), calls=%async_computation.2 | async-start | bytes 327680 | tf_op jit(solution)/shard_map/all_to_all | solution.py:291
  138.4 3.1 %collective-permute-start.8 = (bf16[80,256]{1,0:T(8,128)(2,1)S(1)}, bf16[80,256]{1,0:T(8,128)(2,1)S(1)}, u32[]{:S(2)}, u32[]{:S(2)}) collective-permute-start(bf16[80,256]{1,0:T(8,128)(2,1)S(1)} %get-tuple-element.40), channel_id=1, source_target_pairs={{0,16},{16,0},{1,17},{17,1},{2,18},{18,2},{3,19},{19,3},{4,20},{20... | collective-permute-start | bytes 122888 | tf_op jit(solution)/shard_map/ppermute | solution.py:36

commit v13 on v11

--- a/solution.py
+++ b/solution.py
@@ -249,6 +249,7 @@
         [SMEM, VMEM, VMEM],
         (place, weight, both),
         flops=work,
+        limit=56,
     )
     grad_pre, token = call(
         hidden_grad, [((hid, tokens), BF16), ((8, 128), F32)], [VMEM] * 3, (pre, own, swap(other, "c", 1))

time: 150 us -> 151 us (level)
  Pallas kernels: 14.1 us -> 16.2 us
    pallas_call x11, Pallas kernels: 14.1 us -> 16.2 us  [call(): pl.pallas_call(body, out_shape=[s if isinstance(s, pl.MemoryRef) else jax...]
  transfers between devices with their start and end apart: 15 -> 15, of which waited for: 7 -> 7; matrix products, arithmetic and copies ran while one was open for 0% -> 0% of each run, Pallas kernels for 8% -> 9%
where the time goes in v13:
time: 151 us; the launch traced here: 150 us
  starting transfers between devices  94.6 us (63%)
  waiting for transfers between devices  35.1 us (23%)
  Pallas kernels  16.2 us (11%)
  local copies, waits for them, and re-layouts  3.25 us (2%)
    ppermute x3, starting transfers between devices, shift_both(): return lax.ppermute(value, ('c', 'zh'), pairs)  31.3 us
    ppermute x6, starting transfers between devices, shift(): lax.ppermute(value, axis, [(i, (i + distance) % size) for i in range(size)])  22.8 us
    all_to_all x1, starting transfers between devices, local(): lax.all_to_all(hold(term, u), 'zl', 0, 0)  17.3 us
    pallas_call x11, Pallas kernels, call(): pl.pallas_call(body, out_shape=[s if isinstance(s, pl.MemoryRef) else jax...  16.2 us
    all_to_all x1, waiting for transfers between devices, local(): lax.all_to_all(hold(term, u), 'zl', 0, 0)  12.7 us
    all_to_all x1, waiting for transfers between devices, local(): lax.all_to_all(jnp.broadcast_to(weight_out[None], (n_zl, block, hid)), 'z...  12.7 us
    all_to_all x1, starting transfers between devices, local(): lax.all_to_all(jnp.broadcast_to(weight_out[None], (n_zl, block, hid)), 'z...  12.5 us
    ppermute x3, starting transfers between devices, swap(): return lax.ppermute(value, axis, [(i, i ^ distance) for i in range(size)])  5.87 us
  transfers between devices with their start and end apart: 15, of which 7 were waited for; matrix products, arithmetic and copies ran while one was open for 0% of the time, Pallas kernels for 9%

profile of v13, /device:TPU:2, one launch (start us, length us, event | category | flops | bytes accessed | tf_op | source)
XLA Modules:
  0.0 150.0 jit_solution(4119511985907207490)
XLA Ops:
  0.6 1.6 %broadcast_in_dim.2 = bf16[8,40,432]{2,1,0:T(8,128)(2,1)} broadcast(bf16[40,432]{1,0:T(8,128)(2,1)} %param.5), dimensions={1,2} | broadcast | bytes 311040 | tf_op jit(solution)/shard_map/broadcast_in_dim | solution.py:207
  2.2 12.5 %all-to-all-start = ((bf16[8,40,432]{2,1,0:T(8,128)(2,1)}), bf16[8,40,432]{2,1,0:T(8,128)(2,1)S(1)}, u32[]{:S(2)}, u32[]{:S(2)}) async-start(bf16[8,40,432]{2,1,0:T(8,128)(2,1)} %broadcast_in_dim.2), calls=%async_computation | async-start | bytes 655360 | tf_op jit(solution)/shard_map/all_to_all | solution.py:207
  14.7 0.6 stack.23.place
  15.3 3.8 %shard_map.67 = (bf16[1712,256]{1,0:T(8,128)(2,1)}, bf16[1280,256]{1,0:T(8,128)(2,1)}) custom-call(s32[5]{0:T(128)} %stack.23.place, s32[320,1]{1,0:T(8,128)} %constant.25.clone.base, bf16[256,2560]{1,0:T(8,128)(2,1)} %cot.1, bf16[432,256]{1,0:T(8,128)(2,1)} %bitcast.25), custom_call_target="tpu_custom_call" | custom-call | flops 838860800 | bytes 2299481 | tf_op jit(solution)/shard_map/pallas_call | solution.py:61
  19.2 1.9 %collective-permute-start.3 = (bf16[1712,256]{1,0:T(8,128)(2,1)}, bf16[1712,256]{1,0:T(8,128)(2,1)S(1)}, u32[]{:S(2)}, u32[]{:S(2)}) collective-permute-start(bf16[1712,256]{1,0:T(8,128)(2,1)} %get-tuple-element.25), channel_id=1, source_target_pairs={{0,16},{16,0},{1,17},{17,1},{2,18},{18,2},{3,19},{19,3},{4,20},{20... | collective-permute-start | bytes 2629640 | tf_op jit(solution)/shard_map/ppermute | solution.py:36
  21.1 12.7 %all-to-all-done = bf16[8,40,432]{2,1,0:T(8,128)(2,1)S(1)} async-done(((bf16[8,40,432]{2,1,0:T(8,128)(2,1)}), bf16[8,40,432]{2,1,0:T(8,128)(2,1)S(1)}, u32[]{:S(2)}, u32[]{:S(2)}) %all-to-all-start) | async-done | bytes 276512 | tf_op jit(solution)/shard_map/all_to_all | solution.py:207
  33.8 3.5 %collective-permute-start.2 = (bf16[320,432]{1,0:T(8,128)(2,1)S(1)}, bf16[320,432]{1,0:T(8,128)(2,1)S(1)}, u32[]{:S(2)}, u32[]{:S(2)}) collective-permute-start(bf16[320,432]{1,0:T(8,128)(2,1)S(1)} %bitcast.21), channel_id=1, source_target_pairs={{0,256},{256,512},{512,768},{768,0},{1,257},{257,513},{513,769},{7... | collective-permute-start | bytes 829448 | tf_op jit(solution)/shard_map/ppermute | solution.py:41
  37.3 4.8 %collective-permute-start.1 = (bf16[320,432]{1,0:T(8,128)(2,1)S(1)}, bf16[320,432]{1,0:T(8,128)(2,1)S(1)}, u32[]{:S(2)}, u32[]{:S(2)}) collective-permute-start(bf16[320,432]{1,0:T(8,128)(2,1)S(1)} %bitcast.22), channel_id=1, source_target_pairs={{0,512},{256,768},{512,0},{768,256},{1,513},{257,769},{513,1},{769... | collective-permute-start | bytes 829448 | tf_op jit(solution)/shard_map/ppermute | solution.py:41
  42.1 3.3 %collective-permute-start = (bf16[320,432]{1,0:T(8,128)(2,1)S(1)}, bf16[320,432]{1,0:T(8,128)(2,1)S(1)}, u32[]{:S(2)}, u32[]{:S(2)}) collective-permute-start(bf16[320,432]{1,0:T(8,128)(2,1)S(1)} %bitcast.23), channel_id=1, source_target_pairs={{0,768},{256,0},{512,256},{768,512},{1,769},{257,1},{513,257},{769... | collective-permute-start | bytes 829448 | tf_op jit(solution)/shard_map/ppermute | solution.py:41
  45.3 0.0 collective-permute-done.3.got
  45.3 0.0 copy-done.2
  45.4 0.0 copy-done.3
  45.4 0.0 copy-start.5
  45.4 1.1 copy-done.5
  46.5 2.4 %shard_map.68 = (bf16[432,512]{1,0:T(8,128)(2,1)S(1)}, bf16[320,432]{1,0:T(8,128)(2,1)}, bf16[320,432]{1,0:T(8,128)(2,1)}, bf16[320,432]{1,0:T(8,128)(2,1)}, bf1...) custom-call(s32[5]{0:T(128)S(1)} %copy-done.3, bf16[432,256]{1,0:T(8,128)(2,1)S(1)} %bitcast.26, ...), custom_call_target="tpu_custom_call" | custom-call | flops 566231040 | bytes 2629657 | tf_op jit(solution)/shard_map/pallas_call | solution.py:61
  48.8 0.0 collective-permute-done.2.w3
  48.8 2.2 %collective-permute-done.1.w2 = bf16[320,432]{1,0:T(8,128)(2,1)S(1)} collective-permute-done((bf16[320,432]{1,0:T(8,128)(2,1)S(1)}, bf16[320,432]{1,0:T(8,128)(2,1)S(1)}, u32[]{:S(2)}, u32[]{:S(2)}) %collective-permute-start.1) | collective-permute-done | bytes 276512 | tf_op jit(solution)/shard_map/ppermute | solution.py:41
  51.0 1.7 %collective-permute-done.w1 = bf16[320,432]{1,0:T(8,128)(2,1)S(1)} collective-permute-done((bf16[320,432]{1,0:T(8,128)(2,1)S(1)}, bf16[320,432]{1,0:T(8,128)(2,1)S(1)}, u32[]{:S(2)}, u32[]{:S(2)}) %collective-permute-start) | collective-permute-done | bytes 276512 | tf_op jit(solution)/shard_map/ppermute | solution.py:41
  52.8 2.2 %shard_map.69 = (bf16[4,4,80,512]{3,2,1,0:T(8,128)(2,1)}, bf16[4,320,432]{2,1,0:T(8,128)(2,1)}, f32[8,128]{1,0:T(8,128)S(1)}) custom-call(s32[5]{0:T(128)S(1)} %copy-done.3, bf16[320,432]{1,0:T(8,128)(2,1)S(1)} %bitcast.24, bf16[320,432]{1,0:T(8,128)(2,1)S(1)} %collective-permute-done.w1, bf16[320,432]{1,0:T(8,128)(2,1)S(1)} %collective-permute-done.1.w2, ...), custom_call_target="tpu_custom_call" | custom-call | flops 566231040 | bytes 2322457 | tf_op jit(solution)/shard_map/pallas_call | solution.py:61
  55.0 4.8 %all-to-all-start.1 = ((bf16[4,4,80,512]{3,2,1,0:T(8,128)(2,1)}), bf16[4,4,80,512]{3,2,1,0:T(8,128)(2,1)S(1)}, u32[]{:S(2)}, u32[]{:S(2)}) async-start(bf16[4,4,80,512]{3,2,1,0:T(8,128)(2,1)} %get-tuple-element.27), calls=%async_computation.1 | async-start | bytes 2621440 | tf_op jit(solution)/shard_map/all_to_all | solution.py:242
  59.8 3.8 %shard_map.70 = (f32[432,256]{1,0:T(8,128)}, f32[432,256]{1,0:T(8,128)}) custom-call(s32[5]{0:T(128)} %stack.23.place, bf16[4,320,432]{2,1,0:T(8,128)(2,1)} %get-tuple-element.28.weight, bf16[2,1280,256]{2,1,0:T(8,128)(2,1)} %get-tuple-element.29.both), custom_call_target="tpu_custom_call" | custom-call | flops 566231040 | bytes 3624985 | tf_op jit(solution)/shard_map/pallas_call | solution.py:61
  63.6 2.0 %collective-permute-start.4 = (f32[432,256]{1,0:T(8,128)}, f32[432,256]{1,0:T(8,128)S(1)}, u32[]{:S(2)}, u32[]{:S(2)}) collective-permute-start(f32[432,256]{1,0:T(8,128)} %get-tuple-element.31), channel_id=1, source_target_pairs={{0,16},{16,0},{1,17},{17,1},{2,18},{18,2},{3,19},{19,3},{4,20},{20... | collective-permute-start | bytes 1327112 | tf_op jit(solution)/shard_map/ppermute | solution.py:36
  65.6 0.0 copy-start.6
  65.7 4.1 %collective-permute-start.9 = (bf16[320,432]{1,0:T(8,128)(2,1)}, bf16[320,432]{1,0:T(8,128)(2,1)S(1)}, u32[]{:S(2)}, u32[]{:S(2)}) collective-permute-start(bf16[320,432]{1,0:T(8,128)(2,1)} %shard_map.76), channel_id=1, source_target_pairs={{0,256},{256,512},{512,768},{768,0},{1,257},{257,513},{513,769},{7... | collective-permute-start | bytes 829448 | tf_op jit(solution)/shard_map/ppermute | solution.py:41
  69.8 3.9 %collective-permute-start.10 = (bf16[320,432]{1,0:T(8,128)(2,1)}, bf16[320,432]{1,0:T(8,128)(2,1)S(1)}, u32[]{:S(2)}, u32[]{:S(2)}) collective-permute-start(bf16[320,432]{1,0:T(8,128)(2,1)} %shard_map.77), channel_id=1, source_target_pairs={{0,512},{256,768},{512,0},{768,256},{1,513},{257,769},{513,1},{769... | collective-permute-start | bytes 829448 | tf_op jit(solution)/shard_map/ppermute | solution.py:41
  73.7 0.0 copy-done.6
  73.7 3.2 %collective-permute-start.11 = (bf16[320,432]{1,0:T(8,128)(2,1)S(1)}, bf16[320,432]{1,0:T(8,128)(2,1)S(1)}, u32[]{:S(2)}, u32[]{:S(2)}) collective-permute-start(bf16[320,432]{1,0:T(8,128)(2,1)S(1)} %copy-done.6), channel_id=1, source_target_pairs={{0,768},{256,0},{512,256},{768,512},{1,769},{257,1},{513,257},{769... | collective-permute-start | bytes 829448 | tf_op jit(solution)/shard_map/ppermute | solution.py:41
  76.9 0.0 collective-permute-done.4.other
  76.9 0.0 copy-done
  77.0 1.0 shard_map.71
  78.0 0.0 all-to-all-done.1.parts
  78.0 0.2 shard_map.72
  78.1 15.7 %collective-permute-start.5 = (bf16[80,512]{1,0:T(8,128)(2,1)S(1)}, bf16[80,512]{1,0:T(8,128)(2,1)S(1)}, u32[]{:S(2)}, u32[]{:S(2)}) collective-permute-start(bf16[80,512]{1,0:T(8,128)(2,1)S(1)} %get-tuple-element.35), channel_id=1, source_target_pairs={{0,4},{4,8},{8,12},{12,0},{16,28},{20,16},{24,20},{28,24},{1,5},{5... | collective-permute-start | bytes 245768 | tf_op jit(solution)/shard_map/ppermute | solution.py:51
  93.9 1.9 %collective-permute-start.7 = (bf16[80,512]{1,0:T(8,128)(2,1)S(1)}, bf16[80,512]{1,0:T(8,128)(2,1)S(1)}, u32[]{:S(2)}, u32[]{:S(2)}) collective-permute-start(bf16[80,512]{1,0:T(8,128)(2,1)S(1)} %get-tuple-element.36), channel_id=1, source_target_pairs={{0,12},{4,0},{8,4},{12,8},{16,20},{20,24},{24,28},{28,16},{1,13},{... | collective-permute-start | bytes 245768 | tf_op jit(solution)/shard_map/ppermute | solution.py:51
  95.8 2.8 %collective-permute-done.5.got = bf16[80,512]{1,0:T(8,128)(2,1)S(1)} collective-permute-done((bf16[80,512]{1,0:T(8,128)(2,1)S(1)}, bf16[80,512]{1,0:T(8,128)(2,1)S(1)}, u32[]{:S(2)}, u32[]{:S(2)}) %collective-permute-start.5) | collective-permute-done | bytes 81952 | tf_op jit(solution)/shard_map/ppermute | solution.py:51
  98.6 13.7 %collective-permute-start.6 = (bf16[80,512]{1,0:T(8,128)(2,1)S(1)}, bf16[80,512]{1,0:T(8,128)(2,1)S(1)}, u32[]{:S(2)}, u32[]{:S(2)}) collective-permute-start(bf16[80,512]{1,0:T(8,128)(2,1)S(1)} %shard_map.73.after), channel_id=1, source_target_pairs={{0,4},{4,8},{8,12},{12,0},{16,28},{20,16},{24,20},{28,24},{1,5},{5... | collective-permute-start | bytes 245768 | tf_op jit(solution)/shard_map/ppermute | solution.py:51
  112.3 0.0 collective-permute-done.9
  112.3 0.0 collective-permute-done.10
  112.3 0.0 collective-permute-done.11
  112.3 0.0 collective-permute-done.7.v.then
  112.4 0.9 shard_map.79.value
  113.3 1.7 %collective-permute-done.6.u.after = bf16[80,512]{1,0:T(8,128)(2,1)S(1)} collective-permute-done((bf16[80,512]{1,0:T(8,128)(2,1)S(1)}, bf16[80,512]{1,0:T(8,128)(2,1)S(1)}, u32[]{:S(2)}, u32[]{:S(2)}) %collective-permute-start.6) | collective-permute-done | bytes 81952 | tf_op jit(solution)/shard_map/ppermute | solution.py:51
  115.0 17.3 %all-to-all-start.2 = ((bf16[8,40,432]{2,1,0:T(8,128)(2,1)}), bf16[8,40,432]{2,1,0:T(8,128)(2,1)S(1)}, u32[]{:S(2)}, u32[]{:S(2)}) async-start(bf16[8,40,432]{2,1,0:T(8,128)(2,1)} %shard_map.80), calls=%async_computation.2 | async-start | bytes 655360 | tf_op jit(solution)/shard_map/all_to_all | solution.py:274
  132.3 1.9 %collective-permute-start.8 = (bf16[80,256]{1,0:T(8,128)(2,1)S(1)}, bf16[80,256]{1,0:T(8,128)(2,1)S(1)}, u32[]{:S(2)}, u32[]{:S(2)}) collective-permute-start(bf16[80,256]{1,0:T(8,128)(2,1)S(1)} %get-tuple-element.38), channel_id=1, source_target_pairs={{0,16},{16,0},{1,17},{17,1},{2,18},{18,2},{3,19},{19,3},{4,20},{20... | collective-permute-start | bytes 122888 | tf_op jit(solution)/shard_map/ppermute | solution.py:36
  134.2 1.2 collective-permute-done.8
  135.4 1.2 shard_map.75
  136.6 12.7 %all-to-all-done.2.parts = bf16[8,40,432]{2,1,0:T(8,128)(2,1)S(1)} async-done(((bf16[8,40,432]{2,1,0:T(8,128)(2,1)}), bf16[8,40,432]{2,1,0:T(8,128)(2,1)S(1)}, u32[]{:S(2)}, u32[]{:S(2)}) %all-to-all-start.2) | async-done | bytes 276512 | tf_op jit(solution)/shard_map/all_to_all | solution.py:274
  149.3 0.7 shard_map.81
  (13 shorter events, 0.1 us)
Async XLA Ops:
  2.2 31.6 %all-to-all-start = ((bf16[8,40,432]{2,1,0:T(8,128)(2,1)}), bf16[8,40,432]{2,1,0:T(8,128)(2,1)S(1)}, u32[]{:S(2)}, u32[]{:S(2)}) async-start(bf16[8,40,432]{2,1,0:T(8,128)(2,1)} %broadcast_in_dim.2), calls=%async_computation | async-start | bytes 655360 | tf_op jit(solution)/shard_map/all_to_all | solution.py:207
  15.3 30.0 %copy-start.2 = (bf16[256,432]{0,1:T(8,128)(2,1)S(1)}, bf16[256,432]{0,1:T(8,128)(2,1)}, u32[]{:S(2)}) copy-start(bf16[256,432]{0,1:T(8,128)(2,1)} %param.4) | copy-start | bytes 663556
  15.3 30.0 %copy-start.3 = (s32[5]{0:T(128)S(1)}, s32[5]{0:T(128)}, u32[]{:S(2)}) copy-start(s32[5]{0:T(128)} %stack.23.place) | copy-start | bytes 64
  19.2 26.2 %collective-permute-start.3 = (bf16[1712,256]{1,0:T(8,128)(2,1)}, bf16[1712,256]{1,0:T(8,128)(2,1)S(1)}, u32[]{:S(2)}, u32[]{:S(2)}) collective-permute-start(bf16[1712,256]{1,0:T(8,128)(2,1)} %get-tuple-element.25), channel_id=1, source_target_pairs={{0,16},{16,0},{1,17},{17,1},{2,18},{18,2},{3,19},{19,3},{4,20},{20... | collective-permute-start | bytes 2629640 | tf_op jit(solution)/shard_map/ppermute | solution.py:36
  33.8 15.1 %collective-permute-start.2 = (bf16[320,432]{1,0:T(8,128)(2,1)S(1)}, bf16[320,432]{1,0:T(8,128)(2,1)S(1)}, u32[]{:S(2)}, u32[]{:S(2)}) collective-permute-start(bf16[320,432]{1,0:T(8,128)(2,1)S(1)} %bitcast.21), channel_id=1, source_target_pairs={{0,256},{256,512},{512,768},{768,0},{1,257},{257,513},{513,769},{7... | collective-permute-start | bytes 829448 | tf_op jit(solution)/shard_map/ppermute | solution.py:41
  37.3 13.8 %collective-permute-start.1 = (bf16[320,432]{1,0:T(8,128)(2,1)S(1)}, bf16[320,432]{1,0:T(8,128)(2,1)S(1)}, u32[]{:S(2)}, u32[]{:S(2)}) collective-permute-start(bf16[320,432]{1,0:T(8,128)(2,1)S(1)} %bitcast.22), channel_id=1, source_target_pairs={{0,512},{256,768},{512,0},{768,256},{1,513},{257,769},{513,1},{769... | collective-permute-start | bytes 829448 | tf_op jit(solution)/shard_map/ppermute | solution.py:41
  42.1 10.7 %collective-permute-start = (bf16[320,432]{1,0:T(8,128)(2,1)S(1)}, bf16[320,432]{1,0:T(8,128)(2,1)S(1)}, u32[]{:S(2)}, u32[]{:S(2)}) collective-permute-start(bf16[320,432]{1,0:T(8,128)(2,1)S(1)} %bitcast.23), channel_id=1, source_target_pairs={{0,768},{256,0},{512,256},{768,512},{1,769},{257,1},{513,257},{769... | collective-permute-start | bytes 829448 | tf_op jit(solution)/shard_map/ppermute | solution.py:41
  45.4 1.1 copy-start.5
  55.0 23.0 %all-to-all-start.1 = ((bf16[4,4,80,512]{3,2,1,0:T(8,128)(2,1)}), bf16[4,4,80,512]{3,2,1,0:T(8,128)(2,1)S(1)}, u32[]{:S(2)}, u32[]{:S(2)}) async-start(bf16[4,4,80,512]{3,2,1,0:T(8,128)(2,1)} %get-tuple-element.27), calls=%async_computation.1 | async-start | bytes 2621440 | tf_op jit(solution)/shard_map/all_to_all | solution.py:242
  63.6 13.4 %copy-start = (f32[432,256]{1,0:T(8,128)S(1)}, f32[432,256]{1,0:T(8,128)}, u32[]{:S(2)}) copy-start(f32[432,256]{1,0:T(8,128)} %get-tuple-element.30.own) | copy-start | bytes 1327108
  63.6 13.3 %collective-permute-start.4 = (f32[432,256]{1,0:T(8,128)}, f32[432,256]{1,0:T(8,128)S(1)}, u32[]{:S(2)}, u32[]{:S(2)}) collective-permute-start(f32[432,256]{1,0:T(8,128)} %get-tuple-element.31), channel_id=1, source_target_pairs={{0,16},{16,0},{1,17},{17,1},{2,18},{18,2},{3,19},{19,3},{4,20},{20... | collective-permute-start | bytes 1327112 | tf_op jit(solution)/shard_map/ppermute | solution.py:36
  65.6 8.0 %copy-start.6 = (bf16[320,432]{1,0:T(8,128)(2,1)S(1)}, bf16[320,432]{1,0:T(8,128)(2,1)}, u32[]{:S(2)}) copy-start(bf16[320,432]{1,0:T(8,128)(2,1)} %shard_map.78) | copy-start | bytes 829444
  65.7 46.6 %collective-permute-start.9 = (bf16[320,432]{1,0:T(8,128)(2,1)}, bf16[320,432]{1,0:T(8,128)(2,1)S(1)}, u32[]{:S(2)}, u32[]{:S(2)}) collective-permute-start(bf16[320,432]{1,0:T(8,128)(2,1)} %shard_map.76), channel_id=1, source_target_pairs={{0,256},{256,512},{512,768},{768,0},{1,257},{257,513},{513,769},{7... | collective-permute-start | bytes 829448 | tf_op jit(solution)/shard_map/ppermute | solution.py:41
  69.8 42.5 %collective-permute-start.10 = (bf16[320,432]{1,0:T(8,128)(2,1)}, bf16[320,432]{1,0:T(8,128)(2,1)S(1)}, u32[]{:S(2)}, u32[]{:S(2)}) collective-permute-start(bf16[320,432]{1,0:T(8,128)(2,1)} %shard_map.77), channel_id=1, source_target_pairs={{0,512},{256,768},{512,0},{768,256},{1,513},{257,769},{513,1},{769... | collective-permute-start | bytes 829448 | tf_op jit(solution)/shard_map/ppermute | solution.py:41
  73.7 38.7 %collective-permute-start.11 = (bf16[320,432]{1,0:T(8,128)(2,1)S(1)}, bf16[320,432]{1,0:T(8,128)(2,1)S(1)}, u32[]{:S(2)}, u32[]{:S(2)}) collective-permute-start(bf16[320,432]{1,0:T(8,128)(2,1)S(1)} %copy-done.6), channel_id=1, source_target_pairs={{0,768},{256,0},{512,256},{768,512},{1,769},{257,1},{513,257},{769... | collective-permute-start | bytes 829448 | tf_op jit(solution)/shard_map/ppermute | solution.py:41
  76.9 35.4 %copy-start.1 = (bf16[320,432]{1,0:T(8,128)(2,1)S(1)}, bf16[320,432]{1,0:T(8,128)(2,1)}, u32[]{:S(2)}) copy-start(bf16[320,432]{1,0:T(8,128)(2,1)} %get-tuple-element.40) | copy-start | bytes 829444
  78.1 20.5 %collective-permute-start.5 = (bf16[80,512]{1,0:T(8,128)(2,1)S(1)}, bf16[80,512]{1,0:T(8,128)(2,1)S(1)}, u32[]{:S(2)}, u32[]{:S(2)}) collective-permute-start(bf16[80,512]{1,0:T(8,128)(2,1)S(1)} %get-tuple-element.35), channel_id=1, source_target_pairs={{0,4},{4,8},{8,12},{12,0},{16,28},{20,16},{24,20},{28,24},{1,5},{5... | collective-permute-start | bytes 245768 | tf_op jit(solution)/shard_map/ppermute | solution.py:51
  93.9 18.5 %collective-permute-start.7 = (bf16[80,512]{1,0:T(8,128)(2,1)S(1)}, bf16[80,512]{1,0:T(8,128)(2,1)S(1)}, u32[]{:S(2)}, u32[]{:S(2)}) collective-permute-start(bf16[80,512]{1,0:T(8,128)(2,1)S(1)} %get-tuple-element.36), channel_id=1, source_target_pairs={{0,12},{4,0},{8,4},{12,8},{16,20},{20,24},{24,28},{28,16},{1,13},{... | collective-permute-start | bytes 245768 | tf_op jit(solution)/shard_map/ppermute | solution.py:51
  98.6 16.4 %collective-permute-start.6 = (bf16[80,512]{1,0:T(8,128)(2,1)S(1)}, bf16[80,512]{1,0:T(8,128)(2,1)S(1)}, u32[]{:S(2)}, u32[]{:S(2)}) collective-permute-start(bf16[80,512]{1,0:T(8,128)(2,1)S(1)} %shard_map.73.after), channel_id=1, source_target_pairs={{0,4},{4,8},{8,12},{12,0},{16,28},{20,16},{24,20},{28,24},{1,5},{5... | collective-permute-start | bytes 245768 | tf_op jit(solution)/shard_map/ppermute | solution.py:51
  112.4 23.1 %copy-start.4 = (s32[5]{0:T(128)S(1)}, s32[5]{0:T(128)}, u32[]{:S(2)}) copy-start(s32[5]{0:T(128)} %stack.23.place) | copy-start | bytes 64
  115.0 34.3 %all-to-all-start.2 = ((bf16[8,40,432]{2,1,0:T(8,128)(2,1)}), bf16[8,40,432]{2,1,0:T(8,128)(2,1)S(1)}, u32[]{:S(2)}, u32[]{:S(2)}) async-start(bf16[8,40,432]{2,1,0:T(8,128)(2,1)} %shard_map.80), calls=%async_computation.2 | async-start | bytes 655360 | tf_op jit(solution)/shard_map/all_to_all | solution.py:274
  132.3 3.1 %collective-permute-start.8 = (bf16[80,256]{1,0:T(8,128)(2,1)S(1)}, bf16[80,256]{1,0:T(8,128)(2,1)S(1)}, u32[]{:S(2)}, u32[]{:S(2)}) collective-permute-start(bf16[80,256]{1,0:T(8,128)(2,1)S(1)} %get-tuple-element.38), channel_id=1, source_target_pairs={{0,16},{16,0},{1,17},{17,1},{2,18},{18,2},{3,19},{19,3},{4,20},{20... | collective-permute-start | bytes 122888 | tf_op jit(solution)/shard_map/ppermute | solution.py:36
